TPU v7x, 32 devices: a whole 2x2x4 slice. The times are simulated.
32 devices in a mesh: groups: 2 (over x), wide: 8 (over z, y), ffn: 2 (over core).
Axes of the slice: x: 2, y: 2, z: 4, core: 2. Of those that a mesh axis runs over, the one named last changes fastest.
Arguments:
- tokens: bfloat16 [64, 8192], P('groups', 'wide'), parts along dimension 0, may hold values from -25 to 25
- gate_weight: bfloat16 [8192, 26624], P('wide', 'ffn'), may hold values from -0.09375 to 0.09375
- up_weight: bfloat16 [8192, 26624], P('wide', 'ffn'), may hold values from -0.09375 to 0.09375
- down_weight: bfloat16 [26624, 8192], P('ffn', 'wide'), may hold values from -0.0390625 to 0.0390625
Outputs:
- state: float32 [64, 8192], P('groups', 'wide'), parts along dimension 0
There are 2 independent parts, one for each index of `groups`. A program takes and returns all parts, laid end to end along the dimension named above; an argument that names none is the same for every part. Nothing has to cross between parts.
All inputs are finite; a program needn't handle non-finite values.
Results may differ from a plain program's by a relative error of at most 0.0053.
Values may be sent and summed in bfloat16 or wider, within the bound.
No kernel may reach another device: no remote copies, remote signals or barrier semaphores. Data moves between devices by JAX's collectives and lax.ppermute only.
A program may use at most 192 MiB of HBM per device.

v0:
```python
import jax
import jax.numpy as jnp
from jax import lax
from jax.sharding import PartitionSpec as P

D = 8192
STEPS = 2


def per_device(tokens, gate_weight, up_weight, down_weight):
    state = tokens.astype(jnp.float32)
    rows = tokens.shape[0]
    for step in range(STEPS):
        sumsq = lax.psum(jnp.sum(state * state, axis=1), "wide")
        normed = (state / jnp.sqrt(sumsq[:, None] / D + 1e-05)).astype(jnp.bfloat16)
        gate_part = lax.dot_general(
            gate_weight, normed, (((0,), (1,)), ((), ())), preferred_element_type=jnp.float32
        )
        up_part = lax.dot_general(
            up_weight, normed, (((0,), (1,)), ((), ())), preferred_element_type=jnp.float32
        )
        both = lax.psum_scatter(
            jnp.concatenate([gate_part, up_part], axis=1), "wide", scatter_dimension=0, tiled=True
        )
        hidden = (jax.nn.silu(both[:, :rows]) * both[:, rows:]).astype(jnp.bfloat16)
        partial_value = lax.dot_general(
            lax.all_gather(hidden, "wide", axis=0, tiled=True),
            down_weight,
            (((0,), (0,)), ((), ())),
            preferred_element_type=jnp.float32,
        )
        state = state + lax.psum(partial_value, "ffn")
    return state


def solution(mesh):
    return jax.shard_map(
        per_device,
        mesh=mesh,
        in_specs=(P("groups", "wide"), P("wide", "ffn"), P("wide", "ffn"), P("ffn", "wide")),
        out_specs=P("groups", "wide"),
        check_vma=False,
    )
```

profile of v0, /device:TPU:0, one launch (start us, length us, event | category | flops | bytes accessed | tf_op | source)
XLA Modules:
  0.0 386.2 jit_solution(6353145717499560396)
XLA Ops:
  6.5 0.0 copy-start
  6.5 0.0 reduce-scatter.3.cloned.1.call-start
  6.5 1.0 fusion.2
  7.6 23.1 %psum.28 = f32[32]{0:T(128)S(1)} all-reduce(f32[32]{0:T(128)S(1)} %fusion.2), channel_id=1, replica_groups=mesh['groups'=2,'wide'=8,'ffn'=2] {'wide'}, use_global_device_ids=true, to_apply=%region_1.0 | all-reduce | flops 32 | bytes 256 | tf_op jit(solution)/shard_map/psum | solution.py:14
  30.7 11.2 %convolution_bitcast_fusion.2 = f32[13312,32]{0,1:T(8,128)S(1)} fusion(bf16[1024,13312]{1,0:T(8,128)(2,1)} %param.6, bf16[32,1024]{1,0:T(8,128)(2,1)} %param.4, f32[32]{0:T(128)S(1)} %add_sqrt_fusion.1), kind=kOutput, calls=%fused_computation.2 | convolution fusion | flops 872513536 | bytes 29032576 | tf_op jit(solution)/shard_map/dot_general | solution.py:19
  41.9 0.0 copy-done
  42.0 11.2 %convolution_bitcast_fusion.3 = f32[13312,32]{0,1:T(8,128)S(1)} fusion(bf16[1024,13312]{1,0:T(8,128)(2,1)} %param.5, bf16[32,1024]{1,0:T(8,128)(2,1)S(1)} %copy-done, f32[32]{0:T(128)S(1)} %add_sqrt_fusion.1), kind=kOutput, calls=%fused_computation.3 | convolution fusion | flops 872513536 | bytes 29032576 | tf_op jit(solution)/shard_map/dot_general | solution.py:16
  53.2 2.0 pad_maximum_fusion
  55.2 0.0 reduce-scatter.3.cloned.1.call-update
  55.2 0.0 all-reduce.3.cloned.1.call-start
  55.2 75.2 %reduce-scatter.3.cloned.1.call-done = f32[1664,64]{0,1:T(8,128)} async-done(((f32[13312,64]{0,1:T(8,128)}), f32[1664,64]{0,1:T(8,128)}) %reduce-scatter.3.cloned.1.call-update) | async-done | bytes 426000 | tf_op jit(solution)/shard_map/reduce_scatter | solution.py:22
  130.4 1.1 fusion.1
  131.5 32.3 %all_gather.6 = bf16[13312,32]{0,1:T(8,128)(2,1)S(1)} all-gather(bf16[1664,32]{0,1:T(8,128)(2,1)S(1)} %fusion.1), channel_id=1, replica_groups=mesh['groups'=2,'wide'=8,'ffn'=2] {'wide'}, dimensions={0}, use_global_device_ids=true | all-gather | bytes 958464 | tf_op jit(solution)/shard_map/all_gather | solution.py:27
  163.8 11.9 %fusion.7 = f32[32,1024]{1,0:T(8,128)} fusion(bf16[13312,32]{0,1:T(8,128)(2,1)S(1)} %all_gather.6, bf16[13312,1024]{1,0:T(8,128)(2,1)} %param.7), kind=kOutput, calls=%fused_computation.20 | convolution fusion | flops 872415232 | bytes 28246016 | tf_op jit(solution)/shard_map/dot_general | solution.py:26
  175.7 0.0 all-reduce.3.cloned.1.call-update
  175.7 0.0 reduce-scatter.5.cloned.1.call-start
  175.7 17.3 %all-reduce.3.cloned.1.call-done = f32[32,1024]{1,0:T(8,128)} async-done(((f32[32,1024]{1,0:T(8,128)}), f32[32,1024]{1,0:T(8,128)}) %all-reduce.3.cloned.1.call-update) | async-done | bytes 131088 | tf_op jit(solution)/shard_map/psum | solution.py:32
  193.0 0.0 copy-start.1
  193.1 1.1 multiply_reduce_fusion
  194.2 21.6 %psum.30 = f32[32]{0:T(128)S(1)} all-reduce(f32[32]{0:T(128)S(1)} %multiply_reduce_fusion), channel_id=1, replica_groups=mesh['groups'=2,'wide'=8,'ffn'=2] {'wide'}, use_global_device_ids=true, to_apply=%region_5.6 | all-reduce | flops 32 | bytes 256 | tf_op jit(solution)/shard_map/psum | solution.py:14
  215.8 11.3 %convolution_bitcast_fusion = f32[13312,32]{0,1:T(8,128)S(1)} fusion(bf16[1024,13312]{1,0:T(8,128)(2,1)} %param.6, f32[32]{0:T(128)S(1)} %add_sqrt_fusion, f32[32,1024]{1,0:T(8,128)} %all-reduce.3.cloned.1.call-done, bf16[32,1024]{1,0:T(8,128)(2,1)S(1)} %copy-done), kind=kOutput, calls=%fused_computation | convolution fusion | flops 872546304 | bytes 29163648 | tf_op jit(solution)/shard_map/dot_general | solution.py:19
  227.0 0.0 copy-done.1
  227.1 11.2 %convolution_bitcast_fusion.1 = f32[13312,32]{0,1:T(8,128)S(1)} fusion(bf16[1024,13312]{1,0:T(8,128)(2,1)} %param.5, f32[32]{0:T(128)S(1)} %add_sqrt_fusion, f32[32,1024]{1,0:T(8,128)S(1)} %copy-done.1, bf16[32,1024]{1,0:T(8,128)(2,1)S(1)} %copy-done), kind=kOutput, calls=%fused_computation.1 | convolution fusion | flops 872546304 | bytes 29163648 | tf_op jit(solution)/shard_map/dot_general | solution.py:16
  238.3 2.0 pad_maximum_fusion.1
  240.3 0.0 reduce-scatter.5.cloned.1.call-update
  240.3 0.0 all-reduce.5.cloned.1.call-start
  240.3 75.1 %reduce-scatter.5.cloned.1.call-done = f32[1664,64]{0,1:T(8,128)} async-done(((f32[13312,64]{0,1:T(8,128)}), f32[1664,64]{0,1:T(8,128)}) %reduce-scatter.5.cloned.1.call-update) | async-done | bytes 426000 | tf_op jit(solution)/shard_map/reduce_scatter | solution.py:22
  315.4 1.1 fusion
  316.5 32.3 %all_gather.7 = bf16[13312,32]{0,1:T(8,128)(2,1)S(1)} all-gather(bf16[1664,32]{0,1:T(8,128)(2,1)S(1)} %fusion), channel_id=1, replica_groups=mesh['groups'=2,'wide'=8,'ffn'=2] {'wide'}, dimensions={0}, use_global_device_ids=true | all-gather | bytes 958464 | tf_op jit(solution)/shard_map/all_gather | solution.py:27
  348.8 11.9 %fusion.8 = f32[32,1024]{1,0:T(8,128)} fusion(bf16[13312,32]{0,1:T(8,128)(2,1)S(1)} %all_gather.7, bf16[13312,1024]{1,0:T(8,128)(2,1)} %param.7), kind=kOutput, calls=%fused_computation.21 | convolution fusion | flops 872415232 | bytes 28246016 | tf_op jit(solution)/shard_map/dot_general | solution.py:26
  360.6 0.0 all-reduce.5.cloned.1.call-update
  360.7 17.4 %all-reduce.5.cloned.1.call-done = f32[32,1024]{1,0:T(8,128)} async-done(((f32[32,1024]{1,0:T(8,128)}), f32[32,1024]{1,0:T(8,128)}) %all-reduce.5.cloned.1.call-update) | async-done | bytes 131088 | tf_op jit(solution)/shard_map/psum | solution.py:32
  378.1 1.6 fusion.4
  (2 shorter events, 0.0 us)
Async XLA Ops:
  6.5 35.4 %copy-start = (bf16[32,1024]{1,0:T(8,128)(2,1)S(1)}, bf16[32,1024]{1,0:T(8,128)(2,1)}, u32[]{:S(2)}) copy-start(bf16[32,1024]{1,0:T(8,128)(2,1)} %param.4) | copy-start | bytes 196612
  6.5 123.9 %reduce-scatter.3.cloned.1.call-start = ((), (), s32[]{:S(2)}) async-start(), calls=%async_computation.2 | async-start | bytes 3833856 | tf_op jit(solution)/shard_map/reduce_scatter | solution.py:22
  55.2 137.9 %all-reduce.3.cloned.1.call-start = ((), (), s32[]{:S(2)}) async-start(), calls=%async_computation.3 | async-start | bytes 262144 | tf_op jit(solution)/shard_map/psum | solution.py:32
  175.7 139.7 %reduce-scatter.5.cloned.1.call-start = ((), (), s32[]{:S(2)}) async-start(), calls=%async_computation.4 | async-start | bytes 3833856 | tf_op jit(solution)/shard_map/reduce_scatter | solution.py:22
  193.0 34.0 %copy-start.1 = (f32[32,1024]{1,0:T(8,128)S(1)}, f32[32,1024]{1,0:T(8,128)}, u32[]{:S(2)}) copy-start(f32[32,1024]{1,0:T(8,128)} %all-reduce.3.cloned.1.call-done) | copy-start | bytes 393220
  240.3 137.8 %all-reduce.5.cloned.1.call-start = ((), (), s32[]{:S(2)}) async-start(), calls=%async_computation.5 | async-start | bytes 262144 | tf_op jit(solution)/shard_map/psum | solution.py:32
Sparse Core Ops, SparseCore 0:
  55.3 75.0 reduce-scatter.2
  175.8 17.2 all-reduce.2
  240.4 74.9 reduce-scatter.4
  360.8 17.2 all-reduce.4
where the time goes:
time: 387 us; the launch traced here: 386 us
  waiting for transfers between devices  185 us (48%)
  blocking collectives  109 us (28%)
  matrix products  68.7 us (18%)
  between operations  13.2 us (3%)
  other arithmetic  9.87 us (3%)
    reduce_scatter x2, waiting for transfers between devices, per_device(): lax.psum_scatter(jnp.concatenate([gate_part, up_part], axis=1), 'wide', s...  150 us
    all_gather x2, blocking collectives, per_device(): lax.all_gather(hidden, 'wide', axis=0, tiled=True)  64.6 us
    psum x2, blocking collectives, per_device(): sumsq = lax.psum(jnp.sum(state * state, axis=1), 'wide')  44.7 us
    psum x2, waiting for transfers between devices, per_device(): state = state + lax.psum(partial_value, 'ffn')  34.8 us
    dot_general x2, matrix products, per_device(): lax.dot_general(lax.all_gather(hidden, 'wide', axis=0, tiled=True), down_...  23.7 us
    dot_general x2, matrix products, per_device(): lax.dot_general(up_weight, normed, (((0,), (1,)), ((), ())), preferred_el...  22.5 us
    dot_general x2, matrix products, per_device(): lax.dot_general(gate_weight, normed, (((0,), (1,)), ((), ())), preferred_...  22.5 us
  transfers between devices with their start and end apart: 4, of which 4 were waited for; matrix products, arithmetic and copies ran while one was open for 0% of the time, Pallas kernels for 0%

commit v1 on v0

v1 whole, which is shorter than its diff:
```python
import functools

import jax
import jax.numpy as jnp
from jax import lax
from jax.experimental import pallas as pl
from jax.experimental.pallas import tpu as pltpu
from jax.sharding import PartitionSpec as P

STEPS = 2
CHUNKS = 2
LANES = 128
PIECE = 256
F32 = jnp.float32
BF16 = jnp.bfloat16
SMEM = pl.BlockSpec(memory_space=pltpu.SMEM)
VMEM = pl.BlockSpec(memory_space=pltpu.VMEM)
HBM = pl.BlockSpec(memory_space=pltpu.HBM)
MIB = 2**20


def struct(shape, dtype):
    return jax.ShapeDtypeStruct(shape, dtype)


def cost(flops, moved):
    return pl.CostEstimate(flops=int(flops), bytes_accessed=int(moved), transcendentals=0)


def stages_of(wide):
    found, low = [], 0
    while (1 << low) < wide:
        bits = 1 if low == 0 else min(2, wide.bit_length() - 1 - low)
        found.append((low, 1 << bits))
        low += bits
    return found


def offsets_of(stages):
    found = [0]
    for low, size in reversed(stages):
        found = [(i << low) ^ rest for i in range(size) for rest in found]
    return found


def swap(value, axis, flip, count):
    return lax.ppermute(value, axis, [(i, i ^ flip) for i in range(count)])


def cuts_of(extent, piece):
    return [(a, min(a + piece, extent)) for a in range(0, extent, piece)]


def rows_mean_square(rows):
    total = jnp.sum(rows * rows, axis=1, keepdims=True)
    return jnp.broadcast_to(total, (rows.shape[0], LANES))


def arrange_kernel(offsets, per, groups, where_ref, own_ref, *refs):
    others, (state_ref, x_ref, sumsq_ref, whole) = refs[: groups - 1], refs[groups - 1 :]
    me, group = where_ref[0], where_ref[1]
    rows = own_ref.shape[0]
    for k, ref in enumerate((own_ref,) + tuple(others)):
        start = lax.rem(group + k, groups) * rows
        whole[pl.ds(pl.multiple_of(start, 8), rows), :] = ref[...].astype(F32)
    for p, offset in enumerate(offsets):
        first = (me ^ offset) * per
        if per % 8 == 0:
            first = pl.multiple_of(first, 8)
        state_ref[p * per : (p + 1) * per, :] = whole[pl.ds(first, per), :]
    state = state_ref[...]
    x_ref[...] = state.astype(BF16)
    sumsq_ref[...] = rows_mean_square(state)


def arrange(offsets, per, groups, where, own, others):
    rows, width = own.shape
    rows *= groups
    return pl.pallas_call(
        functools.partial(arrange_kernel, offsets, per, groups),
        out_shape=(struct((rows, width), F32), struct((rows, width), BF16), struct((rows, LANES), F32)),
        in_specs=[SMEM] + [VMEM] * groups,
        out_specs=(VMEM,) * 3,
        scratch_shapes=[pltpu.VMEM((rows, width), F32)],
        name="arrange",
        cost_estimate=cost(rows * width, rows * width * 10),
    )(where, own, *others)


def gate_up_kernel(first, per, base_ref, x_ref, gate_hbm, up_hbm, keep_ref, *refs):
    sends, (gate_vmem, up_vmem, sems) = refs[:-3], refs[-3:]
    depth, width = gate_vmem.shape
    column = pl.multiple_of(base_ref[0] + first, LANES)
    cuts = cuts_of(depth, PIECE)
    copies = []
    for i, (a, b) in enumerate(cuts):
        for k, (source, target) in enumerate(((gate_hbm, gate_vmem), (up_hbm, up_vmem))):
            copy = pltpu.make_async_copy(
                source.at[pl.ds(a, b - a), pl.ds(column, width)], target.at[pl.ds(a, b - a), :], sems.at[k, i]
            )
            copy.start()
            copies.append(copy)
    totals = [None, None]
    for i, (a, b) in enumerate(cuts):
        piece = x_ref[:, a:b]
        for k, held in enumerate((gate_vmem, up_vmem)):
            copies[2 * i + k].wait()
            term = jnp.dot(piece, held[a:b, :], preferred_element_type=F32)
            totals[k] = term if totals[k] is None else totals[k] + term
    group = keep_ref.shape[0]
    for p in range(group * (1 + len(sends))):
        rows = slice(p * per, (p + 1) * per)
        both = jnp.concatenate([totals[0][rows], totals[1][rows]], axis=0)
        target = ((keep_ref,) + tuple(sends))[p // group]
        target[p % group] = both.astype(target.dtype)


def gate_up(first, width, per, size, base, x, gate_weight, up_weight):
    rows, depth = x.shape
    group = rows // per // size
    shape = (group, 2 * per, width)
    return pl.pallas_call(
        functools.partial(gate_up_kernel, first, per),
        out_shape=(struct(shape, F32),) + (struct(shape, BF16),) * (size - 1),
        in_specs=[SMEM, VMEM, HBM, HBM],
        out_specs=(VMEM,) * size,
        scratch_shapes=[
            pltpu.VMEM((depth, width), BF16),
            pltpu.VMEM((depth, width), BF16),
            pltpu.SemaphoreType.DMA((2, len(cuts_of(depth, PIECE)))),
        ],
        name="gate_up",
        compiler_params=pltpu.CompilerParams(vmem_limit_bytes=44 * MIB),
        cost_estimate=cost(4 * rows * depth * width, 4 * depth * width),
    )(base, x, gate_weight, up_weight)


def add_kernel(count, keep_ref, *refs):
    arrived, outs = refs[:count], refs[count:]
    total = keep_ref[...]
    for ref in arrived:
        total = total + ref[...].astype(F32)
    group = outs[0].shape[0]
    for i, out in enumerate(outs):
        out[...] = total[i * group : (i + 1) * group].astype(out.dtype)


def add_stage(keep, arrived, size):
    shape = (keep.shape[0] // size,) + keep.shape[1:]
    return pl.pallas_call(
        functools.partial(add_kernel, len(arrived)),
        out_shape=(struct(shape, F32),) + (struct(shape, BF16),) * (size - 1),
        in_specs=[VMEM] * (1 + len(arrived)),
        out_specs=(VMEM,) * size,
        name="add_partials",
        compiler_params=pltpu.CompilerParams(vmem_limit_bytes=8 * MIB),
        cost_estimate=cost(keep.size * 2, keep.size * 10),
    )(keep, *arrived)


def hidden_kernel(count, width, keep_ref, *refs):
    arrived, (sumsq_ref, out_ref) = refs[:count], refs[count:]
    total = keep_ref[0]
    for ref in arrived:
        total = total + ref[0].astype(F32)
    per = out_ref.shape[0]
    scale = 1.0 / jnp.sqrt(sumsq_ref[...][:, :1] / width + 1e-05)
    gate, up = total[:per] * scale, total[per:] * scale
    out_ref[...] = (gate / (1.0 + jnp.exp(-gate)) * up).astype(BF16)


def hidden_of(keep, arrived, sumsq, features):
    _, both, width = keep.shape
    return pl.pallas_call(
        functools.partial(hidden_kernel, len(arrived), features),
        out_shape=struct((both // 2, width), BF16),
        in_specs=[VMEM] * (2 + len(arrived)),
        out_specs=VMEM,
        name="hidden",
        compiler_params=pltpu.CompilerParams(vmem_limit_bytes=8 * MIB),
        cost_estimate=cost(keep.size * 10, keep.size * 10),
    )(keep, *arrived, sumsq)


def join_kernel(*refs):
    sources, out_ref = refs[:-1], refs[-1]
    out_ref[...] = jnp.concatenate([ref[...].astype(F32) for ref in sources], axis=0).astype(BF16)


def join(parts):
    rows, width = parts[0].shape
    return pl.pallas_call(
        join_kernel,
        out_shape=struct((rows * len(parts), width), BF16),
        in_specs=[VMEM] * len(parts),
        out_specs=VMEM,
        name="join",
        compiler_params=pltpu.CompilerParams(vmem_limit_bytes=8 * MIB),
        cost_estimate=cost(0, rows * len(parts) * width * 4),
    )(*parts)


def down_kernel(first, count, added, base_ref, *refs):
    parts = refs[:count]
    down_hbm = refs[count]
    before = refs[count + 1] if added else None
    out_ref, down_vmem, sems = refs[-3:]
    depth = down_vmem.shape[0]
    row = pl.multiple_of(base_ref[0] + first, LANES)
    cuts = cuts_of(depth, 2 * PIECE)
    copies = []
    for i, (a, b) in enumerate(cuts):
        copy = pltpu.make_async_copy(
            down_hbm.at[pl.ds(row + a, b - a), :], down_vmem.at[pl.ds(a, b - a), :], sems.at[i]
        )
        copy.start()
        copies.append(copy)
    hidden = jnp.concatenate([ref[...] for ref in parts], axis=0)
    total = before[...] if added else None
    for i, (a, b) in enumerate(cuts):
        copies[i].wait()
        term = jnp.dot(hidden[:, a:b], down_vmem[a:b, :], preferred_element_type=F32)
        total = term if total is None else total + term
    out_ref[...] = total


def down(first, base, parts, down_weight, before):
    rows, width = sum(part.shape[0] for part in parts), down_weight.shape[1]
    depth = parts[0].shape[1]
    added = before is not None
    return pl.pallas_call(
        functools.partial(down_kernel, first, len(parts), added),
        out_shape=struct((rows, width), F32),
        in_specs=[SMEM] + [VMEM] * len(parts) + [HBM] + [VMEM] * added,
        out_specs=VMEM,
        scratch_shapes=[
            pltpu.VMEM((depth, width), BF16),
            pltpu.SemaphoreType.DMA((len(cuts_of(depth, 2 * PIECE)),)),
        ],
        name="down",
        compiler_params=pltpu.CompilerParams(vmem_limit_bytes=44 * MIB),
        cost_estimate=cost(2 * rows * depth * width, 2 * depth * width),
    )(base, *parts, down_weight, *([before] if added else []))


def chip_kernel(a_ref, b_ref, state_ref, state_out, send_ref):
    total = a_ref[...] + b_ref[...]
    send_ref[...] = total.astype(BF16)
    state_out[...] = state_ref[...] + total


def renew_kernel(state_ref, *refs):
    arrived, (state_out, x_ref, sumsq_ref) = refs[:-3], refs[-3:]
    state = state_ref[...]
    for ref in arrived:
        state = state + ref[...].astype(F32)
    state_out[...] = state
    x_ref[...] = state.astype(BF16)
    sumsq_ref[...] = rows_mean_square(state)


def finish_kernel(offsets, per, groups, where_ref, a_ref, b_ref, state_ref, out_ref, *refs):
    sends, (change, state) = refs[: groups - 1], refs[groups - 1 :]
    me, group = where_ref[0], where_ref[1]
    for p, offset in enumerate(offsets):
        first = (me ^ offset) * per
        if per % 8 == 0:
            first = pl.multiple_of(first, 8)
        rows = slice(p * per, (p + 1) * per)
        change[pl.ds(first, per), :] = a_ref[rows, :] + b_ref[rows, :]
        state[pl.ds(first, per), :] = state_ref[rows, :]
    rows = out_ref.shape[0]
    own = pl.ds(pl.multiple_of(group * rows, 8), rows)
    out_ref[...] = state[own, :] + change[own, :]
    for k, ref in enumerate(sends):
        other = pl.multiple_of(lax.rem(group + k + 1, groups) * rows, 8)
        ref[...] = change[pl.ds(other, rows), :].astype(BF16)


def per_device(counts, tokens, gate_weight, up_weight, down_weight):
    groups, wide, ffn = counts
    stages = stages_of(wide)
    offsets = offsets_of(stages)
    rows = tokens.shape[0] * groups
    per = rows // wide
    features = tokens.shape[1] * wide
    share = gate_weight.shape[1] // groups
    edges = [share // LANES * k // CHUNKS * LANES for k in range(CHUNKS + 1)]
    chunks = [(a, b - a) for a, b in zip(edges, edges[1:])]
    me, group = lax.axis_index("wide"), lax.axis_index("groups")
    where = jnp.stack([me, group]).astype(jnp.int32)
    base = (group * share).astype(jnp.int32).reshape(1)

    def from_group(value, k):
        return lax.ppermute(value, "groups", [((i + k) % groups, i) for i in range(groups)])

    others = [from_group(tokens, k) for k in range(1, groups)]
    state, x, sumsq = arrange(offsets, per, groups, where, tokens, others)

    def scatter_stage(low, size, sends):
        return [swap(send, "wide", i << low, wide) for i, send in zip(range(1, size), sends)]

    for step in range(STEPS):
        for low, size in stages:
            group_rows = sumsq.shape[0] // size
            blocks = [sumsq[i * group_rows : (i + 1) * group_rows] for i in range(size)]
            sumsq = blocks[0] + sum(scatter_stage(low, size, blocks[1:]))
        change = None
        for first, width in chunks:
            low, size = stages[0]
            keep, *sends = gate_up(first, width, per, size, base, x, gate_weight, up_weight)
            arrived = scatter_stage(low, size, sends)
            for low, size in stages[1:]:
                keep, *sends = add_stage(keep, arrived, size)
                arrived = scatter_stage(low, size, sends)
            parts = [hidden_of(keep, arrived, sumsq, features)]
            for low, size in reversed(stages):
                whole = parts[0] if len(parts) == 1 else join(parts)
                parts = [whole] + [swap(whole, "wide", i << low, wide) for i in range(1, size)]
            change = down(first, base, parts, down_weight, change)
        other = swap(change, "ffn", 1, ffn)
        if step + 1 < STEPS:
            shape = state.shape
            state, send = pl.pallas_call(
                chip_kernel,
                out_shape=(struct(shape, F32), struct(shape, BF16)),
                in_specs=[VMEM] * 3,
                out_specs=(VMEM,) * 2,
                name="chip_sum",
                cost_estimate=cost(state.size, state.size * 16),
            )(change, other, state)
            arrived = [from_group(send, k) for k in range(1, groups)]
            state, x, sumsq = pl.pallas_call(
                renew_kernel,
                out_shape=(struct(shape, F32), struct(shape, BF16), struct((rows, LANES), F32)),
                in_specs=[VMEM] * (1 + len(arrived)),
                out_specs=(VMEM,) * 3,
                name="renew",
                cost_estimate=cost(state.size, state.size * 12),
            )(state, *arrived)
    own = struct(tokens.shape, F32)
    out, *sends = pl.pallas_call(
        functools.partial(finish_kernel, offsets, per, groups),
        out_shape=(own,) + (struct(tokens.shape, BF16),) * (groups - 1),
        in_specs=[SMEM] + [VMEM] * 3,
        out_specs=(VMEM,) * groups,
        scratch_shapes=[pltpu.VMEM(state.shape, F32)] * 2,
        name="finish",
        cost_estimate=cost(state.size, state.size * 16),
    )(where, change, other, state)
    for k, send in enumerate(sends):
        arrived = from_group(send, groups - 1 - k)
        out = out + arrived.astype(F32)
    return out


def solution(mesh):
    counts = tuple(mesh.shape[axis] for axis in ("groups", "wide", "ffn"))
    return jax.shard_map(
        functools.partial(per_device, counts),
        mesh=mesh,
        in_specs=(P("groups", "wide"), P("wide", "ffn"), P("wide", "ffn"), P("ffn", "wide")),
        out_specs=P("groups", "wide"),
        check_vma=False,
    )
```

time: 387 us -> 167 us (0.43)
  waiting for transfers between devices: 185 us -> 43.2 us
  blocking collectives: 109 us -> 0 us
  starting transfers between devices: 0.13 us -> 73.3 us
  matrix products: 68.7 us -> 0 us
  Pallas kernels: 0 us -> 43.1 us
  between operations: 13.2 us -> 0.25 us
  other arithmetic: 9.87 us -> 2.19 us
  local copies, waits for them, and re-layouts: 0.01 us -> 4.51 us
    reduce_scatter x2 -> x0, waiting for transfers between devices: 150 us -> none  [per_device(): lax.psum_scatter(jnp.concatenate([gate_part, up_part], axis=1), 'wide', s...]
    ppermute x0 -> x45, starting transfers between devices: none -> 73.3 us  [the longest x42 66.7 us: swap(): return lax.ppermute(value, axis, [(i, i ^ flip) for i in range(count)])]
    dot_general x6 -> x0, matrix products: 68.7 us -> none  [the longest x2 23.7 us: per_device(): lax.dot_general(lax.all_gather(hidden, 'wide', axis=0, tiled=True), down_...]
    all_gather x2 -> x0, blocking collectives: 64.6 us -> none  [per_device(): lax.all_gather(hidden, 'wide', axis=0, tiled=True)]
    psum x2 -> x0, blocking collectives: 44.7 us -> none  [per_device(): sumsq = lax.psum(jnp.sum(state * state, axis=1), 'wide')]
    ppermute x0 -> x45, waiting for transfers between devices: none -> 43.2 us  [the longest x42 34.7 us: swap(): return lax.ppermute(value, axis, [(i, i ^ flip) for i in range(count)])]
    pallas_call x0 -> x24, Pallas kernels: none -> 43.1 us  [the longest x4 21.9 us: gate_up(): pl.pallas_call(functools.partial(gate_up_kernel, first, per), out_shape=(...]
    psum x2 -> x0, waiting for transfers between devices: 34.8 us -> none  [per_device(): state = state + lax.psum(partial_value, 'ffn')]
  transfers between devices with their start and end apart: 4 -> 45, of which waited for: 4 -> 19; matrix products, arithmetic and copies ran while one was open for 0% -> 0% of each run, Pallas kernels for 0% -> 11%
where the time goes in v1:
time: 167 us; the launch traced here: 166 us
  starting transfers between devices  73.3 us (44%)
  waiting for transfers between devices  43.2 us (26%)
  Pallas kernels  43.1 us (26%)
  local copies, waits for them, and re-layouts  4.51 us (3%)
  other arithmetic  2.19 us (1%)
    ppermute x42, starting transfers between devices, swap(): return lax.ppermute(value, axis, [(i, i ^ flip) for i in range(count)])  66.7 us
    ppermute x42, waiting for transfers between devices, swap(): return lax.ppermute(value, axis, [(i, i ^ flip) for i in range(count)])  34.7 us
    pallas_call x4, Pallas kernels, gate_up(): pl.pallas_call(functools.partial(gate_up_kernel, first, per), out_shape=(...  21.9 us
    pallas_call x4, Pallas kernels, down(): pl.pallas_call(functools.partial(down_kernel, first, len(parts), added),...  13.1 us
    ppermute x3, waiting for transfers between devices, from_group(): lax.ppermute(value, 'groups', [((i + k) % groups, i) for i in range(group...  8.55 us
    ppermute x3, starting transfers between devices, from_group(): lax.ppermute(value, 'groups', [((i + k) % groups, i) for i in range(group...  6.52 us
    unnamed x20, local copies, waits for them, and re-layouts  4.5 us
  transfers between devices with their start and end apart: 45, of which 19 were waited for; matrix products, arithmetic and copies ran while one was open for 0% of the time, Pallas kernels for 11%

profile of v1, /device:TPU:0, one launch (start us, length us, event | category | flops | bytes accessed | tf_op | source)
XLA Modules:
  0.0 166.5 jit_solution(5830957137690273812)
XLA Ops:
  0.0 2.9 %collective-permute-start = (bf16[32,1024]{1,0:T(8,128)(2,1)}, bf16[32,1024]{1,0:T(8,128)(2,1)S(1)}, u32[]{:S(2)}, u32[]{:S(2)}) collective-permute-start(bf16[32,1024]{1,0:T(8,128)(2,1)} %own_ref.1), channel_id=1, source_target_pairs={{16,0},{0,16},{17,1},{1,17},{18,2},{2,18},{19,3},{3,19},{20,4},{4,... | collective-permute-start | bytes 196616 | tf_op jit(solution)/shard_map/ppermute | solution.py:295
  3.5 1.9 %collective-permute-done.refs_0_ = bf16[32,1024]{1,0:T(8,128)(2,1)S(1)} collective-permute-done((bf16[32,1024]{1,0:T(8,128)(2,1)}, bf16[32,1024]{1,0:T(8,128)(2,1)S(1)}, u32[]{:S(2)}, u32[]{:S(2)}) %collective-permute-start) | collective-permute-done | bytes 65568 | tf_op jit(solution)/shard_map/ppermute | solution.py:295
  6.0 1.7 %arrange.1 = (f32[64,1024]{1,0:T(8,128)}, bf16[64,1024]{1,0:T(8,128)(2,1)}, f32[64,128]{1,0:T(8,128)}) custom-call(s32[2]{0:T(128)} %pad_add_fusion.where_ref, bf16[32,1024]{1,0:T(8,128)(2,1)} %own_ref.1, bf16[32,1024]{1,0:T(8,128)(2,1)} %copy-done.7), custom_call_target="tpu_custom_call" | custom-call | flops 65536 | bytes 655360 | tf_op jit(solution)/shard_map/arrange/pallas_call | solution.py:79
  8.6 5.5 %gate_up.5 = (f32[4,16,3328]{2,1,0:T(8,128)S(1)}, bf16[4,16,3328]{2,1,0:T(8,128)(2,1)S(1)}) custom-call(s32[1]{0:T(128)} %bitcast.2.base_ref, bf16[64,1024]{1,0:T(8,128)(2,1)S(1)} %copy-done.3, bf16[1024,13312]{1,0:T(8,128)(2,1)} %gate_hbm.7, bf16[1024,13312]{1,0:T(8,128)(2,1)} %up_hbm.7), custom_call_target="tpu_custom_call" | custom-call | flops 872415232 | bytes 13631488 | tf_op jit(solution)/shard_map/gate_up/pallas_call | solution.py:122
  14.1 2.1 %collective-permute-start.13 = (bf16[4,16,3328]{2,1,0:T(8,128)(2,1)S(1)}, bf16[4,16,3328]{2,1,0:T(8,128)(2,1)S(1)}, u32[]{:S(2)}, u32[]{:S(2)}) collective-permute-start(bf16[4,16,3328]{2,1,0:T(8,128)(2,1)S(1)} %get-tuple-element.48), channel_id=1, source_target_pairs={{0,2},{2,0},{4,6},{6,4},{8,10},{10,8},{12,14},{14,12},{1,3},{3,1},... | collective-permute-start | bytes 1277960 | tf_op jit(solution)/shard_map/ppermute | solution.py:47
  16.3 5.5 %gate_up.4 = (f32[4,16,3328]{2,1,0:T(8,128)S(1)}, bf16[4,16,3328]{2,1,0:T(8,128)(2,1)S(1)}) custom-call(s32[1]{0:T(128)} %bitcast.2.base_ref, bf16[64,1024]{1,0:T(8,128)(2,1)S(1)} %copy-done.3, bf16[1024,13312]{1,0:T(8,128)(2,1)} %gate_hbm.7, bf16[1024,13312]{1,0:T(8,128)(2,1)} %up_hbm.7), custom_call_target="tpu_custom_call" | custom-call | flops 872415232 | bytes 13631488 | tf_op jit(solution)/shard_map/gate_up/pallas_call | solution.py:122
  21.8 2.0 %collective-permute-start.1 = (bf16[4,16,3328]{2,1,0:T(8,128)(2,1)S(1)}, bf16[4,16,3328]{2,1,0:T(8,128)(2,1)S(1)}, u32[]{:S(2)}, u32[]{:S(2)}) collective-permute-start(bf16[4,16,3328]{2,1,0:T(8,128)(2,1)S(1)} %get-tuple-element.41), channel_id=1, source_target_pairs={{0,2},{2,0},{4,6},{6,4},{8,10},{10,8},{12,14},{14,12},{1,3},{3,1},... | collective-permute-start | bytes 1277960 | tf_op jit(solution)/shard_map/ppermute | solution.py:47
  23.8 3.5 %collective-permute-done.5 = f32[32,128]{1,0:T(8,128)S(1)} collective-permute-done((f32[32,128]{1,0:T(8,128)S(1)}, f32[32,128]{1,0:T(8,128)S(1)}, u32[]{:S(2)}, u32[]{:S(2)}) %collective-permute-start.5) | collective-permute-done | bytes 16416 | tf_op jit(solution)/shard_map/ppermute | solution.py:47
  27.4 2.1 %collective-permute-start.14 = (bf16[1,16,3328]{2,1,0:T(8,128)(2,1)S(1)}, bf16[1,16,3328]{2,1,0:T(8,128)(2,1)S(1)}, u32[]{:S(2)}, u32[]{:S(2)}) collective-permute-start(bf16[1,16,3328]{2,1,0:T(8,128)(2,1)S(1)} %get-tuple-element.50), channel_id=1, source_target_pairs={{0,4},{2,6},{4,0},{6,2},{8,12},{10,14},{12,8},{14,10},{1,5},{3,7},... | collective-permute-start | bytes 319496 | tf_op jit(solution)/shard_map/ppermute | solution.py:47
  29.5 2.6 %collective-permute-start.7 = (f32[8,128]{1,0:T(8,128)S(1)}, f32[8,128]{1,0:T(8,128)S(1)}, u32[]{:S(2)}, u32[]{:S(2)}) collective-permute-start(f32[8,128]{1,0:T(8,128)S(1)} %get-tuple-element.76), channel_id=1, source_target_pairs={{0,8},{2,10},{4,12},{6,14},{8,0},{10,2},{12,4},{14,6},{1,9},{3,11}... | collective-permute-start | bytes 12296 | tf_op jit(solution)/shard_map/ppermute | solution.py:47
  34.3 2.8 %collective-permute-start.15 = (bf16[1,16,3328]{2,1,0:T(8,128)(2,1)S(1)}, bf16[1,16,3328]{2,1,0:T(8,128)(2,1)S(1)}, u32[]{:S(2)}, u32[]{:S(2)}) collective-permute-start(bf16[1,16,3328]{2,1,0:T(8,128)(2,1)S(1)} %get-tuple-element.51), channel_id=1, source_target_pairs={{0,8},{2,10},{4,12},{6,14},{8,0},{10,2},{12,4},{14,6},{1,9},{3,11}... | collective-permute-start | bytes 319496 | tf_op jit(solution)/shard_map/ppermute | solution.py:47
  39.0 2.7 %collective-permute-start.3 = (bf16[1,16,3328]{2,1,0:T(8,128)(2,1)S(1)}, bf16[1,16,3328]{2,1,0:T(8,128)(2,1)S(1)}, u32[]{:S(2)}, u32[]{:S(2)}) collective-permute-start(bf16[1,16,3328]{2,1,0:T(8,128)(2,1)S(1)} %get-tuple-element.44), channel_id=1, source_target_pairs={{0,8},{2,10},{4,12},{6,14},{8,0},{10,2},{12,4},{14,6},{1,9},{3,11}... | collective-permute-start | bytes 319496 | tf_op jit(solution)/shard_map/ppermute | solution.py:47
  43.1 3.2 %collective-permute-done.15.refs_1_ = bf16[1,16,3328]{2,1,0:T(8,128)(2,1)S(1)} collective-permute-done((bf16[1,16,3328]{2,1,0:T(8,128)(2,1)S(1)}, bf16[1,16,3328]{2,1,0:T(8,128)(2,1)S(1)}, u32[]{:S(2)}, u32[]{:S(2)}) %collective-permute-start.15) | collective-permute-done | bytes 106528 | tf_op jit(solution)/shard_map/ppermute | solution.py:47
  46.4 6.2 %collective-permute-start.19 = (bf16[8,3328]{1,0:T(8,128)(2,1)S(1)}, bf16[8,3328]{1,0:T(8,128)(2,1)S(1)}, u32[]{:S(2)}, u32[]{:S(2)}) collective-permute-start(bf16[8,3328]{1,0:T(8,128)(2,1)S(1)} %hidden.5.refs_0_), channel_id=1, source_target_pairs={{0,12},{2,14},{4,8},{6,10},{8,4},{10,6},{12,0},{14,2},{1,13},{3,15... | collective-permute-start | bytes 159752 | tf_op jit(solution)/shard_map/ppermute | solution.py:47
  54.7 3.0 %collective-permute-start.11 = (bf16[8,3328]{1,0:T(8,128)(2,1)S(1)}, bf16[8,3328]{1,0:T(8,128)(2,1)S(1)}, u32[]{:S(2)}, u32[]{:S(2)}) collective-permute-start(bf16[8,3328]{1,0:T(8,128)(2,1)S(1)} %hidden.4.refs_0_), channel_id=1, source_target_pairs={{0,12},{2,14},{4,8},{6,10},{8,4},{10,6},{12,0},{14,2},{1,13},{3,15... | collective-permute-start | bytes 159752 | tf_op jit(solution)/shard_map/ppermute | solution.py:47
  57.7 3.2 %collective-permute-start.10 = (bf16[8,3328]{1,0:T(8,128)(2,1)S(1)}, bf16[8,3328]{1,0:T(8,128)(2,1)S(1)}, u32[]{:S(2)}, u32[]{:S(2)}) collective-permute-start(bf16[8,3328]{1,0:T(8,128)(2,1)S(1)} %hidden.4.refs_0_), channel_id=1, source_target_pairs={{0,8},{2,10},{4,12},{6,14},{8,0},{10,2},{12,4},{14,6},{1,9},{3,11}... | collective-permute-start | bytes 159752 | tf_op jit(solution)/shard_map/ppermute | solution.py:47
  65.1 1.6 collective-permute-start.12
  66.7 2.2 %collective-permute-done.20.refs_1_ = bf16[32,3328]{1,0:T(8,128)(2,1)S(1)} collective-permute-done((bf16[32,3328]{1,0:T(8,128)(2,1)S(1)}, bf16[32,3328]{1,0:T(8,128)(2,1)S(1)}, u32[]{:S(2)}, u32[]{:S(2)}) %collective-permute-start.20) | collective-permute-done | bytes 213024 | tf_op jit(solution)/shard_map/ppermute | solution.py:47
  68.9 3.3 %down.4.refs_3_ = f32[64,1024]{1,0:T(8,128)S(1)} custom-call(s32[1]{0:T(128)} %bitcast.2.base_ref, bf16[32,3328]{1,0:T(8,128)(2,1)S(1)} %join.5.refs_0_, bf16[32,3328]{1,0:T(8,128)(2,1)S(1)} %collective-permute-done.20.refs_1_, bf16[13312,1024]{1,0:T(8,128)(2,1)} %refs_2_.7), custom_call_target="tpu_custom_call" | custom-call | flops 436207616 | bytes 6815744 | tf_op jit(solution)/shard_map/down/pallas_call | solution.py:231
  72.2 3.3 %down.5.a_ref = f32[64,1024]{1,0:T(8,128)S(1)} custom-call(s32[1]{0:T(128)} %bitcast.2.base_ref, bf16[32,3328]{1,0:T(8,128)(2,1)S(1)} %join.4.refs_0_, bf16[32,3328]{1,0:T(8,128)(2,1)S(1)} %collective-permute-done.12.refs_1_, bf16[13312,1024]{1,0:T(8,128)(2,1)} %refs_2_.7, f32[64,1024]{1,0:T(8,128)S(1)} %down.4.refs_3_), custom_call_target="tpu_custom_call" | custom-call | flops 436207616 | bytes 6815744 | tf_op jit(solution)/shard_map/down/pallas_call | solution.py:231
  77.8 1.9 %chip_sum.1 = (f32[64,1024]{1,0:T(8,128)}, bf16[64,1024]{1,0:T(8,128)(2,1)}) custom-call(f32[64,1024]{1,0:T(8,128)} %copy-done, f32[64,1024]{1,0:T(8,128)} %copy-done.4, f32[64,1024]{1,0:T(8,128)} %get-tuple-element.53.state_ref), custom_call_target="tpu_custom_call" | custom-call | flops 65536 | bytes 1048576 | tf_op jit(solution)/shard_map/chip_sum/pallas_call | solution.py:324
  79.7 1.8 %collective-permute-start.22 = (bf16[64,1024]{1,0:T(8,128)(2,1)}, bf16[64,1024]{1,0:T(8,128)(2,1)S(1)}, u32[]{:S(2)}, u32[]{:S(2)}) collective-permute-start(bf16[64,1024]{1,0:T(8,128)(2,1)} %get-tuple-element.55), channel_id=1, source_target_pairs={{16,0},{0,16},{17,1},{1,17},{18,2},{2,18},{19,3},{3,19},{20,4},{4,... | collective-permute-start | bytes 393224 | tf_op jit(solution)/shard_map/ppermute | solution.py:295
  81.5 4.0 %collective-permute-done.22.refs_0_ = bf16[64,1024]{1,0:T(8,128)(2,1)S(1)} collective-permute-done((bf16[64,1024]{1,0:T(8,128)(2,1)}, bf16[64,1024]{1,0:T(8,128)(2,1)S(1)}, u32[]{:S(2)}, u32[]{:S(2)}) %collective-permute-start.22) | collective-permute-done | bytes 131104 | tf_op jit(solution)/shard_map/ppermute | solution.py:295
  86.1 1.8 %renew.1 = (f32[64,1024]{1,0:T(8,128)}, bf16[64,1024]{1,0:T(8,128)(2,1)}, f32[64,128]{1,0:T(8,128)}) custom-call(f32[64,1024]{1,0:T(8,128)} %get-tuple-element.54.state_ref, bf16[64,1024]{1,0:T(8,128)(2,1)} %copy-done.6), custom_call_target="tpu_custom_call" | custom-call | flops 65536 | bytes 786432 | tf_op jit(solution)/shard_map/renew/pallas_call | solution.py:333
  88.8 5.5 %gate_up.7 = (f32[4,16,3328]{2,1,0:T(8,128)S(1)}, bf16[4,16,3328]{2,1,0:T(8,128)(2,1)S(1)}) custom-call(s32[1]{0:T(128)} %bitcast.2.base_ref, bf16[64,1024]{1,0:T(8,128)(2,1)S(1)} %copy-done.2, bf16[1024,13312]{1,0:T(8,128)(2,1)} %gate_hbm.7, bf16[1024,13312]{1,0:T(8,128)(2,1)} %up_hbm.7), custom_call_target="tpu_custom_call" | custom-call | flops 872415232 | bytes 13631488 | tf_op jit(solution)/shard_map/gate_up/pallas_call | solution.py:122
  94.3 1.7 %collective-permute-start.35 = (bf16[4,16,3328]{2,1,0:T(8,128)(2,1)S(1)}, bf16[4,16,3328]{2,1,0:T(8,128)(2,1)S(1)}, u32[]{:S(2)}, u32[]{:S(2)}) collective-permute-start(bf16[4,16,3328]{2,1,0:T(8,128)(2,1)S(1)} %get-tuple-element.65), channel_id=1, source_target_pairs={{0,2},{2,0},{4,6},{6,4},{8,10},{10,8},{12,14},{14,12},{1,3},{3,1},... | collective-permute-start | bytes 1277960 | tf_op jit(solution)/shard_map/ppermute | solution.py:47
  96.4 5.5 %gate_up.6 = (f32[4,16,3328]{2,1,0:T(8,128)S(1)}, bf16[4,16,3328]{2,1,0:T(8,128)(2,1)S(1)}) custom-call(s32[1]{0:T(128)} %bitcast.2.base_ref, bf16[64,1024]{1,0:T(8,128)(2,1)S(1)} %copy-done.2, bf16[1024,13312]{1,0:T(8,128)(2,1)} %gate_hbm.7, bf16[1024,13312]{1,0:T(8,128)(2,1)} %up_hbm.7), custom_call_target="tpu_custom_call" | custom-call | flops 872415232 | bytes 13631488 | tf_op jit(solution)/shard_map/gate_up/pallas_call | solution.py:122
  101.9 1.7 %collective-permute-start.23 = (bf16[4,16,3328]{2,1,0:T(8,128)(2,1)S(1)}, bf16[4,16,3328]{2,1,0:T(8,128)(2,1)S(1)}, u32[]{:S(2)}, u32[]{:S(2)}) collective-permute-start(bf16[4,16,3328]{2,1,0:T(8,128)(2,1)S(1)} %get-tuple-element.58), channel_id=1, source_target_pairs={{0,2},{2,0},{4,6},{6,4},{8,10},{10,8},{12,14},{14,12},{1,3},{3,1},... | collective-permute-start | bytes 1277960 | tf_op jit(solution)/shard_map/ppermute | solution.py:47
  103.6 3.9 %collective-permute-done.27 = f32[32,128]{1,0:T(8,128)S(1)} collective-permute-done((f32[32,128]{1,0:T(8,128)S(1)}, f32[32,128]{1,0:T(8,128)S(1)}, u32[]{:S(2)}, u32[]{:S(2)}) %collective-permute-start.27) | collective-permute-done | bytes 16416 | tf_op jit(solution)/shard_map/ppermute | solution.py:47
  108.4 3.2 %collective-permute-start.29 = (f32[8,128]{1,0:T(8,128)S(1)}, f32[8,128]{1,0:T(8,128)S(1)}, u32[]{:S(2)}, u32[]{:S(2)}) collective-permute-start(f32[8,128]{1,0:T(8,128)S(1)} %get-tuple-element.73), channel_id=1, source_target_pairs={{0,8},{2,10},{4,12},{6,14},{8,0},{10,2},{12,4},{14,6},{1,9},{3,11}... | collective-permute-start | bytes 12296 | tf_op jit(solution)/shard_map/ppermute | solution.py:47
  112.2 2.8 %collective-permute-done.23.refs_0_ = bf16[4,16,3328]{2,1,0:T(8,128)(2,1)S(1)} collective-permute-done((bf16[4,16,3328]{2,1,0:T(8,128)(2,1)S(1)}, bf16[4,16,3328]{2,1,0:T(8,128)(2,1)S(1)}, u32[]{:S(2)}, u32[]{:S(2)}) %collective-permute-start.23) | collective-permute-done | bytes 426016 | tf_op jit(solution)/shard_map/ppermute | solution.py:47
  116.3 2.1 %collective-permute-start.38 = (bf16[1,16,3328]{2,1,0:T(8,128)(2,1)S(1)}, bf16[1,16,3328]{2,1,0:T(8,128)(2,1)S(1)}, u32[]{:S(2)}, u32[]{:S(2)}) collective-permute-start(bf16[1,16,3328]{2,1,0:T(8,128)(2,1)S(1)} %get-tuple-element.69), channel_id=1, source_target_pairs={{0,12},{2,14},{4,8},{6,10},{8,4},{10,6},{12,0},{14,2},{1,13},{3,15... | collective-permute-start | bytes 319496 | tf_op jit(solution)/shard_map/ppermute | solution.py:47
  119.1 1.7 %collective-permute-start.25 = (bf16[1,16,3328]{2,1,0:T(8,128)(2,1)S(1)}, bf16[1,16,3328]{2,1,0:T(8,128)(2,1)S(1)}, u32[]{:S(2)}, u32[]{:S(2)}) collective-permute-start(bf16[1,16,3328]{2,1,0:T(8,128)(2,1)S(1)} %get-tuple-element.61), channel_id=1, source_target_pairs={{0,8},{2,10},{4,12},{6,14},{8,0},{10,2},{12,4},{14,6},{1,9},{3,11}... | collective-permute-start | bytes 319496 | tf_op jit(solution)/shard_map/ppermute | solution.py:47
  120.8 2.0 %collective-permute-start.26 = (bf16[1,16,3328]{2,1,0:T(8,128)(2,1)S(1)}, bf16[1,16,3328]{2,1,0:T(8,128)(2,1)S(1)}, u32[]{:S(2)}, u32[]{:S(2)}) collective-permute-start(bf16[1,16,3328]{2,1,0:T(8,128)(2,1)S(1)} %get-tuple-element.62), channel_id=1, source_target_pairs={{0,12},{2,14},{4,8},{6,10},{8,4},{10,6},{12,0},{14,2},{1,13},{3,15... | collective-permute-start | bytes 319496 | tf_op jit(solution)/shard_map/ppermute | solution.py:47
  122.8 7.0 %collective-permute-done.37.refs_1_ = bf16[1,16,3328]{2,1,0:T(8,128)(2,1)S(1)} collective-permute-done((bf16[1,16,3328]{2,1,0:T(8,128)(2,1)S(1)}, bf16[1,16,3328]{2,1,0:T(8,128)(2,1)S(1)}, u32[]{:S(2)}, u32[]{:S(2)}) %collective-permute-start.37) | collective-permute-done | bytes 106528 | tf_op jit(solution)/shard_map/ppermute | solution.py:47
  129.9 2.5 %collective-permute-start.41 = (bf16[8,3328]{1,0:T(8,128)(2,1)S(1)}, bf16[8,3328]{1,0:T(8,128)(2,1)S(1)}, u32[]{:S(2)}, u32[]{:S(2)}) collective-permute-start(bf16[8,3328]{1,0:T(8,128)(2,1)S(1)} %hidden.7.refs_0_), channel_id=1, source_target_pairs={{0,12},{2,14},{4,8},{6,10},{8,4},{10,6},{12,0},{14,2},{1,13},{3,15... | collective-permute-start | bytes 159752 | tf_op jit(solution)/shard_map/ppermute | solution.py:47
  132.4 1.9 %collective-permute-start.40 = (bf16[8,3328]{1,0:T(8,128)(2,1)S(1)}, bf16[8,3328]{1,0:T(8,128)(2,1)S(1)}, u32[]{:S(2)}, u32[]{:S(2)}) collective-permute-start(bf16[8,3328]{1,0:T(8,128)(2,1)S(1)} %hidden.7.refs_0_), channel_id=1, source_target_pairs={{0,8},{2,10},{4,12},{6,14},{8,0},{10,2},{12,4},{14,6},{1,9},{3,11}... | collective-permute-start | bytes 159752 | tf_op jit(solution)/shard_map/ppermute | solution.py:47
  135.1 1.9 %collective-permute-start.33 = (bf16[8,3328]{1,0:T(8,128)(2,1)S(1)}, bf16[8,3328]{1,0:T(8,128)(2,1)S(1)}, u32[]{:S(2)}, u32[]{:S(2)}) collective-permute-start(bf16[8,3328]{1,0:T(8,128)(2,1)S(1)} %hidden.6.refs_0_), channel_id=1, source_target_pairs={{0,12},{2,14},{4,8},{6,10},{8,4},{10,6},{12,0},{14,2},{1,13},{3,15... | collective-permute-start | bytes 159752 | tf_op jit(solution)/shard_map/ppermute | solution.py:47
  137.0 4.1 %collective-permute-start.32 = (bf16[8,3328]{1,0:T(8,128)(2,1)S(1)}, bf16[8,3328]{1,0:T(8,128)(2,1)S(1)}, u32[]{:S(2)}, u32[]{:S(2)}) collective-permute-start(bf16[8,3328]{1,0:T(8,128)(2,1)S(1)} %hidden.6.refs_0_), channel_id=1, source_target_pairs={{0,8},{2,10},{4,12},{6,14},{8,0},{10,2},{12,4},{14,6},{1,9},{3,11}... | collective-permute-start | bytes 159752 | tf_op jit(solution)/shard_map/ppermute | solution.py:47
  142.4 1.6 collective-permute-start.42
  145.3 1.6 collective-permute-start.34
  146.9 2.8 %collective-permute-done.42.refs_1_ = bf16[32,3328]{1,0:T(8,128)(2,1)S(1)} collective-permute-done((bf16[32,3328]{1,0:T(8,128)(2,1)S(1)}, bf16[32,3328]{1,0:T(8,128)(2,1)S(1)}, u32[]{:S(2)}, u32[]{:S(2)}) %collective-permute-start.42) | collective-permute-done | bytes 213024 | tf_op jit(solution)/shard_map/ppermute | solution.py:47
  149.7 3.3 %down.6.refs_3_ = f32[64,1024]{1,0:T(8,128)S(1)} custom-call(s32[1]{0:T(128)} %bitcast.2.base_ref, bf16[32,3328]{1,0:T(8,128)(2,1)S(1)} %join.7.refs_0_, bf16[32,3328]{1,0:T(8,128)(2,1)S(1)} %collective-permute-done.42.refs_1_, bf16[13312,1024]{1,0:T(8,128)(2,1)} %refs_2_.7), custom_call_target="tpu_custom_call" | custom-call | flops 436207616 | bytes 6815744 | tf_op jit(solution)/shard_map/down/pallas_call | solution.py:231
  153.0 3.3 %down.7.a_ref = f32[64,1024]{1,0:T(8,128)S(1)} custom-call(s32[1]{0:T(128)} %bitcast.2.base_ref, bf16[32,3328]{1,0:T(8,128)(2,1)S(1)} %join.6.refs_0_, bf16[32,3328]{1,0:T(8,128)(2,1)S(1)} %collective-permute-done.34.refs_1_, bf16[13312,1024]{1,0:T(8,128)(2,1)} %refs_2_.7, f32[64,1024]{1,0:T(8,128)S(1)} %down.6.refs_3_), custom_call_target="tpu_custom_call" | custom-call | flops 436207616 | bytes 6815744 | tf_op jit(solution)/shard_map/down/pallas_call | solution.py:231
  158.6 1.9 %finish.1 = (f32[32,1024]{1,0:T(8,128)}, bf16[32,1024]{1,0:T(8,128)(2,1)}) custom-call(s32[2]{0:T(128)} %pad_add_fusion.where_ref, f32[64,1024]{1,0:T(8,128)} %copy-done.1, f32[64,1024]{1,0:T(8,128)} %copy-done.5, f32[64,1024]{1,0:T(8,128)} %get-tuple-element.70.state_ref), custom_call_target="tpu_custom_call" | custom-call | flops 65536 | bytes 1048576 | tf_op jit(solution)/shard_map/finish/pallas_call | solution.py:342
  160.4 1.8 %collective-permute-start.44 = (bf16[32,1024]{1,0:T(8,128)(2,1)}, bf16[32,1024]{1,0:T(8,128)(2,1)S(1)}, u32[]{:S(2)}, u32[]{:S(2)}) collective-permute-start(bf16[32,1024]{1,0:T(8,128)(2,1)} %get-tuple-element.72), channel_id=1, source_target_pairs={{16,0},{0,16},{17,1},{1,17},{18,2},{2,18},{19,3},{3,19},{20,4},{4,... | collective-permute-start | bytes 196616 | tf_op jit(solution)/shard_map/ppermute | solution.py:295
  162.2 2.7 %collective-permute-done.44 = bf16[32,1024]{1,0:T(8,128)(2,1)S(1)} collective-permute-done((bf16[32,1024]{1,0:T(8,128)(2,1)}, bf16[32,1024]{1,0:T(8,128)(2,1)S(1)}, u32[]{:S(2)}, u32[]{:S(2)}) %collective-permute-start.44) | collective-permute-done | bytes 65568 | tf_op jit(solution)/shard_map/ppermute | solution.py:295
  164.9 1.6 convert_add_fusion
  (96 shorter events, 27.6 us)
Async XLA Ops:
  0.0 5.4 %collective-permute-start = (bf16[32,1024]{1,0:T(8,128)(2,1)}, bf16[32,1024]{1,0:T(8,128)(2,1)S(1)}, u32[]{:S(2)}, u32[]{:S(2)}) collective-permute-start(bf16[32,1024]{1,0:T(8,128)(2,1)} %own_ref.1), channel_id=1, source_target_pairs={{16,0},{0,16},{17,1},{1,17},{18,2},{2,18},{19,3},{3,19},{20,4},{4,... | collective-permute-start | bytes 196616 | tf_op jit(solution)/shard_map/ppermute | solution.py:295
  8.6 7.6 %copy-start.9 = (f32[64,128]{1,0:T(8,128)S(1)}, f32[64,128]{1,0:T(8,128)}, u32[]{:S(2)}) copy-start(f32[64,128]{1,0:T(8,128)} %get-tuple-element.46) | copy-start | bytes 98308
  14.1 13.2 %collective-permute-start.13 = (bf16[4,16,3328]{2,1,0:T(8,128)(2,1)S(1)}, bf16[4,16,3328]{2,1,0:T(8,128)(2,1)S(1)}, u32[]{:S(2)}, u32[]{:S(2)}) collective-permute-start(bf16[4,16,3328]{2,1,0:T(8,128)(2,1)S(1)} %get-tuple-element.48), channel_id=1, source_target_pairs={{0,2},{2,0},{4,6},{6,4},{8,10},{10,8},{12,14},{14,12},{1,3},{3,1},... | collective-permute-start | bytes 1277960 | tf_op jit(solution)/shard_map/ppermute | solution.py:47
  16.2 11.1 %collective-permute-start.5 = (f32[32,128]{1,0:T(8,128)S(1)}, f32[32,128]{1,0:T(8,128)S(1)}, u32[]{:S(2)}, u32[]{:S(2)}) collective-permute-start(f32[32,128]{1,0:T(8,128)S(1)} %slice.37), channel_id=1, source_target_pairs={{0,2},{2,0},{4,6},{6,4},{8,10},{10,8},{12,14},{14,12},{1,3},{3,1},... | collective-permute-start | bytes 49160 | tf_op jit(solution)/shard_map/ppermute | solution.py:47
  21.8 12.6 %collective-permute-start.1 = (bf16[4,16,3328]{2,1,0:T(8,128)(2,1)S(1)}, bf16[4,16,3328]{2,1,0:T(8,128)(2,1)S(1)}, u32[]{:S(2)}, u32[]{:S(2)}) collective-permute-start(bf16[4,16,3328]{2,1,0:T(8,128)(2,1)S(1)} %get-tuple-element.41), channel_id=1, source_target_pairs={{0,2},{2,0},{4,6},{6,4},{8,10},{10,8},{12,14},{14,12},{1,3},{3,1},... | collective-permute-start | bytes 1277960 | tf_op jit(solution)/shard_map/ppermute | solution.py:47
  27.4 14.3 %collective-permute-start.14 = (bf16[1,16,3328]{2,1,0:T(8,128)(2,1)S(1)}, bf16[1,16,3328]{2,1,0:T(8,128)(2,1)S(1)}, u32[]{:S(2)}, u32[]{:S(2)}) collective-permute-start(bf16[1,16,3328]{2,1,0:T(8,128)(2,1)S(1)} %get-tuple-element.50), channel_id=1, source_target_pairs={{0,4},{2,6},{4,0},{6,2},{8,12},{10,14},{12,8},{14,10},{1,5},{3,7},... | collective-permute-start | bytes 319496 | tf_op jit(solution)/shard_map/ppermute | solution.py:47
  29.5 7.7 %collective-permute-start.7 = (f32[8,128]{1,0:T(8,128)S(1)}, f32[8,128]{1,0:T(8,128)S(1)}, u32[]{:S(2)}, u32[]{:S(2)}) collective-permute-start(f32[8,128]{1,0:T(8,128)S(1)} %get-tuple-element.76), channel_id=1, source_target_pairs={{0,8},{2,10},{4,12},{6,14},{8,0},{10,2},{12,4},{14,6},{1,9},{3,11}... | collective-permute-start | bytes 12296 | tf_op jit(solution)/shard_map/ppermute | solution.py:47
  32.1 6.5 %collective-permute-start.8 = (f32[8,128]{1,0:T(8,128)S(1)}, f32[8,128]{1,0:T(8,128)S(1)}, u32[]{:S(2)}, u32[]{:S(2)}) collective-permute-start(f32[8,128]{1,0:T(8,128)S(1)} %get-tuple-element.77), channel_id=1, source_target_pairs={{0,12},{2,14},{4,8},{6,10},{8,4},{10,6},{12,0},{14,2},{1,13},{3,15... | collective-permute-start | bytes 12296 | tf_op jit(solution)/shard_map/ppermute | solution.py:47
  32.1 6.9 %collective-permute-start.6 = (f32[8,128]{1,0:T(8,128)S(1)}, f32[8,128]{1,0:T(8,128)S(1)}, u32[]{:S(2)}, u32[]{:S(2)}) collective-permute-start(f32[8,128]{1,0:T(8,128)S(1)} %get-tuple-element.78), channel_id=1, source_target_pairs={{0,4},{2,6},{4,0},{6,2},{8,12},{10,14},{12,8},{14,10},{1,5},{3,7},... | collective-permute-start | bytes 12296 | tf_op jit(solution)/shard_map/ppermute | solution.py:47
  34.3 11.9 %collective-permute-start.15 = (bf16[1,16,3328]{2,1,0:T(8,128)(2,1)S(1)}, bf16[1,16,3328]{2,1,0:T(8,128)(2,1)S(1)}, u32[]{:S(2)}, u32[]{:S(2)}) collective-permute-start(bf16[1,16,3328]{2,1,0:T(8,128)(2,1)S(1)} %get-tuple-element.51), channel_id=1, source_target_pairs={{0,8},{2,10},{4,12},{6,14},{8,0},{10,2},{12,4},{14,6},{1,9},{3,11}... | collective-permute-start | bytes 319496 | tf_op jit(solution)/shard_map/ppermute | solution.py:47
  37.2 9.0 %collective-permute-start.16 = (bf16[1,16,3328]{2,1,0:T(8,128)(2,1)S(1)}, bf16[1,16,3328]{2,1,0:T(8,128)(2,1)S(1)}, u32[]{:S(2)}, u32[]{:S(2)}) collective-permute-start(bf16[1,16,3328]{2,1,0:T(8,128)(2,1)S(1)} %get-tuple-element.52), channel_id=1, source_target_pairs={{0,12},{2,14},{4,8},{6,10},{8,4},{10,6},{12,0},{14,2},{1,13},{3,15... | collective-permute-start | bytes 319496 | tf_op jit(solution)/shard_map/ppermute | solution.py:47
  38.6 15.4 %collective-permute-start.2 = (bf16[1,16,3328]{2,1,0:T(8,128)(2,1)S(1)}, bf16[1,16,3328]{2,1,0:T(8,128)(2,1)S(1)}, u32[]{:S(2)}, u32[]{:S(2)}) collective-permute-start(bf16[1,16,3328]{2,1,0:T(8,128)(2,1)S(1)} %get-tuple-element.43), channel_id=1, source_target_pairs={{0,4},{2,6},{4,0},{6,2},{8,12},{10,14},{12,8},{14,10},{1,5},{3,7},... | collective-permute-start | bytes 319496 | tf_op jit(solution)/shard_map/ppermute | solution.py:47
  39.0 15.6 %collective-permute-start.3 = (bf16[1,16,3328]{2,1,0:T(8,128)(2,1)S(1)}, bf16[1,16,3328]{2,1,0:T(8,128)(2,1)S(1)}, u32[]{:S(2)}, u32[]{:S(2)}) collective-permute-start(bf16[1,16,3328]{2,1,0:T(8,128)(2,1)S(1)} %get-tuple-element.44), channel_id=1, source_target_pairs={{0,8},{2,10},{4,12},{6,14},{8,0},{10,2},{12,4},{14,6},{1,9},{3,11}... | collective-permute-start | bytes 319496 | tf_op jit(solution)/shard_map/ppermute | solution.py:47
  41.7 12.9 %collective-permute-start.4 = (bf16[1,16,3328]{2,1,0:T(8,128)(2,1)S(1)}, bf16[1,16,3328]{2,1,0:T(8,128)(2,1)S(1)}, u32[]{:S(2)}, u32[]{:S(2)}) collective-permute-start(bf16[1,16,3328]{2,1,0:T(8,128)(2,1)S(1)} %get-tuple-element.45), channel_id=1, source_target_pairs={{0,12},{2,14},{4,8},{6,10},{8,4},{10,6},{12,0},{14,2},{1,13},{3,15... | collective-permute-start | bytes 319496 | tf_op jit(solution)/shard_map/ppermute | solution.py:47
  46.4 14.5 %collective-permute-start.19 = (bf16[8,3328]{1,0:T(8,128)(2,1)S(1)}, bf16[8,3328]{1,0:T(8,128)(2,1)S(1)}, u32[]{:S(2)}, u32[]{:S(2)}) collective-permute-start(bf16[8,3328]{1,0:T(8,128)(2,1)S(1)} %hidden.5.refs_0_), channel_id=1, source_target_pairs={{0,12},{2,14},{4,8},{6,10},{8,4},{10,6},{12,0},{14,2},{1,13},{3,15... | collective-permute-start | bytes 159752 | tf_op jit(solution)/shard_map/ppermute | solution.py:47
  52.6 8.9 %collective-permute-start.18 = (bf16[8,3328]{1,0:T(8,128)(2,1)S(1)}, bf16[8,3328]{1,0:T(8,128)(2,1)S(1)}, u32[]{:S(2)}, u32[]{:S(2)}) collective-permute-start(bf16[8,3328]{1,0:T(8,128)(2,1)S(1)} %hidden.5.refs_0_), channel_id=1, source_target_pairs={{0,8},{2,10},{4,12},{6,14},{8,0},{10,2},{12,4},{14,6},{1,9},{3,11}... | collective-permute-start | bytes 159752 | tf_op jit(solution)/shard_map/ppermute | solution.py:47
  54.1 7.5 %collective-permute-start.17 = (bf16[8,3328]{1,0:T(8,128)(2,1)S(1)}, bf16[8,3328]{1,0:T(8,128)(2,1)S(1)}, u32[]{:S(2)}, u32[]{:S(2)}) collective-permute-start(bf16[8,3328]{1,0:T(8,128)(2,1)S(1)} %hidden.5.refs_0_), channel_id=1, source_target_pairs={{0,4},{2,6},{4,0},{6,2},{8,12},{10,14},{12,8},{14,10},{1,5},{3,7},... | collective-permute-start | bytes 159752 | tf_op jit(solution)/shard_map/ppermute | solution.py:47
  54.7 8.3 %collective-permute-start.11 = (bf16[8,3328]{1,0:T(8,128)(2,1)S(1)}, bf16[8,3328]{1,0:T(8,128)(2,1)S(1)}, u32[]{:S(2)}, u32[]{:S(2)}) collective-permute-start(bf16[8,3328]{1,0:T(8,128)(2,1)S(1)} %hidden.4.refs_0_), channel_id=1, source_target_pairs={{0,12},{2,14},{4,8},{6,10},{8,4},{10,6},{12,0},{14,2},{1,13},{3,15... | collective-permute-start | bytes 159752 | tf_op jit(solution)/shard_map/ppermute | solution.py:47
  57.7 5.8 %collective-permute-start.10 = (bf16[8,3328]{1,0:T(8,128)(2,1)S(1)}, bf16[8,3328]{1,0:T(8,128)(2,1)S(1)}, u32[]{:S(2)}, u32[]{:S(2)}) collective-permute-start(bf16[8,3328]{1,0:T(8,128)(2,1)S(1)} %hidden.4.refs_0_), channel_id=1, source_target_pairs={{0,8},{2,10},{4,12},{6,14},{8,0},{10,2},{12,4},{14,6},{1,9},{3,11}... | collective-permute-start | bytes 159752 | tf_op jit(solution)/shard_map/ppermute | solution.py:47
  60.9 4.1 %collective-permute-start.9 = (bf16[8,3328]{1,0:T(8,128)(2,1)S(1)}, bf16[8,3328]{1,0:T(8,128)(2,1)S(1)}, u32[]{:S(2)}, u32[]{:S(2)}) collective-permute-start(bf16[8,3328]{1,0:T(8,128)(2,1)S(1)} %hidden.4.refs_0_), channel_id=1, source_target_pairs={{0,4},{2,6},{4,0},{6,2},{8,12},{10,14},{12,8},{14,10},{1,5},{3,7},... | collective-permute-start | bytes 159752 | tf_op jit(solution)/shard_map/ppermute | solution.py:47
  61.6 7.3 %collective-permute-start.20 = (bf16[32,3328]{1,0:T(8,128)(2,1)S(1)}, bf16[32,3328]{1,0:T(8,128)(2,1)S(1)}, u32[]{:S(2)}, u32[]{:S(2)}) collective-permute-start(bf16[32,3328]{1,0:T(8,128)(2,1)S(1)} %join.5.refs_0_), channel_id=1, source_target_pairs={{0,2},{2,0},{4,6},{6,4},{8,10},{10,8},{12,14},{14,12},{1,3},{3,1},... | collective-permute-start | bytes 638984 | tf_op jit(solution)/shard_map/ppermute | solution.py:47
  65.1 7.1 %collective-permute-start.12 = (bf16[32,3328]{1,0:T(8,128)(2,1)S(1)}, bf16[32,3328]{1,0:T(8,128)(2,1)S(1)}, u32[]{:S(2)}, u32[]{:S(2)}) collective-permute-start(bf16[32,3328]{1,0:T(8,128)(2,1)S(1)} %join.4.refs_0_), channel_id=1, source_target_pairs={{0,2},{2,0},{4,6},{6,4},{8,10},{10,8},{12,14},{14,12},{1,3},{3,1},... | collective-permute-start | bytes 638984 | tf_op jit(solution)/shard_map/ppermute | solution.py:47
  75.5 1.6 copy-start
  75.5 1.6 collective-permute-start.21
  79.7 5.8 %collective-permute-start.22 = (bf16[64,1024]{1,0:T(8,128)(2,1)}, bf16[64,1024]{1,0:T(8,128)(2,1)S(1)}, u32[]{:S(2)}, u32[]{:S(2)}) collective-permute-start(bf16[64,1024]{1,0:T(8,128)(2,1)} %get-tuple-element.55), channel_id=1, source_target_pairs={{16,0},{0,16},{17,1},{1,17},{18,2},{2,18},{19,3},{3,19},{20,4},{4,... | collective-permute-start | bytes 393224 | tf_op jit(solution)/shard_map/ppermute | solution.py:295
  88.8 7.2 %copy-start.8 = (f32[64,128]{1,0:T(8,128)S(1)}, f32[64,128]{1,0:T(8,128)}, u32[]{:S(2)}) copy-start(f32[64,128]{1,0:T(8,128)} %get-tuple-element.63) | copy-start | bytes 98308
  94.3 13.2 %collective-permute-start.35 = (bf16[4,16,3328]{2,1,0:T(8,128)(2,1)S(1)}, bf16[4,16,3328]{2,1,0:T(8,128)(2,1)S(1)}, u32[]{:S(2)}, u32[]{:S(2)}) collective-permute-start(bf16[4,16,3328]{2,1,0:T(8,128)(2,1)S(1)} %get-tuple-element.65), channel_id=1, source_target_pairs={{0,2},{2,0},{4,6},{6,4},{8,10},{10,8},{12,14},{14,12},{1,3},{3,1},... | collective-permute-start | bytes 1277960 | tf_op jit(solution)/shard_map/ppermute | solution.py:47
  96.0 11.5 %collective-permute-start.27 = (f32[32,128]{1,0:T(8,128)S(1)}, f32[32,128]{1,0:T(8,128)S(1)}, u32[]{:S(2)}, u32[]{:S(2)}) collective-permute-start(f32[32,128]{1,0:T(8,128)S(1)} %slice.43), channel_id=1, source_target_pairs={{0,2},{2,0},{4,6},{6,4},{8,10},{10,8},{12,14},{14,12},{1,3},{3,1},... | collective-permute-start | bytes 49160 | tf_op jit(solution)/shard_map/ppermute | solution.py:47
  101.9 13.0 %collective-permute-start.23 = (bf16[4,16,3328]{2,1,0:T(8,128)(2,1)S(1)}, bf16[4,16,3328]{2,1,0:T(8,128)(2,1)S(1)}, u32[]{:S(2)}, u32[]{:S(2)}) collective-permute-start(bf16[4,16,3328]{2,1,0:T(8,128)(2,1)S(1)} %get-tuple-element.58), channel_id=1, source_target_pairs={{0,2},{2,0},{4,6},{6,4},{8,10},{10,8},{12,14},{14,12},{1,3},{3,1},... | collective-permute-start | bytes 1277960 | tf_op jit(solution)/shard_map/ppermute | solution.py:47
  107.6 13.2 %collective-permute-start.36 = (bf16[1,16,3328]{2,1,0:T(8,128)(2,1)S(1)}, bf16[1,16,3328]{2,1,0:T(8,128)(2,1)S(1)}, u32[]{:S(2)}, u32[]{:S(2)}) collective-permute-start(bf16[1,16,3328]{2,1,0:T(8,128)(2,1)S(1)} %get-tuple-element.67), channel_id=1, source_target_pairs={{0,4},{2,6},{4,0},{6,2},{8,12},{10,14},{12,8},{14,10},{1,5},{3,7},... | collective-permute-start | bytes 319496 | tf_op jit(solution)/shard_map/ppermute | solution.py:47
  108.4 8.0 %collective-permute-start.29 = (f32[8,128]{1,0:T(8,128)S(1)}, f32[8,128]{1,0:T(8,128)S(1)}, u32[]{:S(2)}, u32[]{:S(2)}) collective-permute-start(f32[8,128]{1,0:T(8,128)S(1)} %get-tuple-element.73), channel_id=1, source_target_pairs={{0,8},{2,10},{4,12},{6,14},{8,0},{10,2},{12,4},{14,6},{1,9},{3,11}... | collective-permute-start | bytes 12296 | tf_op jit(solution)/shard_map/ppermute | solution.py:47
  111.6 6.8 %collective-permute-start.30 = (f32[8,128]{1,0:T(8,128)S(1)}, f32[8,128]{1,0:T(8,128)S(1)}, u32[]{:S(2)}, u32[]{:S(2)}) collective-permute-start(f32[8,128]{1,0:T(8,128)S(1)} %get-tuple-element.74), channel_id=1, source_target_pairs={{0,12},{2,14},{4,8},{6,10},{8,4},{10,6},{12,0},{14,2},{1,13},{3,15... | collective-permute-start | bytes 12296 | tf_op jit(solution)/shard_map/ppermute | solution.py:47
  112.0 7.0 %collective-permute-start.28 = (f32[8,128]{1,0:T(8,128)S(1)}, f32[8,128]{1,0:T(8,128)S(1)}, u32[]{:S(2)}, u32[]{:S(2)}) collective-permute-start(f32[8,128]{1,0:T(8,128)S(1)} %get-tuple-element.75), channel_id=1, source_target_pairs={{0,4},{2,6},{4,0},{6,2},{8,12},{10,14},{12,8},{14,10},{1,5},{3,7},... | collective-permute-start | bytes 12296 | tf_op jit(solution)/shard_map/ppermute | solution.py:47
  114.9 14.9 %collective-permute-start.37 = (bf16[1,16,3328]{2,1,0:T(8,128)(2,1)S(1)}, bf16[1,16,3328]{2,1,0:T(8,128)(2,1)S(1)}, u32[]{:S(2)}, u32[]{:S(2)}) collective-permute-start(bf16[1,16,3328]{2,1,0:T(8,128)(2,1)S(1)} %get-tuple-element.68), channel_id=1, source_target_pairs={{0,8},{2,10},{4,12},{6,14},{8,0},{10,2},{12,4},{14,6},{1,9},{3,11}... | collective-permute-start | bytes 319496 | tf_op jit(solution)/shard_map/ppermute | solution.py:47
  116.3 13.5 %collective-permute-start.38 = (bf16[1,16,3328]{2,1,0:T(8,128)(2,1)S(1)}, bf16[1,16,3328]{2,1,0:T(8,128)(2,1)S(1)}, u32[]{:S(2)}, u32[]{:S(2)}) collective-permute-start(bf16[1,16,3328]{2,1,0:T(8,128)(2,1)S(1)} %get-tuple-element.69), channel_id=1, source_target_pairs={{0,12},{2,14},{4,8},{6,10},{8,4},{10,6},{12,0},{14,2},{1,13},{3,15... | collective-permute-start | bytes 319496 | tf_op jit(solution)/shard_map/ppermute | solution.py:47
  118.4 15.9 %collective-permute-start.24 = (bf16[1,16,3328]{2,1,0:T(8,128)(2,1)S(1)}, bf16[1,16,3328]{2,1,0:T(8,128)(2,1)S(1)}, u32[]{:S(2)}, u32[]{:S(2)}) collective-permute-start(bf16[1,16,3328]{2,1,0:T(8,128)(2,1)S(1)} %get-tuple-element.60), channel_id=1, source_target_pairs={{0,4},{2,6},{4,0},{6,2},{8,12},{10,14},{12,8},{14,10},{1,5},{3,7},... | collective-permute-start | bytes 319496 | tf_op jit(solution)/shard_map/ppermute | solution.py:47
  119.1 15.8 %collective-permute-start.25 = (bf16[1,16,3328]{2,1,0:T(8,128)(2,1)S(1)}, bf16[1,16,3328]{2,1,0:T(8,128)(2,1)S(1)}, u32[]{:S(2)}, u32[]{:S(2)}) collective-permute-start(bf16[1,16,3328]{2,1,0:T(8,128)(2,1)S(1)} %get-tuple-element.61), channel_id=1, source_target_pairs={{0,8},{2,10},{4,12},{6,14},{8,0},{10,2},{12,4},{14,6},{1,9},{3,11}... | collective-permute-start | bytes 319496 | tf_op jit(solution)/shard_map/ppermute | solution.py:47
  120.8 14.1 %collective-permute-start.26 = (bf16[1,16,3328]{2,1,0:T(8,128)(2,1)S(1)}, bf16[1,16,3328]{2,1,0:T(8,128)(2,1)S(1)}, u32[]{:S(2)}, u32[]{:S(2)}) collective-permute-start(bf16[1,16,3328]{2,1,0:T(8,128)(2,1)S(1)} %get-tuple-element.62), channel_id=1, source_target_pairs={{0,12},{2,14},{4,8},{6,10},{8,4},{10,6},{12,0},{14,2},{1,13},{3,15... | collective-permute-start | bytes 319496 | tf_op jit(solution)/shard_map/ppermute | solution.py:47
  129.9 11.2 %collective-permute-start.41 = (bf16[8,3328]{1,0:T(8,128)(2,1)S(1)}, bf16[8,3328]{1,0:T(8,128)(2,1)S(1)}, u32[]{:S(2)}, u32[]{:S(2)}) collective-permute-start(bf16[8,3328]{1,0:T(8,128)(2,1)S(1)} %hidden.7.refs_0_), channel_id=1, source_target_pairs={{0,12},{2,14},{4,8},{6,10},{8,4},{10,6},{12,0},{14,2},{1,13},{3,15... | collective-permute-start | bytes 159752 | tf_op jit(solution)/shard_map/ppermute | solution.py:47
  132.4 9.9 %collective-permute-start.40 = (bf16[8,3328]{1,0:T(8,128)(2,1)S(1)}, bf16[8,3328]{1,0:T(8,128)(2,1)S(1)}, u32[]{:S(2)}, u32[]{:S(2)}) collective-permute-start(bf16[8,3328]{1,0:T(8,128)(2,1)S(1)} %hidden.7.refs_0_), channel_id=1, source_target_pairs={{0,8},{2,10},{4,12},{6,14},{8,0},{10,2},{12,4},{14,6},{1,9},{3,11}... | collective-permute-start | bytes 159752 | tf_op jit(solution)/shard_map/ppermute | solution.py:47
  134.3 8.0 %collective-permute-start.39 = (bf16[8,3328]{1,0:T(8,128)(2,1)S(1)}, bf16[8,3328]{1,0:T(8,128)(2,1)S(1)}, u32[]{:S(2)}, u32[]{:S(2)}) collective-permute-start(bf16[8,3328]{1,0:T(8,128)(2,1)S(1)} %hidden.7.refs_0_), channel_id=1, source_target_pairs={{0,4},{2,6},{4,0},{6,2},{8,12},{10,14},{12,8},{14,10},{1,5},{3,7},... | collective-permute-start | bytes 159752 | tf_op jit(solution)/shard_map/ppermute | solution.py:47
  135.1 8.9 %collective-permute-start.33 = (bf16[8,3328]{1,0:T(8,128)(2,1)S(1)}, bf16[8,3328]{1,0:T(8,128)(2,1)S(1)}, u32[]{:S(2)}, u32[]{:S(2)}) collective-permute-start(bf16[8,3328]{1,0:T(8,128)(2,1)S(1)} %hidden.6.refs_0_), channel_id=1, source_target_pairs={{0,12},{2,14},{4,8},{6,10},{8,4},{10,6},{12,0},{14,2},{1,13},{3,15... | collective-permute-start | bytes 159752 | tf_op jit(solution)/shard_map/ppermute | solution.py:47
  137.0 6.9 %collective-permute-start.32 = (bf16[8,3328]{1,0:T(8,128)(2,1)S(1)}, bf16[8,3328]{1,0:T(8,128)(2,1)S(1)}, u32[]{:S(2)}, u32[]{:S(2)}) collective-permute-start(bf16[8,3328]{1,0:T(8,128)(2,1)S(1)} %hidden.6.refs_0_), channel_id=1, source_target_pairs={{0,8},{2,10},{4,12},{6,14},{8,0},{10,2},{12,4},{14,6},{1,9},{3,11}... | collective-permute-start | bytes 159752 | tf_op jit(solution)/shard_map/ppermute | solution.py:47
  141.1 4.1 %collective-permute-start.31 = (bf16[8,3328]{1,0:T(8,128)(2,1)S(1)}, bf16[8,3328]{1,0:T(8,128)(2,1)S(1)}, u32[]{:S(2)}, u32[]{:S(2)}) collective-permute-start(bf16[8,3328]{1,0:T(8,128)(2,1)S(1)} %hidden.6.refs_0_), channel_id=1, source_target_pairs={{0,4},{2,6},{4,0},{6,2},{8,12},{10,14},{12,8},{14,10},{1,5},{3,7},... | collective-permute-start | bytes 159752 | tf_op jit(solution)/shard_map/ppermute | solution.py:47
  142.4 7.3 %collective-permute-start.42 = (bf16[32,3328]{1,0:T(8,128)(2,1)S(1)}, bf16[32,3328]{1,0:T(8,128)(2,1)S(1)}, u32[]{:S(2)}, u32[]{:S(2)}) collective-permute-start(bf16[32,3328]{1,0:T(8,128)(2,1)S(1)} %join.7.refs_0_), channel_id=1, source_target_pairs={{0,2},{2,0},{4,6},{6,4},{8,10},{10,8},{12,14},{14,12},{1,3},{3,1},... | collective-permute-start | bytes 638984 | tf_op jit(solution)/shard_map/ppermute | solution.py:47
  145.3 7.7 %collective-permute-start.34 = (bf16[32,3328]{1,0:T(8,128)(2,1)S(1)}, bf16[32,3328]{1,0:T(8,128)(2,1)S(1)}, u32[]{:S(2)}, u32[]{:S(2)}) collective-permute-start(bf16[32,3328]{1,0:T(8,128)(2,1)S(1)} %join.6.refs_0_), channel_id=1, source_target_pairs={{0,2},{2,0},{4,6},{6,4},{8,10},{10,8},{12,14},{14,12},{1,3},{3,1},... | collective-permute-start | bytes 638984 | tf_op jit(solution)/shard_map/ppermute | solution.py:47
  156.3 1.6 collective-permute-start.43
  160.4 4.5 %collective-permute-start.44 = (bf16[32,1024]{1,0:T(8,128)(2,1)}, bf16[32,1024]{1,0:T(8,128)(2,1)S(1)}, u32[]{:S(2)}, u32[]{:S(2)}) collective-permute-start(bf16[32,1024]{1,0:T(8,128)(2,1)} %get-tuple-element.72), channel_id=1, source_target_pairs={{16,0},{0,16},{17,1},{1,17},{18,2},{2,18},{19,3},{3,19},{20,4},{4,... | collective-permute-start | bytes 196616 | tf_op jit(solution)/shard_map/ppermute | solution.py:295
  (7 other events, 6.1 us)

commit v2 on v1

--- a/solution.py
+++ b/solution.py
@@ -17,10 +17,15 @@
 VMEM = pl.BlockSpec(memory_space=pltpu.VMEM)
 HBM = pl.BlockSpec(memory_space=pltpu.HBM)
 MIB = 2**20
+LOAD_LIMIT, FRESH_LIMIT, DOWN_LIMIT, HELD_LIMIT = 10, 10, 10, 10
 
 
 def struct(shape, dtype):
     return jax.ShapeDtypeStruct(shape, dtype)
+
+
+def in_hbm(value):
+    return pltpu.with_memory_space_constraint(value, pltpu.HBM)
 
 
 def cost(flops, moved):
@@ -83,72 +88,146 @@
         out_specs=(VMEM,) * 3,
         scratch_shapes=[pltpu.VMEM((rows, width), F32)],
         name="arrange",
+        compiler_params=pltpu.CompilerParams(vmem_limit_bytes=8 * MIB),
         cost_estimate=cost(rows * width, rows * width * 10),
     )(where, own, *others)
 
 
-def gate_up_kernel(first, per, base_ref, x_ref, gate_hbm, up_hbm, keep_ref, *refs):
-    sends, (gate_vmem, up_vmem, sems) = refs[:-3], refs[-3:]
-    depth, width = gate_vmem.shape
+def squeeze(value):
+    return (value * jnp.abs(value)).astype(BF16)
+
+
+def expand(ref, index=slice(None)):
+    sent = ref[index].astype(F32)
+    return sent * lax.rsqrt(jnp.maximum(jnp.abs(sent), 1e-37))
+
+
+def three_lanes(value):
+    shape = value.shape[:-1] + (LANES,)
+    value = jnp.broadcast_to(value, shape)
+    lane = lax.broadcasted_iota(jnp.int32, shape, len(shape) - 1)
+    out = jnp.zeros(shape, F32)
+    for k in range(3):
+        part = value.astype(BF16).astype(F32)
+        out = jnp.where(lane == k, part, out)
+        value = value - part
+    return out.astype(BF16)
+
+
+def start_copies(pairs, sems):
+    copies = [pltpu.make_async_copy(source, target, sems.at[i]) for i, (source, target) in enumerate(pairs)]
+    for copy in copies:
+        copy.start()
+    return copies
+
+
+def column_pairs(column, width, sources, targets):
+    pairs = []
+    for a, b in cuts_of(targets[0].shape[0], PIECE):
+        for source, target in zip(sources, targets):
+            pairs.append((source.at[pl.ds(a, b - a), pl.ds(column, width)], target.at[pl.ds(a, b - a), :]))
+    return pairs
+
+
+def load_kernel(first, base_ref, gate_hbm, up_hbm, gate_ref, up_ref, sems):
     column = pl.multiple_of(base_ref[0] + first, LANES)
-    cuts = cuts_of(depth, PIECE)
-    copies = []
-    for i, (a, b) in enumerate(cuts):
-        for k, (source, target) in enumerate(((gate_hbm, gate_vmem), (up_hbm, up_vmem))):
-            copy = pltpu.make_async_copy(
-                source.at[pl.ds(a, b - a), pl.ds(column, width)], target.at[pl.ds(a, b - a), :], sems.at[k, i]
-            )
-            copy.start()
-            copies.append(copy)
+    for copy in start_copies(column_pairs(column, gate_ref.shape[1], (gate_hbm, up_hbm), (gate_ref, up_ref)), sems):
+        copy.wait()
+
+
+def load(first, width, base, gate_weight, up_weight):
+    depth = gate_weight.shape[0]
+    shape = struct((depth, width), BF16)
+    return pl.pallas_call(
+        functools.partial(load_kernel, first),
+        out_shape=(shape,) * 2,
+        in_specs=[SMEM, HBM, HBM],
+        out_specs=(VMEM,) * 2,
+        scratch_shapes=[pltpu.SemaphoreType.DMA((2 * len(cuts_of(depth, PIECE)),))],
+        name="load",
+        compiler_params=pltpu.CompilerParams(vmem_limit_bytes=LOAD_LIMIT * MIB),
+        cost_estimate=cost(0, 4 * depth * width),
+    )(base, gate_weight, up_weight)
+
+
+def gate_up_kernel(first, per, size, fresh, summed, base_ref, x_ref, *refs):
+    refs = list(refs)
+    sumsq_ref = refs.pop(0) if summed else None
+    weights, refs = refs[:2], refs[2:]
+    outs, refs = refs[:size], refs[size:]
+    copies = None
+    if fresh:
+        held, sems = refs[:2], refs[2]
+        column = pl.multiple_of(base_ref[0] + first, LANES)
+        copies = start_copies(column_pairs(column, held[0].shape[1], weights, held), sems)
+    else:
+        held = weights
+    depth, width = held[0].shape
     totals = [None, None]
-    for i, (a, b) in enumerate(cuts):
+    for i, (a, b) in enumerate(cuts_of(depth, PIECE)):
         piece = x_ref[:, a:b]
-        for k, held in enumerate((gate_vmem, up_vmem)):
-            copies[2 * i + k].wait()
-            term = jnp.dot(piece, held[a:b, :], preferred_element_type=F32)
+        for k, weight in enumerate(held):
+            if fresh:
+                copies[2 * i + k].wait()
+            term = jnp.dot(piece, weight[a:b, :], preferred_element_type=F32)
             totals[k] = term if totals[k] is None else totals[k] + term
-    group = keep_ref.shape[0]
-    for p in range(group * (1 + len(sends))):
+    group = outs[0].shape[0]
+    for p in range(group * size):
         rows = slice(p * per, (p + 1) * per)
         both = jnp.concatenate([totals[0][rows], totals[1][rows]], axis=0)
-        target = ((keep_ref,) + tuple(sends))[p // group]
-        target[p % group] = both.astype(target.dtype)
-
-
-def gate_up(first, width, per, size, base, x, gate_weight, up_weight):
+        target = outs[p // group]
+        target[p % group, :, :width] = both if p < group else squeeze(both)
+        if summed:
+            square = sumsq_ref[rows]
+            square = jnp.concatenate([square, square], axis=0)
+            target[p % group, :, width:] = square if p < group else three_lanes(square[:, :1])
+
+
+def gate_up(first, width, per, size, base, x, sumsq, weights, fresh):
     rows, depth = x.shape
     group = rows // per // size
-    shape = (group, 2 * per, width)
-    return pl.pallas_call(
-        functools.partial(gate_up_kernel, first, per),
-        out_shape=(struct(shape, F32),) + (struct(shape, BF16),) * (size - 1),
-        in_specs=[SMEM, VMEM, HBM, HBM],
-        out_specs=(VMEM,) * size,
-        scratch_shapes=[
-            pltpu.VMEM((depth, width), BF16),
-            pltpu.VMEM((depth, width), BF16),
-            pltpu.SemaphoreType.DMA((2, len(cuts_of(depth, PIECE)))),
-        ],
+    summed = sumsq is not None
+    shape = (group, 2 * per, width + LANES * summed)
+    held = struct((depth, width), BF16)
+    return pl.pallas_call(
+        functools.partial(gate_up_kernel, first, per, size, fresh, summed),
+        out_shape=(struct(shape, F32),) + (struct(shape, BF16),) * (size - 1) + (held,) * (2 * fresh),
+        in_specs=[SMEM, VMEM] + [VMEM] * summed + [HBM if fresh else VMEM] * 2,
+        out_specs=(VMEM,) * (size + 2 * fresh),
+        scratch_shapes=[pltpu.SemaphoreType.DMA((2 * len(cuts_of(depth, PIECE)),))] * fresh,
         name="gate_up",
-        compiler_params=pltpu.CompilerParams(vmem_limit_bytes=44 * MIB),
+        compiler_params=pltpu.CompilerParams(vmem_limit_bytes=(FRESH_LIMIT if fresh else HELD_LIMIT) * MIB),
         cost_estimate=cost(4 * rows * depth * width, 4 * depth * width),
-    )(base, x, gate_weight, up_weight)
-
-
-def add_kernel(count, keep_ref, *refs):
+    )(base, x, *([sumsq] if summed else []), *weights)
+
+
+def arrived_sum(keep, width, refs):
+    total = keep[..., :width]
+    for ref in refs:
+        total = total + expand(ref, (slice(None), slice(None), slice(0, width)))
+    if keep.shape[-1] == width:
+        return total, None
+    square = keep[..., width:]
+    for ref in refs:
+        square = square + jnp.sum(ref[:, :, width:].astype(F32), axis=-1, keepdims=True)
+    return total, square
+
+
+def add_kernel(count, width, keep_ref, *refs):
     arrived, outs = refs[:count], refs[count:]
-    total = keep_ref[...]
-    for ref in arrived:
-        total = total + ref[...].astype(F32)
+    total, square = arrived_sum(keep_ref[...], width, arrived)
     group = outs[0].shape[0]
     for i, out in enumerate(outs):
-        out[...] = total[i * group : (i + 1) * group].astype(out.dtype)
-
-
-def add_stage(keep, arrived, size):
+        rows = slice(i * group, (i + 1) * group)
+        out[:, :, :width] = total[rows] if i == 0 else squeeze(total[rows])
+        if square is not None:
+            out[:, :, width:] = square[rows] if i == 0 else three_lanes(square[rows][..., :1])
+
+
+def add_stage(keep, width, arrived, size):
     shape = (keep.shape[0] // size,) + keep.shape[1:]
     return pl.pallas_call(
-        functools.partial(add_kernel, len(arrived)),
+        functools.partial(add_kernel, len(arrived), width),
         out_shape=(struct(shape, F32),) + (struct(shape, BF16),) * (size - 1),
         in_specs=[VMEM] * (1 + len(arrived)),
         out_specs=(VMEM,) * size,
@@ -158,28 +237,35 @@
     )(keep, *arrived)
 
 
-def hidden_kernel(count, width, keep_ref, *refs):
-    arrived, (sumsq_ref, out_ref) = refs[:count], refs[count:]
-    total = keep_ref[0]
-    for ref in arrived:
-        total = total + ref[0].astype(F32)
+def hidden_kernel(count, width, summed, features, keep_ref, *refs):
+    arrived, refs = refs[:count], refs[count:]
+    total, square = arrived_sum(keep_ref[...], width, arrived)
+    total = total[0]
+    out_ref = refs[0] if summed else refs[1]
     per = out_ref.shape[0]
-    scale = 1.0 / jnp.sqrt(sumsq_ref[...][:, :1] / width + 1e-05)
+    if summed:
+        scale = 1.0 / jnp.sqrt(square[0][:per] / features + 1e-05)
+        refs[1][...] = scale
+    else:
+        scale = refs[0][...]
+    scale = scale[:, :1]
     gate, up = total[:per] * scale, total[per:] * scale
     out_ref[...] = (gate / (1.0 + jnp.exp(-gate)) * up).astype(BF16)
 
 
-def hidden_of(keep, arrived, sumsq, features):
-    _, both, width = keep.shape
-    return pl.pallas_call(
-        functools.partial(hidden_kernel, len(arrived), features),
-        out_shape=struct((both // 2, width), BF16),
-        in_specs=[VMEM] * (2 + len(arrived)),
-        out_specs=VMEM,
+def hidden_of(keep, width, arrived, scale, features):
+    per = keep.shape[1] // 2
+    summed = scale is None
+    out = struct((per, width), BF16)
+    return pl.pallas_call(
+        functools.partial(hidden_kernel, len(arrived), width, summed, features),
+        out_shape=(out, struct((per, LANES), F32)) if summed else (out,),
+        in_specs=[VMEM] * (1 + len(arrived) + (not summed)),
+        out_specs=(VMEM,) * (1 + summed),
         name="hidden",
         compiler_params=pltpu.CompilerParams(vmem_limit_bytes=8 * MIB),
         cost_estimate=cost(keep.size * 10, keep.size * 10),
-    )(keep, *arrived, sumsq)
+    )(keep, *arrived, *([] if summed else [scale]))
 
 
 def join_kernel(*refs):
@@ -200,47 +286,42 @@
     )(*parts)
 
 
-def down_kernel(first, count, added, base_ref, *refs):
-    parts = refs[:count]
-    down_hbm = refs[count]
-    before = refs[count + 1] if added else None
-    out_ref, down_vmem, sems = refs[-3:]
-    depth = down_vmem.shape[0]
-    row = pl.multiple_of(base_ref[0] + first, LANES)
-    cuts = cuts_of(depth, 2 * PIECE)
-    copies = []
-    for i, (a, b) in enumerate(cuts):
-        copy = pltpu.make_async_copy(
-            down_hbm.at[pl.ds(row + a, b - a), :], down_vmem.at[pl.ds(a, b - a), :], sems.at[i]
-        )
-        copy.start()
-        copies.append(copy)
+def down_kernel(first, count, added, fresh, base_ref, *refs):
+    refs = list(refs)
+    parts, weight, refs = refs[:count], refs[count], refs[count + 1 :]
+    before = refs.pop(0) if added else None
+    out_ref = refs.pop(0)
+    if fresh:
+        held, sems = refs
+        row = pl.multiple_of(base_ref[0] + first, LANES)
+        cuts = cuts_of(held.shape[0], 2 * PIECE)
+        copies = start_copies([(weight.at[pl.ds(row + a, b - a), :], held.at[pl.ds(a, b - a), :]) for a, b in cuts], sems)
+    else:
+        held, cuts = weight, [(0, weight.shape[0])]
     hidden = jnp.concatenate([ref[...] for ref in parts], axis=0)
     total = before[...] if added else None
     for i, (a, b) in enumerate(cuts):
-        copies[i].wait()
-        term = jnp.dot(hidden[:, a:b], down_vmem[a:b, :], preferred_element_type=F32)
+        if fresh:
+            copies[i].wait()
+        term = jnp.dot(hidden[:, a:b], held[a:b, :], preferred_element_type=F32)
         total = term if total is None else total + term
     out_ref[...] = total
 
 
-def down(first, base, parts, down_weight, before):
-    rows, width = sum(part.shape[0] for part in parts), down_weight.shape[1]
+def down(first, base, parts, weight, before, fresh):
+    rows, width = sum(part.shape[0] for part in parts), weight.shape[1]
     depth = parts[0].shape[1]
     added = before is not None
     return pl.pallas_call(
-        functools.partial(down_kernel, first, len(parts), added),
-        out_shape=struct((rows, width), F32),
-        in_specs=[SMEM] + [VMEM] * len(parts) + [HBM] + [VMEM] * added,
-        out_specs=VMEM,
-        scratch_shapes=[
-            pltpu.VMEM((depth, width), BF16),
-            pltpu.SemaphoreType.DMA((len(cuts_of(depth, 2 * PIECE)),)),
-        ],
+        functools.partial(down_kernel, first, len(parts), added, fresh),
+        out_shape=(struct((rows, width), F32),) + (struct((depth, width), BF16),) * fresh,
+        in_specs=[SMEM] + [VMEM] * len(parts) + [HBM if fresh else VMEM] + [VMEM] * added,
+        out_specs=(VMEM,) * (1 + fresh),
+        scratch_shapes=[pltpu.SemaphoreType.DMA((len(cuts_of(depth, 2 * PIECE)),))] * fresh,
         name="down",
-        compiler_params=pltpu.CompilerParams(vmem_limit_bytes=44 * MIB),
+        compiler_params=pltpu.CompilerParams(vmem_limit_bytes=(DOWN_LIMIT if fresh else HELD_LIMIT) * MIB),
         cost_estimate=cost(2 * rows * depth * width, 2 * depth * width),
-    )(base, *parts, down_weight, *([before] if added else []))
+    )(base, *parts, weight, *([before] if added else []))
 
 
 def chip_kernel(a_ref, b_ref, state_ref, state_out, send_ref):
@@ -300,24 +381,37 @@
     def scatter_stage(low, size, sends):
         return [swap(send, "wide", i << low, wide) for i, send in zip(range(1, size), sends)]
 
+    gates, downs = {}, {}
+    gate_weight, up_weight, down_weight = (in_hbm(w) for w in (gate_weight, up_weight, down_weight))
+    gates[0] = load(*chunks[0], base, gate_weight, up_weight)
     for step in range(STEPS):
-        for low, size in stages:
-            group_rows = sumsq.shape[0] // size
-            blocks = [sumsq[i * group_rows : (i + 1) * group_rows] for i in range(size)]
-            sumsq = blocks[0] + sum(scatter_stage(low, size, blocks[1:]))
-        change = None
-        for first, width in chunks:
+        change = scale = None
+        for c, (first, width) in enumerate(chunks):
             low, size = stages[0]
-            keep, *sends = gate_up(first, width, per, size, base, x, gate_weight, up_weight)
+            fresh = c not in gates
+            found = gate_up(
+                first, width, per, size, base, x, sumsq if c == 0 else None,
+                (gate_weight, up_weight) if fresh else gates[c], fresh,
+            )
+            keep, *sends = found[:size]
+            if fresh:
+                gates[c] = found[size:]
             arrived = scatter_stage(low, size, sends)
             for low, size in stages[1:]:
-                keep, *sends = add_stage(keep, arrived, size)
+                keep, *sends = add_stage(keep, width, arrived, size)
                 arrived = scatter_stage(low, size, sends)
-            parts = [hidden_of(keep, arrived, sumsq, features)]
+            made = hidden_of(keep, width, arrived, scale, features)
+            parts = [made[0]]
+            if scale is None:
+                scale = made[1]
             for low, size in reversed(stages):
                 whole = parts[0] if len(parts) == 1 else join(parts)
                 parts = [whole] + [swap(whole, "wide", i << low, wide) for i in range(1, size)]
-            change = down(first, base, parts, down_weight, change)
+            fresh = c not in downs
+            found = down(first, base, parts, down_weight if fresh else downs[c], change, fresh)
+            change = found[0]
+            if fresh:
+                downs[c] = found[1]
         other = swap(change, "ffn", 1, ffn)
         if step + 1 < STEPS:
             shape = state.shape
@@ -327,6 +421,7 @@
                 in_specs=[VMEM] * 3,
                 out_specs=(VMEM,) * 2,
                 name="chip_sum",
+                compiler_params=pltpu.CompilerParams(vmem_limit_bytes=8 * MIB),
                 cost_estimate=cost(state.size, state.size * 16),
             )(change, other, state)
             arrived = [from_group(send, k) for k in range(1, groups)]
@@ -336,6 +431,7 @@
                 in_specs=[VMEM] * (1 + len(arrived)),
                 out_specs=(VMEM,) * 3,
                 name="renew",
+                compiler_params=pltpu.CompilerParams(vmem_limit_bytes=8 * MIB),
                 cost_estimate=cost(state.size, state.size * 12),
             )(state, *arrived)
     own = struct(tokens.shape, F32)
@@ -346,6 +442,7 @@
         out_specs=(VMEM,) * groups,
         scratch_shapes=[pltpu.VMEM(state.shape, F32)] * 2,
         name="finish",
+        compiler_params=pltpu.CompilerParams(vmem_limit_bytes=8 * MIB),
         cost_estimate=cost(state.size, state.size * 16),
     )(where, change, other, state)
     for k, send in enumerate(sends):

time: 167 us -> 135 us (0.81)
  starting transfers between devices: 73.3 us -> 51.6 us
  Pallas kernels: 43.1 us -> 31.1 us
  waiting for transfers between devices: 43.2 us -> 50.7 us
  local copies, waits for them, and re-layouts: 4.51 us -> 0.01 us
    ppermute x42 -> x34, starting transfers between devices: 66.7 us -> 47.2 us  [swap(): return lax.ppermute(value, axis, [(i, i ^ flip) for i in range(count)])]
    ppermute x42 -> x34, waiting for transfers between devices: 34.7 us -> 42.2 us  [swap(): return lax.ppermute(value, axis, [(i, i ^ flip) for i in range(count)])]
    pallas_call x16 -> x17, Pallas kernels: 35.8 us -> 29.6 us  [the longest x4 13 us: gate_up(): pl.pallas_call(functools.partial(gate_up_kernel, first, per, size, fresh,...]
    unnamed x20 -> x2, local copies, waits for them, and re-layouts: 4.5 us -> 0.01 us
    ppermute x3, starting transfers between devices: 6.52 us -> 4.41 us  [from_group(): lax.ppermute(value, 'groups', [((i + k) % groups, i) for i in range(group...]
    pallas_call x1, Pallas kernels: 1.9 us -> 0.05 us  [per_device(): pl.pallas_call(chip_kernel, out_shape=(struct(shape, F32), struct(shape,...]
    pallas_call x1, Pallas kernels: 1.79 us -> 0.12 us  [per_device(): pl.pallas_call(renew_kernel, out_shape=(struct(shape, F32), struct(shape,...]
  transfers between devices with their start and end apart: 45 -> 37, of which waited for: 19 -> 18; matrix products, arithmetic and copies ran while one was open for 0% -> 0% of each run, Pallas kernels for 11% -> 15%
where the time goes in v2:
time: 135 us; the launch traced here: 134 us
  starting transfers between devices  51.6 us (38%)
  waiting for transfers between devices  50.7 us (38%)
  Pallas kernels  31.1 us (23%)
    ppermute x34, starting transfers between devices, swap(): return lax.ppermute(value, axis, [(i, i ^ flip) for i in range(count)])  47.2 us
    ppermute x34, waiting for transfers between devices, swap(): return lax.ppermute(value, axis, [(i, i ^ flip) for i in range(count)])  42.2 us
    pallas_call x4, Pallas kernels, gate_up(): pl.pallas_call(functools.partial(gate_up_kernel, first, per, size, fresh,...  13 us
    pallas_call x4, Pallas kernels, down(): pl.pallas_call(functools.partial(down_kernel, first, len(parts), added, f...  9.14 us
    ppermute x3, waiting for transfers between devices, from_group(): lax.ppermute(value, 'groups', [((i + k) % groups, i) for i in range(group...  8.47 us
    pallas_call x1, Pallas kernels, load(): pl.pallas_call(functools.partial(load_kernel, first), out_shape=(shape,)...  5.03 us
    ppermute x3, starting transfers between devices, from_group(): lax.ppermute(value, 'groups', [((i + k) % groups, i) for i in range(group...  4.41 us
  transfers between devices with their start and end apart: 37, of which 18 were waited for; matrix products, arithmetic and copies ran while one was open for 0% of the time, Pallas kernels for 15%

profile of v2, /device:TPU:0, one launch (start us, length us, event | category | flops | bytes accessed | tf_op | source)
XLA Modules:
  0.0 134.4 jit_solution(17518902208860913481)
XLA Ops:
  0.0 2.9 %collective-permute-start = (bf16[32,1024]{1,0:T(8,128)(2,1)}, bf16[32,1024]{1,0:T(8,128)(2,1)S(1)}, u32[]{:S(2)}, u32[]{:S(2)}) collective-permute-start(bf16[32,1024]{1,0:T(8,128)(2,1)} %own_ref.1), channel_id=1, source_target_pairs={{16,0},{0,16},{17,1},{1,17},{18,2},{2,18},{19,3},{3,19},{20,4},{4,... | collective-permute-start | bytes 196616 | tf_op jit(solution)/shard_map/ppermute | solution.py:376
  2.9 5.0 %load.1 = (bf16[1024,3328]{1,0:T(8,128)(2,1)S(1)}, bf16[1024,3328]{1,0:T(8,128)(2,1)S(1)}) custom-call(s32[1]{0:T(128)} %bitcast.2.base_ref, bf16[1024,13312]{1,0:T(8,128)(2,1)} %gate_hbm.1, bf16[1024,13312]{1,0:T(8,128)(2,1)} %up_hbm.1), custom_call_target="tpu_custom_call" | custom-call | bytes 13631488 | tf_op jit(solution)/shard_map/load/pallas_call | solution.py:141
  8.7 2.5 %gate_up.5 = (f32[4,16,3456]{2,1,0:T(8,128)S(1)}, bf16[4,16,3456]{2,1,0:T(8,128)(2,1)S(1)}) custom-call(s32[1]{0:T(128)} %bitcast.2.base_ref, bf16[64,1024]{1,0:T(8,128)(2,1)S(1)} %get-tuple-element.51.x_ref, f32[64,128]{1,0:T(8,128)S(1)} %get-tuple-element.58.refs_0_, bf16[1024,3328]{1,0:T(8,128)(2,1)S(1)} %get-tuple-element.59.refs_1_, ...), custom_call_target="tpu_custom_call" | custom-call | flops 872415232 | bytes 13631488 | tf_op jit(solution)/shard_map/gate_up/pallas_call | solution.py:192
  11.2 1.6 %collective-permute-start.5 = (bf16[4,16,3456]{2,1,0:T(8,128)(2,1)S(1)}, bf16[4,16,3456]{2,1,0:T(8,128)(2,1)S(1)}, u32[]{:S(2)}, u32[]{:S(2)}) collective-permute-start(bf16[4,16,3456]{2,1,0:T(8,128)(2,1)S(1)} %get-tuple-element.62), channel_id=1, source_target_pairs={{0,2},{2,0},{4,6},{6,4},{8,10},{10,8},{12,14},{14,12},{1,3},{3,1},... | collective-permute-start | bytes 1327112 | tf_op jit(solution)/shard_map/ppermute | solution.py:52
  12.8 5.5 %gate_up.4 = (f32[4,16,3328]{2,1,0:T(8,128)S(1)}, bf16[4,16,3328]{2,1,0:T(8,128)(2,1)S(1)}, bf16[1024,3328]{1,0:T(8,128)(2,1)S(1)}, bf16[1024,3328]{1,0:T(8,128)(2,1)S(1)}) custom-call(s32[1]{0:T(128)} %bitcast.2.base_ref, bf16[64,1024]{1,0:T(8,128)(2,1)S(1)} %get-tuple-element.51.x_ref, bf16[1024,13312]{1,0:T(8,128)(2,1)} %gate_hbm.1, ...), custom_call_target="tpu_custom_call" | custom-call | flops 872415232 | bytes 13631488 | tf_op jit(solution)/shard_map/gate_up/pallas_call | solution.py:192
  18.8 5.5 %collective-permute-done.5.refs_0_ = bf16[4,16,3456]{2,1,0:T(8,128)(2,1)S(1)} collective-permute-done((bf16[4,16,3456]{2,1,0:T(8,128)(2,1)S(1)}, bf16[4,16,3456]{2,1,0:T(8,128)(2,1)S(1)}, u32[]{:S(2)}, u32[]{:S(2)}) %collective-permute-start.5) | collective-permute-done | bytes 442400 | tf_op jit(solution)/shard_map/ppermute | solution.py:52
  24.9 1.6 %collective-permute-start.6 = (bf16[1,16,3456]{2,1,0:T(8,128)(2,1)S(1)}, bf16[1,16,3456]{2,1,0:T(8,128)(2,1)S(1)}, u32[]{:S(2)}, u32[]{:S(2)}) collective-permute-start(bf16[1,16,3456]{2,1,0:T(8,128)(2,1)S(1)} %get-tuple-element.64), channel_id=1, source_target_pairs={{0,4},{2,6},{4,0},{6,2},{8,12},{10,14},{12,8},{14,10},{1,5},{3,7},... | collective-permute-start | bytes 331784 | tf_op jit(solution)/shard_map/ppermute | solution.py:52
  26.5 2.6 %collective-permute-start.7 = (bf16[1,16,3456]{2,1,0:T(8,128)(2,1)S(1)}, bf16[1,16,3456]{2,1,0:T(8,128)(2,1)S(1)}, u32[]{:S(2)}, u32[]{:S(2)}) collective-permute-start(bf16[1,16,3456]{2,1,0:T(8,128)(2,1)S(1)} %get-tuple-element.65), channel_id=1, source_target_pairs={{0,8},{2,10},{4,12},{6,14},{8,0},{10,2},{12,4},{14,6},{1,9},{3,11}... | collective-permute-start | bytes 331784 | tf_op jit(solution)/shard_map/ppermute | solution.py:52
  29.3 2.7 %collective-permute-done.1.refs_0_ = bf16[4,16,3328]{2,1,0:T(8,128)(2,1)S(1)} collective-permute-done((bf16[4,16,3328]{2,1,0:T(8,128)(2,1)S(1)}, bf16[4,16,3328]{2,1,0:T(8,128)(2,1)S(1)}, u32[]{:S(2)}, u32[]{:S(2)}) %collective-permute-start.1) | collective-permute-done | bytes 426016 | tf_op jit(solution)/shard_map/ppermute | solution.py:52
  32.3 1.6 %collective-permute-start.2 = (bf16[1,16,3328]{2,1,0:T(8,128)(2,1)S(1)}, bf16[1,16,3328]{2,1,0:T(8,128)(2,1)S(1)}, u32[]{:S(2)}, u32[]{:S(2)}) collective-permute-start(bf16[1,16,3328]{2,1,0:T(8,128)(2,1)S(1)} %get-tuple-element.55), channel_id=1, source_target_pairs={{0,4},{2,6},{4,0},{6,2},{8,12},{10,14},{12,8},{14,10},{1,5},{3,7},... | collective-permute-start | bytes 319496 | tf_op jit(solution)/shard_map/ppermute | solution.py:52
  33.9 2.6 %collective-permute-start.3 = (bf16[1,16,3328]{2,1,0:T(8,128)(2,1)S(1)}, bf16[1,16,3328]{2,1,0:T(8,128)(2,1)S(1)}, u32[]{:S(2)}, u32[]{:S(2)}) collective-permute-start(bf16[1,16,3328]{2,1,0:T(8,128)(2,1)S(1)} %get-tuple-element.56), channel_id=1, source_target_pairs={{0,8},{2,10},{4,12},{6,14},{8,0},{10,2},{12,4},{14,6},{1,9},{3,11}... | collective-permute-start | bytes 319496 | tf_op jit(solution)/shard_map/ppermute | solution.py:52
  37.0 3.7 %collective-permute-start.15 = (bf16[8,3328]{1,0:T(8,128)(2,1)S(1)}, bf16[8,3328]{1,0:T(8,128)(2,1)S(1)}, u32[]{:S(2)}, u32[]{:S(2)}) collective-permute-start(bf16[8,3328]{1,0:T(8,128)(2,1)S(1)} %get-tuple-element.68.refs_0_), channel_id=1, source_target_pairs={{0,12},{2,14},{4,8},{6,10},{8,4},{10,6},{12,0},{14,2},{1,13},{3,15... | collective-permute-start | bytes 159752 | tf_op jit(solution)/shard_map/ppermute | solution.py:52
  41.5 5.5 %collective-permute-done.3.refs_1_ = bf16[1,16,3328]{2,1,0:T(8,128)(2,1)S(1)} collective-permute-done((bf16[1,16,3328]{2,1,0:T(8,128)(2,1)S(1)}, bf16[1,16,3328]{2,1,0:T(8,128)(2,1)S(1)}, u32[]{:S(2)}, u32[]{:S(2)}) %collective-permute-start.3) | collective-permute-done | bytes 106528 | tf_op jit(solution)/shard_map/ppermute | solution.py:52
  47.2 2.9 %collective-permute-start.11 = (bf16[8,3328]{1,0:T(8,128)(2,1)S(1)}, bf16[8,3328]{1,0:T(8,128)(2,1)S(1)}, u32[]{:S(2)}, u32[]{:S(2)}) collective-permute-start(bf16[8,3328]{1,0:T(8,128)(2,1)S(1)} %hidden.5.refs_0_), channel_id=1, source_target_pairs={{0,12},{2,14},{4,8},{6,10},{8,4},{10,6},{12,0},{14,2},{1,13},{3,15... | collective-permute-start | bytes 159752 | tf_op jit(solution)/shard_map/ppermute | solution.py:52
  50.1 1.5 %collective-permute-start.10 = (bf16[8,3328]{1,0:T(8,128)(2,1)S(1)}, bf16[8,3328]{1,0:T(8,128)(2,1)S(1)}, u32[]{:S(2)}, u32[]{:S(2)}) collective-permute-start(bf16[8,3328]{1,0:T(8,128)(2,1)S(1)} %hidden.5.refs_0_), channel_id=1, source_target_pairs={{0,8},{2,10},{4,12},{6,14},{8,0},{10,2},{12,4},{14,6},{1,9},{3,11}... | collective-permute-start | bytes 159752 | tf_op jit(solution)/shard_map/ppermute | solution.py:52
  52.0 1.6 %collective-permute-start.16 = (bf16[32,3328]{1,0:T(8,128)(2,1)S(1)}, bf16[32,3328]{1,0:T(8,128)(2,1)S(1)}, u32[]{:S(2)}, u32[]{:S(2)}) collective-permute-start(bf16[32,3328]{1,0:T(8,128)(2,1)S(1)} %join.5.refs_0_), channel_id=1, source_target_pairs={{0,2},{2,0},{4,6},{6,4},{8,10},{10,8},{12,14},{14,12},{1,3},{3,1},... | collective-permute-start | bytes 638984 | tf_op jit(solution)/shard_map/ppermute | solution.py:52
  53.7 1.4 %collective-permute-done.10.refs_2_ = bf16[8,3328]{1,0:T(8,128)(2,1)S(1)} collective-permute-done((bf16[8,3328]{1,0:T(8,128)(2,1)S(1)}, bf16[8,3328]{1,0:T(8,128)(2,1)S(1)}, u32[]{:S(2)}, u32[]{:S(2)}) %collective-permute-start.10) | collective-permute-done | bytes 53280 | tf_op jit(solution)/shard_map/ppermute | solution.py:52
  55.7 1.6 %collective-permute-start.12 = (bf16[32,3328]{1,0:T(8,128)(2,1)S(1)}, bf16[32,3328]{1,0:T(8,128)(2,1)S(1)}, u32[]{:S(2)}, u32[]{:S(2)}) collective-permute-start(bf16[32,3328]{1,0:T(8,128)(2,1)S(1)} %join.4.refs_0_), channel_id=1, source_target_pairs={{0,2},{2,0},{4,6},{6,4},{8,10},{10,8},{12,14},{14,12},{1,3},{3,1},... | collective-permute-start | bytes 638984 | tf_op jit(solution)/shard_map/ppermute | solution.py:52
  57.3 2.2 %collective-permute-done.16.refs_1_ = bf16[32,3328]{1,0:T(8,128)(2,1)S(1)} collective-permute-done((bf16[32,3328]{1,0:T(8,128)(2,1)S(1)}, bf16[32,3328]{1,0:T(8,128)(2,1)S(1)}, u32[]{:S(2)}, u32[]{:S(2)}) %collective-permute-start.16) | collective-permute-done | bytes 213024 | tf_op jit(solution)/shard_map/ppermute | solution.py:52
  59.5 3.3 %down.4 = (f32[64,1024]{1,0:T(8,128)S(1)}, bf16[3328,1024]{1,0:T(8,128)(2,1)S(1)}) custom-call(s32[1]{0:T(128)} %bitcast.2.base_ref, bf16[32,3328]{1,0:T(8,128)(2,1)S(1)} %join.5.refs_0_, bf16[32,3328]{1,0:T(8,128)(2,1)S(1)} %collective-permute-done.16.refs_1_, bf16[13312,1024]{1,0:T(8,128)(2,1)} %refs_2_.3), custom_call_target="tpu_custom_call" | custom-call | flops 436207616 | bytes 6815744 | tf_op jit(solution)/shard_map/down/pallas_call | solution.py:315
  62.8 3.3 %down.5 = (f32[64,1024]{1,0:T(8,128)S(1)}, bf16[3328,1024]{1,0:T(8,128)(2,1)S(1)}) custom-call(s32[1]{0:T(128)} %bitcast.2.base_ref, bf16[32,3328]{1,0:T(8,128)(2,1)S(1)} %join.4.refs_0_, bf16[32,3328]{1,0:T(8,128)(2,1)S(1)} %collective-permute-done.12.refs_1_, bf16[13312,1024]{1,0:T(8,128)(2,1)} %refs_2_.3, f32[64,1024]{1,0:T(8,128)S(1)} %get-tuple-element.69.refs_3_), custom_call_target="tpu_custom_call" | custom-call | flops 436207616 | bytes 6815744 | tf_op jit(solution)/shard_map/down/pallas_call | solution.py:315
  66.2 1.5 %collective-permute-done.17.b_ref = f32[64,1024]{1,0:T(8,128)S(1)} collective-permute-done((f32[64,1024]{1,0:T(8,128)S(1)}, f32[64,1024]{1,0:T(8,128)S(1)}, u32[]{:S(2)}, u32[]{:S(2)}) %collective-permute-start.17) | collective-permute-done | bytes 262176 | tf_op jit(solution)/shard_map/ppermute | solution.py:52
  68.5 4.9 %collective-permute-done.18.refs_0_ = bf16[64,1024]{1,0:T(8,128)(2,1)S(1)} collective-permute-done((bf16[64,1024]{1,0:T(8,128)(2,1)S(1)}, bf16[64,1024]{1,0:T(8,128)(2,1)S(1)}, u32[]{:S(2)}, u32[]{:S(2)}) %collective-permute-start.18) | collective-permute-done | bytes 131104 | tf_op jit(solution)/shard_map/ppermute | solution.py:376
  73.5 2.5 %gate_up.7 = (f32[4,16,3456]{2,1,0:T(8,128)S(1)}, bf16[4,16,3456]{2,1,0:T(8,128)(2,1)S(1)}) custom-call(s32[1]{0:T(128)} %bitcast.2.base_ref, bf16[64,1024]{1,0:T(8,128)(2,1)S(1)} %get-tuple-element.74.x_ref, f32[64,128]{1,0:T(8,128)S(1)} %get-tuple-element.83.refs_0_, bf16[1024,3328]{1,0:T(8,128)(2,1)S(1)} %get-tuple-element.59.refs_1_, ...), custom_call_target="tpu_custom_call" | custom-call | flops 872415232 | bytes 13631488 | tf_op jit(solution)/shard_map/gate_up/pallas_call | solution.py:192
  76.0 1.6 %collective-permute-start.23 = (bf16[4,16,3456]{2,1,0:T(8,128)(2,1)S(1)}, bf16[4,16,3456]{2,1,0:T(8,128)(2,1)S(1)}, u32[]{:S(2)}, u32[]{:S(2)}) collective-permute-start(bf16[4,16,3456]{2,1,0:T(8,128)(2,1)S(1)} %get-tuple-element.85), channel_id=1, source_target_pairs={{0,2},{2,0},{4,6},{6,4},{8,10},{10,8},{12,14},{14,12},{1,3},{3,1},... | collective-permute-start | bytes 1327112 | tf_op jit(solution)/shard_map/ppermute | solution.py:52
  77.5 2.6 %gate_up.6 = (f32[4,16,3328]{2,1,0:T(8,128)S(1)}, bf16[4,16,3328]{2,1,0:T(8,128)(2,1)S(1)}) custom-call(s32[1]{0:T(128)} %bitcast.2.base_ref, bf16[64,1024]{1,0:T(8,128)(2,1)S(1)} %get-tuple-element.74.x_ref, bf16[1024,3328]{1,0:T(8,128)(2,1)S(1)} %get-tuple-element.75.refs_0_, bf16[1024,3328]{1,0:T(8,128)(2,1)S(1)} %get-tuple-element.76.refs_1_), custom_call_target="tpu_custom_call" | custom-call | flops 872415232 | bytes 13631488 | tf_op jit(solution)/shard_map/gate_up/pallas_call | solution.py:192
  80.8 8.4 %collective-permute-done.23.refs_0_ = bf16[4,16,3456]{2,1,0:T(8,128)(2,1)S(1)} collective-permute-done((bf16[4,16,3456]{2,1,0:T(8,128)(2,1)S(1)}, bf16[4,16,3456]{2,1,0:T(8,128)(2,1)S(1)}, u32[]{:S(2)}, u32[]{:S(2)}) %collective-permute-start.23) | collective-permute-done | bytes 442400 | tf_op jit(solution)/shard_map/ppermute | solution.py:52
  89.6 1.1 collective-permute-start.24
  90.8 1.9 %collective-permute-start.25 = (bf16[1,16,3456]{2,1,0:T(8,128)(2,1)S(1)}, bf16[1,16,3456]{2,1,0:T(8,128)(2,1)S(1)}, u32[]{:S(2)}, u32[]{:S(2)}) collective-permute-start(bf16[1,16,3456]{2,1,0:T(8,128)(2,1)S(1)} %get-tuple-element.88), channel_id=1, source_target_pairs={{0,8},{2,10},{4,12},{6,14},{8,0},{10,2},{12,4},{14,6},{1,9},{3,11}... | collective-permute-start | bytes 331784 | tf_op jit(solution)/shard_map/ppermute | solution.py:52
  92.7 1.4 %collective-permute-start.26 = (bf16[1,16,3456]{2,1,0:T(8,128)(2,1)S(1)}, bf16[1,16,3456]{2,1,0:T(8,128)(2,1)S(1)}, u32[]{:S(2)}, u32[]{:S(2)}) collective-permute-start(bf16[1,16,3456]{2,1,0:T(8,128)(2,1)S(1)} %get-tuple-element.89), channel_id=1, source_target_pairs={{0,12},{2,14},{4,8},{6,10},{8,4},{10,6},{12,0},{14,2},{1,13},{3,15... | collective-permute-start | bytes 331784 | tf_op jit(solution)/shard_map/ppermute | solution.py:52
  94.1 2.5 %collective-permute-done.19.refs_0_ = bf16[4,16,3328]{2,1,0:T(8,128)(2,1)S(1)} collective-permute-done((bf16[4,16,3328]{2,1,0:T(8,128)(2,1)S(1)}, bf16[4,16,3328]{2,1,0:T(8,128)(2,1)S(1)}, u32[]{:S(2)}, u32[]{:S(2)}) %collective-permute-start.19) | collective-permute-done | bytes 426016 | tf_op jit(solution)/shard_map/ppermute | solution.py:52
  96.8 1.1 collective-permute-start.20
  97.9 1.9 %collective-permute-start.21 = (bf16[1,16,3328]{2,1,0:T(8,128)(2,1)S(1)}, bf16[1,16,3328]{2,1,0:T(8,128)(2,1)S(1)}, u32[]{:S(2)}, u32[]{:S(2)}) collective-permute-start(bf16[1,16,3328]{2,1,0:T(8,128)(2,1)S(1)} %get-tuple-element.81), channel_id=1, source_target_pairs={{0,8},{2,10},{4,12},{6,14},{8,0},{10,2},{12,4},{14,6},{1,9},{3,11}... | collective-permute-start | bytes 319496 | tf_op jit(solution)/shard_map/ppermute | solution.py:52
  99.8 1.4 %collective-permute-start.22 = (bf16[1,16,3328]{2,1,0:T(8,128)(2,1)S(1)}, bf16[1,16,3328]{2,1,0:T(8,128)(2,1)S(1)}, u32[]{:S(2)}, u32[]{:S(2)}) collective-permute-start(bf16[1,16,3328]{2,1,0:T(8,128)(2,1)S(1)} %get-tuple-element.82), channel_id=1, source_target_pairs={{0,12},{2,14},{4,8},{6,10},{8,4},{10,6},{12,0},{14,2},{1,13},{3,15... | collective-permute-start | bytes 319496 | tf_op jit(solution)/shard_map/ppermute | solution.py:52
  101.5 2.5 %collective-permute-start.33 = (bf16[8,3328]{1,0:T(8,128)(2,1)S(1)}, bf16[8,3328]{1,0:T(8,128)(2,1)S(1)}, u32[]{:S(2)}, u32[]{:S(2)}) collective-permute-start(bf16[8,3328]{1,0:T(8,128)(2,1)S(1)} %get-tuple-element.92.refs_0_), channel_id=1, source_target_pairs={{0,12},{2,14},{4,8},{6,10},{8,4},{10,6},{12,0},{14,2},{1,13},{3,15... | collective-permute-start | bytes 159752 | tf_op jit(solution)/shard_map/ppermute | solution.py:52
  104.2 1.8 %collective-permute-start.31 = (bf16[8,3328]{1,0:T(8,128)(2,1)S(1)}, bf16[8,3328]{1,0:T(8,128)(2,1)S(1)}, u32[]{:S(2)}, u32[]{:S(2)}) collective-permute-start(bf16[8,3328]{1,0:T(8,128)(2,1)S(1)} %get-tuple-element.92.refs_0_), channel_id=1, source_target_pairs={{0,4},{2,6},{4,0},{6,2},{8,12},{10,14},{12,8},{14,10},{1,5},{3,7},... | collective-permute-start | bytes 159752 | tf_op jit(solution)/shard_map/ppermute | solution.py:52
  106.0 4.2 %collective-permute-done.21.refs_1_ = bf16[1,16,3328]{2,1,0:T(8,128)(2,1)S(1)} collective-permute-done((bf16[1,16,3328]{2,1,0:T(8,128)(2,1)S(1)}, bf16[1,16,3328]{2,1,0:T(8,128)(2,1)S(1)}, u32[]{:S(2)}, u32[]{:S(2)}) %collective-permute-start.21) | collective-permute-done | bytes 106528 | tf_op jit(solution)/shard_map/ppermute | solution.py:52
  110.5 2.0 %collective-permute-start.29 = (bf16[8,3328]{1,0:T(8,128)(2,1)S(1)}, bf16[8,3328]{1,0:T(8,128)(2,1)S(1)}, u32[]{:S(2)}, u32[]{:S(2)}) collective-permute-start(bf16[8,3328]{1,0:T(8,128)(2,1)S(1)} %hidden.7.refs_0_), channel_id=1, source_target_pairs={{0,12},{2,14},{4,8},{6,10},{8,4},{10,6},{12,0},{14,2},{1,13},{3,15... | collective-permute-start | bytes 159752 | tf_op jit(solution)/shard_map/ppermute | solution.py:52
  112.5 2.9 %collective-permute-start.28 = (bf16[8,3328]{1,0:T(8,128)(2,1)S(1)}, bf16[8,3328]{1,0:T(8,128)(2,1)S(1)}, u32[]{:S(2)}, u32[]{:S(2)}) collective-permute-start(bf16[8,3328]{1,0:T(8,128)(2,1)S(1)} %hidden.7.refs_0_), channel_id=1, source_target_pairs={{0,8},{2,10},{4,12},{6,14},{8,0},{10,2},{12,4},{14,6},{1,9},{3,11}... | collective-permute-start | bytes 159752 | tf_op jit(solution)/shard_map/ppermute | solution.py:52
  115.4 1.6 %collective-permute-start.34 = (bf16[32,3328]{1,0:T(8,128)(2,1)S(1)}, bf16[32,3328]{1,0:T(8,128)(2,1)S(1)}, u32[]{:S(2)}, u32[]{:S(2)}) collective-permute-start(bf16[32,3328]{1,0:T(8,128)(2,1)S(1)} %join.7.refs_0_), channel_id=1, source_target_pairs={{0,2},{2,0},{4,6},{6,4},{8,10},{10,8},{12,14},{14,12},{1,3},{3,1},... | collective-permute-start | bytes 638984 | tf_op jit(solution)/shard_map/ppermute | solution.py:52
  117.0 1.1 collective-permute-done.28.refs_2_
  118.1 1.4 %collective-permute-done.27.refs_1_ = bf16[8,3328]{1,0:T(8,128)(2,1)S(1)} collective-permute-done((bf16[8,3328]{1,0:T(8,128)(2,1)S(1)}, bf16[8,3328]{1,0:T(8,128)(2,1)S(1)}, u32[]{:S(2)}, u32[]{:S(2)}) %collective-permute-start.27) | collective-permute-done | bytes 53280 | tf_op jit(solution)/shard_map/ppermute | solution.py:52
  119.5 1.6 %collective-permute-start.30 = (bf16[32,3328]{1,0:T(8,128)(2,1)S(1)}, bf16[32,3328]{1,0:T(8,128)(2,1)S(1)}, u32[]{:S(2)}, u32[]{:S(2)}) collective-permute-start(bf16[32,3328]{1,0:T(8,128)(2,1)S(1)} %join.6.refs_0_), channel_id=1, source_target_pairs={{0,2},{2,0},{4,6},{6,4},{8,10},{10,8},{12,14},{14,12},{1,3},{3,1},... | collective-permute-start | bytes 638984 | tf_op jit(solution)/shard_map/ppermute | solution.py:52
  121.1 2.5 %collective-permute-done.34.refs_1_ = bf16[32,3328]{1,0:T(8,128)(2,1)S(1)} collective-permute-done((bf16[32,3328]{1,0:T(8,128)(2,1)S(1)}, bf16[32,3328]{1,0:T(8,128)(2,1)S(1)}, u32[]{:S(2)}, u32[]{:S(2)}) %collective-permute-start.34) | collective-permute-done | bytes 213024 | tf_op jit(solution)/shard_map/ppermute | solution.py:52
  123.6 1.3 down.6.refs_3_
  125.9 1.3 down.7.a_ref
  127.3 1.5 %collective-permute-done.35.b_ref = f32[64,1024]{1,0:T(8,128)S(1)} collective-permute-done((f32[64,1024]{1,0:T(8,128)S(1)}, f32[64,1024]{1,0:T(8,128)S(1)}, u32[]{:S(2)}, u32[]{:S(2)}) %collective-permute-start.35) | collective-permute-done | bytes 262176 | tf_op jit(solution)/shard_map/ppermute | solution.py:52
  130.2 3.6 %collective-permute-done.36 = bf16[32,1024]{1,0:T(8,128)(2,1)S(1)} collective-permute-done((bf16[32,1024]{1,0:T(8,128)(2,1)S(1)}, bf16[32,1024]{1,0:T(8,128)(2,1)S(1)}, u32[]{:S(2)}, u32[]{:S(2)}) %collective-permute-start.36) | collective-permute-done | bytes 65568 | tf_op jit(solution)/shard_map/ppermute | solution.py:376
  (55 shorter events, 11.1 us)
Async XLA Ops:
  0.0 8.1 %collective-permute-start = (bf16[32,1024]{1,0:T(8,128)(2,1)}, bf16[32,1024]{1,0:T(8,128)(2,1)S(1)}, u32[]{:S(2)}, u32[]{:S(2)}) collective-permute-start(bf16[32,1024]{1,0:T(8,128)(2,1)} %own_ref.1), channel_id=1, source_target_pairs={{16,0},{0,16},{17,1},{1,17},{18,2},{2,18},{19,3},{3,19},{20,4},{4,... | collective-permute-start | bytes 196616 | tf_op jit(solution)/shard_map/ppermute | solution.py:376
  2.9 5.1 %copy-start = (bf16[32,1024]{1,0:T(8,128)(2,1)S(1)}, bf16[32,1024]{1,0:T(8,128)(2,1)}, u32[]{:S(2)}) copy-start(bf16[32,1024]{1,0:T(8,128)(2,1)} %own_ref.1) | copy-start | bytes 196612
  11.2 13.2 %collective-permute-start.5 = (bf16[4,16,3456]{2,1,0:T(8,128)(2,1)S(1)}, bf16[4,16,3456]{2,1,0:T(8,128)(2,1)S(1)}, u32[]{:S(2)}, u32[]{:S(2)}) collective-permute-start(bf16[4,16,3456]{2,1,0:T(8,128)(2,1)S(1)} %get-tuple-element.62), channel_id=1, source_target_pairs={{0,2},{2,0},{4,6},{6,4},{8,10},{10,8},{12,14},{14,12},{1,3},{3,1},... | collective-permute-start | bytes 1327112 | tf_op jit(solution)/shard_map/ppermute | solution.py:52
  18.3 13.8 %collective-permute-start.1 = (bf16[4,16,3328]{2,1,0:T(8,128)(2,1)S(1)}, bf16[4,16,3328]{2,1,0:T(8,128)(2,1)S(1)}, u32[]{:S(2)}, u32[]{:S(2)}) collective-permute-start(bf16[4,16,3328]{2,1,0:T(8,128)(2,1)S(1)} %get-tuple-element.53), channel_id=1, source_target_pairs={{0,2},{2,0},{4,6},{6,4},{8,10},{10,8},{12,14},{14,12},{1,3},{3,1},... | collective-permute-start | bytes 1277960 | tf_op jit(solution)/shard_map/ppermute | solution.py:52
  24.9 11.6 %collective-permute-start.6 = (bf16[1,16,3456]{2,1,0:T(8,128)(2,1)S(1)}, bf16[1,16,3456]{2,1,0:T(8,128)(2,1)S(1)}, u32[]{:S(2)}, u32[]{:S(2)}) collective-permute-start(bf16[1,16,3456]{2,1,0:T(8,128)(2,1)S(1)} %get-tuple-element.64), channel_id=1, source_target_pairs={{0,4},{2,6},{4,0},{6,2},{8,12},{10,14},{12,8},{14,10},{1,5},{3,7},... | collective-permute-start | bytes 331784 | tf_op jit(solution)/shard_map/ppermute | solution.py:52
  26.5 10.2 %collective-permute-start.7 = (bf16[1,16,3456]{2,1,0:T(8,128)(2,1)S(1)}, bf16[1,16,3456]{2,1,0:T(8,128)(2,1)S(1)}, u32[]{:S(2)}, u32[]{:S(2)}) collective-permute-start(bf16[1,16,3456]{2,1,0:T(8,128)(2,1)S(1)} %get-tuple-element.65), channel_id=1, source_target_pairs={{0,8},{2,10},{4,12},{6,14},{8,0},{10,2},{12,4},{14,6},{1,9},{3,11}... | collective-permute-start | bytes 331784 | tf_op jit(solution)/shard_map/ppermute | solution.py:52
  29.1 7.6 %collective-permute-start.8 = (bf16[1,16,3456]{2,1,0:T(8,128)(2,1)S(1)}, bf16[1,16,3456]{2,1,0:T(8,128)(2,1)S(1)}, u32[]{:S(2)}, u32[]{:S(2)}) collective-permute-start(bf16[1,16,3456]{2,1,0:T(8,128)(2,1)S(1)} %get-tuple-element.66), channel_id=1, source_target_pairs={{0,12},{2,14},{4,8},{6,10},{8,4},{10,6},{12,0},{14,2},{1,13},{3,15... | collective-permute-start | bytes 331784 | tf_op jit(solution)/shard_map/ppermute | solution.py:52
  32.3 8.4 %collective-permute-start.2 = (bf16[1,16,3328]{2,1,0:T(8,128)(2,1)S(1)}, bf16[1,16,3328]{2,1,0:T(8,128)(2,1)S(1)}, u32[]{:S(2)}, u32[]{:S(2)}) collective-permute-start(bf16[1,16,3328]{2,1,0:T(8,128)(2,1)S(1)} %get-tuple-element.55), channel_id=1, source_target_pairs={{0,4},{2,6},{4,0},{6,2},{8,12},{10,14},{12,8},{14,10},{1,5},{3,7},... | collective-permute-start | bytes 319496 | tf_op jit(solution)/shard_map/ppermute | solution.py:52
  33.9 13.1 %collective-permute-start.3 = (bf16[1,16,3328]{2,1,0:T(8,128)(2,1)S(1)}, bf16[1,16,3328]{2,1,0:T(8,128)(2,1)S(1)}, u32[]{:S(2)}, u32[]{:S(2)}) collective-permute-start(bf16[1,16,3328]{2,1,0:T(8,128)(2,1)S(1)} %get-tuple-element.56), channel_id=1, source_target_pairs={{0,8},{2,10},{4,12},{6,14},{8,0},{10,2},{12,4},{14,6},{1,9},{3,11}... | collective-permute-start | bytes 319496 | tf_op jit(solution)/shard_map/ppermute | solution.py:52
  36.5 10.5 %collective-permute-start.4 = (bf16[1,16,3328]{2,1,0:T(8,128)(2,1)S(1)}, bf16[1,16,3328]{2,1,0:T(8,128)(2,1)S(1)}, u32[]{:S(2)}, u32[]{:S(2)}) collective-permute-start(bf16[1,16,3328]{2,1,0:T(8,128)(2,1)S(1)} %get-tuple-element.57), channel_id=1, source_target_pairs={{0,12},{2,14},{4,8},{6,10},{8,4},{10,6},{12,0},{14,2},{1,13},{3,15... | collective-permute-start | bytes 319496 | tf_op jit(solution)/shard_map/ppermute | solution.py:52
  37.0 14.5 %collective-permute-start.15 = (bf16[8,3328]{1,0:T(8,128)(2,1)S(1)}, bf16[8,3328]{1,0:T(8,128)(2,1)S(1)}, u32[]{:S(2)}, u32[]{:S(2)}) collective-permute-start(bf16[8,3328]{1,0:T(8,128)(2,1)S(1)} %get-tuple-element.68.refs_0_), channel_id=1, source_target_pairs={{0,12},{2,14},{4,8},{6,10},{8,4},{10,6},{12,0},{14,2},{1,13},{3,15... | collective-permute-start | bytes 159752 | tf_op jit(solution)/shard_map/ppermute | solution.py:52
  40.7 11.3 %collective-permute-start.14 = (bf16[8,3328]{1,0:T(8,128)(2,1)S(1)}, bf16[8,3328]{1,0:T(8,128)(2,1)S(1)}, u32[]{:S(2)}, u32[]{:S(2)}) collective-permute-start(bf16[8,3328]{1,0:T(8,128)(2,1)S(1)} %get-tuple-element.68.refs_0_), channel_id=1, source_target_pairs={{0,8},{2,10},{4,12},{6,14},{8,0},{10,2},{12,4},{14,6},{1,9},{3,11}... | collective-permute-start | bytes 159752 | tf_op jit(solution)/shard_map/ppermute | solution.py:52
  40.7 11.3 %collective-permute-start.13 = (bf16[8,3328]{1,0:T(8,128)(2,1)S(1)}, bf16[8,3328]{1,0:T(8,128)(2,1)S(1)}, u32[]{:S(2)}, u32[]{:S(2)}) collective-permute-start(bf16[8,3328]{1,0:T(8,128)(2,1)S(1)} %get-tuple-element.68.refs_0_), channel_id=1, source_target_pairs={{0,4},{2,6},{4,0},{6,2},{8,12},{10,14},{12,8},{14,10},{1,5},{3,7},... | collective-permute-start | bytes 159752 | tf_op jit(solution)/shard_map/ppermute | solution.py:52
  47.2 6.5 %collective-permute-start.11 = (bf16[8,3328]{1,0:T(8,128)(2,1)S(1)}, bf16[8,3328]{1,0:T(8,128)(2,1)S(1)}, u32[]{:S(2)}, u32[]{:S(2)}) collective-permute-start(bf16[8,3328]{1,0:T(8,128)(2,1)S(1)} %hidden.5.refs_0_), channel_id=1, source_target_pairs={{0,12},{2,14},{4,8},{6,10},{8,4},{10,6},{12,0},{14,2},{1,13},{3,15... | collective-permute-start | bytes 159752 | tf_op jit(solution)/shard_map/ppermute | solution.py:52
  50.1 5.0 %collective-permute-start.10 = (bf16[8,3328]{1,0:T(8,128)(2,1)S(1)}, bf16[8,3328]{1,0:T(8,128)(2,1)S(1)}, u32[]{:S(2)}, u32[]{:S(2)}) collective-permute-start(bf16[8,3328]{1,0:T(8,128)(2,1)S(1)} %hidden.5.refs_0_), channel_id=1, source_target_pairs={{0,8},{2,10},{4,12},{6,14},{8,0},{10,2},{12,4},{14,6},{1,9},{3,11}... | collective-permute-start | bytes 159752 | tf_op jit(solution)/shard_map/ppermute | solution.py:52
  51.6 4.1 %collective-permute-start.9 = (bf16[8,3328]{1,0:T(8,128)(2,1)S(1)}, bf16[8,3328]{1,0:T(8,128)(2,1)S(1)}, u32[]{:S(2)}, u32[]{:S(2)}) collective-permute-start(bf16[8,3328]{1,0:T(8,128)(2,1)S(1)} %hidden.5.refs_0_), channel_id=1, source_target_pairs={{0,4},{2,6},{4,0},{6,2},{8,12},{10,14},{12,8},{14,10},{1,5},{3,7},... | collective-permute-start | bytes 159752 | tf_op jit(solution)/shard_map/ppermute | solution.py:52
  52.0 7.6 %collective-permute-start.16 = (bf16[32,3328]{1,0:T(8,128)(2,1)S(1)}, bf16[32,3328]{1,0:T(8,128)(2,1)S(1)}, u32[]{:S(2)}, u32[]{:S(2)}) collective-permute-start(bf16[32,3328]{1,0:T(8,128)(2,1)S(1)} %join.5.refs_0_), channel_id=1, source_target_pairs={{0,2},{2,0},{4,6},{6,4},{8,10},{10,8},{12,14},{14,12},{1,3},{3,1},... | collective-permute-start | bytes 638984 | tf_op jit(solution)/shard_map/ppermute | solution.py:52
  55.7 7.1 %collective-permute-start.12 = (bf16[32,3328]{1,0:T(8,128)(2,1)S(1)}, bf16[32,3328]{1,0:T(8,128)(2,1)S(1)}, u32[]{:S(2)}, u32[]{:S(2)}) collective-permute-start(bf16[32,3328]{1,0:T(8,128)(2,1)S(1)} %join.4.refs_0_), channel_id=1, source_target_pairs={{0,2},{2,0},{4,6},{6,4},{8,10},{10,8},{12,14},{14,12},{1,3},{3,1},... | collective-permute-start | bytes 638984 | tf_op jit(solution)/shard_map/ppermute | solution.py:52
  66.1 1.6 %collective-permute-start.17 = (f32[64,1024]{1,0:T(8,128)S(1)}, f32[64,1024]{1,0:T(8,128)S(1)}, u32[]{:S(2)}, u32[]{:S(2)}) collective-permute-start(f32[64,1024]{1,0:T(8,128)S(1)} %get-tuple-element.70.a_ref), channel_id=1, source_target_pairs={{0,1},{1,0},{2,3},{3,2},{4,5},{5,4},{6,7},{7,6},{8,9},{9,8},{10,11... | collective-permute-start | bytes 786440 | tf_op jit(solution)/shard_map/ppermute | solution.py:52
  67.8 5.6 %collective-permute-start.18 = (bf16[64,1024]{1,0:T(8,128)(2,1)S(1)}, bf16[64,1024]{1,0:T(8,128)(2,1)S(1)}, u32[]{:S(2)}, u32[]{:S(2)}) collective-permute-start(bf16[64,1024]{1,0:T(8,128)(2,1)S(1)} %get-tuple-element.73), channel_id=1, source_target_pairs={{16,0},{0,16},{17,1},{1,17},{18,2},{2,18},{19,3},{3,19},{20,4},{4,... | collective-permute-start | bytes 393224 | tf_op jit(solution)/shard_map/ppermute | solution.py:376
  76.0 13.2 %collective-permute-start.23 = (bf16[4,16,3456]{2,1,0:T(8,128)(2,1)S(1)}, bf16[4,16,3456]{2,1,0:T(8,128)(2,1)S(1)}, u32[]{:S(2)}, u32[]{:S(2)}) collective-permute-start(bf16[4,16,3456]{2,1,0:T(8,128)(2,1)S(1)} %get-tuple-element.85), channel_id=1, source_target_pairs={{0,2},{2,0},{4,6},{6,4},{8,10},{10,8},{12,14},{14,12},{1,3},{3,1},... | collective-permute-start | bytes 1327112 | tf_op jit(solution)/shard_map/ppermute | solution.py:52
  80.2 16.4 %collective-permute-start.19 = (bf16[4,16,3328]{2,1,0:T(8,128)(2,1)S(1)}, bf16[4,16,3328]{2,1,0:T(8,128)(2,1)S(1)}, u32[]{:S(2)}, u32[]{:S(2)}) collective-permute-start(bf16[4,16,3328]{2,1,0:T(8,128)(2,1)S(1)} %get-tuple-element.78), channel_id=1, source_target_pairs={{0,2},{2,0},{4,6},{6,4},{8,10},{10,8},{12,14},{14,12},{1,3},{3,1},... | collective-permute-start | bytes 1277960 | tf_op jit(solution)/shard_map/ppermute | solution.py:52
  89.6 10.2 %collective-permute-start.24 = (bf16[1,16,3456]{2,1,0:T(8,128)(2,1)S(1)}, bf16[1,16,3456]{2,1,0:T(8,128)(2,1)S(1)}, u32[]{:S(2)}, u32[]{:S(2)}) collective-permute-start(bf16[1,16,3456]{2,1,0:T(8,128)(2,1)S(1)} %get-tuple-element.87), channel_id=1, source_target_pairs={{0,4},{2,6},{4,0},{6,2},{8,12},{10,14},{12,8},{14,10},{1,5},{3,7},... | collective-permute-start | bytes 331784 | tf_op jit(solution)/shard_map/ppermute | solution.py:52
  90.8 10.5 %collective-permute-start.25 = (bf16[1,16,3456]{2,1,0:T(8,128)(2,1)S(1)}, bf16[1,16,3456]{2,1,0:T(8,128)(2,1)S(1)}, u32[]{:S(2)}, u32[]{:S(2)}) collective-permute-start(bf16[1,16,3456]{2,1,0:T(8,128)(2,1)S(1)} %get-tuple-element.88), channel_id=1, source_target_pairs={{0,8},{2,10},{4,12},{6,14},{8,0},{10,2},{12,4},{14,6},{1,9},{3,11}... | collective-permute-start | bytes 331784 | tf_op jit(solution)/shard_map/ppermute | solution.py:52
  92.7 8.6 %collective-permute-start.26 = (bf16[1,16,3456]{2,1,0:T(8,128)(2,1)S(1)}, bf16[1,16,3456]{2,1,0:T(8,128)(2,1)S(1)}, u32[]{:S(2)}, u32[]{:S(2)}) collective-permute-start(bf16[1,16,3456]{2,1,0:T(8,128)(2,1)S(1)} %get-tuple-element.89), channel_id=1, source_target_pairs={{0,12},{2,14},{4,8},{6,10},{8,4},{10,6},{12,0},{14,2},{1,13},{3,15... | collective-permute-start | bytes 331784 | tf_op jit(solution)/shard_map/ppermute | solution.py:52
  96.8 7.4 %collective-permute-start.20 = (bf16[1,16,3328]{2,1,0:T(8,128)(2,1)S(1)}, bf16[1,16,3328]{2,1,0:T(8,128)(2,1)S(1)}, u32[]{:S(2)}, u32[]{:S(2)}) collective-permute-start(bf16[1,16,3328]{2,1,0:T(8,128)(2,1)S(1)} %get-tuple-element.80), channel_id=1, source_target_pairs={{0,4},{2,6},{4,0},{6,2},{8,12},{10,14},{12,8},{14,10},{1,5},{3,7},... | collective-permute-start | bytes 319496 | tf_op jit(solution)/shard_map/ppermute | solution.py:52
  97.9 12.3 %collective-permute-start.21 = (bf16[1,16,3328]{2,1,0:T(8,128)(2,1)S(1)}, bf16[1,16,3328]{2,1,0:T(8,128)(2,1)S(1)}, u32[]{:S(2)}, u32[]{:S(2)}) collective-permute-start(bf16[1,16,3328]{2,1,0:T(8,128)(2,1)S(1)} %get-tuple-element.81), channel_id=1, source_target_pairs={{0,8},{2,10},{4,12},{6,14},{8,0},{10,2},{12,4},{14,6},{1,9},{3,11}... | collective-permute-start | bytes 319496 | tf_op jit(solution)/shard_map/ppermute | solution.py:52
  99.8 10.4 %collective-permute-start.22 = (bf16[1,16,3328]{2,1,0:T(8,128)(2,1)S(1)}, bf16[1,16,3328]{2,1,0:T(8,128)(2,1)S(1)}, u32[]{:S(2)}, u32[]{:S(2)}) collective-permute-start(bf16[1,16,3328]{2,1,0:T(8,128)(2,1)S(1)} %get-tuple-element.82), channel_id=1, source_target_pairs={{0,12},{2,14},{4,8},{6,10},{8,4},{10,6},{12,0},{14,2},{1,13},{3,15... | collective-permute-start | bytes 319496 | tf_op jit(solution)/shard_map/ppermute | solution.py:52
  101.5 13.8 %collective-permute-start.33 = (bf16[8,3328]{1,0:T(8,128)(2,1)S(1)}, bf16[8,3328]{1,0:T(8,128)(2,1)S(1)}, u32[]{:S(2)}, u32[]{:S(2)}) collective-permute-start(bf16[8,3328]{1,0:T(8,128)(2,1)S(1)} %get-tuple-element.92.refs_0_), channel_id=1, source_target_pairs={{0,12},{2,14},{4,8},{6,10},{8,4},{10,6},{12,0},{14,2},{1,13},{3,15... | collective-permute-start | bytes 159752 | tf_op jit(solution)/shard_map/ppermute | solution.py:52
  104.0 11.4 %collective-permute-start.32 = (bf16[8,3328]{1,0:T(8,128)(2,1)S(1)}, bf16[8,3328]{1,0:T(8,128)(2,1)S(1)}, u32[]{:S(2)}, u32[]{:S(2)}) collective-permute-start(bf16[8,3328]{1,0:T(8,128)(2,1)S(1)} %get-tuple-element.92.refs_0_), channel_id=1, source_target_pairs={{0,8},{2,10},{4,12},{6,14},{8,0},{10,2},{12,4},{14,6},{1,9},{3,11}... | collective-permute-start | bytes 159752 | tf_op jit(solution)/shard_map/ppermute | solution.py:52
  104.2 11.2 %collective-permute-start.31 = (bf16[8,3328]{1,0:T(8,128)(2,1)S(1)}, bf16[8,3328]{1,0:T(8,128)(2,1)S(1)}, u32[]{:S(2)}, u32[]{:S(2)}) collective-permute-start(bf16[8,3328]{1,0:T(8,128)(2,1)S(1)} %get-tuple-element.92.refs_0_), channel_id=1, source_target_pairs={{0,4},{2,6},{4,0},{6,2},{8,12},{10,14},{12,8},{14,10},{1,5},{3,7},... | collective-permute-start | bytes 159752 | tf_op jit(solution)/shard_map/ppermute | solution.py:52
  110.5 6.6 %collective-permute-start.29 = (bf16[8,3328]{1,0:T(8,128)(2,1)S(1)}, bf16[8,3328]{1,0:T(8,128)(2,1)S(1)}, u32[]{:S(2)}, u32[]{:S(2)}) collective-permute-start(bf16[8,3328]{1,0:T(8,128)(2,1)S(1)} %hidden.7.refs_0_), channel_id=1, source_target_pairs={{0,12},{2,14},{4,8},{6,10},{8,4},{10,6},{12,0},{14,2},{1,13},{3,15... | collective-permute-start | bytes 159752 | tf_op jit(solution)/shard_map/ppermute | solution.py:52
  112.5 5.6 %collective-permute-start.28 = (bf16[8,3328]{1,0:T(8,128)(2,1)S(1)}, bf16[8,3328]{1,0:T(8,128)(2,1)S(1)}, u32[]{:S(2)}, u32[]{:S(2)}) collective-permute-start(bf16[8,3328]{1,0:T(8,128)(2,1)S(1)} %hidden.7.refs_0_), channel_id=1, source_target_pairs={{0,8},{2,10},{4,12},{6,14},{8,0},{10,2},{12,4},{14,6},{1,9},{3,11}... | collective-permute-start | bytes 159752 | tf_op jit(solution)/shard_map/ppermute | solution.py:52
  115.4 4.1 %collective-permute-start.27 = (bf16[8,3328]{1,0:T(8,128)(2,1)S(1)}, bf16[8,3328]{1,0:T(8,128)(2,1)S(1)}, u32[]{:S(2)}, u32[]{:S(2)}) collective-permute-start(bf16[8,3328]{1,0:T(8,128)(2,1)S(1)} %hidden.7.refs_0_), channel_id=1, source_target_pairs={{0,4},{2,6},{4,0},{6,2},{8,12},{10,14},{12,8},{14,10},{1,5},{3,7},... | collective-permute-start | bytes 159752 | tf_op jit(solution)/shard_map/ppermute | solution.py:52
  115.4 8.2 %collective-permute-start.34 = (bf16[32,3328]{1,0:T(8,128)(2,1)S(1)}, bf16[32,3328]{1,0:T(8,128)(2,1)S(1)}, u32[]{:S(2)}, u32[]{:S(2)}) collective-permute-start(bf16[32,3328]{1,0:T(8,128)(2,1)S(1)} %join.7.refs_0_), channel_id=1, source_target_pairs={{0,2},{2,0},{4,6},{6,4},{8,10},{10,8},{12,14},{14,12},{1,3},{3,1},... | collective-permute-start | bytes 638984 | tf_op jit(solution)/shard_map/ppermute | solution.py:52
  119.5 6.4 %collective-permute-start.30 = (bf16[32,3328]{1,0:T(8,128)(2,1)S(1)}, bf16[32,3328]{1,0:T(8,128)(2,1)S(1)}, u32[]{:S(2)}, u32[]{:S(2)}) collective-permute-start(bf16[32,3328]{1,0:T(8,128)(2,1)S(1)} %join.6.refs_0_), channel_id=1, source_target_pairs={{0,2},{2,0},{4,6},{6,4},{8,10},{10,8},{12,14},{14,12},{1,3},{3,1},... | collective-permute-start | bytes 638984 | tf_op jit(solution)/shard_map/ppermute | solution.py:52
  127.2 1.6 %collective-permute-start.35 = (f32[64,1024]{1,0:T(8,128)S(1)}, f32[64,1024]{1,0:T(8,128)S(1)}, u32[]{:S(2)}, u32[]{:S(2)}) collective-permute-start(f32[64,1024]{1,0:T(8,128)S(1)} %down.7.a_ref), channel_id=1, source_target_pairs={{0,1},{1,0},{2,3},{3,2},{4,5},{5,4},{6,7},{7,6},{8,9},{9,8},{10,11... | collective-permute-start | bytes 786440 | tf_op jit(solution)/shard_map/ppermute | solution.py:52
  129.4 4.3 %collective-permute-start.36 = (bf16[32,1024]{1,0:T(8,128)(2,1)S(1)}, bf16[32,1024]{1,0:T(8,128)(2,1)S(1)}, u32[]{:S(2)}, u32[]{:S(2)}) collective-permute-start(bf16[32,1024]{1,0:T(8,128)(2,1)S(1)} %get-tuple-element.96), channel_id=1, source_target_pairs={{16,0},{0,16},{17,1},{1,17},{18,2},{2,18},{19,3},{3,19},{20,4},{4,... | collective-permute-start | bytes 196616 | tf_op jit(solution)/shard_map/ppermute | solution.py:376

commit v3 on v2

--- a/solution.py
+++ b/solution.py
@@ -8,7 +8,10 @@
 from jax.sharding import PartitionSpec as P
 
 STEPS = 2
-CHUNKS = 2
+CHUNKS = (27, 25)
+SCATTER_BITS, GATHER_BITS = 2, 2
+PRELOAD = True
+TIE, PAIR = False, True
 LANES = 128
 PIECE = 256
 F32 = jnp.float32
@@ -28,24 +31,25 @@
     return pltpu.with_memory_space_constraint(value, pltpu.HBM)
 
 
+def after(value, *earlier):
+    return lax.optimization_barrier((value,) + earlier)[0]
+
+
 def cost(flops, moved):
     return pl.CostEstimate(flops=int(flops), bytes_accessed=int(moved), transcendentals=0)
 
 
-def stages_of(wide):
-    found, low = [], 0
-    while (1 << low) < wide:
-        bits = 1 if low == 0 else min(2, wide.bit_length() - 1 - low)
-        found.append((low, 1 << bits))
+def stages_of(wide, most):
+    found, low, total = [], 0, wide.bit_length() - 1
+    while low < total:
+        bits = min(most, total - low)
+        found.append([reverse(i, bits) << low for i in range(1 << bits)])
         low += bits
     return found
 
 
-def offsets_of(stages):
-    found = [0]
-    for low, size in reversed(stages):
-        found = [(i << low) ^ rest for i in range(size) for rest in found]
-    return found
+def reverse(value, bits):
+    return sum(((value >> k) & 1) << (bits - 1 - k) for k in range(bits))
 
 
 def swap(value, axis, flip, count):
@@ -129,25 +133,24 @@
     return pairs
 
 
-def load_kernel(first, base_ref, gate_hbm, up_hbm, gate_ref, up_ref, sems):
+def load_kernel(first, base_ref, weight_hbm, held_ref, sems):
     column = pl.multiple_of(base_ref[0] + first, LANES)
-    for copy in start_copies(column_pairs(column, gate_ref.shape[1], (gate_hbm, up_hbm), (gate_ref, up_ref)), sems):
+    for copy in start_copies(column_pairs(column, held_ref.shape[1], (weight_hbm,), (held_ref,)), sems):
         copy.wait()
 
 
-def load(first, width, base, gate_weight, up_weight):
-    depth = gate_weight.shape[0]
-    shape = struct((depth, width), BF16)
+def load(first, width, base, weight):
+    depth = weight.shape[0]
     return pl.pallas_call(
         functools.partial(load_kernel, first),
-        out_shape=(shape,) * 2,
-        in_specs=[SMEM, HBM, HBM],
-        out_specs=(VMEM,) * 2,
-        scratch_shapes=[pltpu.SemaphoreType.DMA((2 * len(cuts_of(depth, PIECE)),))],
+        out_shape=struct((depth, width), BF16),
+        in_specs=[SMEM, HBM],
+        out_specs=VMEM,
+        scratch_shapes=[pltpu.SemaphoreType.DMA((len(cuts_of(depth, PIECE)),))],
         name="load",
         compiler_params=pltpu.CompilerParams(vmem_limit_bytes=LOAD_LIMIT * MIB),
         cost_estimate=cost(0, 4 * depth * width),
-    )(base, gate_weight, up_weight)
+    )(base, weight)
 
 
 def gate_up_kernel(first, per, size, fresh, summed, base_ref, x_ref, *refs):
@@ -155,22 +158,28 @@
     sumsq_ref = refs.pop(0) if summed else None
     weights, refs = refs[:2], refs[2:]
     outs, refs = refs[:size], refs[size:]
-    copies = None
-    if fresh:
-        held, sems = refs[:2], refs[2]
-        column = pl.multiple_of(base_ref[0] + first, LANES)
-        copies = start_copies(column_pairs(column, held[0].shape[1], weights, held), sems)
-    else:
-        held = weights
+    column = pl.multiple_of(base_ref[0] + first, LANES)
+    held, copies = [], []
+    for k in range(2):
+        target = refs.pop(0) if fresh[k] else weights[k]
+        held.append(target)
+        copies.append((weights[k], target) if fresh[k] else None)
     depth, width = held[0].shape
+    cuts = cuts_of(depth, PIECE)
+    for k in range(2):
+        if fresh[k]:
+            sems = refs.pop(0)
+            copies[k] = start_copies(column_pairs(column, width, copies[k][:1], copies[k][1:]), sems)
     totals = [None, None]
-    for i, (a, b) in enumerate(cuts_of(depth, PIECE)):
-        piece = x_ref[:, a:b]
-        for k, weight in enumerate(held):
-            if fresh:
-                copies[2 * i + k].wait()
-            term = jnp.dot(piece, weight[a:b, :], preferred_element_type=F32)
-            totals[k] = term if totals[k] is None else totals[k] + term
+    order = [(i, k) for i in range(len(cuts)) for k in range(2)]
+    if fresh[0] != fresh[1]:
+        order.sort(key=lambda one: fresh[one[1]])
+    for i, k in order:
+        a, b = cuts[i]
+        if fresh[k]:
+            copies[k][i].wait()
+        term = jnp.dot(x_ref[:, a:b], held[k][a:b, :], preferred_element_type=F32)
+        totals[k] = term if totals[k] is None else totals[k] + term
     group = outs[0].shape[0]
     for p in range(group * size):
         rows = slice(p * per, (p + 1) * per)
@@ -191,12 +200,12 @@
     held = struct((depth, width), BF16)
     return pl.pallas_call(
         functools.partial(gate_up_kernel, first, per, size, fresh, summed),
-        out_shape=(struct(shape, F32),) + (struct(shape, BF16),) * (size - 1) + (held,) * (2 * fresh),
-        in_specs=[SMEM, VMEM] + [VMEM] * summed + [HBM if fresh else VMEM] * 2,
-        out_specs=(VMEM,) * (size + 2 * fresh),
-        scratch_shapes=[pltpu.SemaphoreType.DMA((2 * len(cuts_of(depth, PIECE)),))] * fresh,
+        out_shape=(struct(shape, F32),) + (struct(shape, BF16),) * (size - 1) + (held,) * sum(fresh),
+        in_specs=[SMEM, VMEM] + [VMEM] * summed + [HBM if one else VMEM for one in fresh],
+        out_specs=(VMEM,) * (size + sum(fresh)),
+        scratch_shapes=[pltpu.SemaphoreType.DMA((len(cuts_of(depth, PIECE)),))] * sum(fresh),
         name="gate_up",
-        compiler_params=pltpu.CompilerParams(vmem_limit_bytes=(FRESH_LIMIT if fresh else HELD_LIMIT) * MIB),
+        compiler_params=pltpu.CompilerParams(vmem_limit_bytes=(FRESH_LIMIT if any(fresh) else HELD_LIMIT) * MIB),
         cost_estimate=cost(4 * rows * depth * width, 4 * depth * width),
     )(base, x, *([sumsq] if summed else []), *weights)
 
@@ -213,21 +222,21 @@
     return total, square
 
 
-def add_kernel(count, width, keep_ref, *refs):
+def add_kernel(count, width, pair, keep_ref, *refs):
     arrived, outs = refs[:count], refs[count:]
     total, square = arrived_sum(keep_ref[...], width, arrived)
     group = outs[0].shape[0]
     for i, out in enumerate(outs):
-        rows = slice(i * group, (i + 1) * group)
+        rows = slice(None) if pair else slice(i * group, (i + 1) * group)
         out[:, :, :width] = total[rows] if i == 0 else squeeze(total[rows])
         if square is not None:
             out[:, :, width:] = square[rows] if i == 0 else three_lanes(square[rows][..., :1])
 
 
-def add_stage(keep, width, arrived, size):
-    shape = (keep.shape[0] // size,) + keep.shape[1:]
-    return pl.pallas_call(
-        functools.partial(add_kernel, len(arrived), width),
+def add_stage(keep, width, arrived, size, pair):
+    shape = (keep.shape[0] if pair else keep.shape[0] // size,) + keep.shape[1:]
+    return pl.pallas_call(
+        functools.partial(add_kernel, len(arrived), width, pair),
         out_shape=(struct(shape, F32),) + (struct(shape, BF16),) * (size - 1),
         in_specs=[VMEM] * (1 + len(arrived)),
         out_specs=(VMEM,) * size,
@@ -237,29 +246,35 @@
     )(keep, *arrived)
 
 
-def hidden_kernel(count, width, summed, features, keep_ref, *refs):
+def hidden_kernel(count, width, summed, features, pair, keep_ref, *refs):
     arrived, refs = refs[:count], refs[count:]
-    total, square = arrived_sum(keep_ref[...], width, arrived)
-    total = total[0]
     out_ref = refs[0] if summed else refs[1]
-    per = out_ref.shape[0]
-    if summed:
-        scale = 1.0 / jnp.sqrt(square[0][:per] / features + 1e-05)
-        refs[1][...] = scale
-    else:
-        scale = refs[0][...]
-    scale = scale[:, :1]
-    gate, up = total[:per] * scale, total[per:] * scale
-    out_ref[...] = (gate / (1.0 + jnp.exp(-gate)) * up).astype(BF16)
-
-
-def hidden_of(keep, width, arrived, scale, features):
-    per = keep.shape[1] // 2
+    group = keep_ref.shape[0]
+    per = keep_ref.shape[1] // 2
+    made = []
+    for p in range(group):
+        total, square = arrived_sum(keep_ref[p : p + 1], width, [ref.at[pl.ds(group - 1 - p, 1)] for ref in arrived])
+        total = total[0]
+        rows = slice(p * per, (p + 1) * per)
+        if summed:
+            scale = 1.0 / jnp.sqrt(square[0][:per] / features + 1e-05)
+            refs[1][rows] = scale
+        else:
+            scale = refs[0][rows]
+        scale = scale[:, :1]
+        gate, up = total[:per] * scale, total[per:] * scale
+        made.append(gate / (1.0 + jnp.exp(-gate)) * up)
+    out_ref[...] = jnp.concatenate(made, axis=0).astype(BF16)
+
+
+def hidden_of(keep, width, arrived, scale, features, pair):
+    group, both, _ = keep.shape
+    rows = group * both // 2
     summed = scale is None
-    out = struct((per, width), BF16)
-    return pl.pallas_call(
-        functools.partial(hidden_kernel, len(arrived), width, summed, features),
-        out_shape=(out, struct((per, LANES), F32)) if summed else (out,),
+    out = struct((rows, width), BF16)
+    return pl.pallas_call(
+        functools.partial(hidden_kernel, len(arrived), width, summed, features, pair),
+        out_shape=(out, struct((rows, LANES), F32)) if summed else (out,),
         in_specs=[VMEM] * (1 + len(arrived) + (not summed)),
         out_specs=(VMEM,) * (1 + summed),
         name="hidden",
@@ -284,6 +299,27 @@
         compiler_params=pltpu.CompilerParams(vmem_limit_bytes=8 * MIB),
         cost_estimate=cost(0, rows * len(parts) * width * 4),
     )(*parts)
+
+
+def load_down_kernel(first, base_ref, down_hbm, after_ref, held, sems):
+    row = pl.multiple_of(base_ref[0] + first, LANES)
+    cuts = cuts_of(held.shape[0], 2 * PIECE)
+    pairs = [(down_hbm.at[pl.ds(row + a, b - a), :], held.at[pl.ds(a, b - a), :]) for a, b in cuts]
+    for copy in start_copies(pairs, sems):
+        copy.wait()
+
+
+def load_down(first, depth, base, weight, after):
+    return pl.pallas_call(
+        functools.partial(load_down_kernel, first),
+        out_shape=struct((depth, weight.shape[1]), BF16),
+        in_specs=[SMEM, HBM, VMEM],
+        out_specs=VMEM,
+        scratch_shapes=[pltpu.SemaphoreType.DMA((len(cuts_of(depth, 2 * PIECE)),))],
+        name="load_down",
+        compiler_params=pltpu.CompilerParams(vmem_limit_bytes=LOAD_LIMIT * MIB),
+        cost_estimate=cost(0, 2 * depth * weight.shape[1]),
+    )(base, weight, after)
 
 
 def down_kernel(first, count, added, fresh, base_ref, *refs):
@@ -360,13 +396,13 @@
 
 def per_device(counts, tokens, gate_weight, up_weight, down_weight):
     groups, wide, ffn = counts
-    stages = stages_of(wide)
-    offsets = offsets_of(stages)
+    stages, gathers = stages_of(wide, SCATTER_BITS), stages_of(wide, GATHER_BITS)
+    offsets = [reverse(p, wide.bit_length() - 1) for p in range(wide)]
     rows = tokens.shape[0] * groups
     per = rows // wide
     features = tokens.shape[1] * wide
     share = gate_weight.shape[1] // groups
-    edges = [share // LANES * k // CHUNKS * LANES for k in range(CHUNKS + 1)]
+    edges = [share // LANES * sum(CHUNKS[:k]) // sum(CHUNKS) * LANES for k in range(len(CHUNKS) + 1)]
     chunks = [(a, b - a) for a, b in zip(edges, edges[1:])]
     me, group = lax.axis_index("wide"), lax.axis_index("groups")
     where = jnp.stack([me, group]).astype(jnp.int32)
@@ -378,37 +414,70 @@
     others = [from_group(tokens, k) for k in range(1, groups)]
     state, x, sumsq = arrange(offsets, per, groups, where, tokens, others)
 
-    def scatter_stage(low, size, sends):
-        return [swap(send, "wide", i << low, wide) for i, send in zip(range(1, size), sends)]
-
+    def scatter_stage(flips, sends):
+        return [swap(send, "wide", flip, wide) for flip, send in zip(flips[1:], sends)]
+
+    gate_weight, up_weight, down_weight = (in_hbm(w) for w in (gate_weight, up_weight, down_weight))
+    last = len(chunks) - 1
     gates, downs = {}, {}
-    gate_weight, up_weight, down_weight = (in_hbm(w) for w in (gate_weight, up_weight, down_weight))
-    gates[0] = load(*chunks[0], base, gate_weight, up_weight)
+    early = load(*chunks[0], base, gate_weight)
     for step in range(STEPS):
-        change = scale = None
+        work, previous = [], x
         for c, (first, width) in enumerate(chunks):
-            low, size = stages[0]
-            fresh = c not in gates
+            weights, fresh = gates.get(c, (gate_weight, up_weight)), (c not in gates,) * 2
+            if fresh[0] and c == 0:
+                weights, fresh = (early, up_weight), (False, True)
+            size = len(stages[0])
             found = gate_up(
-                first, width, per, size, base, x, sumsq if c == 0 else None,
-                (gate_weight, up_weight) if fresh else gates[c], fresh,
+                first, width, per, size, base, after(x, previous), sumsq if c == 0 else None, weights, fresh
             )
-            keep, *sends = found[:size]
-            if fresh:
-                gates[c] = found[size:]
-            arrived = scatter_stage(low, size, sends)
-            for low, size in stages[1:]:
-                keep, *sends = add_stage(keep, width, arrived, size)
-                arrived = scatter_stage(low, size, sends)
-            made = hidden_of(keep, width, arrived, scale, features)
-            parts = [made[0]]
-            if scale is None:
-                scale = made[1]
-            for low, size in reversed(stages):
-                whole = parts[0] if len(parts) == 1 else join(parts)
-                parts = [whole] + [swap(whole, "wide", i << low, wide) for i in range(1, size)]
+            previous = found[0]
+            if c not in gates:
+                gates[c] = tuple(found[size:]) if c else (early, found[size])
+            sends = list(found[1:size])
+            if TIE and work:
+                sends = [after(send, work[-1][1][0]) for send in sends]
+            work.append((found[0], scatter_stage(stages[0], sends)))
+        for at, flips in enumerate(stages[1:], 1):
+            pair = PAIR and at + 1 == len(stages) and len(flips) == 2
+            done = []
+            for c, (first, width) in enumerate(chunks):
+                keep, arrived = work[c]
+                if c < last:
+                    keep = after(keep, work[c + 1][0])
+                elif c - 1 in downs and PRELOAD and step == 0:
+                    keep = after(keep, downs[c - 1])
+                keep, *sends = add_stage(keep, width, arrived, len(flips), pair)
+                done.append((keep, scatter_stage(flips, sends)))
+                if PRELOAD and c not in downs:
+                    downs[c] = load_down(first, width, base, down_weight, keep)
+            work = done
+        scale, parts = None, []
+        for c, (first, width) in enumerate(chunks):
+            keep, arrived = work[c]
+            if c < last:
+                keep = after(keep, work[c + 1][0])
+            elif c in downs:
+                keep = after(keep, downs[c])
+            made = hidden_of(keep, width, arrived, scale, features, pair)
+            scale = made[1] if scale is None else scale
+            parts.append([made[0]])
+        for flips in reversed(gathers[:-1] if pair else gathers):
+            done = []
+            for c in range(len(chunks)):
+                pieces = parts[c]
+                if c < last and len(pieces) > 1:
+                    pieces = [after(pieces[0], parts[c + 1][0])] + pieces[1:]
+                done.append(pieces[0] if len(pieces) == 1 else join(pieces))
+            for c in range(len(chunks)):
+                whole = done[c]
+                parts[c] = [whole] + [swap(whole, "wide", flip, wide) for flip in flips[1:]]
+        change = None
+        for c, (first, width) in enumerate(chunks):
             fresh = c not in downs
-            found = down(first, base, parts, down_weight if fresh else downs[c], change, fresh)
+            if c < last:
+                parts[c][0] = after(parts[c][0], parts[c + 1][0])
+            found = down(first, base, parts[c], down_weight if fresh else downs[c], change, fresh)
             change = found[0]
             if fresh:
                 downs[c] = found[1]

time: 135 us -> 119 us (0.88)
  starting transfers between devices: 51.6 us -> 38.3 us
  waiting for transfers between devices: 50.7 us -> 48.1 us
    ppermute x34 -> x30, starting transfers between devices: 47.2 us -> 34.5 us  [swap(): return lax.ppermute(value, axis, [(i, i ^ flip) for i in range(count)])]
    pallas_call x9 -> x7, Pallas kernels: 6.53 us -> 10.8 us  [the longest x2 5.95 us: load_down(): pl.pallas_call(functools.partial(load_down_kernel, first), out_shape=stru...]
    pallas_call x4, Pallas kernels: 9.14 us -> 5.27 us  [down(): pl.pallas_call(functools.partial(down_kernel, first, len(parts), added, f...]
    ppermute x34 -> x30, waiting for transfers between devices: 42.2 us -> 39 us  [swap(): return lax.ppermute(value, axis, [(i, i ^ flip) for i in range(count)])]
  transfers between devices with their start and end apart: 37 -> 33, of which waited for: 18 -> 22; matrix products, arithmetic and copies ran while one was open for 0% -> 0% of each run, Pallas kernels for 15% -> 18%
where the time goes in v3:
time: 119 us
  waiting for transfers between devices  48.1 us (40%)
  starting transfers between devices  38.3 us (32%)
  Pallas kernels  31.9 us (27%)
    ppermute x30, waiting for transfers between devices, swap(): return lax.ppermute(value, axis, [(i, i ^ flip) for i in range(count)])  39 us
    ppermute x30, starting transfers between devices, swap(): return lax.ppermute(value, axis, [(i, i ^ flip) for i in range(count)])  34.5 us
    pallas_call x4, Pallas kernels, gate_up(): pl.pallas_call(functools.partial(gate_up_kernel, first, per, size, fresh,...  13.4 us
    ppermute x3, waiting for transfers between devices, from_group(): lax.ppermute(value, 'groups', [((i + k) % groups, i) for i in range(group...  9.05 us
    pallas_call x2, Pallas kernels, load_down(): pl.pallas_call(functools.partial(load_down_kernel, first), out_shape=stru...  5.95 us
    pallas_call x4, Pallas kernels, down(): pl.pallas_call(functools.partial(down_kernel, first, len(parts), added, f...  5.27 us
    ppermute x3, starting transfers between devices, from_group(): lax.ppermute(value, 'groups', [((i + k) % groups, i) for i in range(group...  3.82 us
    pallas_call x1, Pallas kernels, load(): pl.pallas_call(functools.partial(load_kernel, first), out_shape=struct((d...  3.13 us
  transfers between devices with their start and end apart: 33, of which 22 were waited for; matrix products, arithmetic and copies ran while one was open for 0% of the time, Pallas kernels for 18%

profile of v3, /device:TPU:0, one launch (start us, length us, event | category | flops | bytes accessed | tf_op | source)
XLA Modules:
  0.0 119.3 jit_solution(8090823136260880635)
XLA Ops:
  0.0 2.9 %collective-permute-start = (bf16[32,1024]{1,0:T(8,128)(2,1)}, bf16[32,1024]{1,0:T(8,128)(2,1)S(1)}, u32[]{:S(2)}, u32[]{:S(2)}) collective-permute-start(bf16[32,1024]{1,0:T(8,128)(2,1)} %own_ref.1), channel_id=1, source_target_pairs={{16,0},{0,16},{17,1},{1,17},{18,2},{2,18},{19,3},{3,19},{20,4},{4,... | collective-permute-start | bytes 196616 | tf_op jit(solution)/shard_map/ppermute | solution.py:412
  2.9 3.1 %load.1.refs_1_ = bf16[1024,3456]{1,0:T(8,128)(2,1)S(1)} custom-call(s32[1]{0:T(128)} %bitcast.2.base_ref, bf16[1024,13312]{1,0:T(8,128)(2,1)} %refs_0_.1), custom_call_target="tpu_custom_call" | custom-call | bytes 14155776 | tf_op jit(solution)/shard_map/load/pallas_call | solution.py:144
  6.2 0.7 arrange.1
  6.8 3.6 %gate_up.4 = (f32[2,16,3584]{2,1,0:T(8,128)S(1)}, bf16[2,16,3584]{2,1,0:T(8,128)(2,1)S(1)}, bf16[2,16,3584]{2,1,0:T(8,128)(2,1)S(1)}, bf16[2,16,3584]{2,1,0:T(8,128)(2,1)S(1)}, bf16[1024,3456]{1,0:T(8,128)(2,1)S(1)}) custom-call(s32[1]{0:T(128)} %bitcast.2.base_ref, bf16[64,1024]{1,0:T(8,128)(2,1)S(1)} %get-tuple-element.63.x_ref, ...), custom_call_target="tpu_custom_call" | custom-call | flops 905969664 | bytes 14155776 | tf_op jit(solution)/shard_map/gate_up/pallas_call | solution.py:201
  10.4 1.6 %collective-permute-start.1 = (bf16[2,16,3584]{2,1,0:T(8,128)(2,1)S(1)}, bf16[2,16,3584]{2,1,0:T(8,128)(2,1)S(1)}, u32[]{:S(2)}, u32[]{:S(2)}) collective-permute-start(bf16[2,16,3584]{2,1,0:T(8,128)(2,1)S(1)} %get-tuple-element.66), channel_id=1, source_target_pairs={{0,4},{2,6},{4,0},{6,2},{8,12},{10,14},{12,8},{14,10},{1,5},{3,7},... | collective-permute-start | bytes 688136 | tf_op jit(solution)/shard_map/ppermute | solution.py:56
  12.1 1.5 %collective-permute-start.2 = (bf16[2,16,3584]{2,1,0:T(8,128)(2,1)S(1)}, bf16[2,16,3584]{2,1,0:T(8,128)(2,1)S(1)}, u32[]{:S(2)}, u32[]{:S(2)}) collective-permute-start(bf16[2,16,3584]{2,1,0:T(8,128)(2,1)S(1)} %get-tuple-element.67), channel_id=1, source_target_pairs={{0,2},{2,0},{4,6},{6,4},{8,10},{10,8},{12,14},{14,12},{1,3},{3,1},... | collective-permute-start | bytes 688136 | tf_op jit(solution)/shard_map/ppermute | solution.py:56
  14.0 5.3 %gate_up.5 = (f32[2,16,3200]{2,1,0:T(8,128)S(1)}, bf16[2,16,3200]{2,1,0:T(8,128)(2,1)S(1)}, bf16[2,16,3200]{2,1,0:T(8,128)(2,1)S(1)}, bf16[2,16,3200]{2,1,0:T(8,...) custom-call(s32[1]{0:T(128)} %bitcast.2.base_ref, ...), custom_call_target="tpu_custom_call" | custom-call | flops 838860800 | bytes 13107200 | tf_op jit(solution)/shard_map/gate_up/pallas_call | solution.py:201
  19.3 1.6 %collective-permute-start.4 = (bf16[2,16,3200]{2,1,0:T(8,128)(2,1)S(1)}, bf16[2,16,3200]{2,1,0:T(8,128)(2,1)S(1)}, u32[]{:S(2)}, u32[]{:S(2)}) collective-permute-start(bf16[2,16,3200]{2,1,0:T(8,128)(2,1)S(1)} %get-tuple-element.71), channel_id=1, source_target_pairs={{0,4},{2,6},{4,0},{6,2},{8,12},{10,14},{12,8},{14,10},{1,5},{3,7},... | collective-permute-start | bytes 614408 | tf_op jit(solution)/shard_map/ppermute | solution.py:56
  21.0 1.5 %collective-permute-start.5 = (bf16[2,16,3200]{2,1,0:T(8,128)(2,1)S(1)}, bf16[2,16,3200]{2,1,0:T(8,128)(2,1)S(1)}, u32[]{:S(2)}, u32[]{:S(2)}) collective-permute-start(bf16[2,16,3200]{2,1,0:T(8,128)(2,1)S(1)} %get-tuple-element.72), channel_id=1, source_target_pairs={{0,2},{2,0},{4,6},{6,4},{8,10},{10,8},{12,14},{14,12},{1,3},{3,1},... | collective-permute-start | bytes 614408 | tf_op jit(solution)/shard_map/ppermute | solution.py:56
  23.4 1.5 %collective-permute-done.3.refs_2_ = bf16[2,16,3584]{2,1,0:T(8,128)(2,1)S(1)} collective-permute-done((bf16[2,16,3584]{2,1,0:T(8,128)(2,1)S(1)}, bf16[2,16,3584]{2,1,0:T(8,128)(2,1)S(1)}, u32[]{:S(2)}, u32[]{:S(2)}) %collective-permute-start.3) | collective-permute-done | bytes 229408 | tf_op jit(solution)/shard_map/ppermute | solution.py:56
  25.5 2.7 %collective-permute-start.8 = (bf16[2,16,3584]{2,1,0:T(8,128)(2,1)S(1)}, bf16[2,16,3584]{2,1,0:T(8,128)(2,1)S(1)}, u32[]{:S(2)}, u32[]{:S(2)}) collective-permute-start(bf16[2,16,3584]{2,1,0:T(8,128)(2,1)S(1)} %get-tuple-element.78), channel_id=1, source_target_pairs={{0,8},{2,10},{4,12},{6,14},{8,0},{10,2},{12,4},{14,6},{1,9},{3,11}... | collective-permute-start | bytes 688136 | tf_op jit(solution)/shard_map/ppermute | solution.py:56
  28.2 3.1 %load_down.2.refs_4_ = bf16[3456,1024]{1,0:T(8,128)(2,1)S(1)} custom-call(s32[1]{0:T(128)} %bitcast.2.base_ref, bf16[13312,1024]{1,0:T(8,128)(2,1)} %down_hbm.3, f32[2,16,3584]{2,1,0:T(8,128)S(1)} %get-tuple-element.77.after_ref.keep_ref), custom_call_target="tpu_custom_call" | custom-call | bytes 7077888 | tf_op jit(solution)/shard_map/load_down/pallas_call | solution.py:313
  31.2 2.1 %collective-permute-done.4.refs_0_ = bf16[2,16,3200]{2,1,0:T(8,128)(2,1)S(1)} collective-permute-done((bf16[2,16,3200]{2,1,0:T(8,128)(2,1)S(1)}, bf16[2,16,3200]{2,1,0:T(8,128)(2,1)S(1)}, u32[]{:S(2)}, u32[]{:S(2)}) %collective-permute-start.4) | collective-permute-done | bytes 204832 | tf_op jit(solution)/shard_map/ppermute | solution.py:56
  33.3 3.9 %collective-permute-done.6.refs_2_ = bf16[2,16,3200]{2,1,0:T(8,128)(2,1)S(1)} collective-permute-done((bf16[2,16,3200]{2,1,0:T(8,128)(2,1)S(1)}, bf16[2,16,3200]{2,1,0:T(8,128)(2,1)S(1)}, u32[]{:S(2)}, u32[]{:S(2)}) %collective-permute-start.6) | collective-permute-done | bytes 204832 | tf_op jit(solution)/shard_map/ppermute | solution.py:56
  37.8 3.1 %collective-permute-start.14 = (bf16[16,3456]{1,0:T(8,128)(2,1)S(1)}, bf16[16,3456]{1,0:T(8,128)(2,1)S(1)}, u32[]{:S(2)}, u32[]{:S(2)}) collective-permute-start(bf16[16,3456]{1,0:T(8,128)(2,1)S(1)} %get-tuple-element.81.refs_0_), channel_id=1, source_target_pairs={{0,6},{2,4},{4,2},{6,0},{8,14},{10,12},{12,10},{14,8},{1,7},{3,5},... | collective-permute-start | bytes 331784 | tf_op jit(solution)/shard_map/ppermute | solution.py:56
  40.9 2.2 %collective-permute-start.13 = (bf16[16,3456]{1,0:T(8,128)(2,1)S(1)}, bf16[16,3456]{1,0:T(8,128)(2,1)S(1)}, u32[]{:S(2)}, u32[]{:S(2)}) collective-permute-start(bf16[16,3456]{1,0:T(8,128)(2,1)S(1)} %get-tuple-element.81.refs_0_), channel_id=1, source_target_pairs={{0,2},{2,0},{4,6},{6,4},{8,10},{10,8},{12,14},{14,12},{1,3},{3,1},... | collective-permute-start | bytes 331784 | tf_op jit(solution)/shard_map/ppermute | solution.py:56
  43.1 2.9 %load_down.3.refs_4_ = bf16[3200,1024]{1,0:T(8,128)(2,1)S(1)} custom-call(s32[1]{0:T(128)} %bitcast.2.base_ref, bf16[13312,1024]{1,0:T(8,128)(2,1)} %down_hbm.3, f32[2,16,3200]{2,1,0:T(8,128)S(1)} %get-tuple-element.75.after_ref.keep_ref), custom_call_target="tpu_custom_call" | custom-call | bytes 6553600 | tf_op jit(solution)/shard_map/load_down/pallas_call | solution.py:313
  46.0 2.5 %collective-permute-done.7.refs_0_ = bf16[2,16,3200]{2,1,0:T(8,128)(2,1)S(1)} collective-permute-done((bf16[2,16,3200]{2,1,0:T(8,128)(2,1)S(1)}, bf16[2,16,3200]{2,1,0:T(8,128)(2,1)S(1)}, u32[]{:S(2)}, u32[]{:S(2)}) %collective-permute-start.7) | collective-permute-done | bytes 204832 | tf_op jit(solution)/shard_map/ppermute | solution.py:56
  48.8 1.0 collective-permute-start.10
  49.7 2.5 %collective-permute-start.9 = (bf16[16,3200]{1,0:T(8,128)(2,1)S(1)}, bf16[16,3200]{1,0:T(8,128)(2,1)S(1)}, u32[]{:S(2)}, u32[]{:S(2)}) collective-permute-start(bf16[16,3200]{1,0:T(8,128)(2,1)S(1)} %hidden.5.refs_0_), channel_id=1, source_target_pairs={{0,4},{2,6},{4,0},{6,2},{8,12},{10,14},{12,8},{14,10},{1,5},{3,7},... | collective-permute-start | bytes 307208 | tf_op jit(solution)/shard_map/ppermute | solution.py:56
  52.3 1.4 %down.4.refs_5_ = f32[64,1024]{1,0:T(8,128)S(1)} custom-call(s32[1]{0:T(128)} %bitcast.2.base_ref, bf16[16,3456]{1,0:T(8,128)(2,1)S(1)} %get-tuple-element.81.refs_0_, bf16[16,3456]{1,0:T(8,128)(2,1)S(1)} %collective-permute-done.12.refs_1_, bf16[16,3456]{1,0:T(8,128)(2,1)S(1)} %collective-permute-done.13.refs_2_, ...), custom_call_target="tpu_custom_call" | custom-call | flops 452984832 | bytes 7077888 | tf_op jit(solution)/shard_map/down/pallas_call | solution.py:351
  53.7 1.4 %collective-permute-done.11.refs_3_ = bf16[16,3200]{1,0:T(8,128)(2,1)S(1)} collective-permute-done((bf16[16,3200]{1,0:T(8,128)(2,1)S(1)}, bf16[16,3200]{1,0:T(8,128)(2,1)S(1)}, u32[]{:S(2)}, u32[]{:S(2)}) %collective-permute-start.11) | collective-permute-done | bytes 102432 | tf_op jit(solution)/shard_map/ppermute | solution.py:56
  55.6 1.3 %down.5.a_ref = f32[64,1024]{1,0:T(8,128)S(1)} custom-call(s32[1]{0:T(128)} %bitcast.2.base_ref, bf16[16,3200]{1,0:T(8,128)(2,1)S(1)} %hidden.5.refs_0_, bf16[16,3200]{1,0:T(8,128)(2,1)S(1)} %collective-permute-done.9.refs_1_, bf16[16,3200]{1,0:T(8,128)(2,1)S(1)} %collective-permute-done.10.refs_2_, bf16[16,3200]{1,0:T(8,128)(2,1)S(1)} %collective-permute-done.11.refs_3_, ...), custom_call_target="tpu_custom_call" | custom-call | flops 419430400 | bytes 6553600 | tf_op jit(solution)/shard_map/down/pallas_call | solution.py:351
  57.0 1.5 %collective-permute-done.15.b_ref = f32[64,1024]{1,0:T(8,128)S(1)} collective-permute-done((f32[64,1024]{1,0:T(8,128)S(1)}, f32[64,1024]{1,0:T(8,128)S(1)}, u32[]{:S(2)}, u32[]{:S(2)}) %collective-permute-start.15) | collective-permute-done | bytes 262176 | tf_op jit(solution)/shard_map/ppermute | solution.py:56
  58.9 5.2 %collective-permute-done.16.refs_0_ = bf16[64,1024]{1,0:T(8,128)(2,1)S(1)} collective-permute-done((bf16[64,1024]{1,0:T(8,128)(2,1)S(1)}, bf16[64,1024]{1,0:T(8,128)(2,1)S(1)}, u32[]{:S(2)}, u32[]{:S(2)}) %collective-permute-start.16) | collective-permute-done | bytes 131104 | tf_op jit(solution)/shard_map/ppermute | solution.py:412
  64.3 2.3 %gate_up.6 = (f32[2,16,3584]{2,1,0:T(8,128)S(1)}, bf16[2,16,3584]{2,1,0:T(8,128)(2,1)S(1)}, bf16[2,16,3584]{2,1,0:T(8,128)(2,1)S(1)}, bf16[2,16,3584]{2,1,0:T(8,128)(2,1)S(1)}) custom-call(s32[1]{0:T(128)} %bitcast.2.base_ref, bf16[64,1024]{1,0:T(8,128)(2,1)S(1)} %get-tuple-element.90.x_ref, f32[64,128]{1,0:T(8,128)S(1)} %get-tuple-element.87.refs_0_, ...), custom_call_target="tpu_custom_call" | custom-call | flops 905969664 | bytes 14155776 | tf_op jit(solution)/shard_map/gate_up/pallas_call | solution.py:201
  66.5 1.4 %collective-permute-start.21 = (bf16[2,16,3584]{2,1,0:T(8,128)(2,1)S(1)}, bf16[2,16,3584]{2,1,0:T(8,128)(2,1)S(1)}, u32[]{:S(2)}, u32[]{:S(2)}) collective-permute-start(bf16[2,16,3584]{2,1,0:T(8,128)(2,1)S(1)} %get-tuple-element.101), channel_id=1, source_target_pairs={{0,4},{2,6},{4,0},{6,2},{8,12},{10,14},{12,8},{14,10},{1,5},{3,7},... | collective-permute-start | bytes 688136 | tf_op jit(solution)/shard_map/ppermute | solution.py:56
  68.3 1.8 %collective-permute-start.23 = (bf16[2,16,3584]{2,1,0:T(8,128)(2,1)S(1)}, bf16[2,16,3584]{2,1,0:T(8,128)(2,1)S(1)}, u32[]{:S(2)}, u32[]{:S(2)}) collective-permute-start(bf16[2,16,3584]{2,1,0:T(8,128)(2,1)S(1)} %get-tuple-element.103), channel_id=1, source_target_pairs={{0,6},{2,4},{4,2},{6,0},{8,14},{10,12},{12,10},{14,8},{1,7},{3,5},... | collective-permute-start | bytes 688136 | tf_op jit(solution)/shard_map/ppermute | solution.py:56
  70.1 2.3 %gate_up.7 = (f32[2,16,3200]{2,1,0:T(8,128)S(1)}, bf16[2,16,3200]{2,1,0:T(8,128)(2,1)S(1)}, bf16[2,16,3200]{2,1,0:T(8,128)(2,1)S(1)}, bf16[2,16,3200]{2,1,0:T(8,128)(2,1)S(1)}) custom-call(s32[1]{0:T(128)} %bitcast.2.base_ref, bf16[64,1024]{1,0:T(8,128)(2,1)S(1)} %get-tuple-element.90.x_ref, bf16[1024,3200]{1,0:T(8,128)(2,1)S(1)} %get-tuple-element.91.refs_0_, ...), custom_call_target="tpu_custom_call" | custom-call | flops 838860800 | bytes 13107200 | tf_op jit(solution)/shard_map/gate_up/pallas_call | solution.py:201
  72.4 1.4 %collective-permute-start.17 = (bf16[2,16,3200]{2,1,0:T(8,128)(2,1)S(1)}, bf16[2,16,3200]{2,1,0:T(8,128)(2,1)S(1)}, u32[]{:S(2)}, u32[]{:S(2)}) collective-permute-start(bf16[2,16,3200]{2,1,0:T(8,128)(2,1)S(1)} %get-tuple-element.94), channel_id=1, source_target_pairs={{0,4},{2,6},{4,0},{6,2},{8,12},{10,14},{12,8},{14,10},{1,5},{3,7},... | collective-permute-start | bytes 614408 | tf_op jit(solution)/shard_map/ppermute | solution.py:56
  74.2 1.0 collective-permute-done.21.refs_0_
  75.1 1.2 collective-permute-start.19
  76.3 4.0 %collective-permute-done.22.refs_1_ = bf16[2,16,3584]{2,1,0:T(8,128)(2,1)S(1)} collective-permute-done((bf16[2,16,3584]{2,1,0:T(8,128)(2,1)S(1)}, bf16[2,16,3584]{2,1,0:T(8,128)(2,1)S(1)}, u32[]{:S(2)}, u32[]{:S(2)}) %collective-permute-start.22) | collective-permute-done | bytes 229408 | tf_op jit(solution)/shard_map/ppermute | solution.py:56
  81.1 1.7 %collective-permute-start.24 = (bf16[2,16,3584]{2,1,0:T(8,128)(2,1)S(1)}, bf16[2,16,3584]{2,1,0:T(8,128)(2,1)S(1)}, u32[]{:S(2)}, u32[]{:S(2)}) collective-permute-start(bf16[2,16,3584]{2,1,0:T(8,128)(2,1)S(1)} %get-tuple-element.106), channel_id=1, source_target_pairs={{0,8},{2,10},{4,12},{6,14},{8,0},{10,2},{12,4},{14,6},{1,9},{3,11}... | collective-permute-start | bytes 688136 | tf_op jit(solution)/shard_map/ppermute | solution.py:56
  82.8 5.9 %collective-permute-done.17.refs_0_ = bf16[2,16,3200]{2,1,0:T(8,128)(2,1)S(1)} collective-permute-done((bf16[2,16,3200]{2,1,0:T(8,128)(2,1)S(1)}, bf16[2,16,3200]{2,1,0:T(8,128)(2,1)S(1)}, u32[]{:S(2)}, u32[]{:S(2)}) %collective-permute-start.17) | collective-permute-done | bytes 204832 | tf_op jit(solution)/shard_map/ppermute | solution.py:56
  88.7 3.8 %collective-permute-done.19.refs_2_ = bf16[2,16,3200]{2,1,0:T(8,128)(2,1)S(1)} collective-permute-done((bf16[2,16,3200]{2,1,0:T(8,128)(2,1)S(1)}, bf16[2,16,3200]{2,1,0:T(8,128)(2,1)S(1)}, u32[]{:S(2)}, u32[]{:S(2)}) %collective-permute-start.19) | collective-permute-done | bytes 204832 | tf_op jit(solution)/shard_map/ppermute | solution.py:56
  93.3 3.3 %collective-permute-start.30 = (bf16[16,3456]{1,0:T(8,128)(2,1)S(1)}, bf16[16,3456]{1,0:T(8,128)(2,1)S(1)}, u32[]{:S(2)}, u32[]{:S(2)}) collective-permute-start(bf16[16,3456]{1,0:T(8,128)(2,1)S(1)} %get-tuple-element.109.refs_0_), channel_id=1, source_target_pairs={{0,6},{2,4},{4,2},{6,0},{8,14},{10,12},{12,10},{14,8},{1,7},{3,5},... | collective-permute-start | bytes 331784 | tf_op jit(solution)/shard_map/ppermute | solution.py:56
  97.2 5.1 %collective-permute-done.20.refs_0_ = bf16[2,16,3200]{2,1,0:T(8,128)(2,1)S(1)} collective-permute-done((bf16[2,16,3200]{2,1,0:T(8,128)(2,1)S(1)}, bf16[2,16,3200]{2,1,0:T(8,128)(2,1)S(1)}, u32[]{:S(2)}, u32[]{:S(2)}) %collective-permute-start.20) | collective-permute-done | bytes 204832 | tf_op jit(solution)/shard_map/ppermute | solution.py:56
  102.5 2.1 %collective-permute-start.26 = (bf16[16,3200]{1,0:T(8,128)(2,1)S(1)}, bf16[16,3200]{1,0:T(8,128)(2,1)S(1)}, u32[]{:S(2)}, u32[]{:S(2)}) collective-permute-start(bf16[16,3200]{1,0:T(8,128)(2,1)S(1)} %hidden.7.refs_0_), channel_id=1, source_target_pairs={{0,2},{2,0},{4,6},{6,4},{8,10},{10,8},{12,14},{14,12},{1,3},{3,1},... | collective-permute-start | bytes 307208 | tf_op jit(solution)/shard_map/ppermute | solution.py:56
  104.6 1.4 %collective-permute-start.25 = (bf16[16,3200]{1,0:T(8,128)(2,1)S(1)}, bf16[16,3200]{1,0:T(8,128)(2,1)S(1)}, u32[]{:S(2)}, u32[]{:S(2)}) collective-permute-start(bf16[16,3200]{1,0:T(8,128)(2,1)S(1)} %hidden.7.refs_0_), channel_id=1, source_target_pairs={{0,4},{2,6},{4,0},{6,2},{8,12},{10,14},{12,8},{14,10},{1,5},{3,7},... | collective-permute-start | bytes 307208 | tf_op jit(solution)/shard_map/ppermute | solution.py:56
  106.0 1.4 %down.6.refs_5_ = f32[64,1024]{1,0:T(8,128)S(1)} custom-call(s32[1]{0:T(128)} %bitcast.2.base_ref, bf16[16,3456]{1,0:T(8,128)(2,1)S(1)} %get-tuple-element.109.refs_0_, bf16[16,3456]{1,0:T(8,128)(2,1)S(1)} %collective-permute-done.28.refs_1_, bf16[16,3456]{1,0:T(8,128)(2,1)S(1)} %collective-permute-done.29.refs_2_, ...), custom_call_target="tpu_custom_call" | custom-call | flops 452984832 | bytes 7077888 | tf_op jit(solution)/shard_map/down/pallas_call | solution.py:351
  107.4 1.2 %collective-permute-done.27.refs_3_ = bf16[16,3200]{1,0:T(8,128)(2,1)S(1)} collective-permute-done((bf16[16,3200]{1,0:T(8,128)(2,1)S(1)}, bf16[16,3200]{1,0:T(8,128)(2,1)S(1)}, u32[]{:S(2)}, u32[]{:S(2)}) %collective-permute-start.27) | collective-permute-done | bytes 102432 | tf_op jit(solution)/shard_map/ppermute | solution.py:56
  108.6 1.0 collective-permute-done.26.refs_2_
  109.6 1.1 collective-permute-done.25.refs_1_
  110.8 1.3 %down.7.a_ref = f32[64,1024]{1,0:T(8,128)S(1)} custom-call(s32[1]{0:T(128)} %bitcast.2.base_ref, bf16[16,3200]{1,0:T(8,128)(2,1)S(1)} %hidden.7.refs_0_, bf16[16,3200]{1,0:T(8,128)(2,1)S(1)} %collective-permute-done.25.refs_1_, bf16[16,3200]{1,0:T(8,128)(2,1)S(1)} %collective-permute-done.26.refs_2_, bf16[16,3200]{1,0:T(8,128)(2,1)S(1)} %collective-permute-done.27.refs_3_, ...), custom_call_target="tpu_custom_call" | custom-call | flops 419430400 | bytes 6553600 | tf_op jit(solution)/shard_map/down/pallas_call | solution.py:351
  112.2 1.5 %collective-permute-done.31.b_ref = f32[64,1024]{1,0:T(8,128)S(1)} collective-permute-done((f32[64,1024]{1,0:T(8,128)S(1)}, f32[64,1024]{1,0:T(8,128)S(1)}, u32[]{:S(2)}, u32[]{:S(2)}) %collective-permute-start.31) | collective-permute-done | bytes 262176 | tf_op jit(solution)/shard_map/ppermute | solution.py:56
  114.8 3.8 %collective-permute-done.32 = bf16[32,1024]{1,0:T(8,128)(2,1)S(1)} collective-permute-done((bf16[32,1024]{1,0:T(8,128)(2,1)S(1)}, bf16[32,1024]{1,0:T(8,128)(2,1)S(1)}, u32[]{:S(2)}, u32[]{:S(2)}) %collective-permute-start.32) | collective-permute-done | bytes 65568 | tf_op jit(solution)/shard_map/ppermute | solution.py:412
  118.6 0.7 convert_add_fusion
  (45 shorter events, 8.5 us)
Async XLA Ops:
  0.0 6.2 %collective-permute-start = (bf16[32,1024]{1,0:T(8,128)(2,1)}, bf16[32,1024]{1,0:T(8,128)(2,1)S(1)}, u32[]{:S(2)}, u32[]{:S(2)}) collective-permute-start(bf16[32,1024]{1,0:T(8,128)(2,1)} %own_ref.1), channel_id=1, source_target_pairs={{16,0},{0,16},{17,1},{1,17},{18,2},{2,18},{19,3},{3,19},{20,4},{4,... | collective-permute-start | bytes 196616 | tf_op jit(solution)/shard_map/ppermute | solution.py:412
  2.9 3.2 %copy-start = (bf16[32,1024]{1,0:T(8,128)(2,1)S(1)}, bf16[32,1024]{1,0:T(8,128)(2,1)}, u32[]{:S(2)}) copy-start(bf16[32,1024]{1,0:T(8,128)(2,1)} %own_ref.1) | copy-start | bytes 196612
  10.4 12.1 %collective-permute-start.1 = (bf16[2,16,3584]{2,1,0:T(8,128)(2,1)S(1)}, bf16[2,16,3584]{2,1,0:T(8,128)(2,1)S(1)}, u32[]{:S(2)}, u32[]{:S(2)}) collective-permute-start(bf16[2,16,3584]{2,1,0:T(8,128)(2,1)S(1)} %get-tuple-element.66), channel_id=1, source_target_pairs={{0,4},{2,6},{4,0},{6,2},{8,12},{10,14},{12,8},{14,10},{1,5},{3,7},... | collective-permute-start | bytes 688136 | tf_op jit(solution)/shard_map/ppermute | solution.py:56
  12.1 11.3 %collective-permute-start.2 = (bf16[2,16,3584]{2,1,0:T(8,128)(2,1)S(1)}, bf16[2,16,3584]{2,1,0:T(8,128)(2,1)S(1)}, u32[]{:S(2)}, u32[]{:S(2)}) collective-permute-start(bf16[2,16,3584]{2,1,0:T(8,128)(2,1)S(1)} %get-tuple-element.67), channel_id=1, source_target_pairs={{0,2},{2,0},{4,6},{6,4},{8,10},{10,8},{12,14},{14,12},{1,3},{3,1},... | collective-permute-start | bytes 688136 | tf_op jit(solution)/shard_map/ppermute | solution.py:56
  13.6 11.4 %collective-permute-start.3 = (bf16[2,16,3584]{2,1,0:T(8,128)(2,1)S(1)}, bf16[2,16,3584]{2,1,0:T(8,128)(2,1)S(1)}, u32[]{:S(2)}, u32[]{:S(2)}) collective-permute-start(bf16[2,16,3584]{2,1,0:T(8,128)(2,1)S(1)} %get-tuple-element.68), channel_id=1, source_target_pairs={{0,6},{2,4},{4,2},{6,0},{8,14},{10,12},{12,10},{14,8},{1,7},{3,5},... | collective-permute-start | bytes 688136 | tf_op jit(solution)/shard_map/ppermute | solution.py:56
  19.3 14.0 %collective-permute-start.4 = (bf16[2,16,3200]{2,1,0:T(8,128)(2,1)S(1)}, bf16[2,16,3200]{2,1,0:T(8,128)(2,1)S(1)}, u32[]{:S(2)}, u32[]{:S(2)}) collective-permute-start(bf16[2,16,3200]{2,1,0:T(8,128)(2,1)S(1)} %get-tuple-element.71), channel_id=1, source_target_pairs={{0,4},{2,6},{4,0},{6,2},{8,12},{10,14},{12,8},{14,10},{1,5},{3,7},... | collective-permute-start | bytes 614408 | tf_op jit(solution)/shard_map/ppermute | solution.py:56
  21.0 12.3 %collective-permute-start.5 = (bf16[2,16,3200]{2,1,0:T(8,128)(2,1)S(1)}, bf16[2,16,3200]{2,1,0:T(8,128)(2,1)S(1)}, u32[]{:S(2)}, u32[]{:S(2)}) collective-permute-start(bf16[2,16,3200]{2,1,0:T(8,128)(2,1)S(1)} %get-tuple-element.72), channel_id=1, source_target_pairs={{0,2},{2,0},{4,6},{6,4},{8,10},{10,8},{12,14},{14,12},{1,3},{3,1},... | collective-permute-start | bytes 614408 | tf_op jit(solution)/shard_map/ppermute | solution.py:56
  22.5 14.7 %collective-permute-start.6 = (bf16[2,16,3200]{2,1,0:T(8,128)(2,1)S(1)}, bf16[2,16,3200]{2,1,0:T(8,128)(2,1)S(1)}, u32[]{:S(2)}, u32[]{:S(2)}) collective-permute-start(bf16[2,16,3200]{2,1,0:T(8,128)(2,1)S(1)} %get-tuple-element.73), channel_id=1, source_target_pairs={{0,6},{2,4},{4,2},{6,0},{8,14},{10,12},{12,10},{14,8},{1,7},{3,5},... | collective-permute-start | bytes 614408 | tf_op jit(solution)/shard_map/ppermute | solution.py:56
  25.5 12.0 %collective-permute-start.8 = (bf16[2,16,3584]{2,1,0:T(8,128)(2,1)S(1)}, bf16[2,16,3584]{2,1,0:T(8,128)(2,1)S(1)}, u32[]{:S(2)}, u32[]{:S(2)}) collective-permute-start(bf16[2,16,3584]{2,1,0:T(8,128)(2,1)S(1)} %get-tuple-element.78), channel_id=1, source_target_pairs={{0,8},{2,10},{4,12},{6,14},{8,0},{10,2},{12,4},{14,6},{1,9},{3,11}... | collective-permute-start | bytes 688136 | tf_op jit(solution)/shard_map/ppermute | solution.py:56
  37.4 11.1 %collective-permute-start.7 = (bf16[2,16,3200]{2,1,0:T(8,128)(2,1)S(1)}, bf16[2,16,3200]{2,1,0:T(8,128)(2,1)S(1)}, u32[]{:S(2)}, u32[]{:S(2)}) collective-permute-start(bf16[2,16,3200]{2,1,0:T(8,128)(2,1)S(1)} %get-tuple-element.76), channel_id=1, source_target_pairs={{0,8},{2,10},{4,12},{6,14},{8,0},{10,2},{12,4},{14,6},{1,9},{3,11}... | collective-permute-start | bytes 614408 | tf_op jit(solution)/shard_map/ppermute | solution.py:56
  37.8 11.9 %collective-permute-start.14 = (bf16[16,3456]{1,0:T(8,128)(2,1)S(1)}, bf16[16,3456]{1,0:T(8,128)(2,1)S(1)}, u32[]{:S(2)}, u32[]{:S(2)}) collective-permute-start(bf16[16,3456]{1,0:T(8,128)(2,1)S(1)} %get-tuple-element.81.refs_0_), channel_id=1, source_target_pairs={{0,6},{2,4},{4,2},{6,0},{8,14},{10,12},{12,10},{14,8},{1,7},{3,5},... | collective-permute-start | bytes 331784 | tf_op jit(solution)/shard_map/ppermute | solution.py:56
  40.9 11.4 %collective-permute-start.13 = (bf16[16,3456]{1,0:T(8,128)(2,1)S(1)}, bf16[16,3456]{1,0:T(8,128)(2,1)S(1)}, u32[]{:S(2)}, u32[]{:S(2)}) collective-permute-start(bf16[16,3456]{1,0:T(8,128)(2,1)S(1)} %get-tuple-element.81.refs_0_), channel_id=1, source_target_pairs={{0,2},{2,0},{4,6},{6,4},{8,10},{10,8},{12,14},{14,12},{1,3},{3,1},... | collective-permute-start | bytes 331784 | tf_op jit(solution)/shard_map/ppermute | solution.py:56
  43.1 9.2 %collective-permute-start.12 = (bf16[16,3456]{1,0:T(8,128)(2,1)S(1)}, bf16[16,3456]{1,0:T(8,128)(2,1)S(1)}, u32[]{:S(2)}, u32[]{:S(2)}) collective-permute-start(bf16[16,3456]{1,0:T(8,128)(2,1)S(1)} %get-tuple-element.81.refs_0_), channel_id=1, source_target_pairs={{0,4},{2,6},{4,0},{6,2},{8,12},{10,14},{12,8},{14,10},{1,5},{3,7},... | collective-permute-start | bytes 331784 | tf_op jit(solution)/shard_map/ppermute | solution.py:56
  48.7 6.3 %collective-permute-start.11 = (bf16[16,3200]{1,0:T(8,128)(2,1)S(1)}, bf16[16,3200]{1,0:T(8,128)(2,1)S(1)}, u32[]{:S(2)}, u32[]{:S(2)}) collective-permute-start(bf16[16,3200]{1,0:T(8,128)(2,1)S(1)} %hidden.5.refs_0_), channel_id=1, source_target_pairs={{0,6},{2,4},{4,2},{6,0},{8,14},{10,12},{12,10},{14,8},{1,7},{3,5},... | collective-permute-start | bytes 307208 | tf_op jit(solution)/shard_map/ppermute | solution.py:56
  48.8 6.4 %collective-permute-start.10 = (bf16[16,3200]{1,0:T(8,128)(2,1)S(1)}, bf16[16,3200]{1,0:T(8,128)(2,1)S(1)}, u32[]{:S(2)}, u32[]{:S(2)}) collective-permute-start(bf16[16,3200]{1,0:T(8,128)(2,1)S(1)} %hidden.5.refs_0_), channel_id=1, source_target_pairs={{0,2},{2,0},{4,6},{6,4},{8,10},{10,8},{12,14},{14,12},{1,3},{3,1},... | collective-permute-start | bytes 307208 | tf_op jit(solution)/shard_map/ppermute | solution.py:56
  49.7 5.9 %collective-permute-start.9 = (bf16[16,3200]{1,0:T(8,128)(2,1)S(1)}, bf16[16,3200]{1,0:T(8,128)(2,1)S(1)}, u32[]{:S(2)}, u32[]{:S(2)}) collective-permute-start(bf16[16,3200]{1,0:T(8,128)(2,1)S(1)} %hidden.5.refs_0_), channel_id=1, source_target_pairs={{0,4},{2,6},{4,0},{6,2},{8,12},{10,14},{12,8},{14,10},{1,5},{3,7},... | collective-permute-start | bytes 307208 | tf_op jit(solution)/shard_map/ppermute | solution.py:56
  56.9 1.6 %collective-permute-start.15 = (f32[64,1024]{1,0:T(8,128)S(1)}, f32[64,1024]{1,0:T(8,128)S(1)}, u32[]{:S(2)}, u32[]{:S(2)}) collective-permute-start(f32[64,1024]{1,0:T(8,128)S(1)} %down.5.a_ref), channel_id=1, source_target_pairs={{0,1},{1,0},{2,3},{3,2},{4,5},{5,4},{6,7},{7,6},{8,9},{9,8},{10,11... | collective-permute-start | bytes 786440 | tf_op jit(solution)/shard_map/ppermute | solution.py:56
  58.5 5.6 %collective-permute-start.16 = (bf16[64,1024]{1,0:T(8,128)(2,1)S(1)}, bf16[64,1024]{1,0:T(8,128)(2,1)S(1)}, u32[]{:S(2)}, u32[]{:S(2)}) collective-permute-start(bf16[64,1024]{1,0:T(8,128)(2,1)S(1)} %get-tuple-element.84), channel_id=1, source_target_pairs={{16,0},{0,16},{17,1},{1,17},{18,2},{2,18},{19,3},{3,19},{20,4},{4,... | collective-permute-start | bytes 393224 | tf_op jit(solution)/shard_map/ppermute | solution.py:412
  66.5 8.6 %collective-permute-start.21 = (bf16[2,16,3584]{2,1,0:T(8,128)(2,1)S(1)}, bf16[2,16,3584]{2,1,0:T(8,128)(2,1)S(1)}, u32[]{:S(2)}, u32[]{:S(2)}) collective-permute-start(bf16[2,16,3584]{2,1,0:T(8,128)(2,1)S(1)} %get-tuple-element.101), channel_id=1, source_target_pairs={{0,4},{2,6},{4,0},{6,2},{8,12},{10,14},{12,8},{14,10},{1,5},{3,7},... | collective-permute-start | bytes 688136 | tf_op jit(solution)/shard_map/ppermute | solution.py:56
  67.9 12.4 %collective-permute-start.22 = (bf16[2,16,3584]{2,1,0:T(8,128)(2,1)S(1)}, bf16[2,16,3584]{2,1,0:T(8,128)(2,1)S(1)}, u32[]{:S(2)}, u32[]{:S(2)}) collective-permute-start(bf16[2,16,3584]{2,1,0:T(8,128)(2,1)S(1)} %get-tuple-element.102), channel_id=1, source_target_pairs={{0,2},{2,0},{4,6},{6,4},{8,10},{10,8},{12,14},{14,12},{1,3},{3,1},... | collective-permute-start | bytes 688136 | tf_op jit(solution)/shard_map/ppermute | solution.py:56
  68.3 12.2 %collective-permute-start.23 = (bf16[2,16,3584]{2,1,0:T(8,128)(2,1)S(1)}, bf16[2,16,3584]{2,1,0:T(8,128)(2,1)S(1)}, u32[]{:S(2)}, u32[]{:S(2)}) collective-permute-start(bf16[2,16,3584]{2,1,0:T(8,128)(2,1)S(1)} %get-tuple-element.103), channel_id=1, source_target_pairs={{0,6},{2,4},{4,2},{6,0},{8,14},{10,12},{12,10},{14,8},{1,7},{3,5},... | collective-permute-start | bytes 688136 | tf_op jit(solution)/shard_map/ppermute | solution.py:56
  72.4 16.3 %collective-permute-start.17 = (bf16[2,16,3200]{2,1,0:T(8,128)(2,1)S(1)}, bf16[2,16,3200]{2,1,0:T(8,128)(2,1)S(1)}, u32[]{:S(2)}, u32[]{:S(2)}) collective-permute-start(bf16[2,16,3200]{2,1,0:T(8,128)(2,1)S(1)} %get-tuple-element.94), channel_id=1, source_target_pairs={{0,4},{2,6},{4,0},{6,2},{8,12},{10,14},{12,8},{14,10},{1,5},{3,7},... | collective-permute-start | bytes 614408 | tf_op jit(solution)/shard_map/ppermute | solution.py:56
  73.8 14.9 %collective-permute-start.18 = (bf16[2,16,3200]{2,1,0:T(8,128)(2,1)S(1)}, bf16[2,16,3200]{2,1,0:T(8,128)(2,1)S(1)}, u32[]{:S(2)}, u32[]{:S(2)}) collective-permute-start(bf16[2,16,3200]{2,1,0:T(8,128)(2,1)S(1)} %get-tuple-element.95), channel_id=1, source_target_pairs={{0,2},{2,0},{4,6},{6,4},{8,10},{10,8},{12,14},{14,12},{1,3},{3,1},... | collective-permute-start | bytes 614408 | tf_op jit(solution)/shard_map/ppermute | solution.py:56
  75.1 17.4 %collective-permute-start.19 = (bf16[2,16,3200]{2,1,0:T(8,128)(2,1)S(1)}, bf16[2,16,3200]{2,1,0:T(8,128)(2,1)S(1)}, u32[]{:S(2)}, u32[]{:S(2)}) collective-permute-start(bf16[2,16,3200]{2,1,0:T(8,128)(2,1)S(1)} %get-tuple-element.96), channel_id=1, source_target_pairs={{0,6},{2,4},{4,2},{6,0},{8,14},{10,12},{12,10},{14,8},{1,7},{3,5},... | collective-permute-start | bytes 614408 | tf_op jit(solution)/shard_map/ppermute | solution.py:56
  81.1 11.9 %collective-permute-start.24 = (bf16[2,16,3584]{2,1,0:T(8,128)(2,1)S(1)}, bf16[2,16,3584]{2,1,0:T(8,128)(2,1)S(1)}, u32[]{:S(2)}, u32[]{:S(2)}) collective-permute-start(bf16[2,16,3584]{2,1,0:T(8,128)(2,1)S(1)} %get-tuple-element.106), channel_id=1, source_target_pairs={{0,8},{2,10},{4,12},{6,14},{8,0},{10,2},{12,4},{14,6},{1,9},{3,11}... | collective-permute-start | bytes 688136 | tf_op jit(solution)/shard_map/ppermute | solution.py:56
  92.8 9.5 %collective-permute-start.20 = (bf16[2,16,3200]{2,1,0:T(8,128)(2,1)S(1)}, bf16[2,16,3200]{2,1,0:T(8,128)(2,1)S(1)}, u32[]{:S(2)}, u32[]{:S(2)}) collective-permute-start(bf16[2,16,3200]{2,1,0:T(8,128)(2,1)S(1)} %get-tuple-element.99), channel_id=1, source_target_pairs={{0,8},{2,10},{4,12},{6,14},{8,0},{10,2},{12,4},{14,6},{1,9},{3,11}... | collective-permute-start | bytes 614408 | tf_op jit(solution)/shard_map/ppermute | solution.py:56
  93.3 11.3 %collective-permute-start.30 = (bf16[16,3456]{1,0:T(8,128)(2,1)S(1)}, bf16[16,3456]{1,0:T(8,128)(2,1)S(1)}, u32[]{:S(2)}, u32[]{:S(2)}) collective-permute-start(bf16[16,3456]{1,0:T(8,128)(2,1)S(1)} %get-tuple-element.109.refs_0_), channel_id=1, source_target_pairs={{0,6},{2,4},{4,2},{6,0},{8,14},{10,12},{12,10},{14,8},{1,7},{3,5},... | collective-permute-start | bytes 331784 | tf_op jit(solution)/shard_map/ppermute | solution.py:56
  96.5 9.5 %collective-permute-start.29 = (bf16[16,3456]{1,0:T(8,128)(2,1)S(1)}, bf16[16,3456]{1,0:T(8,128)(2,1)S(1)}, u32[]{:S(2)}, u32[]{:S(2)}) collective-permute-start(bf16[16,3456]{1,0:T(8,128)(2,1)S(1)} %get-tuple-element.109.refs_0_), channel_id=1, source_target_pairs={{0,2},{2,0},{4,6},{6,4},{8,10},{10,8},{12,14},{14,12},{1,3},{3,1},... | collective-permute-start | bytes 331784 | tf_op jit(solution)/shard_map/ppermute | solution.py:56
  96.6 9.5 %collective-permute-start.28 = (bf16[16,3456]{1,0:T(8,128)(2,1)S(1)}, bf16[16,3456]{1,0:T(8,128)(2,1)S(1)}, u32[]{:S(2)}, u32[]{:S(2)}) collective-permute-start(bf16[16,3456]{1,0:T(8,128)(2,1)S(1)} %get-tuple-element.109.refs_0_), channel_id=1, source_target_pairs={{0,4},{2,6},{4,0},{6,2},{8,12},{10,14},{12,8},{14,10},{1,5},{3,7},... | collective-permute-start | bytes 331784 | tf_op jit(solution)/shard_map/ppermute | solution.py:56
  102.4 6.2 %collective-permute-start.27 = (bf16[16,3200]{1,0:T(8,128)(2,1)S(1)}, bf16[16,3200]{1,0:T(8,128)(2,1)S(1)}, u32[]{:S(2)}, u32[]{:S(2)}) collective-permute-start(bf16[16,3200]{1,0:T(8,128)(2,1)S(1)} %hidden.7.refs_0_), channel_id=1, source_target_pairs={{0,6},{2,4},{4,2},{6,0},{8,14},{10,12},{12,10},{14,8},{1,7},{3,5},... | collective-permute-start | bytes 307208 | tf_op jit(solution)/shard_map/ppermute | solution.py:56
  102.5 7.1 %collective-permute-start.26 = (bf16[16,3200]{1,0:T(8,128)(2,1)S(1)}, bf16[16,3200]{1,0:T(8,128)(2,1)S(1)}, u32[]{:S(2)}, u32[]{:S(2)}) collective-permute-start(bf16[16,3200]{1,0:T(8,128)(2,1)S(1)} %hidden.7.refs_0_), channel_id=1, source_target_pairs={{0,2},{2,0},{4,6},{6,4},{8,10},{10,8},{12,14},{14,12},{1,3},{3,1},... | collective-permute-start | bytes 307208 | tf_op jit(solution)/shard_map/ppermute | solution.py:56
  104.6 6.1 %collective-permute-start.25 = (bf16[16,3200]{1,0:T(8,128)(2,1)S(1)}, bf16[16,3200]{1,0:T(8,128)(2,1)S(1)}, u32[]{:S(2)}, u32[]{:S(2)}) collective-permute-start(bf16[16,3200]{1,0:T(8,128)(2,1)S(1)} %hidden.7.refs_0_), channel_id=1, source_target_pairs={{0,4},{2,6},{4,0},{6,2},{8,12},{10,14},{12,8},{14,10},{1,5},{3,7},... | collective-permute-start | bytes 307208 | tf_op jit(solution)/shard_map/ppermute | solution.py:56
  112.1 1.6 %collective-permute-start.31 = (f32[64,1024]{1,0:T(8,128)S(1)}, f32[64,1024]{1,0:T(8,128)S(1)}, u32[]{:S(2)}, u32[]{:S(2)}) collective-permute-start(f32[64,1024]{1,0:T(8,128)S(1)} %down.7.a_ref), channel_id=1, source_target_pairs={{0,1},{1,0},{2,3},{3,2},{4,5},{5,4},{6,7},{7,6},{8,9},{9,8},{10,11... | collective-permute-start | bytes 786440 | tf_op jit(solution)/shard_map/ppermute | solution.py:56
  114.3 4.3 %collective-permute-start.32 = (bf16[32,1024]{1,0:T(8,128)(2,1)S(1)}, bf16[32,1024]{1,0:T(8,128)(2,1)S(1)}, u32[]{:S(2)}, u32[]{:S(2)}) collective-permute-start(bf16[32,1024]{1,0:T(8,128)(2,1)S(1)} %get-tuple-element.112), channel_id=1, source_target_pairs={{16,0},{0,16},{17,1},{1,17},{18,2},{2,18},{19,3},{3,19},{20,4},{4,... | collective-permute-start | bytes 196616 | tf_op jit(solution)/shard_map/ppermute | solution.py:412

commit v4 on v3

--- a/solution.py
+++ b/solution.py
@@ -322,11 +322,12 @@
     )(base, weight, after)
 
 
-def down_kernel(first, count, added, fresh, base_ref, *refs):
+def down_kernel(first, count, added, fresh, sent, base_ref, *refs):
     refs = list(refs)
     parts, weight, refs = refs[:count], refs[count], refs[count + 1 :]
     before = refs.pop(0) if added else None
     out_ref = refs.pop(0)
+    send_ref = refs.pop(0) if sent else None
     if fresh:
         held, sems = refs
         row = pl.multiple_of(base_ref[0] + first, LANES)
@@ -342,17 +343,21 @@
         term = jnp.dot(hidden[:, a:b], held[a:b, :], preferred_element_type=F32)
         total = term if total is None else total + term
     out_ref[...] = total
-
-
-def down(first, base, parts, weight, before, fresh):
+    if sent:
+        send_ref[...] = total.astype(BF16)
+
+
+def down(first, base, parts, weight, before, fresh, sent):
     rows, width = sum(part.shape[0] for part in parts), weight.shape[1]
     depth = parts[0].shape[1]
     added = before is not None
     return pl.pallas_call(
-        functools.partial(down_kernel, first, len(parts), added, fresh),
-        out_shape=(struct((rows, width), F32),) + (struct((depth, width), BF16),) * fresh,
+        functools.partial(down_kernel, first, len(parts), added, fresh, sent),
+        out_shape=(struct((rows, width), F32),)
+        + (struct((rows, width), BF16),) * sent
+        + (struct((depth, width), BF16),) * fresh,
         in_specs=[SMEM] + [VMEM] * len(parts) + [HBM if fresh else VMEM] + [VMEM] * added,
-        out_specs=(VMEM,) * (1 + fresh),
+        out_specs=(VMEM,) * (1 + sent + fresh),
         scratch_shapes=[pltpu.SemaphoreType.DMA((len(cuts_of(depth, 2 * PIECE)),))] * fresh,
         name="down",
         compiler_params=pltpu.CompilerParams(vmem_limit_bytes=(DOWN_LIMIT if fresh else HELD_LIMIT) * MIB),
@@ -361,7 +366,7 @@
 
 
 def chip_kernel(a_ref, b_ref, state_ref, state_out, send_ref):
-    total = a_ref[...] + b_ref[...]
+    total = a_ref[...] + b_ref[...].astype(F32)
     send_ref[...] = total.astype(BF16)
     state_out[...] = state_ref[...] + total
 
@@ -379,12 +384,13 @@
 def finish_kernel(offsets, per, groups, where_ref, a_ref, b_ref, state_ref, out_ref, *refs):
     sends, (change, state) = refs[: groups - 1], refs[groups - 1 :]
     me, group = where_ref[0], where_ref[1]
+    other = b_ref[...].astype(F32)
     for p, offset in enumerate(offsets):
         first = (me ^ offset) * per
         if per % 8 == 0:
             first = pl.multiple_of(first, 8)
         rows = slice(p * per, (p + 1) * per)
-        change[pl.ds(first, per), :] = a_ref[rows, :] + b_ref[rows, :]
+        change[pl.ds(first, per), :] = a_ref[rows, :] + other[rows, :]
         state[pl.ds(first, per), :] = state_ref[rows, :]
     rows = out_ref.shape[0]
     own = pl.ds(pl.multiple_of(group * rows, 8), rows)
@@ -477,11 +483,11 @@
             fresh = c not in downs
             if c < last:
                 parts[c][0] = after(parts[c][0], parts[c + 1][0])
-            found = down(first, base, parts[c], down_weight if fresh else downs[c], change, fresh)
+            found = down(first, base, parts[c], down_weight if fresh else downs[c], change, fresh, c == last)
             change = found[0]
             if fresh:
-                downs[c] = found[1]
-        other = swap(change, "ffn", 1, ffn)
+                downs[c] = found[-1]
+        other = swap(found[1], "ffn", 1, ffn)
         if step + 1 < STEPS:
             shape = state.shape
             state, send = pl.pallas_call(

time: 119 us -> 119 us (level)
  transfers between devices with their start and end apart: 33 -> 33, of which waited for: 22 -> 22; matrix products, arithmetic and copies ran while one was open for 0% -> 0% of each run, Pallas kernels for 18% -> 19%
where the time goes in v4:
time: 119 us
  waiting for transfers between devices  47.8 us (40%)
  starting transfers between devices  38.4 us (32%)
  Pallas kernels  31.9 us (27%)
    ppermute x30, waiting for transfers between devices, swap(): return lax.ppermute(value, axis, [(i, i ^ flip) for i in range(count)])  38.7 us
    ppermute x30, starting transfers between devices, swap(): return lax.ppermute(value, axis, [(i, i ^ flip) for i in range(count)])  34.5 us
    pallas_call x4, Pallas kernels, gate_up(): pl.pallas_call(functools.partial(gate_up_kernel, first, per, size, fresh,...  13.4 us
    ppermute x3, waiting for transfers between devices, from_group(): lax.ppermute(value, 'groups', [((i + k) % groups, i) for i in range(group...  9.04 us
    pallas_call x2, Pallas kernels, load_down(): pl.pallas_call(functools.partial(load_down_kernel, first), out_shape=stru...  5.95 us
    pallas_call x4, Pallas kernels, down(): pl.pallas_call(functools.partial(down_kernel, first, len(parts), added, f...  5.26 us
    ppermute x3, starting transfers between devices, from_group(): lax.ppermute(value, 'groups', [((i + k) % groups, i) for i in range(group...  3.85 us
    pallas_call x1, Pallas kernels, load(): pl.pallas_call(functools.partial(load_kernel, first), out_shape=struct((d...  3.13 us
  transfers between devices with their start and end apart: 33, of which 22 were waited for; matrix products, arithmetic and copies ran while one was open for 0% of the time, Pallas kernels for 19%

profile of v4, /device:TPU:0, one launch (start us, length us, event | category | flops | bytes accessed | tf_op | source)
XLA Modules:
  0.0 118.9 jit_solution(5996642753505479841)
XLA Ops:
  0.0 2.9 %collective-permute-start = (bf16[32,1024]{1,0:T(8,128)(2,1)}, bf16[32,1024]{1,0:T(8,128)(2,1)S(1)}, u32[]{:S(2)}, u32[]{:S(2)}) collective-permute-start(bf16[32,1024]{1,0:T(8,128)(2,1)} %own_ref.1), channel_id=1, source_target_pairs={{16,0},{0,16},{17,1},{1,17},{18,2},{2,18},{19,3},{3,19},{20,4},{4,... | collective-permute-start | bytes 196616 | tf_op jit(solution)/shard_map/ppermute | solution.py:418
  2.9 3.1 %load.1.refs_1_ = bf16[1024,3456]{1,0:T(8,128)(2,1)S(1)} custom-call(s32[1]{0:T(128)} %bitcast.2.base_ref, bf16[1024,13312]{1,0:T(8,128)(2,1)} %refs_0_.1), custom_call_target="tpu_custom_call" | custom-call | bytes 14155776 | tf_op jit(solution)/shard_map/load/pallas_call | solution.py:144
  6.2 0.7 arrange.1
  6.8 3.6 %gate_up.4 = (f32[2,16,3584]{2,1,0:T(8,128)S(1)}, bf16[2,16,3584]{2,1,0:T(8,128)(2,1)S(1)}, bf16[2,16,3584]{2,1,0:T(8,128)(2,1)S(1)}, bf16[2,16,3584]{2,1,0:T(8,128)(2,1)S(1)}, bf16[1024,3456]{1,0:T(8,128)(2,1)S(1)}) custom-call(s32[1]{0:T(128)} %bitcast.2.base_ref, bf16[64,1024]{1,0:T(8,128)(2,1)S(1)} %get-tuple-element.67.x_ref, ...), custom_call_target="tpu_custom_call" | custom-call | flops 905969664 | bytes 14155776 | tf_op jit(solution)/shard_map/gate_up/pallas_call | solution.py:201
  10.4 1.6 %collective-permute-start.1 = (bf16[2,16,3584]{2,1,0:T(8,128)(2,1)S(1)}, bf16[2,16,3584]{2,1,0:T(8,128)(2,1)S(1)}, u32[]{:S(2)}, u32[]{:S(2)}) collective-permute-start(bf16[2,16,3584]{2,1,0:T(8,128)(2,1)S(1)} %get-tuple-element.70), channel_id=1, source_target_pairs={{0,4},{2,6},{4,0},{6,2},{8,12},{10,14},{12,8},{14,10},{1,5},{3,7},... | collective-permute-start | bytes 688136 | tf_op jit(solution)/shard_map/ppermute | solution.py:56
  12.1 1.5 %collective-permute-start.2 = (bf16[2,16,3584]{2,1,0:T(8,128)(2,1)S(1)}, bf16[2,16,3584]{2,1,0:T(8,128)(2,1)S(1)}, u32[]{:S(2)}, u32[]{:S(2)}) collective-permute-start(bf16[2,16,3584]{2,1,0:T(8,128)(2,1)S(1)} %get-tuple-element.71), channel_id=1, source_target_pairs={{0,2},{2,0},{4,6},{6,4},{8,10},{10,8},{12,14},{14,12},{1,3},{3,1},... | collective-permute-start | bytes 688136 | tf_op jit(solution)/shard_map/ppermute | solution.py:56
  14.0 5.3 %gate_up.5 = (f32[2,16,3200]{2,1,0:T(8,128)S(1)}, bf16[2,16,3200]{2,1,0:T(8,128)(2,1)S(1)}, bf16[2,16,3200]{2,1,0:T(8,128)(2,1)S(1)}, bf16[2,16,3200]{2,1,0:T(8,...) custom-call(s32[1]{0:T(128)} %bitcast.2.base_ref, ...), custom_call_target="tpu_custom_call" | custom-call | flops 838860800 | bytes 13107200 | tf_op jit(solution)/shard_map/gate_up/pallas_call | solution.py:201
  19.3 1.6 %collective-permute-start.4 = (bf16[2,16,3200]{2,1,0:T(8,128)(2,1)S(1)}, bf16[2,16,3200]{2,1,0:T(8,128)(2,1)S(1)}, u32[]{:S(2)}, u32[]{:S(2)}) collective-permute-start(bf16[2,16,3200]{2,1,0:T(8,128)(2,1)S(1)} %get-tuple-element.75), channel_id=1, source_target_pairs={{0,4},{2,6},{4,0},{6,2},{8,12},{10,14},{12,8},{14,10},{1,5},{3,7},... | collective-permute-start | bytes 614408 | tf_op jit(solution)/shard_map/ppermute | solution.py:56
  21.0 1.5 %collective-permute-start.5 = (bf16[2,16,3200]{2,1,0:T(8,128)(2,1)S(1)}, bf16[2,16,3200]{2,1,0:T(8,128)(2,1)S(1)}, u32[]{:S(2)}, u32[]{:S(2)}) collective-permute-start(bf16[2,16,3200]{2,1,0:T(8,128)(2,1)S(1)} %get-tuple-element.76), channel_id=1, source_target_pairs={{0,2},{2,0},{4,6},{6,4},{8,10},{10,8},{12,14},{14,12},{1,3},{3,1},... | collective-permute-start | bytes 614408 | tf_op jit(solution)/shard_map/ppermute | solution.py:56
  23.4 1.5 %collective-permute-done.3.refs_2_ = bf16[2,16,3584]{2,1,0:T(8,128)(2,1)S(1)} collective-permute-done((bf16[2,16,3584]{2,1,0:T(8,128)(2,1)S(1)}, bf16[2,16,3584]{2,1,0:T(8,128)(2,1)S(1)}, u32[]{:S(2)}, u32[]{:S(2)}) %collective-permute-start.3) | collective-permute-done | bytes 229408 | tf_op jit(solution)/shard_map/ppermute | solution.py:56
  25.5 2.7 %collective-permute-start.8 = (bf16[2,16,3584]{2,1,0:T(8,128)(2,1)S(1)}, bf16[2,16,3584]{2,1,0:T(8,128)(2,1)S(1)}, u32[]{:S(2)}, u32[]{:S(2)}) collective-permute-start(bf16[2,16,3584]{2,1,0:T(8,128)(2,1)S(1)} %get-tuple-element.82), channel_id=1, source_target_pairs={{0,8},{2,10},{4,12},{6,14},{8,0},{10,2},{12,4},{14,6},{1,9},{3,11}... | collective-permute-start | bytes 688136 | tf_op jit(solution)/shard_map/ppermute | solution.py:56
  28.2 3.1 %load_down.2.refs_4_ = bf16[3456,1024]{1,0:T(8,128)(2,1)S(1)} custom-call(s32[1]{0:T(128)} %bitcast.2.base_ref, bf16[13312,1024]{1,0:T(8,128)(2,1)} %down_hbm.3, f32[2,16,3584]{2,1,0:T(8,128)S(1)} %get-tuple-element.81.after_ref.keep_ref), custom_call_target="tpu_custom_call" | custom-call | bytes 7077888 | tf_op jit(solution)/shard_map/load_down/pallas_call | solution.py:313
  31.2 2.1 %collective-permute-done.4.refs_0_ = bf16[2,16,3200]{2,1,0:T(8,128)(2,1)S(1)} collective-permute-done((bf16[2,16,3200]{2,1,0:T(8,128)(2,1)S(1)}, bf16[2,16,3200]{2,1,0:T(8,128)(2,1)S(1)}, u32[]{:S(2)}, u32[]{:S(2)}) %collective-permute-start.4) | collective-permute-done | bytes 204832 | tf_op jit(solution)/shard_map/ppermute | solution.py:56
  33.3 3.9 %collective-permute-done.6.refs_2_ = bf16[2,16,3200]{2,1,0:T(8,128)(2,1)S(1)} collective-permute-done((bf16[2,16,3200]{2,1,0:T(8,128)(2,1)S(1)}, bf16[2,16,3200]{2,1,0:T(8,128)(2,1)S(1)}, u32[]{:S(2)}, u32[]{:S(2)}) %collective-permute-start.6) | collective-permute-done | bytes 204832 | tf_op jit(solution)/shard_map/ppermute | solution.py:56
  37.8 3.1 %collective-permute-start.14 = (bf16[16,3456]{1,0:T(8,128)(2,1)S(1)}, bf16[16,3456]{1,0:T(8,128)(2,1)S(1)}, u32[]{:S(2)}, u32[]{:S(2)}) collective-permute-start(bf16[16,3456]{1,0:T(8,128)(2,1)S(1)} %get-tuple-element.85.refs_0_), channel_id=1, source_target_pairs={{0,6},{2,4},{4,2},{6,0},{8,14},{10,12},{12,10},{14,8},{1,7},{3,5},... | collective-permute-start | bytes 331784 | tf_op jit(solution)/shard_map/ppermute | solution.py:56
  40.9 2.2 %collective-permute-start.13 = (bf16[16,3456]{1,0:T(8,128)(2,1)S(1)}, bf16[16,3456]{1,0:T(8,128)(2,1)S(1)}, u32[]{:S(2)}, u32[]{:S(2)}) collective-permute-start(bf16[16,3456]{1,0:T(8,128)(2,1)S(1)} %get-tuple-element.85.refs_0_), channel_id=1, source_target_pairs={{0,2},{2,0},{4,6},{6,4},{8,10},{10,8},{12,14},{14,12},{1,3},{3,1},... | collective-permute-start | bytes 331784 | tf_op jit(solution)/shard_map/ppermute | solution.py:56
  43.1 2.9 %load_down.3.refs_4_ = bf16[3200,1024]{1,0:T(8,128)(2,1)S(1)} custom-call(s32[1]{0:T(128)} %bitcast.2.base_ref, bf16[13312,1024]{1,0:T(8,128)(2,1)} %down_hbm.3, f32[2,16,3200]{2,1,0:T(8,128)S(1)} %get-tuple-element.79.after_ref.keep_ref), custom_call_target="tpu_custom_call" | custom-call | bytes 6553600 | tf_op jit(solution)/shard_map/load_down/pallas_call | solution.py:313
  46.0 2.5 %collective-permute-done.7.refs_0_ = bf16[2,16,3200]{2,1,0:T(8,128)(2,1)S(1)} collective-permute-done((bf16[2,16,3200]{2,1,0:T(8,128)(2,1)S(1)}, bf16[2,16,3200]{2,1,0:T(8,128)(2,1)S(1)}, u32[]{:S(2)}, u32[]{:S(2)}) %collective-permute-start.7) | collective-permute-done | bytes 204832 | tf_op jit(solution)/shard_map/ppermute | solution.py:56
  48.8 1.0 collective-permute-start.10
  49.7 2.5 %collective-permute-start.9 = (bf16[16,3200]{1,0:T(8,128)(2,1)S(1)}, bf16[16,3200]{1,0:T(8,128)(2,1)S(1)}, u32[]{:S(2)}, u32[]{:S(2)}) collective-permute-start(bf16[16,3200]{1,0:T(8,128)(2,1)S(1)} %hidden.5.refs_0_), channel_id=1, source_target_pairs={{0,4},{2,6},{4,0},{6,2},{8,12},{10,14},{12,8},{14,10},{1,5},{3,7},... | collective-permute-start | bytes 307208 | tf_op jit(solution)/shard_map/ppermute | solution.py:56
  52.3 1.4 %down.4.refs_5_ = f32[64,1024]{1,0:T(8,128)S(1)} custom-call(s32[1]{0:T(128)} %bitcast.2.base_ref, bf16[16,3456]{1,0:T(8,128)(2,1)S(1)} %get-tuple-element.85.refs_0_, bf16[16,3456]{1,0:T(8,128)(2,1)S(1)} %collective-permute-done.12.refs_1_, bf16[16,3456]{1,0:T(8,128)(2,1)S(1)} %collective-permute-done.13.refs_2_, ...), custom_call_target="tpu_custom_call" | custom-call | flops 452984832 | bytes 7077888 | tf_op jit(solution)/shard_map/down/pallas_call | solution.py:354
  53.6 1.4 %collective-permute-done.11.refs_3_ = bf16[16,3200]{1,0:T(8,128)(2,1)S(1)} collective-permute-done((bf16[16,3200]{1,0:T(8,128)(2,1)S(1)}, bf16[16,3200]{1,0:T(8,128)(2,1)S(1)}, u32[]{:S(2)}, u32[]{:S(2)}) %collective-permute-start.11) | collective-permute-done | bytes 102432 | tf_op jit(solution)/shard_map/ppermute | solution.py:56
  55.6 1.3 %down.5 = (f32[64,1024]{1,0:T(8,128)S(1)}, bf16[64,1024]{1,0:T(8,128)(2,1)S(1)}) custom-call(s32[1]{0:T(128)} %bitcast.2.base_ref, bf16[16,3200]{1,0:T(8,128)(2,1)S(1)} %hidden.5.refs_0_, bf16[16,3200]{1,0:T(8,128)(2,1)S(1)} %collective-permute-done.9.refs_1_, bf16[16,3200]{1,0:T(8,128)(2,1)S(1)} %collective-permute-done.10.refs_2_, ...), custom_call_target="tpu_custom_call" | custom-call | flops 419430400 | bytes 6553600 | tf_op jit(solution)/shard_map/down/pallas_call | solution.py:354
  57.0 1.3 %collective-permute-done.15.b_ref = bf16[64,1024]{1,0:T(8,128)(2,1)S(1)} collective-permute-done((bf16[64,1024]{1,0:T(8,128)(2,1)S(1)}, bf16[64,1024]{1,0:T(8,128)(2,1)S(1)}, u32[]{:S(2)}, u32[]{:S(2)}) %collective-permute-start.15) | collective-permute-done | bytes 131104 | tf_op jit(solution)/shard_map/ppermute | solution.py:56
  58.7 5.2 %collective-permute-done.16.refs_0_ = bf16[64,1024]{1,0:T(8,128)(2,1)S(1)} collective-permute-done((bf16[64,1024]{1,0:T(8,128)(2,1)S(1)}, bf16[64,1024]{1,0:T(8,128)(2,1)S(1)}, u32[]{:S(2)}, u32[]{:S(2)}) %collective-permute-start.16) | collective-permute-done | bytes 131104 | tf_op jit(solution)/shard_map/ppermute | solution.py:418
  64.1 2.3 %gate_up.6 = (f32[2,16,3584]{2,1,0:T(8,128)S(1)}, bf16[2,16,3584]{2,1,0:T(8,128)(2,1)S(1)}, bf16[2,16,3584]{2,1,0:T(8,128)(2,1)S(1)}, bf16[2,16,3584]{2,1,0:T(8,128)(2,1)S(1)}) custom-call(s32[1]{0:T(128)} %bitcast.2.base_ref, bf16[64,1024]{1,0:T(8,128)(2,1)S(1)} %get-tuple-element.96.x_ref, f32[64,128]{1,0:T(8,128)S(1)} %get-tuple-element.93.refs_0_, ...), custom_call_target="tpu_custom_call" | custom-call | flops 905969664 | bytes 14155776 | tf_op jit(solution)/shard_map/gate_up/pallas_call | solution.py:201
  66.3 1.4 %collective-permute-start.21 = (bf16[2,16,3584]{2,1,0:T(8,128)(2,1)S(1)}, bf16[2,16,3584]{2,1,0:T(8,128)(2,1)S(1)}, u32[]{:S(2)}, u32[]{:S(2)}) collective-permute-start(bf16[2,16,3584]{2,1,0:T(8,128)(2,1)S(1)} %get-tuple-element.107), channel_id=1, source_target_pairs={{0,4},{2,6},{4,0},{6,2},{8,12},{10,14},{12,8},{14,10},{1,5},{3,7},... | collective-permute-start | bytes 688136 | tf_op jit(solution)/shard_map/ppermute | solution.py:56
  68.1 1.8 %collective-permute-start.23 = (bf16[2,16,3584]{2,1,0:T(8,128)(2,1)S(1)}, bf16[2,16,3584]{2,1,0:T(8,128)(2,1)S(1)}, u32[]{:S(2)}, u32[]{:S(2)}) collective-permute-start(bf16[2,16,3584]{2,1,0:T(8,128)(2,1)S(1)} %get-tuple-element.109), channel_id=1, source_target_pairs={{0,6},{2,4},{4,2},{6,0},{8,14},{10,12},{12,10},{14,8},{1,7},{3,5},... | collective-permute-start | bytes 688136 | tf_op jit(solution)/shard_map/ppermute | solution.py:56
  69.9 2.3 %gate_up.7 = (f32[2,16,3200]{2,1,0:T(8,128)S(1)}, bf16[2,16,3200]{2,1,0:T(8,128)(2,1)S(1)}, bf16[2,16,3200]{2,1,0:T(8,128)(2,1)S(1)}, bf16[2,16,3200]{2,1,0:T(8,128)(2,1)S(1)}) custom-call(s32[1]{0:T(128)} %bitcast.2.base_ref, bf16[64,1024]{1,0:T(8,128)(2,1)S(1)} %get-tuple-element.96.x_ref, bf16[1024,3200]{1,0:T(8,128)(2,1)S(1)} %get-tuple-element.97.refs_0_, ...), custom_call_target="tpu_custom_call" | custom-call | flops 838860800 | bytes 13107200 | tf_op jit(solution)/shard_map/gate_up/pallas_call | solution.py:201
  72.2 1.4 %collective-permute-start.17 = (bf16[2,16,3200]{2,1,0:T(8,128)(2,1)S(1)}, bf16[2,16,3200]{2,1,0:T(8,128)(2,1)S(1)}, u32[]{:S(2)}, u32[]{:S(2)}) collective-permute-start(bf16[2,16,3200]{2,1,0:T(8,128)(2,1)S(1)} %get-tuple-element.100), channel_id=1, source_target_pairs={{0,4},{2,6},{4,0},{6,2},{8,12},{10,14},{12,8},{14,10},{1,5},{3,7},... | collective-permute-start | bytes 614408 | tf_op jit(solution)/shard_map/ppermute | solution.py:56
  74.0 1.0 collective-permute-done.21.refs_0_
  75.0 1.2 collective-permute-start.19
  76.1 4.0 %collective-permute-done.22.refs_1_ = bf16[2,16,3584]{2,1,0:T(8,128)(2,1)S(1)} collective-permute-done((bf16[2,16,3584]{2,1,0:T(8,128)(2,1)S(1)}, bf16[2,16,3584]{2,1,0:T(8,128)(2,1)S(1)}, u32[]{:S(2)}, u32[]{:S(2)}) %collective-permute-start.22) | collective-permute-done | bytes 229408 | tf_op jit(solution)/shard_map/ppermute | solution.py:56
  80.9 1.7 %collective-permute-start.24 = (bf16[2,16,3584]{2,1,0:T(8,128)(2,1)S(1)}, bf16[2,16,3584]{2,1,0:T(8,128)(2,1)S(1)}, u32[]{:S(2)}, u32[]{:S(2)}) collective-permute-start(bf16[2,16,3584]{2,1,0:T(8,128)(2,1)S(1)} %get-tuple-element.112), channel_id=1, source_target_pairs={{0,8},{2,10},{4,12},{6,14},{8,0},{10,2},{12,4},{14,6},{1,9},{3,11}... | collective-permute-start | bytes 688136 | tf_op jit(solution)/shard_map/ppermute | solution.py:56
  82.6 5.9 %collective-permute-done.17.refs_0_ = bf16[2,16,3200]{2,1,0:T(8,128)(2,1)S(1)} collective-permute-done((bf16[2,16,3200]{2,1,0:T(8,128)(2,1)S(1)}, bf16[2,16,3200]{2,1,0:T(8,128)(2,1)S(1)}, u32[]{:S(2)}, u32[]{:S(2)}) %collective-permute-start.17) | collective-permute-done | bytes 204832 | tf_op jit(solution)/shard_map/ppermute | solution.py:56
  88.5 3.8 %collective-permute-done.19.refs_2_ = bf16[2,16,3200]{2,1,0:T(8,128)(2,1)S(1)} collective-permute-done((bf16[2,16,3200]{2,1,0:T(8,128)(2,1)S(1)}, bf16[2,16,3200]{2,1,0:T(8,128)(2,1)S(1)}, u32[]{:S(2)}, u32[]{:S(2)}) %collective-permute-start.19) | collective-permute-done | bytes 204832 | tf_op jit(solution)/shard_map/ppermute | solution.py:56
  93.1 3.3 %collective-permute-start.30 = (bf16[16,3456]{1,0:T(8,128)(2,1)S(1)}, bf16[16,3456]{1,0:T(8,128)(2,1)S(1)}, u32[]{:S(2)}, u32[]{:S(2)}) collective-permute-start(bf16[16,3456]{1,0:T(8,128)(2,1)S(1)} %get-tuple-element.115.refs_0_), channel_id=1, source_target_pairs={{0,6},{2,4},{4,2},{6,0},{8,14},{10,12},{12,10},{14,8},{1,7},{3,5},... | collective-permute-start | bytes 331784 | tf_op jit(solution)/shard_map/ppermute | solution.py:56
  97.0 5.1 %collective-permute-done.20.refs_0_ = bf16[2,16,3200]{2,1,0:T(8,128)(2,1)S(1)} collective-permute-done((bf16[2,16,3200]{2,1,0:T(8,128)(2,1)S(1)}, bf16[2,16,3200]{2,1,0:T(8,128)(2,1)S(1)}, u32[]{:S(2)}, u32[]{:S(2)}) %collective-permute-start.20) | collective-permute-done | bytes 204832 | tf_op jit(solution)/shard_map/ppermute | solution.py:56
  102.4 2.1 %collective-permute-start.26 = (bf16[16,3200]{1,0:T(8,128)(2,1)S(1)}, bf16[16,3200]{1,0:T(8,128)(2,1)S(1)}, u32[]{:S(2)}, u32[]{:S(2)}) collective-permute-start(bf16[16,3200]{1,0:T(8,128)(2,1)S(1)} %hidden.7.refs_0_), channel_id=1, source_target_pairs={{0,2},{2,0},{4,6},{6,4},{8,10},{10,8},{12,14},{14,12},{1,3},{3,1},... | collective-permute-start | bytes 307208 | tf_op jit(solution)/shard_map/ppermute | solution.py:56
  104.5 1.4 %collective-permute-start.25 = (bf16[16,3200]{1,0:T(8,128)(2,1)S(1)}, bf16[16,3200]{1,0:T(8,128)(2,1)S(1)}, u32[]{:S(2)}, u32[]{:S(2)}) collective-permute-start(bf16[16,3200]{1,0:T(8,128)(2,1)S(1)} %hidden.7.refs_0_), channel_id=1, source_target_pairs={{0,4},{2,6},{4,0},{6,2},{8,12},{10,14},{12,8},{14,10},{1,5},{3,7},... | collective-permute-start | bytes 307208 | tf_op jit(solution)/shard_map/ppermute | solution.py:56
  105.9 1.4 %down.6.refs_5_ = f32[64,1024]{1,0:T(8,128)S(1)} custom-call(s32[1]{0:T(128)} %bitcast.2.base_ref, bf16[16,3456]{1,0:T(8,128)(2,1)S(1)} %get-tuple-element.115.refs_0_, bf16[16,3456]{1,0:T(8,128)(2,1)S(1)} %collective-permute-done.28.refs_1_, bf16[16,3456]{1,0:T(8,128)(2,1)S(1)} %collective-permute-done.29.refs_2_, ...), custom_call_target="tpu_custom_call" | custom-call | flops 452984832 | bytes 7077888 | tf_op jit(solution)/shard_map/down/pallas_call | solution.py:354
  107.2 1.3 %collective-permute-done.27.refs_3_ = bf16[16,3200]{1,0:T(8,128)(2,1)S(1)} collective-permute-done((bf16[16,3200]{1,0:T(8,128)(2,1)S(1)}, bf16[16,3200]{1,0:T(8,128)(2,1)S(1)}, u32[]{:S(2)}, u32[]{:S(2)}) %collective-permute-start.27) | collective-permute-done | bytes 102432 | tf_op jit(solution)/shard_map/ppermute | solution.py:56
  108.5 1.0 collective-permute-done.26.refs_2_
  109.5 1.1 collective-permute-done.25.refs_1_
  110.6 1.3 %down.7 = (f32[64,1024]{1,0:T(8,128)S(1)}, bf16[64,1024]{1,0:T(8,128)(2,1)S(1)}) custom-call(s32[1]{0:T(128)} %bitcast.2.base_ref, bf16[16,3200]{1,0:T(8,128)(2,1)S(1)} %hidden.7.refs_0_, bf16[16,3200]{1,0:T(8,128)(2,1)S(1)} %collective-permute-done.25.refs_1_, bf16[16,3200]{1,0:T(8,128)(2,1)S(1)} %collective-permute-done.26.refs_2_, ...), custom_call_target="tpu_custom_call" | custom-call | flops 419430400 | bytes 6553600 | tf_op jit(solution)/shard_map/down/pallas_call | solution.py:354
  112.0 1.3 %collective-permute-done.31.b_ref = bf16[64,1024]{1,0:T(8,128)(2,1)S(1)} collective-permute-done((bf16[64,1024]{1,0:T(8,128)(2,1)S(1)}, bf16[64,1024]{1,0:T(8,128)(2,1)S(1)}, u32[]{:S(2)}, u32[]{:S(2)}) %collective-permute-start.31) | collective-permute-done | bytes 131104 | tf_op jit(solution)/shard_map/ppermute | solution.py:56
  114.5 3.8 %collective-permute-done.32 = bf16[32,1024]{1,0:T(8,128)(2,1)S(1)} collective-permute-done((bf16[32,1024]{1,0:T(8,128)(2,1)S(1)}, bf16[32,1024]{1,0:T(8,128)(2,1)S(1)}, u32[]{:S(2)}, u32[]{:S(2)}) %collective-permute-start.32) | collective-permute-done | bytes 65568 | tf_op jit(solution)/shard_map/ppermute | solution.py:418
  118.3 0.7 convert_add_fusion
  (45 shorter events, 8.5 us)
Async XLA Ops:
  0.0 6.2 %collective-permute-start = (bf16[32,1024]{1,0:T(8,128)(2,1)}, bf16[32,1024]{1,0:T(8,128)(2,1)S(1)}, u32[]{:S(2)}, u32[]{:S(2)}) collective-permute-start(bf16[32,1024]{1,0:T(8,128)(2,1)} %own_ref.1), channel_id=1, source_target_pairs={{16,0},{0,16},{17,1},{1,17},{18,2},{2,18},{19,3},{3,19},{20,4},{4,... | collective-permute-start | bytes 196616 | tf_op jit(solution)/shard_map/ppermute | solution.py:418
  2.9 3.2 %copy-start = (bf16[32,1024]{1,0:T(8,128)(2,1)S(1)}, bf16[32,1024]{1,0:T(8,128)(2,1)}, u32[]{:S(2)}) copy-start(bf16[32,1024]{1,0:T(8,128)(2,1)} %own_ref.1) | copy-start | bytes 196612
  10.4 12.1 %collective-permute-start.1 = (bf16[2,16,3584]{2,1,0:T(8,128)(2,1)S(1)}, bf16[2,16,3584]{2,1,0:T(8,128)(2,1)S(1)}, u32[]{:S(2)}, u32[]{:S(2)}) collective-permute-start(bf16[2,16,3584]{2,1,0:T(8,128)(2,1)S(1)} %get-tuple-element.70), channel_id=1, source_target_pairs={{0,4},{2,6},{4,0},{6,2},{8,12},{10,14},{12,8},{14,10},{1,5},{3,7},... | collective-permute-start | bytes 688136 | tf_op jit(solution)/shard_map/ppermute | solution.py:56
  12.1 11.3 %collective-permute-start.2 = (bf16[2,16,3584]{2,1,0:T(8,128)(2,1)S(1)}, bf16[2,16,3584]{2,1,0:T(8,128)(2,1)S(1)}, u32[]{:S(2)}, u32[]{:S(2)}) collective-permute-start(bf16[2,16,3584]{2,1,0:T(8,128)(2,1)S(1)} %get-tuple-element.71), channel_id=1, source_target_pairs={{0,2},{2,0},{4,6},{6,4},{8,10},{10,8},{12,14},{14,12},{1,3},{3,1},... | collective-permute-start | bytes 688136 | tf_op jit(solution)/shard_map/ppermute | solution.py:56
  13.6 11.4 %collective-permute-start.3 = (bf16[2,16,3584]{2,1,0:T(8,128)(2,1)S(1)}, bf16[2,16,3584]{2,1,0:T(8,128)(2,1)S(1)}, u32[]{:S(2)}, u32[]{:S(2)}) collective-permute-start(bf16[2,16,3584]{2,1,0:T(8,128)(2,1)S(1)} %get-tuple-element.72), channel_id=1, source_target_pairs={{0,6},{2,4},{4,2},{6,0},{8,14},{10,12},{12,10},{14,8},{1,7},{3,5},... | collective-permute-start | bytes 688136 | tf_op jit(solution)/shard_map/ppermute | solution.py:56
  19.3 14.0 %collective-permute-start.4 = (bf16[2,16,3200]{2,1,0:T(8,128)(2,1)S(1)}, bf16[2,16,3200]{2,1,0:T(8,128)(2,1)S(1)}, u32[]{:S(2)}, u32[]{:S(2)}) collective-permute-start(bf16[2,16,3200]{2,1,0:T(8,128)(2,1)S(1)} %get-tuple-element.75), channel_id=1, source_target_pairs={{0,4},{2,6},{4,0},{6,2},{8,12},{10,14},{12,8},{14,10},{1,5},{3,7},... | collective-permute-start | bytes 614408 | tf_op jit(solution)/shard_map/ppermute | solution.py:56
  21.0 12.3 %collective-permute-start.5 = (bf16[2,16,3200]{2,1,0:T(8,128)(2,1)S(1)}, bf16[2,16,3200]{2,1,0:T(8,128)(2,1)S(1)}, u32[]{:S(2)}, u32[]{:S(2)}) collective-permute-start(bf16[2,16,3200]{2,1,0:T(8,128)(2,1)S(1)} %get-tuple-element.76), channel_id=1, source_target_pairs={{0,2},{2,0},{4,6},{6,4},{8,10},{10,8},{12,14},{14,12},{1,3},{3,1},... | collective-permute-start | bytes 614408 | tf_op jit(solution)/shard_map/ppermute | solution.py:56
  22.5 14.7 %collective-permute-start.6 = (bf16[2,16,3200]{2,1,0:T(8,128)(2,1)S(1)}, bf16[2,16,3200]{2,1,0:T(8,128)(2,1)S(1)}, u32[]{:S(2)}, u32[]{:S(2)}) collective-permute-start(bf16[2,16,3200]{2,1,0:T(8,128)(2,1)S(1)} %get-tuple-element.77), channel_id=1, source_target_pairs={{0,6},{2,4},{4,2},{6,0},{8,14},{10,12},{12,10},{14,8},{1,7},{3,5},... | collective-permute-start | bytes 614408 | tf_op jit(solution)/shard_map/ppermute | solution.py:56
  25.5 12.0 %collective-permute-start.8 = (bf16[2,16,3584]{2,1,0:T(8,128)(2,1)S(1)}, bf16[2,16,3584]{2,1,0:T(8,128)(2,1)S(1)}, u32[]{:S(2)}, u32[]{:S(2)}) collective-permute-start(bf16[2,16,3584]{2,1,0:T(8,128)(2,1)S(1)} %get-tuple-element.82), channel_id=1, source_target_pairs={{0,8},{2,10},{4,12},{6,14},{8,0},{10,2},{12,4},{14,6},{1,9},{3,11}... | collective-permute-start | bytes 688136 | tf_op jit(solution)/shard_map/ppermute | solution.py:56
  37.4 11.1 %collective-permute-start.7 = (bf16[2,16,3200]{2,1,0:T(8,128)(2,1)S(1)}, bf16[2,16,3200]{2,1,0:T(8,128)(2,1)S(1)}, u32[]{:S(2)}, u32[]{:S(2)}) collective-permute-start(bf16[2,16,3200]{2,1,0:T(8,128)(2,1)S(1)} %get-tuple-element.80), channel_id=1, source_target_pairs={{0,8},{2,10},{4,12},{6,14},{8,0},{10,2},{12,4},{14,6},{1,9},{3,11}... | collective-permute-start | bytes 614408 | tf_op jit(solution)/shard_map/ppermute | solution.py:56
  37.8 11.9 %collective-permute-start.14 = (bf16[16,3456]{1,0:T(8,128)(2,1)S(1)}, bf16[16,3456]{1,0:T(8,128)(2,1)S(1)}, u32[]{:S(2)}, u32[]{:S(2)}) collective-permute-start(bf16[16,3456]{1,0:T(8,128)(2,1)S(1)} %get-tuple-element.85.refs_0_), channel_id=1, source_target_pairs={{0,6},{2,4},{4,2},{6,0},{8,14},{10,12},{12,10},{14,8},{1,7},{3,5},... | collective-permute-start | bytes 331784 | tf_op jit(solution)/shard_map/ppermute | solution.py:56
  40.9 11.4 %collective-permute-start.13 = (bf16[16,3456]{1,0:T(8,128)(2,1)S(1)}, bf16[16,3456]{1,0:T(8,128)(2,1)S(1)}, u32[]{:S(2)}, u32[]{:S(2)}) collective-permute-start(bf16[16,3456]{1,0:T(8,128)(2,1)S(1)} %get-tuple-element.85.refs_0_), channel_id=1, source_target_pairs={{0,2},{2,0},{4,6},{6,4},{8,10},{10,8},{12,14},{14,12},{1,3},{3,1},... | collective-permute-start | bytes 331784 | tf_op jit(solution)/shard_map/ppermute | solution.py:56
  43.1 9.2 %collective-permute-start.12 = (bf16[16,3456]{1,0:T(8,128)(2,1)S(1)}, bf16[16,3456]{1,0:T(8,128)(2,1)S(1)}, u32[]{:S(2)}, u32[]{:S(2)}) collective-permute-start(bf16[16,3456]{1,0:T(8,128)(2,1)S(1)} %get-tuple-element.85.refs_0_), channel_id=1, source_target_pairs={{0,4},{2,6},{4,0},{6,2},{8,12},{10,14},{12,8},{14,10},{1,5},{3,7},... | collective-permute-start | bytes 331784 | tf_op jit(solution)/shard_map/ppermute | solution.py:56
  48.7 6.3 %collective-permute-start.11 = (bf16[16,3200]{1,0:T(8,128)(2,1)S(1)}, bf16[16,3200]{1,0:T(8,128)(2,1)S(1)}, u32[]{:S(2)}, u32[]{:S(2)}) collective-permute-start(bf16[16,3200]{1,0:T(8,128)(2,1)S(1)} %hidden.5.refs_0_), channel_id=1, source_target_pairs={{0,6},{2,4},{4,2},{6,0},{8,14},{10,12},{12,10},{14,8},{1,7},{3,5},... | collective-permute-start | bytes 307208 | tf_op jit(solution)/shard_map/ppermute | solution.py:56
  48.8 6.4 %collective-permute-start.10 = (bf16[16,3200]{1,0:T(8,128)(2,1)S(1)}, bf16[16,3200]{1,0:T(8,128)(2,1)S(1)}, u32[]{:S(2)}, u32[]{:S(2)}) collective-permute-start(bf16[16,3200]{1,0:T(8,128)(2,1)S(1)} %hidden.5.refs_0_), channel_id=1, source_target_pairs={{0,2},{2,0},{4,6},{6,4},{8,10},{10,8},{12,14},{14,12},{1,3},{3,1},... | collective-permute-start | bytes 307208 | tf_op jit(solution)/shard_map/ppermute | solution.py:56
  49.7 5.9 %collective-permute-start.9 = (bf16[16,3200]{1,0:T(8,128)(2,1)S(1)}, bf16[16,3200]{1,0:T(8,128)(2,1)S(1)}, u32[]{:S(2)}, u32[]{:S(2)}) collective-permute-start(bf16[16,3200]{1,0:T(8,128)(2,1)S(1)} %hidden.5.refs_0_), channel_id=1, source_target_pairs={{0,4},{2,6},{4,0},{6,2},{8,12},{10,14},{12,8},{14,10},{1,5},{3,7},... | collective-permute-start | bytes 307208 | tf_op jit(solution)/shard_map/ppermute | solution.py:56
  56.9 1.4 %collective-permute-start.15 = (bf16[64,1024]{1,0:T(8,128)(2,1)S(1)}, bf16[64,1024]{1,0:T(8,128)(2,1)S(1)}, u32[]{:S(2)}, u32[]{:S(2)}) collective-permute-start(bf16[64,1024]{1,0:T(8,128)(2,1)S(1)} %get-tuple-element.87), channel_id=1, source_target_pairs={{0,1},{1,0},{2,3},{3,2},{4,5},{5,4},{6,7},{7,6},{8,9},{9,8},{10,11... | collective-permute-start | bytes 393224 | tf_op jit(solution)/shard_map/ppermute | solution.py:56
  58.4 5.6 %collective-permute-start.16 = (bf16[64,1024]{1,0:T(8,128)(2,1)S(1)}, bf16[64,1024]{1,0:T(8,128)(2,1)S(1)}, u32[]{:S(2)}, u32[]{:S(2)}) collective-permute-start(bf16[64,1024]{1,0:T(8,128)(2,1)S(1)} %get-tuple-element.90), channel_id=1, source_target_pairs={{16,0},{0,16},{17,1},{1,17},{18,2},{2,18},{19,3},{3,19},{20,4},{4,... | collective-permute-start | bytes 393224 | tf_op jit(solution)/shard_map/ppermute | solution.py:418
  66.3 8.6 %collective-permute-start.21 = (bf16[2,16,3584]{2,1,0:T(8,128)(2,1)S(1)}, bf16[2,16,3584]{2,1,0:T(8,128)(2,1)S(1)}, u32[]{:S(2)}, u32[]{:S(2)}) collective-permute-start(bf16[2,16,3584]{2,1,0:T(8,128)(2,1)S(1)} %get-tuple-element.107), channel_id=1, source_target_pairs={{0,4},{2,6},{4,0},{6,2},{8,12},{10,14},{12,8},{14,10},{1,5},{3,7},... | collective-permute-start | bytes 688136 | tf_op jit(solution)/shard_map/ppermute | solution.py:56
  67.7 12.4 %collective-permute-start.22 = (bf16[2,16,3584]{2,1,0:T(8,128)(2,1)S(1)}, bf16[2,16,3584]{2,1,0:T(8,128)(2,1)S(1)}, u32[]{:S(2)}, u32[]{:S(2)}) collective-permute-start(bf16[2,16,3584]{2,1,0:T(8,128)(2,1)S(1)} %get-tuple-element.108), channel_id=1, source_target_pairs={{0,2},{2,0},{4,6},{6,4},{8,10},{10,8},{12,14},{14,12},{1,3},{3,1},... | collective-permute-start | bytes 688136 | tf_op jit(solution)/shard_map/ppermute | solution.py:56
  68.1 12.2 %collective-permute-start.23 = (bf16[2,16,3584]{2,1,0:T(8,128)(2,1)S(1)}, bf16[2,16,3584]{2,1,0:T(8,128)(2,1)S(1)}, u32[]{:S(2)}, u32[]{:S(2)}) collective-permute-start(bf16[2,16,3584]{2,1,0:T(8,128)(2,1)S(1)} %get-tuple-element.109), channel_id=1, source_target_pairs={{0,6},{2,4},{4,2},{6,0},{8,14},{10,12},{12,10},{14,8},{1,7},{3,5},... | collective-permute-start | bytes 688136 | tf_op jit(solution)/shard_map/ppermute | solution.py:56
  72.2 16.3 %collective-permute-start.17 = (bf16[2,16,3200]{2,1,0:T(8,128)(2,1)S(1)}, bf16[2,16,3200]{2,1,0:T(8,128)(2,1)S(1)}, u32[]{:S(2)}, u32[]{:S(2)}) collective-permute-start(bf16[2,16,3200]{2,1,0:T(8,128)(2,1)S(1)} %get-tuple-element.100), channel_id=1, source_target_pairs={{0,4},{2,6},{4,0},{6,2},{8,12},{10,14},{12,8},{14,10},{1,5},{3,7},... | collective-permute-start | bytes 614408 | tf_op jit(solution)/shard_map/ppermute | solution.py:56
  73.6 14.9 %collective-permute-start.18 = (bf16[2,16,3200]{2,1,0:T(8,128)(2,1)S(1)}, bf16[2,16,3200]{2,1,0:T(8,128)(2,1)S(1)}, u32[]{:S(2)}, u32[]{:S(2)}) collective-permute-start(bf16[2,16,3200]{2,1,0:T(8,128)(2,1)S(1)} %get-tuple-element.101), channel_id=1, source_target_pairs={{0,2},{2,0},{4,6},{6,4},{8,10},{10,8},{12,14},{14,12},{1,3},{3,1},... | collective-permute-start | bytes 614408 | tf_op jit(solution)/shard_map/ppermute | solution.py:56
  75.0 17.4 %collective-permute-start.19 = (bf16[2,16,3200]{2,1,0:T(8,128)(2,1)S(1)}, bf16[2,16,3200]{2,1,0:T(8,128)(2,1)S(1)}, u32[]{:S(2)}, u32[]{:S(2)}) collective-permute-start(bf16[2,16,3200]{2,1,0:T(8,128)(2,1)S(1)} %get-tuple-element.102), channel_id=1, source_target_pairs={{0,6},{2,4},{4,2},{6,0},{8,14},{10,12},{12,10},{14,8},{1,7},{3,5},... | collective-permute-start | bytes 614408 | tf_op jit(solution)/shard_map/ppermute | solution.py:56
  80.9 11.9 %collective-permute-start.24 = (bf16[2,16,3584]{2,1,0:T(8,128)(2,1)S(1)}, bf16[2,16,3584]{2,1,0:T(8,128)(2,1)S(1)}, u32[]{:S(2)}, u32[]{:S(2)}) collective-permute-start(bf16[2,16,3584]{2,1,0:T(8,128)(2,1)S(1)} %get-tuple-element.112), channel_id=1, source_target_pairs={{0,8},{2,10},{4,12},{6,14},{8,0},{10,2},{12,4},{14,6},{1,9},{3,11}... | collective-permute-start | bytes 688136 | tf_op jit(solution)/shard_map/ppermute | solution.py:56
  92.6 9.5 %collective-permute-start.20 = (bf16[2,16,3200]{2,1,0:T(8,128)(2,1)S(1)}, bf16[2,16,3200]{2,1,0:T(8,128)(2,1)S(1)}, u32[]{:S(2)}, u32[]{:S(2)}) collective-permute-start(bf16[2,16,3200]{2,1,0:T(8,128)(2,1)S(1)} %get-tuple-element.105), channel_id=1, source_target_pairs={{0,8},{2,10},{4,12},{6,14},{8,0},{10,2},{12,4},{14,6},{1,9},{3,11}... | collective-permute-start | bytes 614408 | tf_op jit(solution)/shard_map/ppermute | solution.py:56
  93.1 11.4 %collective-permute-start.30 = (bf16[16,3456]{1,0:T(8,128)(2,1)S(1)}, bf16[16,3456]{1,0:T(8,128)(2,1)S(1)}, u32[]{:S(2)}, u32[]{:S(2)}) collective-permute-start(bf16[16,3456]{1,0:T(8,128)(2,1)S(1)} %get-tuple-element.115.refs_0_), channel_id=1, source_target_pairs={{0,6},{2,4},{4,2},{6,0},{8,14},{10,12},{12,10},{14,8},{1,7},{3,5},... | collective-permute-start | bytes 331784 | tf_op jit(solution)/shard_map/ppermute | solution.py:56
  96.4 9.5 %collective-permute-start.29 = (bf16[16,3456]{1,0:T(8,128)(2,1)S(1)}, bf16[16,3456]{1,0:T(8,128)(2,1)S(1)}, u32[]{:S(2)}, u32[]{:S(2)}) collective-permute-start(bf16[16,3456]{1,0:T(8,128)(2,1)S(1)} %get-tuple-element.115.refs_0_), channel_id=1, source_target_pairs={{0,2},{2,0},{4,6},{6,4},{8,10},{10,8},{12,14},{14,12},{1,3},{3,1},... | collective-permute-start | bytes 331784 | tf_op jit(solution)/shard_map/ppermute | solution.py:56
  96.4 9.5 %collective-permute-start.28 = (bf16[16,3456]{1,0:T(8,128)(2,1)S(1)}, bf16[16,3456]{1,0:T(8,128)(2,1)S(1)}, u32[]{:S(2)}, u32[]{:S(2)}) collective-permute-start(bf16[16,3456]{1,0:T(8,128)(2,1)S(1)} %get-tuple-element.115.refs_0_), channel_id=1, source_target_pairs={{0,4},{2,6},{4,0},{6,2},{8,12},{10,14},{12,8},{14,10},{1,5},{3,7},... | collective-permute-start | bytes 331784 | tf_op jit(solution)/shard_map/ppermute | solution.py:56
  102.3 6.2 %collective-permute-start.27 = (bf16[16,3200]{1,0:T(8,128)(2,1)S(1)}, bf16[16,3200]{1,0:T(8,128)(2,1)S(1)}, u32[]{:S(2)}, u32[]{:S(2)}) collective-permute-start(bf16[16,3200]{1,0:T(8,128)(2,1)S(1)} %hidden.7.refs_0_), channel_id=1, source_target_pairs={{0,6},{2,4},{4,2},{6,0},{8,14},{10,12},{12,10},{14,8},{1,7},{3,5},... | collective-permute-start | bytes 307208 | tf_op jit(solution)/shard_map/ppermute | solution.py:56
  102.4 7.1 %collective-permute-start.26 = (bf16[16,3200]{1,0:T(8,128)(2,1)S(1)}, bf16[16,3200]{1,0:T(8,128)(2,1)S(1)}, u32[]{:S(2)}, u32[]{:S(2)}) collective-permute-start(bf16[16,3200]{1,0:T(8,128)(2,1)S(1)} %hidden.7.refs_0_), channel_id=1, source_target_pairs={{0,2},{2,0},{4,6},{6,4},{8,10},{10,8},{12,14},{14,12},{1,3},{3,1},... | collective-permute-start | bytes 307208 | tf_op jit(solution)/shard_map/ppermute | solution.py:56
  104.5 6.2 %collective-permute-start.25 = (bf16[16,3200]{1,0:T(8,128)(2,1)S(1)}, bf16[16,3200]{1,0:T(8,128)(2,1)S(1)}, u32[]{:S(2)}, u32[]{:S(2)}) collective-permute-start(bf16[16,3200]{1,0:T(8,128)(2,1)S(1)} %hidden.7.refs_0_), channel_id=1, source_target_pairs={{0,4},{2,6},{4,0},{6,2},{8,12},{10,14},{12,8},{14,10},{1,5},{3,7},... | collective-permute-start | bytes 307208 | tf_op jit(solution)/shard_map/ppermute | solution.py:56
  111.9 1.4 %collective-permute-start.31 = (bf16[64,1024]{1,0:T(8,128)(2,1)S(1)}, bf16[64,1024]{1,0:T(8,128)(2,1)S(1)}, u32[]{:S(2)}, u32[]{:S(2)}) collective-permute-start(bf16[64,1024]{1,0:T(8,128)(2,1)S(1)} %get-tuple-element.117), channel_id=1, source_target_pairs={{0,1},{1,0},{2,3},{3,2},{4,5},{5,4},{6,7},{7,6},{8,9},{9,8},{10,11... | collective-permute-start | bytes 393224 | tf_op jit(solution)/shard_map/ppermute | solution.py:56
  113.9 4.3 %collective-permute-start.32 = (bf16[32,1024]{1,0:T(8,128)(2,1)S(1)}, bf16[32,1024]{1,0:T(8,128)(2,1)S(1)}, u32[]{:S(2)}, u32[]{:S(2)}) collective-permute-start(bf16[32,1024]{1,0:T(8,128)(2,1)S(1)} %get-tuple-element.120), channel_id=1, source_target_pairs={{16,0},{0,16},{17,1},{1,17},{18,2},{2,18},{19,3},{3,19},{20,4},{4,... | collective-permute-start | bytes 196616 | tf_op jit(solution)/shard_map/ppermute | solution.py:418

commit v5 on v4

--- a/solution.py
+++ b/solution.py
@@ -344,7 +344,7 @@
         total = term if total is None else total + term
     out_ref[...] = total
     if sent:
-        send_ref[...] = total.astype(BF16)
+        send_ref[...] = squeeze(total)
 
 
 def down(first, base, parts, weight, before, fresh, sent):
@@ -366,8 +366,8 @@
 
 
 def chip_kernel(a_ref, b_ref, state_ref, state_out, send_ref):
-    total = a_ref[...] + b_ref[...].astype(F32)
-    send_ref[...] = total.astype(BF16)
+    total = a_ref[...] + expand(b_ref)
+    send_ref[...] = squeeze(total)
     state_out[...] = state_ref[...] + total
 
 
@@ -375,7 +375,7 @@
     arrived, (state_out, x_ref, sumsq_ref) = refs[:-3], refs[-3:]
     state = state_ref[...]
     for ref in arrived:
-        state = state + ref[...].astype(F32)
+        state = state + expand(ref)
     state_out[...] = state
     x_ref[...] = state.astype(BF16)
     sumsq_ref[...] = rows_mean_square(state)
@@ -384,7 +384,7 @@
 def finish_kernel(offsets, per, groups, where_ref, a_ref, b_ref, state_ref, out_ref, *refs):
     sends, (change, state) = refs[: groups - 1], refs[groups - 1 :]
     me, group = where_ref[0], where_ref[1]
-    other = b_ref[...].astype(F32)
+    other = expand(b_ref)
     for p, offset in enumerate(offsets):
         first = (me ^ offset) * per
         if per % 8 == 0:
@@ -397,7 +397,7 @@
     out_ref[...] = state[own, :] + change[own, :]
     for k, ref in enumerate(sends):
         other = pl.multiple_of(lax.rem(group + k + 1, groups) * rows, 8)
-        ref[...] = change[pl.ds(other, rows), :].astype(BF16)
+        ref[...] = squeeze(change[pl.ds(other, rows), :])
 
 
 def per_device(counts, tokens, gate_weight, up_weight, down_weight):
@@ -522,7 +522,7 @@
     )(where, change, other, state)
     for k, send in enumerate(sends):
         arrived = from_group(send, groups - 1 - k)
-        out = out + arrived.astype(F32)
+        out = out + expand(arrived)
     return out
 
 

time: 119 us -> 119 us (level)
  transfers between devices with their start and end apart: 33 -> 33, of which waited for: 22 -> 22; matrix products, arithmetic and copies ran while one was open for 0% -> 0% of each run, Pallas kernels for 19% -> 18%
where the time goes in v5:
time: 119 us
  waiting for transfers between devices  47.8 us (40%)
  starting transfers between devices  38.3 us (32%)
  Pallas kernels  32 us (27%)
    ppermute x30, waiting for transfers between devices, swap(): return lax.ppermute(value, axis, [(i, i ^ flip) for i in range(count)])  38.8 us
    ppermute x30, starting transfers between devices, swap(): return lax.ppermute(value, axis, [(i, i ^ flip) for i in range(count)])  34.5 us
    pallas_call x4, Pallas kernels, gate_up(): pl.pallas_call(functools.partial(gate_up_kernel, first, per, size, fresh,...  13.4 us
    ppermute x3, waiting for transfers between devices, from_group(): lax.ppermute(value, 'groups', [((i + k) % groups, i) for i in range(group...  9.05 us
    pallas_call x2, Pallas kernels, load_down(): pl.pallas_call(functools.partial(load_down_kernel, first), out_shape=stru...  5.95 us
    pallas_call x4, Pallas kernels, down(): pl.pallas_call(functools.partial(down_kernel, first, len(parts), added, f...  5.27 us
    ppermute x3, starting transfers between devices, from_group(): lax.ppermute(value, 'groups', [((i + k) % groups, i) for i in range(group...  3.83 us
    pallas_call x1, Pallas kernels, load(): pl.pallas_call(functools.partial(load_kernel, first), out_shape=struct((d...  3.13 us
  transfers between devices with their start and end apart: 33, of which 22 were waited for; matrix products, arithmetic and copies ran while one was open for 0% of the time, Pallas kernels for 18%

profile of v5, /device:TPU:0, one launch (start us, length us, event | category | flops | bytes accessed | tf_op | source)
XLA Modules:
  0.0 119.1 jit_solution(251527872164617080)
XLA Ops:
  0.0 2.9 %collective-permute-start = (bf16[32,1024]{1,0:T(8,128)(2,1)}, bf16[32,1024]{1,0:T(8,128)(2,1)S(1)}, u32[]{:S(2)}, u32[]{:S(2)}) collective-permute-start(bf16[32,1024]{1,0:T(8,128)(2,1)} %own_ref.1), channel_id=1, source_target_pairs={{16,0},{0,16},{17,1},{1,17},{18,2},{2,18},{19,3},{3,19},{20,4},{4,... | collective-permute-start | bytes 196616 | tf_op jit(solution)/shard_map/ppermute | solution.py:418
  2.9 3.1 %load.1.refs_1_ = bf16[1024,3456]{1,0:T(8,128)(2,1)S(1)} custom-call(s32[1]{0:T(128)} %bitcast.2.base_ref, bf16[1024,13312]{1,0:T(8,128)(2,1)} %refs_0_.1), custom_call_target="tpu_custom_call" | custom-call | bytes 14155776 | tf_op jit(solution)/shard_map/load/pallas_call | solution.py:144
  6.2 0.7 arrange.1
  6.8 3.6 %gate_up.4 = (f32[2,16,3584]{2,1,0:T(8,128)S(1)}, bf16[2,16,3584]{2,1,0:T(8,128)(2,1)S(1)}, bf16[2,16,3584]{2,1,0:T(8,128)(2,1)S(1)}, bf16[2,16,3584]{2,1,0:T(8,128)(2,1)S(1)}, bf16[1024,3456]{1,0:T(8,128)(2,1)S(1)}) custom-call(s32[1]{0:T(128)} %bitcast.2.base_ref, bf16[64,1024]{1,0:T(8,128)(2,1)S(1)} %get-tuple-element.67.x_ref, ...), custom_call_target="tpu_custom_call" | custom-call | flops 905969664 | bytes 14155776 | tf_op jit(solution)/shard_map/gate_up/pallas_call | solution.py:201
  10.4 1.6 %collective-permute-start.1 = (bf16[2,16,3584]{2,1,0:T(8,128)(2,1)S(1)}, bf16[2,16,3584]{2,1,0:T(8,128)(2,1)S(1)}, u32[]{:S(2)}, u32[]{:S(2)}) collective-permute-start(bf16[2,16,3584]{2,1,0:T(8,128)(2,1)S(1)} %get-tuple-element.70), channel_id=1, source_target_pairs={{0,4},{2,6},{4,0},{6,2},{8,12},{10,14},{12,8},{14,10},{1,5},{3,7},... | collective-permute-start | bytes 688136 | tf_op jit(solution)/shard_map/ppermute | solution.py:56
  12.1 1.5 %collective-permute-start.2 = (bf16[2,16,3584]{2,1,0:T(8,128)(2,1)S(1)}, bf16[2,16,3584]{2,1,0:T(8,128)(2,1)S(1)}, u32[]{:S(2)}, u32[]{:S(2)}) collective-permute-start(bf16[2,16,3584]{2,1,0:T(8,128)(2,1)S(1)} %get-tuple-element.71), channel_id=1, source_target_pairs={{0,2},{2,0},{4,6},{6,4},{8,10},{10,8},{12,14},{14,12},{1,3},{3,1},... | collective-permute-start | bytes 688136 | tf_op jit(solution)/shard_map/ppermute | solution.py:56
  14.0 5.3 %gate_up.5 = (f32[2,16,3200]{2,1,0:T(8,128)S(1)}, bf16[2,16,3200]{2,1,0:T(8,128)(2,1)S(1)}, bf16[2,16,3200]{2,1,0:T(8,128)(2,1)S(1)}, bf16[2,16,3200]{2,1,0:T(8,...) custom-call(s32[1]{0:T(128)} %bitcast.2.base_ref, ...), custom_call_target="tpu_custom_call" | custom-call | flops 838860800 | bytes 13107200 | tf_op jit(solution)/shard_map/gate_up/pallas_call | solution.py:201
  19.3 1.6 %collective-permute-start.4 = (bf16[2,16,3200]{2,1,0:T(8,128)(2,1)S(1)}, bf16[2,16,3200]{2,1,0:T(8,128)(2,1)S(1)}, u32[]{:S(2)}, u32[]{:S(2)}) collective-permute-start(bf16[2,16,3200]{2,1,0:T(8,128)(2,1)S(1)} %get-tuple-element.75), channel_id=1, source_target_pairs={{0,4},{2,6},{4,0},{6,2},{8,12},{10,14},{12,8},{14,10},{1,5},{3,7},... | collective-permute-start | bytes 614408 | tf_op jit(solution)/shard_map/ppermute | solution.py:56
  21.0 1.5 %collective-permute-start.5 = (bf16[2,16,3200]{2,1,0:T(8,128)(2,1)S(1)}, bf16[2,16,3200]{2,1,0:T(8,128)(2,1)S(1)}, u32[]{:S(2)}, u32[]{:S(2)}) collective-permute-start(bf16[2,16,3200]{2,1,0:T(8,128)(2,1)S(1)} %get-tuple-element.76), channel_id=1, source_target_pairs={{0,2},{2,0},{4,6},{6,4},{8,10},{10,8},{12,14},{14,12},{1,3},{3,1},... | collective-permute-start | bytes 614408 | tf_op jit(solution)/shard_map/ppermute | solution.py:56
  23.4 1.5 %collective-permute-done.3.refs_2_ = bf16[2,16,3584]{2,1,0:T(8,128)(2,1)S(1)} collective-permute-done((bf16[2,16,3584]{2,1,0:T(8,128)(2,1)S(1)}, bf16[2,16,3584]{2,1,0:T(8,128)(2,1)S(1)}, u32[]{:S(2)}, u32[]{:S(2)}) %collective-permute-start.3) | collective-permute-done | bytes 229408 | tf_op jit(solution)/shard_map/ppermute | solution.py:56
  25.5 2.7 %collective-permute-start.8 = (bf16[2,16,3584]{2,1,0:T(8,128)(2,1)S(1)}, bf16[2,16,3584]{2,1,0:T(8,128)(2,1)S(1)}, u32[]{:S(2)}, u32[]{:S(2)}) collective-permute-start(bf16[2,16,3584]{2,1,0:T(8,128)(2,1)S(1)} %get-tuple-element.82), channel_id=1, source_target_pairs={{0,8},{2,10},{4,12},{6,14},{8,0},{10,2},{12,4},{14,6},{1,9},{3,11}... | collective-permute-start | bytes 688136 | tf_op jit(solution)/shard_map/ppermute | solution.py:56
  28.2 3.1 %load_down.2.refs_4_ = bf16[3456,1024]{1,0:T(8,128)(2,1)S(1)} custom-call(s32[1]{0:T(128)} %bitcast.2.base_ref, bf16[13312,1024]{1,0:T(8,128)(2,1)} %down_hbm.3, f32[2,16,3584]{2,1,0:T(8,128)S(1)} %get-tuple-element.81.after_ref.keep_ref), custom_call_target="tpu_custom_call" | custom-call | bytes 7077888 | tf_op jit(solution)/shard_map/load_down/pallas_call | solution.py:313
  31.2 2.1 %collective-permute-done.4.refs_0_ = bf16[2,16,3200]{2,1,0:T(8,128)(2,1)S(1)} collective-permute-done((bf16[2,16,3200]{2,1,0:T(8,128)(2,1)S(1)}, bf16[2,16,3200]{2,1,0:T(8,128)(2,1)S(1)}, u32[]{:S(2)}, u32[]{:S(2)}) %collective-permute-start.4) | collective-permute-done | bytes 204832 | tf_op jit(solution)/shard_map/ppermute | solution.py:56
  33.3 3.9 %collective-permute-done.6.refs_2_ = bf16[2,16,3200]{2,1,0:T(8,128)(2,1)S(1)} collective-permute-done((bf16[2,16,3200]{2,1,0:T(8,128)(2,1)S(1)}, bf16[2,16,3200]{2,1,0:T(8,128)(2,1)S(1)}, u32[]{:S(2)}, u32[]{:S(2)}) %collective-permute-start.6) | collective-permute-done | bytes 204832 | tf_op jit(solution)/shard_map/ppermute | solution.py:56
  37.8 3.1 %collective-permute-start.14 = (bf16[16,3456]{1,0:T(8,128)(2,1)S(1)}, bf16[16,3456]{1,0:T(8,128)(2,1)S(1)}, u32[]{:S(2)}, u32[]{:S(2)}) collective-permute-start(bf16[16,3456]{1,0:T(8,128)(2,1)S(1)} %get-tuple-element.85.refs_0_), channel_id=1, source_target_pairs={{0,6},{2,4},{4,2},{6,0},{8,14},{10,12},{12,10},{14,8},{1,7},{3,5},... | collective-permute-start | bytes 331784 | tf_op jit(solution)/shard_map/ppermute | solution.py:56
  40.9 2.2 %collective-permute-start.13 = (bf16[16,3456]{1,0:T(8,128)(2,1)S(1)}, bf16[16,3456]{1,0:T(8,128)(2,1)S(1)}, u32[]{:S(2)}, u32[]{:S(2)}) collective-permute-start(bf16[16,3456]{1,0:T(8,128)(2,1)S(1)} %get-tuple-element.85.refs_0_), channel_id=1, source_target_pairs={{0,2},{2,0},{4,6},{6,4},{8,10},{10,8},{12,14},{14,12},{1,3},{3,1},... | collective-permute-start | bytes 331784 | tf_op jit(solution)/shard_map/ppermute | solution.py:56
  43.1 2.9 %load_down.3.refs_4_ = bf16[3200,1024]{1,0:T(8,128)(2,1)S(1)} custom-call(s32[1]{0:T(128)} %bitcast.2.base_ref, bf16[13312,1024]{1,0:T(8,128)(2,1)} %down_hbm.3, f32[2,16,3200]{2,1,0:T(8,128)S(1)} %get-tuple-element.79.after_ref.keep_ref), custom_call_target="tpu_custom_call" | custom-call | bytes 6553600 | tf_op jit(solution)/shard_map/load_down/pallas_call | solution.py:313
  46.0 2.5 %collective-permute-done.7.refs_0_ = bf16[2,16,3200]{2,1,0:T(8,128)(2,1)S(1)} collective-permute-done((bf16[2,16,3200]{2,1,0:T(8,128)(2,1)S(1)}, bf16[2,16,3200]{2,1,0:T(8,128)(2,1)S(1)}, u32[]{:S(2)}, u32[]{:S(2)}) %collective-permute-start.7) | collective-permute-done | bytes 204832 | tf_op jit(solution)/shard_map/ppermute | solution.py:56
  48.8 1.0 collective-permute-start.10
  49.7 2.5 %collective-permute-start.9 = (bf16[16,3200]{1,0:T(8,128)(2,1)S(1)}, bf16[16,3200]{1,0:T(8,128)(2,1)S(1)}, u32[]{:S(2)}, u32[]{:S(2)}) collective-permute-start(bf16[16,3200]{1,0:T(8,128)(2,1)S(1)} %hidden.5.refs_0_), channel_id=1, source_target_pairs={{0,4},{2,6},{4,0},{6,2},{8,12},{10,14},{12,8},{14,10},{1,5},{3,7},... | collective-permute-start | bytes 307208 | tf_op jit(solution)/shard_map/ppermute | solution.py:56
  52.3 1.4 %down.4.refs_5_ = f32[64,1024]{1,0:T(8,128)S(1)} custom-call(s32[1]{0:T(128)} %bitcast.2.base_ref, bf16[16,3456]{1,0:T(8,128)(2,1)S(1)} %get-tuple-element.85.refs_0_, bf16[16,3456]{1,0:T(8,128)(2,1)S(1)} %collective-permute-done.12.refs_1_, bf16[16,3456]{1,0:T(8,128)(2,1)S(1)} %collective-permute-done.13.refs_2_, ...), custom_call_target="tpu_custom_call" | custom-call | flops 452984832 | bytes 7077888 | tf_op jit(solution)/shard_map/down/pallas_call | solution.py:354
  53.6 1.4 %collective-permute-done.11.refs_3_ = bf16[16,3200]{1,0:T(8,128)(2,1)S(1)} collective-permute-done((bf16[16,3200]{1,0:T(8,128)(2,1)S(1)}, bf16[16,3200]{1,0:T(8,128)(2,1)S(1)}, u32[]{:S(2)}, u32[]{:S(2)}) %collective-permute-start.11) | collective-permute-done | bytes 102432 | tf_op jit(solution)/shard_map/ppermute | solution.py:56
  55.6 1.3 %down.5 = (f32[64,1024]{1,0:T(8,128)S(1)}, bf16[64,1024]{1,0:T(8,128)(2,1)S(1)}) custom-call(s32[1]{0:T(128)} %bitcast.2.base_ref, bf16[16,3200]{1,0:T(8,128)(2,1)S(1)} %hidden.5.refs_0_, bf16[16,3200]{1,0:T(8,128)(2,1)S(1)} %collective-permute-done.9.refs_1_, bf16[16,3200]{1,0:T(8,128)(2,1)S(1)} %collective-permute-done.10.refs_2_, ...), custom_call_target="tpu_custom_call" | custom-call | flops 419430400 | bytes 6553600 | tf_op jit(solution)/shard_map/down/pallas_call | solution.py:354
  57.0 1.3 %collective-permute-done.15.b_ref = bf16[64,1024]{1,0:T(8,128)(2,1)S(1)} collective-permute-done((bf16[64,1024]{1,0:T(8,128)(2,1)S(1)}, bf16[64,1024]{1,0:T(8,128)(2,1)S(1)}, u32[]{:S(2)}, u32[]{:S(2)}) %collective-permute-start.15) | collective-permute-done | bytes 131104 | tf_op jit(solution)/shard_map/ppermute | solution.py:56
  58.8 5.2 %collective-permute-done.16.refs_0_ = bf16[64,1024]{1,0:T(8,128)(2,1)S(1)} collective-permute-done((bf16[64,1024]{1,0:T(8,128)(2,1)S(1)}, bf16[64,1024]{1,0:T(8,128)(2,1)S(1)}, u32[]{:S(2)}, u32[]{:S(2)}) %collective-permute-start.16) | collective-permute-done | bytes 131104 | tf_op jit(solution)/shard_map/ppermute | solution.py:418
  64.2 2.3 %gate_up.6 = (f32[2,16,3584]{2,1,0:T(8,128)S(1)}, bf16[2,16,3584]{2,1,0:T(8,128)(2,1)S(1)}, bf16[2,16,3584]{2,1,0:T(8,128)(2,1)S(1)}, bf16[2,16,3584]{2,1,0:T(8,128)(2,1)S(1)}) custom-call(s32[1]{0:T(128)} %bitcast.2.base_ref, bf16[64,1024]{1,0:T(8,128)(2,1)S(1)} %get-tuple-element.96.x_ref, f32[64,128]{1,0:T(8,128)S(1)} %get-tuple-element.93.refs_0_, ...), custom_call_target="tpu_custom_call" | custom-call | flops 905969664 | bytes 14155776 | tf_op jit(solution)/shard_map/gate_up/pallas_call | solution.py:201
  66.4 1.4 %collective-permute-start.21 = (bf16[2,16,3584]{2,1,0:T(8,128)(2,1)S(1)}, bf16[2,16,3584]{2,1,0:T(8,128)(2,1)S(1)}, u32[]{:S(2)}, u32[]{:S(2)}) collective-permute-start(bf16[2,16,3584]{2,1,0:T(8,128)(2,1)S(1)} %get-tuple-element.107), channel_id=1, source_target_pairs={{0,4},{2,6},{4,0},{6,2},{8,12},{10,14},{12,8},{14,10},{1,5},{3,7},... | collective-permute-start | bytes 688136 | tf_op jit(solution)/shard_map/ppermute | solution.py:56
  68.2 1.8 %collective-permute-start.23 = (bf16[2,16,3584]{2,1,0:T(8,128)(2,1)S(1)}, bf16[2,16,3584]{2,1,0:T(8,128)(2,1)S(1)}, u32[]{:S(2)}, u32[]{:S(2)}) collective-permute-start(bf16[2,16,3584]{2,1,0:T(8,128)(2,1)S(1)} %get-tuple-element.109), channel_id=1, source_target_pairs={{0,6},{2,4},{4,2},{6,0},{8,14},{10,12},{12,10},{14,8},{1,7},{3,5},... | collective-permute-start | bytes 688136 | tf_op jit(solution)/shard_map/ppermute | solution.py:56
  70.0 2.3 %gate_up.7 = (f32[2,16,3200]{2,1,0:T(8,128)S(1)}, bf16[2,16,3200]{2,1,0:T(8,128)(2,1)S(1)}, bf16[2,16,3200]{2,1,0:T(8,128)(2,1)S(1)}, bf16[2,16,3200]{2,1,0:T(8,128)(2,1)S(1)}) custom-call(s32[1]{0:T(128)} %bitcast.2.base_ref, bf16[64,1024]{1,0:T(8,128)(2,1)S(1)} %get-tuple-element.96.x_ref, bf16[1024,3200]{1,0:T(8,128)(2,1)S(1)} %get-tuple-element.97.refs_0_, ...), custom_call_target="tpu_custom_call" | custom-call | flops 838860800 | bytes 13107200 | tf_op jit(solution)/shard_map/gate_up/pallas_call | solution.py:201
  72.3 1.4 %collective-permute-start.17 = (bf16[2,16,3200]{2,1,0:T(8,128)(2,1)S(1)}, bf16[2,16,3200]{2,1,0:T(8,128)(2,1)S(1)}, u32[]{:S(2)}, u32[]{:S(2)}) collective-permute-start(bf16[2,16,3200]{2,1,0:T(8,128)(2,1)S(1)} %get-tuple-element.100), channel_id=1, source_target_pairs={{0,4},{2,6},{4,0},{6,2},{8,12},{10,14},{12,8},{14,10},{1,5},{3,7},... | collective-permute-start | bytes 614408 | tf_op jit(solution)/shard_map/ppermute | solution.py:56
  74.1 1.0 collective-permute-done.21.refs_0_
  75.0 1.2 collective-permute-start.19
  76.2 4.0 %collective-permute-done.22.refs_1_ = bf16[2,16,3584]{2,1,0:T(8,128)(2,1)S(1)} collective-permute-done((bf16[2,16,3584]{2,1,0:T(8,128)(2,1)S(1)}, bf16[2,16,3584]{2,1,0:T(8,128)(2,1)S(1)}, u32[]{:S(2)}, u32[]{:S(2)}) %collective-permute-start.22) | collective-permute-done | bytes 229408 | tf_op jit(solution)/shard_map/ppermute | solution.py:56
  81.0 1.7 %collective-permute-start.24 = (bf16[2,16,3584]{2,1,0:T(8,128)(2,1)S(1)}, bf16[2,16,3584]{2,1,0:T(8,128)(2,1)S(1)}, u32[]{:S(2)}, u32[]{:S(2)}) collective-permute-start(bf16[2,16,3584]{2,1,0:T(8,128)(2,1)S(1)} %get-tuple-element.112), channel_id=1, source_target_pairs={{0,8},{2,10},{4,12},{6,14},{8,0},{10,2},{12,4},{14,6},{1,9},{3,11}... | collective-permute-start | bytes 688136 | tf_op jit(solution)/shard_map/ppermute | solution.py:56
  82.7 6.0 %collective-permute-done.17.refs_0_ = bf16[2,16,3200]{2,1,0:T(8,128)(2,1)S(1)} collective-permute-done((bf16[2,16,3200]{2,1,0:T(8,128)(2,1)S(1)}, bf16[2,16,3200]{2,1,0:T(8,128)(2,1)S(1)}, u32[]{:S(2)}, u32[]{:S(2)}) %collective-permute-start.17) | collective-permute-done | bytes 204832 | tf_op jit(solution)/shard_map/ppermute | solution.py:56
  88.6 3.8 %collective-permute-done.19.refs_2_ = bf16[2,16,3200]{2,1,0:T(8,128)(2,1)S(1)} collective-permute-done((bf16[2,16,3200]{2,1,0:T(8,128)(2,1)S(1)}, bf16[2,16,3200]{2,1,0:T(8,128)(2,1)S(1)}, u32[]{:S(2)}, u32[]{:S(2)}) %collective-permute-start.19) | collective-permute-done | bytes 204832 | tf_op jit(solution)/shard_map/ppermute | solution.py:56
  93.2 3.3 %collective-permute-start.30 = (bf16[16,3456]{1,0:T(8,128)(2,1)S(1)}, bf16[16,3456]{1,0:T(8,128)(2,1)S(1)}, u32[]{:S(2)}, u32[]{:S(2)}) collective-permute-start(bf16[16,3456]{1,0:T(8,128)(2,1)S(1)} %get-tuple-element.115.refs_0_), channel_id=1, source_target_pairs={{0,6},{2,4},{4,2},{6,0},{8,14},{10,12},{12,10},{14,8},{1,7},{3,5},... | collective-permute-start | bytes 331784 | tf_op jit(solution)/shard_map/ppermute | solution.py:56
  97.1 5.1 %collective-permute-done.20.refs_0_ = bf16[2,16,3200]{2,1,0:T(8,128)(2,1)S(1)} collective-permute-done((bf16[2,16,3200]{2,1,0:T(8,128)(2,1)S(1)}, bf16[2,16,3200]{2,1,0:T(8,128)(2,1)S(1)}, u32[]{:S(2)}, u32[]{:S(2)}) %collective-permute-start.20) | collective-permute-done | bytes 204832 | tf_op jit(solution)/shard_map/ppermute | solution.py:56
  102.5 2.1 %collective-permute-start.26 = (bf16[16,3200]{1,0:T(8,128)(2,1)S(1)}, bf16[16,3200]{1,0:T(8,128)(2,1)S(1)}, u32[]{:S(2)}, u32[]{:S(2)}) collective-permute-start(bf16[16,3200]{1,0:T(8,128)(2,1)S(1)} %hidden.7.refs_0_), channel_id=1, source_target_pairs={{0,2},{2,0},{4,6},{6,4},{8,10},{10,8},{12,14},{14,12},{1,3},{3,1},... | collective-permute-start | bytes 307208 | tf_op jit(solution)/shard_map/ppermute | solution.py:56
  104.6 1.4 %collective-permute-start.25 = (bf16[16,3200]{1,0:T(8,128)(2,1)S(1)}, bf16[16,3200]{1,0:T(8,128)(2,1)S(1)}, u32[]{:S(2)}, u32[]{:S(2)}) collective-permute-start(bf16[16,3200]{1,0:T(8,128)(2,1)S(1)} %hidden.7.refs_0_), channel_id=1, source_target_pairs={{0,4},{2,6},{4,0},{6,2},{8,12},{10,14},{12,8},{14,10},{1,5},{3,7},... | collective-permute-start | bytes 307208 | tf_op jit(solution)/shard_map/ppermute | solution.py:56
  106.0 1.4 %down.6.refs_5_ = f32[64,1024]{1,0:T(8,128)S(1)} custom-call(s32[1]{0:T(128)} %bitcast.2.base_ref, bf16[16,3456]{1,0:T(8,128)(2,1)S(1)} %get-tuple-element.115.refs_0_, bf16[16,3456]{1,0:T(8,128)(2,1)S(1)} %collective-permute-done.28.refs_1_, bf16[16,3456]{1,0:T(8,128)(2,1)S(1)} %collective-permute-done.29.refs_2_, ...), custom_call_target="tpu_custom_call" | custom-call | flops 452984832 | bytes 7077888 | tf_op jit(solution)/shard_map/down/pallas_call | solution.py:354
  107.3 1.3 %collective-permute-done.27.refs_3_ = bf16[16,3200]{1,0:T(8,128)(2,1)S(1)} collective-permute-done((bf16[16,3200]{1,0:T(8,128)(2,1)S(1)}, bf16[16,3200]{1,0:T(8,128)(2,1)S(1)}, u32[]{:S(2)}, u32[]{:S(2)}) %collective-permute-start.27) | collective-permute-done | bytes 102432 | tf_op jit(solution)/shard_map/ppermute | solution.py:56
  108.6 1.0 collective-permute-done.26.refs_2_
  109.6 1.1 collective-permute-done.25.refs_1_
  110.7 1.3 %down.7 = (f32[64,1024]{1,0:T(8,128)S(1)}, bf16[64,1024]{1,0:T(8,128)(2,1)S(1)}) custom-call(s32[1]{0:T(128)} %bitcast.2.base_ref, bf16[16,3200]{1,0:T(8,128)(2,1)S(1)} %hidden.7.refs_0_, bf16[16,3200]{1,0:T(8,128)(2,1)S(1)} %collective-permute-done.25.refs_1_, bf16[16,3200]{1,0:T(8,128)(2,1)S(1)} %collective-permute-done.26.refs_2_, ...), custom_call_target="tpu_custom_call" | custom-call | flops 419430400 | bytes 6553600 | tf_op jit(solution)/shard_map/down/pallas_call | solution.py:354
  112.1 1.3 %collective-permute-done.31.b_ref = bf16[64,1024]{1,0:T(8,128)(2,1)S(1)} collective-permute-done((bf16[64,1024]{1,0:T(8,128)(2,1)S(1)}, bf16[64,1024]{1,0:T(8,128)(2,1)S(1)}, u32[]{:S(2)}, u32[]{:S(2)}) %collective-permute-start.31) | collective-permute-done | bytes 131104 | tf_op jit(solution)/shard_map/ppermute | solution.py:56
  114.6 3.8 %collective-permute-done.32 = bf16[32,1024]{1,0:T(8,128)(2,1)S(1)} collective-permute-done((bf16[32,1024]{1,0:T(8,128)(2,1)S(1)}, bf16[32,1024]{1,0:T(8,128)(2,1)S(1)}, u32[]{:S(2)}, u32[]{:S(2)}) %collective-permute-start.32) | collective-permute-done | bytes 65568 | tf_op jit(solution)/shard_map/ppermute | solution.py:418
  118.4 0.7 fusion.2
  (45 shorter events, 8.6 us)
Async XLA Ops:
  0.0 6.2 %collective-permute-start = (bf16[32,1024]{1,0:T(8,128)(2,1)}, bf16[32,1024]{1,0:T(8,128)(2,1)S(1)}, u32[]{:S(2)}, u32[]{:S(2)}) collective-permute-start(bf16[32,1024]{1,0:T(8,128)(2,1)} %own_ref.1), channel_id=1, source_target_pairs={{16,0},{0,16},{17,1},{1,17},{18,2},{2,18},{19,3},{3,19},{20,4},{4,... | collective-permute-start | bytes 196616 | tf_op jit(solution)/shard_map/ppermute | solution.py:418
  2.9 3.2 %copy-start = (bf16[32,1024]{1,0:T(8,128)(2,1)S(1)}, bf16[32,1024]{1,0:T(8,128)(2,1)}, u32[]{:S(2)}) copy-start(bf16[32,1024]{1,0:T(8,128)(2,1)} %own_ref.1) | copy-start | bytes 196612
  10.4 12.1 %collective-permute-start.1 = (bf16[2,16,3584]{2,1,0:T(8,128)(2,1)S(1)}, bf16[2,16,3584]{2,1,0:T(8,128)(2,1)S(1)}, u32[]{:S(2)}, u32[]{:S(2)}) collective-permute-start(bf16[2,16,3584]{2,1,0:T(8,128)(2,1)S(1)} %get-tuple-element.70), channel_id=1, source_target_pairs={{0,4},{2,6},{4,0},{6,2},{8,12},{10,14},{12,8},{14,10},{1,5},{3,7},... | collective-permute-start | bytes 688136 | tf_op jit(solution)/shard_map/ppermute | solution.py:56
  12.1 11.3 %collective-permute-start.2 = (bf16[2,16,3584]{2,1,0:T(8,128)(2,1)S(1)}, bf16[2,16,3584]{2,1,0:T(8,128)(2,1)S(1)}, u32[]{:S(2)}, u32[]{:S(2)}) collective-permute-start(bf16[2,16,3584]{2,1,0:T(8,128)(2,1)S(1)} %get-tuple-element.71), channel_id=1, source_target_pairs={{0,2},{2,0},{4,6},{6,4},{8,10},{10,8},{12,14},{14,12},{1,3},{3,1},... | collective-permute-start | bytes 688136 | tf_op jit(solution)/shard_map/ppermute | solution.py:56
  13.6 11.4 %collective-permute-start.3 = (bf16[2,16,3584]{2,1,0:T(8,128)(2,1)S(1)}, bf16[2,16,3584]{2,1,0:T(8,128)(2,1)S(1)}, u32[]{:S(2)}, u32[]{:S(2)}) collective-permute-start(bf16[2,16,3584]{2,1,0:T(8,128)(2,1)S(1)} %get-tuple-element.72), channel_id=1, source_target_pairs={{0,6},{2,4},{4,2},{6,0},{8,14},{10,12},{12,10},{14,8},{1,7},{3,5},... | collective-permute-start | bytes 688136 | tf_op jit(solution)/shard_map/ppermute | solution.py:56
  19.3 14.0 %collective-permute-start.4 = (bf16[2,16,3200]{2,1,0:T(8,128)(2,1)S(1)}, bf16[2,16,3200]{2,1,0:T(8,128)(2,1)S(1)}, u32[]{:S(2)}, u32[]{:S(2)}) collective-permute-start(bf16[2,16,3200]{2,1,0:T(8,128)(2,1)S(1)} %get-tuple-element.75), channel_id=1, source_target_pairs={{0,4},{2,6},{4,0},{6,2},{8,12},{10,14},{12,8},{14,10},{1,5},{3,7},... | collective-permute-start | bytes 614408 | tf_op jit(solution)/shard_map/ppermute | solution.py:56
  21.0 12.3 %collective-permute-start.5 = (bf16[2,16,3200]{2,1,0:T(8,128)(2,1)S(1)}, bf16[2,16,3200]{2,1,0:T(8,128)(2,1)S(1)}, u32[]{:S(2)}, u32[]{:S(2)}) collective-permute-start(bf16[2,16,3200]{2,1,0:T(8,128)(2,1)S(1)} %get-tuple-element.76), channel_id=1, source_target_pairs={{0,2},{2,0},{4,6},{6,4},{8,10},{10,8},{12,14},{14,12},{1,3},{3,1},... | collective-permute-start | bytes 614408 | tf_op jit(solution)/shard_map/ppermute | solution.py:56
  22.5 14.7 %collective-permute-start.6 = (bf16[2,16,3200]{2,1,0:T(8,128)(2,1)S(1)}, bf16[2,16,3200]{2,1,0:T(8,128)(2,1)S(1)}, u32[]{:S(2)}, u32[]{:S(2)}) collective-permute-start(bf16[2,16,3200]{2,1,0:T(8,128)(2,1)S(1)} %get-tuple-element.77), channel_id=1, source_target_pairs={{0,6},{2,4},{4,2},{6,0},{8,14},{10,12},{12,10},{14,8},{1,7},{3,5},... | collective-permute-start | bytes 614408 | tf_op jit(solution)/shard_map/ppermute | solution.py:56
  25.5 12.0 %collective-permute-start.8 = (bf16[2,16,3584]{2,1,0:T(8,128)(2,1)S(1)}, bf16[2,16,3584]{2,1,0:T(8,128)(2,1)S(1)}, u32[]{:S(2)}, u32[]{:S(2)}) collective-permute-start(bf16[2,16,3584]{2,1,0:T(8,128)(2,1)S(1)} %get-tuple-element.82), channel_id=1, source_target_pairs={{0,8},{2,10},{4,12},{6,14},{8,0},{10,2},{12,4},{14,6},{1,9},{3,11}... | collective-permute-start | bytes 688136 | tf_op jit(solution)/shard_map/ppermute | solution.py:56
  37.4 11.1 %collective-permute-start.7 = (bf16[2,16,3200]{2,1,0:T(8,128)(2,1)S(1)}, bf16[2,16,3200]{2,1,0:T(8,128)(2,1)S(1)}, u32[]{:S(2)}, u32[]{:S(2)}) collective-permute-start(bf16[2,16,3200]{2,1,0:T(8,128)(2,1)S(1)} %get-tuple-element.80), channel_id=1, source_target_pairs={{0,8},{2,10},{4,12},{6,14},{8,0},{10,2},{12,4},{14,6},{1,9},{3,11}... | collective-permute-start | bytes 614408 | tf_op jit(solution)/shard_map/ppermute | solution.py:56
  37.8 11.9 %collective-permute-start.14 = (bf16[16,3456]{1,0:T(8,128)(2,1)S(1)}, bf16[16,3456]{1,0:T(8,128)(2,1)S(1)}, u32[]{:S(2)}, u32[]{:S(2)}) collective-permute-start(bf16[16,3456]{1,0:T(8,128)(2,1)S(1)} %get-tuple-element.85.refs_0_), channel_id=1, source_target_pairs={{0,6},{2,4},{4,2},{6,0},{8,14},{10,12},{12,10},{14,8},{1,7},{3,5},... | collective-permute-start | bytes 331784 | tf_op jit(solution)/shard_map/ppermute | solution.py:56
  40.9 11.4 %collective-permute-start.13 = (bf16[16,3456]{1,0:T(8,128)(2,1)S(1)}, bf16[16,3456]{1,0:T(8,128)(2,1)S(1)}, u32[]{:S(2)}, u32[]{:S(2)}) collective-permute-start(bf16[16,3456]{1,0:T(8,128)(2,1)S(1)} %get-tuple-element.85.refs_0_), channel_id=1, source_target_pairs={{0,2},{2,0},{4,6},{6,4},{8,10},{10,8},{12,14},{14,12},{1,3},{3,1},... | collective-permute-start | bytes 331784 | tf_op jit(solution)/shard_map/ppermute | solution.py:56
  43.1 9.2 %collective-permute-start.12 = (bf16[16,3456]{1,0:T(8,128)(2,1)S(1)}, bf16[16,3456]{1,0:T(8,128)(2,1)S(1)}, u32[]{:S(2)}, u32[]{:S(2)}) collective-permute-start(bf16[16,3456]{1,0:T(8,128)(2,1)S(1)} %get-tuple-element.85.refs_0_), channel_id=1, source_target_pairs={{0,4},{2,6},{4,0},{6,2},{8,12},{10,14},{12,8},{14,10},{1,5},{3,7},... | collective-permute-start | bytes 331784 | tf_op jit(solution)/shard_map/ppermute | solution.py:56
  48.7 6.3 %collective-permute-start.11 = (bf16[16,3200]{1,0:T(8,128)(2,1)S(1)}, bf16[16,3200]{1,0:T(8,128)(2,1)S(1)}, u32[]{:S(2)}, u32[]{:S(2)}) collective-permute-start(bf16[16,3200]{1,0:T(8,128)(2,1)S(1)} %hidden.5.refs_0_), channel_id=1, source_target_pairs={{0,6},{2,4},{4,2},{6,0},{8,14},{10,12},{12,10},{14,8},{1,7},{3,5},... | collective-permute-start | bytes 307208 | tf_op jit(solution)/shard_map/ppermute | solution.py:56
  48.8 6.4 %collective-permute-start.10 = (bf16[16,3200]{1,0:T(8,128)(2,1)S(1)}, bf16[16,3200]{1,0:T(8,128)(2,1)S(1)}, u32[]{:S(2)}, u32[]{:S(2)}) collective-permute-start(bf16[16,3200]{1,0:T(8,128)(2,1)S(1)} %hidden.5.refs_0_), channel_id=1, source_target_pairs={{0,2},{2,0},{4,6},{6,4},{8,10},{10,8},{12,14},{14,12},{1,3},{3,1},... | collective-permute-start | bytes 307208 | tf_op jit(solution)/shard_map/ppermute | solution.py:56
  49.7 5.9 %collective-permute-start.9 = (bf16[16,3200]{1,0:T(8,128)(2,1)S(1)}, bf16[16,3200]{1,0:T(8,128)(2,1)S(1)}, u32[]{:S(2)}, u32[]{:S(2)}) collective-permute-start(bf16[16,3200]{1,0:T(8,128)(2,1)S(1)} %hidden.5.refs_0_), channel_id=1, source_target_pairs={{0,4},{2,6},{4,0},{6,2},{8,12},{10,14},{12,8},{14,10},{1,5},{3,7},... | collective-permute-start | bytes 307208 | tf_op jit(solution)/shard_map/ppermute | solution.py:56
  56.9 1.4 %collective-permute-start.15 = (bf16[64,1024]{1,0:T(8,128)(2,1)S(1)}, bf16[64,1024]{1,0:T(8,128)(2,1)S(1)}, u32[]{:S(2)}, u32[]{:S(2)}) collective-permute-start(bf16[64,1024]{1,0:T(8,128)(2,1)S(1)} %get-tuple-element.87), channel_id=1, source_target_pairs={{0,1},{1,0},{2,3},{3,2},{4,5},{5,4},{6,7},{7,6},{8,9},{9,8},{10,11... | collective-permute-start | bytes 393224 | tf_op jit(solution)/shard_map/ppermute | solution.py:56
  58.4 5.6 %collective-permute-start.16 = (bf16[64,1024]{1,0:T(8,128)(2,1)S(1)}, bf16[64,1024]{1,0:T(8,128)(2,1)S(1)}, u32[]{:S(2)}, u32[]{:S(2)}) collective-permute-start(bf16[64,1024]{1,0:T(8,128)(2,1)S(1)} %get-tuple-element.90), channel_id=1, source_target_pairs={{16,0},{0,16},{17,1},{1,17},{18,2},{2,18},{19,3},{3,19},{20,4},{4,... | collective-permute-start | bytes 393224 | tf_op jit(solution)/shard_map/ppermute | solution.py:418
  66.4 8.6 %collective-permute-start.21 = (bf16[2,16,3584]{2,1,0:T(8,128)(2,1)S(1)}, bf16[2,16,3584]{2,1,0:T(8,128)(2,1)S(1)}, u32[]{:S(2)}, u32[]{:S(2)}) collective-permute-start(bf16[2,16,3584]{2,1,0:T(8,128)(2,1)S(1)} %get-tuple-element.107), channel_id=1, source_target_pairs={{0,4},{2,6},{4,0},{6,2},{8,12},{10,14},{12,8},{14,10},{1,5},{3,7},... | collective-permute-start | bytes 688136 | tf_op jit(solution)/shard_map/ppermute | solution.py:56
  67.8 12.4 %collective-permute-start.22 = (bf16[2,16,3584]{2,1,0:T(8,128)(2,1)S(1)}, bf16[2,16,3584]{2,1,0:T(8,128)(2,1)S(1)}, u32[]{:S(2)}, u32[]{:S(2)}) collective-permute-start(bf16[2,16,3584]{2,1,0:T(8,128)(2,1)S(1)} %get-tuple-element.108), channel_id=1, source_target_pairs={{0,2},{2,0},{4,6},{6,4},{8,10},{10,8},{12,14},{14,12},{1,3},{3,1},... | collective-permute-start | bytes 688136 | tf_op jit(solution)/shard_map/ppermute | solution.py:56
  68.2 12.2 %collective-permute-start.23 = (bf16[2,16,3584]{2,1,0:T(8,128)(2,1)S(1)}, bf16[2,16,3584]{2,1,0:T(8,128)(2,1)S(1)}, u32[]{:S(2)}, u32[]{:S(2)}) collective-permute-start(bf16[2,16,3584]{2,1,0:T(8,128)(2,1)S(1)} %get-tuple-element.109), channel_id=1, source_target_pairs={{0,6},{2,4},{4,2},{6,0},{8,14},{10,12},{12,10},{14,8},{1,7},{3,5},... | collective-permute-start | bytes 688136 | tf_op jit(solution)/shard_map/ppermute | solution.py:56
  72.3 16.4 %collective-permute-start.17 = (bf16[2,16,3200]{2,1,0:T(8,128)(2,1)S(1)}, bf16[2,16,3200]{2,1,0:T(8,128)(2,1)S(1)}, u32[]{:S(2)}, u32[]{:S(2)}) collective-permute-start(bf16[2,16,3200]{2,1,0:T(8,128)(2,1)S(1)} %get-tuple-element.100), channel_id=1, source_target_pairs={{0,4},{2,6},{4,0},{6,2},{8,12},{10,14},{12,8},{14,10},{1,5},{3,7},... | collective-permute-start | bytes 614408 | tf_op jit(solution)/shard_map/ppermute | solution.py:56
  73.7 15.0 %collective-permute-start.18 = (bf16[2,16,3200]{2,1,0:T(8,128)(2,1)S(1)}, bf16[2,16,3200]{2,1,0:T(8,128)(2,1)S(1)}, u32[]{:S(2)}, u32[]{:S(2)}) collective-permute-start(bf16[2,16,3200]{2,1,0:T(8,128)(2,1)S(1)} %get-tuple-element.101), channel_id=1, source_target_pairs={{0,2},{2,0},{4,6},{6,4},{8,10},{10,8},{12,14},{14,12},{1,3},{3,1},... | collective-permute-start | bytes 614408 | tf_op jit(solution)/shard_map/ppermute | solution.py:56
  75.0 17.4 %collective-permute-start.19 = (bf16[2,16,3200]{2,1,0:T(8,128)(2,1)S(1)}, bf16[2,16,3200]{2,1,0:T(8,128)(2,1)S(1)}, u32[]{:S(2)}, u32[]{:S(2)}) collective-permute-start(bf16[2,16,3200]{2,1,0:T(8,128)(2,1)S(1)} %get-tuple-element.102), channel_id=1, source_target_pairs={{0,6},{2,4},{4,2},{6,0},{8,14},{10,12},{12,10},{14,8},{1,7},{3,5},... | collective-permute-start | bytes 614408 | tf_op jit(solution)/shard_map/ppermute | solution.py:56
  81.0 11.9 %collective-permute-start.24 = (bf16[2,16,3584]{2,1,0:T(8,128)(2,1)S(1)}, bf16[2,16,3584]{2,1,0:T(8,128)(2,1)S(1)}, u32[]{:S(2)}, u32[]{:S(2)}) collective-permute-start(bf16[2,16,3584]{2,1,0:T(8,128)(2,1)S(1)} %get-tuple-element.112), channel_id=1, source_target_pairs={{0,8},{2,10},{4,12},{6,14},{8,0},{10,2},{12,4},{14,6},{1,9},{3,11}... | collective-permute-start | bytes 688136 | tf_op jit(solution)/shard_map/ppermute | solution.py:56
  92.7 9.5 %collective-permute-start.20 = (bf16[2,16,3200]{2,1,0:T(8,128)(2,1)S(1)}, bf16[2,16,3200]{2,1,0:T(8,128)(2,1)S(1)}, u32[]{:S(2)}, u32[]{:S(2)}) collective-permute-start(bf16[2,16,3200]{2,1,0:T(8,128)(2,1)S(1)} %get-tuple-element.105), channel_id=1, source_target_pairs={{0,8},{2,10},{4,12},{6,14},{8,0},{10,2},{12,4},{14,6},{1,9},{3,11}... | collective-permute-start | bytes 614408 | tf_op jit(solution)/shard_map/ppermute | solution.py:56
  93.2 11.4 %collective-permute-start.30 = (bf16[16,3456]{1,0:T(8,128)(2,1)S(1)}, bf16[16,3456]{1,0:T(8,128)(2,1)S(1)}, u32[]{:S(2)}, u32[]{:S(2)}) collective-permute-start(bf16[16,3456]{1,0:T(8,128)(2,1)S(1)} %get-tuple-element.115.refs_0_), channel_id=1, source_target_pairs={{0,6},{2,4},{4,2},{6,0},{8,14},{10,12},{12,10},{14,8},{1,7},{3,5},... | collective-permute-start | bytes 331784 | tf_op jit(solution)/shard_map/ppermute | solution.py:56
  96.5 9.5 %collective-permute-start.29 = (bf16[16,3456]{1,0:T(8,128)(2,1)S(1)}, bf16[16,3456]{1,0:T(8,128)(2,1)S(1)}, u32[]{:S(2)}, u32[]{:S(2)}) collective-permute-start(bf16[16,3456]{1,0:T(8,128)(2,1)S(1)} %get-tuple-element.115.refs_0_), channel_id=1, source_target_pairs={{0,2},{2,0},{4,6},{6,4},{8,10},{10,8},{12,14},{14,12},{1,3},{3,1},... | collective-permute-start | bytes 331784 | tf_op jit(solution)/shard_map/ppermute | solution.py:56
  96.5 9.5 %collective-permute-start.28 = (bf16[16,3456]{1,0:T(8,128)(2,1)S(1)}, bf16[16,3456]{1,0:T(8,128)(2,1)S(1)}, u32[]{:S(2)}, u32[]{:S(2)}) collective-permute-start(bf16[16,3456]{1,0:T(8,128)(2,1)S(1)} %get-tuple-element.115.refs_0_), channel_id=1, source_target_pairs={{0,4},{2,6},{4,0},{6,2},{8,12},{10,14},{12,8},{14,10},{1,5},{3,7},... | collective-permute-start | bytes 331784 | tf_op jit(solution)/shard_map/ppermute | solution.py:56
  102.4 6.2 %collective-permute-start.27 = (bf16[16,3200]{1,0:T(8,128)(2,1)S(1)}, bf16[16,3200]{1,0:T(8,128)(2,1)S(1)}, u32[]{:S(2)}, u32[]{:S(2)}) collective-permute-start(bf16[16,3200]{1,0:T(8,128)(2,1)S(1)} %hidden.7.refs_0_), channel_id=1, source_target_pairs={{0,6},{2,4},{4,2},{6,0},{8,14},{10,12},{12,10},{14,8},{1,7},{3,5},... | collective-permute-start | bytes 307208 | tf_op jit(solution)/shard_map/ppermute | solution.py:56
  102.5 7.1 %collective-permute-start.26 = (bf16[16,3200]{1,0:T(8,128)(2,1)S(1)}, bf16[16,3200]{1,0:T(8,128)(2,1)S(1)}, u32[]{:S(2)}, u32[]{:S(2)}) collective-permute-start(bf16[16,3200]{1,0:T(8,128)(2,1)S(1)} %hidden.7.refs_0_), channel_id=1, source_target_pairs={{0,2},{2,0},{4,6},{6,4},{8,10},{10,8},{12,14},{14,12},{1,3},{3,1},... | collective-permute-start | bytes 307208 | tf_op jit(solution)/shard_map/ppermute | solution.py:56
  104.6 6.2 %collective-permute-start.25 = (bf16[16,3200]{1,0:T(8,128)(2,1)S(1)}, bf16[16,3200]{1,0:T(8,128)(2,1)S(1)}, u32[]{:S(2)}, u32[]{:S(2)}) collective-permute-start(bf16[16,3200]{1,0:T(8,128)(2,1)S(1)} %hidden.7.refs_0_), channel_id=1, source_target_pairs={{0,4},{2,6},{4,0},{6,2},{8,12},{10,14},{12,8},{14,10},{1,5},{3,7},... | collective-permute-start | bytes 307208 | tf_op jit(solution)/shard_map/ppermute | solution.py:56
  112.0 1.4 %collective-permute-start.31 = (bf16[64,1024]{1,0:T(8,128)(2,1)S(1)}, bf16[64,1024]{1,0:T(8,128)(2,1)S(1)}, u32[]{:S(2)}, u32[]{:S(2)}) collective-permute-start(bf16[64,1024]{1,0:T(8,128)(2,1)S(1)} %get-tuple-element.117), channel_id=1, source_target_pairs={{0,1},{1,0},{2,3},{3,2},{4,5},{5,4},{6,7},{7,6},{8,9},{9,8},{10,11... | collective-permute-start | bytes 393224 | tf_op jit(solution)/shard_map/ppermute | solution.py:56
  114.1 4.3 %collective-permute-start.32 = (bf16[32,1024]{1,0:T(8,128)(2,1)S(1)}, bf16[32,1024]{1,0:T(8,128)(2,1)S(1)}, u32[]{:S(2)}, u32[]{:S(2)}) collective-permute-start(bf16[32,1024]{1,0:T(8,128)(2,1)S(1)} %get-tuple-element.120), channel_id=1, source_target_pairs={{16,0},{0,16},{17,1},{1,17},{18,2},{2,18},{19,3},{3,19},{20,4},{4,... | collective-permute-start | bytes 196616 | tf_op jit(solution)/shard_map/ppermute | solution.py:418

commit v6 on v5

--- a/solution.py
+++ b/solution.py
@@ -180,16 +180,81 @@
             copies[k][i].wait()
         term = jnp.dot(x_ref[:, a:b], held[k][a:b, :], preferred_element_type=F32)
         totals[k] = term if totals[k] is None else totals[k] + term
-    group = outs[0].shape[0]
+    hand_out(totals, outs, width, per, sumsq_ref[...] if summed else None)
+
+
+def hand_out(totals, outs, width, per, squares):
+    size, group = len(outs), outs[0].shape[0]
     for p in range(group * size):
         rows = slice(p * per, (p + 1) * per)
         both = jnp.concatenate([totals[0][rows], totals[1][rows]], axis=0)
         target = outs[p // group]
         target[p % group, :, :width] = both if p < group else squeeze(both)
-        if summed:
-            square = sumsq_ref[rows]
-            square = jnp.concatenate([square, square], axis=0)
+        if squares is not None:
+            square = jnp.concatenate([squares[rows], squares[rows]], axis=0)
             target[p % group, :, width:] = square if p < group else three_lanes(square[:, :1])
+
+
+def renewed(state_ref, arrived):
+    state = state_ref[...]
+    for ref in arrived:
+        state = state + expand(ref)
+    return state
+
+
+def begin_kernel(count, state_ref, *refs):
+    arrived, (gate_ref, up_ref, state_out, x_ref, sumsq_ref, gate_out, up_out) = refs[:count], refs[count:]
+    state = renewed(state_ref, arrived)
+    half = state.shape[1]
+    x = state.astype(BF16)
+    state_out[...] = state
+    x_ref[...] = x
+    sumsq_ref[...] = rows_mean_square(state)
+    gate_out[...] = jnp.dot(x, gate_ref[:half, :], preferred_element_type=F32)
+    up_out[...] = jnp.dot(x, up_ref[:half, :], preferred_element_type=F32)
+
+
+def end_kernel(count, per, size, state_ref, *refs):
+    arrived, refs = refs[:count], refs[count:]
+    gate_ref, up_ref, first_state, first_x, sumsq_ref, gate_in, up_in, *outs = refs
+    outs, (state_out, x_ref) = outs[:size], outs[size:]
+    state = renewed(state_ref, arrived)
+    half, width = state.shape[1], gate_ref.shape[1]
+    x = state.astype(BF16)
+    state_out[:, :half] = first_state[...]
+    state_out[:, half:] = state
+    x_ref[:, :half] = first_x[...]
+    x_ref[:, half:] = x
+    totals = [gate_in[...] + jnp.dot(x, gate_ref[half:, :], preferred_element_type=F32)]
+    totals.append(up_in[...] + jnp.dot(x, up_ref[half:, :], preferred_element_type=F32))
+    hand_out(totals, outs, width, per, sumsq_ref[...] + rows_mean_square(state))
+
+
+def renew_and_gate_up(per, size, states, sends, weights):
+    rows, half = states[0].shape
+    depth, width = weights[0].shape
+    params = dict(compiler_params=pltpu.CompilerParams(vmem_limit_bytes=HELD_LIMIT * MIB))
+    params["cost_estimate"] = cost(2 * rows * depth * width, 2 * depth * width)
+    total = struct((rows, width), F32)
+    made = pl.pallas_call(
+        functools.partial(begin_kernel, len(sends[0])),
+        out_shape=(struct((rows, half), F32), struct((rows, half), BF16), struct((rows, LANES), F32), total, total),
+        in_specs=[VMEM] * (3 + len(sends[0])),
+        out_specs=(VMEM,) * 5,
+        name="begin",
+        **params,
+    )(states[0], *sends[0], *weights)
+    shape = (rows // per // size, 2 * per, width + LANES)
+    return pl.pallas_call(
+        functools.partial(end_kernel, len(sends[1]), per, size),
+        out_shape=(struct(shape, F32),)
+        + (struct(shape, BF16),) * (size - 1)
+        + (struct((rows, depth), F32), struct((rows, depth), BF16)),
+        in_specs=[VMEM] * (8 + len(sends[1])),
+        out_specs=(VMEM,) * (size + 2),
+        name="end",
+        **params,
+    )(states[1], *sends[1], *weights, *made)
 
 
 def gate_up(first, width, per, size, base, x, sumsq, weights, fresh):
@@ -365,20 +430,14 @@
     )(base, *parts, weight, *([before] if added else []))
 
 
-def chip_kernel(a_ref, b_ref, state_ref, state_out, send_ref):
+def chip_kernel(a_ref, b_ref, state_ref, *outs):
     total = a_ref[...] + expand(b_ref)
-    send_ref[...] = squeeze(total)
-    state_out[...] = state_ref[...] + total
-
-
-def renew_kernel(state_ref, *refs):
-    arrived, (state_out, x_ref, sumsq_ref) = refs[:-3], refs[-3:]
-    state = state_ref[...]
-    for ref in arrived:
-        state = state + expand(ref)
-    state_out[...] = state
-    x_ref[...] = state.astype(BF16)
-    sumsq_ref[...] = rows_mean_square(state)
+    state = state_ref[...] + total
+    half = outs[0].shape[1]
+    for k in range(2):
+        columns = slice(k * half, (k + 1) * half)
+        outs[k][...] = state[:, columns]
+        outs[2 + k][...] = squeeze(total[:, columns])
 
 
 def finish_kernel(offsets, per, groups, where_ref, a_ref, b_ref, state_ref, out_ref, *refs):
@@ -434,9 +493,12 @@
             if fresh[0] and c == 0:
                 weights, fresh = (early, up_weight), (False, True)
             size = len(stages[0])
-            found = gate_up(
-                first, width, per, size, base, after(x, previous), sumsq if c == 0 else None, weights, fresh
-            )
+            if step > 0 and c == 0:
+                *found, state, x = renew_and_gate_up(per, size, states, halves, weights)
+            else:
+                found = gate_up(
+                    first, width, per, size, base, after(x, previous), sumsq if c == 0 else None, weights, fresh
+                )
             previous = found[0]
             if c not in gates:
                 gates[c] = tuple(found[size:]) if c else (early, found[size])
@@ -489,26 +551,18 @@
                 downs[c] = found[-1]
         other = swap(found[1], "ffn", 1, ffn)
         if step + 1 < STEPS:
-            shape = state.shape
-            state, send = pl.pallas_call(
+            half = struct((rows, state.shape[1] // 2), F32)
+            sent = struct(half.shape, BF16)
+            *states, first_send, second_send = pl.pallas_call(
                 chip_kernel,
-                out_shape=(struct(shape, F32), struct(shape, BF16)),
+                out_shape=(half, half, sent, sent),
                 in_specs=[VMEM] * 3,
-                out_specs=(VMEM,) * 2,
+                out_specs=(VMEM,) * 4,
                 name="chip_sum",
                 compiler_params=pltpu.CompilerParams(vmem_limit_bytes=8 * MIB),
                 cost_estimate=cost(state.size, state.size * 16),
             )(change, other, state)
-            arrived = [from_group(send, k) for k in range(1, groups)]
-            state, x, sumsq = pl.pallas_call(
-                renew_kernel,
-                out_shape=(struct(shape, F32), struct(shape, BF16), struct((rows, LANES), F32)),
-                in_specs=[VMEM] * (1 + len(arrived)),
-                out_specs=(VMEM,) * 3,
-                name="renew",
-                compiler_params=pltpu.CompilerParams(vmem_limit_bytes=8 * MIB),
-                cost_estimate=cost(state.size, state.size * 12),
-            )(state, *arrived)
+            halves = [[from_group(send, k) for k in range(1, groups)] for send in (first_send, second_send)]
     own = struct(tokens.shape, F32)
     out, *sends = pl.pallas_call(
         functools.partial(finish_kernel, offsets, per, groups),

time: 119 us -> 117 us (0.983)
  waiting for transfers between devices: 47.8 us -> 39.4 us
  starting transfers between devices: 38.3 us -> 41.7 us
  local copies, waits for them, and re-layouts: 0.01 us -> 2.72 us
    ppermute x30, waiting for transfers between devices: 38.8 us -> 32.8 us  [swap(): return lax.ppermute(value, axis, [(i, i ^ flip) for i in range(count)])]
    unnamed x2 -> x8, local copies, waits for them, and re-layouts: 0.01 us -> 2.72 us
    pallas_call x2 -> x3, Pallas kernels: 0.25 us -> 2.77 us  [the longest x1 1.35 us: renew_and_gate_up(): pl.pallas_call(functools.partial(end_kernel, len(sends[1]), per, size), o...]
    ppermute x3 -> x4, waiting for transfers between devices: 9.05 us -> 6.61 us  [from_group(): lax.ppermute(value, 'groups', [((i + k) % groups, i) for i in range(group...]
    pallas_call x4 -> x3, Pallas kernels: 13.4 us -> 11.2 us  [gate_up(): pl.pallas_call(functools.partial(gate_up_kernel, first, per, size, fresh,...]
    ppermute x3 -> x4, starting transfers between devices: 3.83 us -> 5.57 us  [from_group(): lax.ppermute(value, 'groups', [((i + k) % groups, i) for i in range(group...]
    ppermute x30, starting transfers between devices: 34.5 us -> 36.1 us  [swap(): return lax.ppermute(value, axis, [(i, i ^ flip) for i in range(count)])]
  transfers between devices with their start and end apart: 33 -> 34, of which waited for: 22 -> 19; matrix products, arithmetic and copies ran while one was open for 0% -> 0% of each run, Pallas kernels for 18% -> 20%
where the time goes in v6:
time: 117 us
  starting transfers between devices  41.7 us (36%)
  waiting for transfers between devices  39.4 us (34%)
  Pallas kernels  32.3 us (28%)
  local copies, waits for them, and re-layouts  2.72 us (2%)
    ppermute x30, starting transfers between devices, swap(): return lax.ppermute(value, axis, [(i, i ^ flip) for i in range(count)])  36.1 us
    ppermute x30, waiting for transfers between devices, swap(): return lax.ppermute(value, axis, [(i, i ^ flip) for i in range(count)])  32.8 us
    pallas_call x3, Pallas kernels, gate_up(): pl.pallas_call(functools.partial(gate_up_kernel, first, per, size, fresh,...  11.2 us
    ppermute x4, waiting for transfers between devices, from_group(): lax.ppermute(value, 'groups', [((i + k) % groups, i) for i in range(group...  6.61 us
    pallas_call x2, Pallas kernels, load_down(): pl.pallas_call(functools.partial(load_down_kernel, first), out_shape=stru...  5.95 us
    ppermute x4, starting transfers between devices, from_group(): lax.ppermute(value, 'groups', [((i + k) % groups, i) for i in range(group...  5.57 us
    pallas_call x4, Pallas kernels, down(): pl.pallas_call(functools.partial(down_kernel, first, len(parts), added, f...  5.29 us
    pallas_call x1, Pallas kernels, load(): pl.pallas_call(functools.partial(load_kernel, first), out_shape=struct((d...  3.13 us
  transfers between devices with their start and end apart: 34, of which 19 were waited for; matrix products, arithmetic and copies ran while one was open for 0% of the time, Pallas kernels for 20%

profile of v6, /device:TPU:0, one launch (start us, length us, event | category | flops | bytes accessed | tf_op | source)
XLA Modules:
  0.0 117.0 jit_solution(16504014974243353571)
XLA Ops:
  0.0 2.9 %collective-permute-start = (bf16[32,1024]{1,0:T(8,128)(2,1)}, bf16[32,1024]{1,0:T(8,128)(2,1)S(1)}, u32[]{:S(2)}, u32[]{:S(2)}) collective-permute-start(bf16[32,1024]{1,0:T(8,128)(2,1)} %own_ref.1), channel_id=1, source_target_pairs={{16,0},{0,16},{17,1},{1,17},{18,2},{2,18},{19,3},{3,19},{20,4},{4,... | collective-permute-start | bytes 196616 | tf_op jit(solution)/shard_map/ppermute | solution.py:477
  2.9 3.1 %load.1.refs_1_ = bf16[1024,3456]{1,0:T(8,128)(2,1)S(1)} custom-call(s32[1]{0:T(128)} %bitcast.2.base_ref, bf16[1024,13312]{1,0:T(8,128)(2,1)} %refs_0_.1), custom_call_target="tpu_custom_call" | custom-call | bytes 14155776 | tf_op jit(solution)/shard_map/load/pallas_call | solution.py:144
  6.8 3.6 %gate_up.3 = (f32[2,16,3584]{2,1,0:T(8,128)S(1)}, bf16[2,16,3584]{2,1,0:T(8,128)(2,1)S(1)}, bf16[2,16,3584]{2,1,0:T(8,128)(2,1)S(1)}, bf16[2,16,3584]{2,1,0:T(8,128)(2,1)S(1)}, bf16[1024,3456]{1,0:T(8,128)(2,1)S(1)}) custom-call(s32[1]{0:T(128)} %bitcast.2.base_ref, bf16[64,1024]{1,0:T(8,128)(2,1)S(1)} %get-tuple-element.72.x_ref, ...), custom_call_target="tpu_custom_call" | custom-call | flops 905969664 | bytes 14155776 | tf_op jit(solution)/shard_map/gate_up/pallas_call | solution.py:266
  10.4 1.6 %collective-permute-start.1 = (bf16[2,16,3584]{2,1,0:T(8,128)(2,1)S(1)}, bf16[2,16,3584]{2,1,0:T(8,128)(2,1)S(1)}, u32[]{:S(2)}, u32[]{:S(2)}) collective-permute-start(bf16[2,16,3584]{2,1,0:T(8,128)(2,1)S(1)} %get-tuple-element.75), channel_id=1, source_target_pairs={{0,4},{2,6},{4,0},{6,2},{8,12},{10,14},{12,8},{14,10},{1,5},{3,7},... | collective-permute-start | bytes 688136 | tf_op jit(solution)/shard_map/ppermute | solution.py:56
  12.1 1.5 %collective-permute-start.2 = (bf16[2,16,3584]{2,1,0:T(8,128)(2,1)S(1)}, bf16[2,16,3584]{2,1,0:T(8,128)(2,1)S(1)}, u32[]{:S(2)}, u32[]{:S(2)}) collective-permute-start(bf16[2,16,3584]{2,1,0:T(8,128)(2,1)S(1)} %get-tuple-element.76), channel_id=1, source_target_pairs={{0,2},{2,0},{4,6},{6,4},{8,10},{10,8},{12,14},{14,12},{1,3},{3,1},... | collective-permute-start | bytes 688136 | tf_op jit(solution)/shard_map/ppermute | solution.py:56
  14.0 5.3 %gate_up.4 = (f32[2,16,3200]{2,1,0:T(8,128)S(1)}, bf16[2,16,3200]{2,1,0:T(8,128)(2,1)S(1)}, bf16[2,16,3200]{2,1,0:T(8,128)(2,1)S(1)}, bf16[2,16,3200]{2,1,0:T(8,...) custom-call(s32[1]{0:T(128)} %bitcast.2.base_ref, ...), custom_call_target="tpu_custom_call" | custom-call | flops 838860800 | bytes 13107200 | tf_op jit(solution)/shard_map/gate_up/pallas_call | solution.py:266
  19.3 2.7 %copy-done = bf16[1024,3200]{1,0:T(8,128)(2,1)} copy-done((bf16[1024,3200]{1,0:T(8,128)(2,1)}, bf16[1024,3200]{1,0:T(8,128)(2,1)S(1)}, u32[]{:S(2)}) %copy-start) | copy-done | bytes 6553624
  22.0 1.6 %collective-permute-start.4 = (bf16[2,16,3200]{2,1,0:T(8,128)(2,1)S(1)}, bf16[2,16,3200]{2,1,0:T(8,128)(2,1)S(1)}, u32[]{:S(2)}, u32[]{:S(2)}) collective-permute-start(bf16[2,16,3200]{2,1,0:T(8,128)(2,1)S(1)} %get-tuple-element.80), channel_id=1, source_target_pairs={{0,4},{2,6},{4,0},{6,2},{8,12},{10,14},{12,8},{14,10},{1,5},{3,7},... | collective-permute-start | bytes 614408 | tf_op jit(solution)/shard_map/ppermute | solution.py:56
  23.6 1.5 %collective-permute-start.5 = (bf16[2,16,3200]{2,1,0:T(8,128)(2,1)S(1)}, bf16[2,16,3200]{2,1,0:T(8,128)(2,1)S(1)}, u32[]{:S(2)}, u32[]{:S(2)}) collective-permute-start(bf16[2,16,3200]{2,1,0:T(8,128)(2,1)S(1)} %get-tuple-element.81), channel_id=1, source_target_pairs={{0,2},{2,0},{4,6},{6,4},{8,10},{10,8},{12,14},{14,12},{1,3},{3,1},... | collective-permute-start | bytes 614408 | tf_op jit(solution)/shard_map/ppermute | solution.py:56
  26.1 2.7 %collective-permute-start.8 = (bf16[2,16,3584]{2,1,0:T(8,128)(2,1)S(1)}, bf16[2,16,3584]{2,1,0:T(8,128)(2,1)S(1)}, u32[]{:S(2)}, u32[]{:S(2)}) collective-permute-start(bf16[2,16,3584]{2,1,0:T(8,128)(2,1)S(1)} %get-tuple-element.87), channel_id=1, source_target_pairs={{0,8},{2,10},{4,12},{6,14},{8,0},{10,2},{12,4},{14,6},{1,9},{3,11}... | collective-permute-start | bytes 688136 | tf_op jit(solution)/shard_map/ppermute | solution.py:56
  28.7 3.1 %load_down.2.refs_4_ = bf16[3456,1024]{1,0:T(8,128)(2,1)S(1)} custom-call(s32[1]{0:T(128)} %bitcast.2.base_ref, bf16[13312,1024]{1,0:T(8,128)(2,1)} %down_hbm.3, f32[2,16,3584]{2,1,0:T(8,128)S(1)} %get-tuple-element.86.after_ref.keep_ref), custom_call_target="tpu_custom_call" | custom-call | bytes 7077888 | tf_op jit(solution)/shard_map/load_down/pallas_call | solution.py:378
  31.8 2.9 %collective-permute-done.4.refs_0_ = bf16[2,16,3200]{2,1,0:T(8,128)(2,1)S(1)} collective-permute-done((bf16[2,16,3200]{2,1,0:T(8,128)(2,1)S(1)}, bf16[2,16,3200]{2,1,0:T(8,128)(2,1)S(1)}, u32[]{:S(2)}, u32[]{:S(2)}) %collective-permute-start.4) | collective-permute-done | bytes 204832 | tf_op jit(solution)/shard_map/ppermute | solution.py:56
  34.7 3.4 %collective-permute-done.6.refs_2_ = bf16[2,16,3200]{2,1,0:T(8,128)(2,1)S(1)} collective-permute-done((bf16[2,16,3200]{2,1,0:T(8,128)(2,1)S(1)}, bf16[2,16,3200]{2,1,0:T(8,128)(2,1)S(1)}, u32[]{:S(2)}, u32[]{:S(2)}) %collective-permute-start.6) | collective-permute-done | bytes 204832 | tf_op jit(solution)/shard_map/ppermute | solution.py:56
  38.8 3.5 %collective-permute-start.14 = (bf16[16,3456]{1,0:T(8,128)(2,1)S(1)}, bf16[16,3456]{1,0:T(8,128)(2,1)S(1)}, u32[]{:S(2)}, u32[]{:S(2)}) collective-permute-start(bf16[16,3456]{1,0:T(8,128)(2,1)S(1)} %get-tuple-element.90.refs_0_), channel_id=1, source_target_pairs={{0,6},{2,4},{4,2},{6,0},{8,14},{10,12},{12,10},{14,8},{1,7},{3,5},... | collective-permute-start | bytes 331784 | tf_op jit(solution)/shard_map/ppermute | solution.py:56
  42.3 1.5 %collective-permute-start.13 = (bf16[16,3456]{1,0:T(8,128)(2,1)S(1)}, bf16[16,3456]{1,0:T(8,128)(2,1)S(1)}, u32[]{:S(2)}, u32[]{:S(2)}) collective-permute-start(bf16[16,3456]{1,0:T(8,128)(2,1)S(1)} %get-tuple-element.90.refs_0_), channel_id=1, source_target_pairs={{0,2},{2,0},{4,6},{6,4},{8,10},{10,8},{12,14},{14,12},{1,3},{3,1},... | collective-permute-start | bytes 331784 | tf_op jit(solution)/shard_map/ppermute | solution.py:56
  43.8 2.9 %load_down.3.refs_4_ = bf16[3200,1024]{1,0:T(8,128)(2,1)S(1)} custom-call(s32[1]{0:T(128)} %bitcast.2.base_ref, bf16[13312,1024]{1,0:T(8,128)(2,1)} %down_hbm.3, f32[2,16,3200]{2,1,0:T(8,128)S(1)} %get-tuple-element.84.after_ref.keep_ref), custom_call_target="tpu_custom_call" | custom-call | bytes 6553600 | tf_op jit(solution)/shard_map/load_down/pallas_call | solution.py:378
  46.7 2.0 %collective-permute-done.7.refs_0_ = bf16[2,16,3200]{2,1,0:T(8,128)(2,1)S(1)} collective-permute-done((bf16[2,16,3200]{2,1,0:T(8,128)(2,1)S(1)}, bf16[2,16,3200]{2,1,0:T(8,128)(2,1)S(1)}, u32[]{:S(2)}, u32[]{:S(2)}) %collective-permute-start.7) | collective-permute-done | bytes 204832 | tf_op jit(solution)/shard_map/ppermute | solution.py:56
  48.9 1.5 %collective-permute-start.10 = (bf16[16,3200]{1,0:T(8,128)(2,1)S(1)}, bf16[16,3200]{1,0:T(8,128)(2,1)S(1)}, u32[]{:S(2)}, u32[]{:S(2)}) collective-permute-start(bf16[16,3200]{1,0:T(8,128)(2,1)S(1)} %hidden.5.refs_0_), channel_id=1, source_target_pairs={{0,2},{2,0},{4,6},{6,4},{8,10},{10,8},{12,14},{14,12},{1,3},{3,1},... | collective-permute-start | bytes 307208 | tf_op jit(solution)/shard_map/ppermute | solution.py:56
  50.4 2.0 %collective-permute-start.9 = (bf16[16,3200]{1,0:T(8,128)(2,1)S(1)}, bf16[16,3200]{1,0:T(8,128)(2,1)S(1)}, u32[]{:S(2)}, u32[]{:S(2)}) collective-permute-start(bf16[16,3200]{1,0:T(8,128)(2,1)S(1)} %hidden.5.refs_0_), channel_id=1, source_target_pairs={{0,4},{2,6},{4,0},{6,2},{8,12},{10,14},{12,8},{14,10},{1,5},{3,7},... | collective-permute-start | bytes 307208 | tf_op jit(solution)/shard_map/ppermute | solution.py:56
  52.4 1.4 %down.4.refs_5_ = f32[64,1024]{1,0:T(8,128)S(1)} custom-call(s32[1]{0:T(128)} %bitcast.2.base_ref, bf16[16,3456]{1,0:T(8,128)(2,1)S(1)} %get-tuple-element.90.refs_0_, bf16[16,3456]{1,0:T(8,128)(2,1)S(1)} %collective-permute-done.12.refs_1_, bf16[16,3456]{1,0:T(8,128)(2,1)S(1)} %collective-permute-done.13.refs_2_, ...), custom_call_target="tpu_custom_call" | custom-call | flops 452984832 | bytes 7077888 | tf_op jit(solution)/shard_map/down/pallas_call | solution.py:419
  53.8 1.1 collective-permute-done.11.refs_3_
  55.7 1.3 %down.5 = (f32[64,1024]{1,0:T(8,128)S(1)}, bf16[64,1024]{1,0:T(8,128)(2,1)S(1)}) custom-call(s32[1]{0:T(128)} %bitcast.2.base_ref, bf16[16,3200]{1,0:T(8,128)(2,1)S(1)} %hidden.5.refs_0_, bf16[16,3200]{1,0:T(8,128)(2,1)S(1)} %collective-permute-done.9.refs_1_, bf16[16,3200]{1,0:T(8,128)(2,1)S(1)} %collective-permute-done.10.refs_2_, ...), custom_call_target="tpu_custom_call" | custom-call | flops 419430400 | bytes 6553600 | tf_op jit(solution)/shard_map/down/pallas_call | solution.py:419
  57.1 1.3 %collective-permute-done.15.b_ref = bf16[64,1024]{1,0:T(8,128)(2,1)S(1)} collective-permute-done((bf16[64,1024]{1,0:T(8,128)(2,1)S(1)}, bf16[64,1024]{1,0:T(8,128)(2,1)S(1)}, u32[]{:S(2)}, u32[]{:S(2)}) %collective-permute-start.15) | collective-permute-done | bytes 131104 | tf_op jit(solution)/shard_map/ppermute | solution.py:56
  59.4 1.2 %collective-permute-start.16 = (bf16[64,512]{1,0:T(8,128)(2,1)S(1)}, bf16[64,512]{1,0:T(8,128)(2,1)S(1)}, u32[]{:S(2)}, u32[]{:S(2)}) collective-permute-start(bf16[64,512]{1,0:T(8,128)(2,1)S(1)} %get-tuple-element.95), channel_id=1, source_target_pairs={{16,0},{0,16},{17,1},{1,17},{18,2},{2,18},{19,3},{3,19},{20,4},{4,... | collective-permute-start | bytes 196616 | tf_op jit(solution)/shard_map/ppermute | solution.py:477
  60.6 2.8 %collective-permute-done.17.refs_0_ = bf16[64,512]{1,0:T(8,128)(2,1)S(1)} collective-permute-done((bf16[64,512]{1,0:T(8,128)(2,1)S(1)}, bf16[64,512]{1,0:T(8,128)(2,1)S(1)}, u32[]{:S(2)}, u32[]{:S(2)}) %collective-permute-start.17) | collective-permute-done | bytes 65568 | tf_op jit(solution)/shard_map/ppermute | solution.py:477
  63.4 1.3 %begin.1 = (f32[64,512]{1,0:T(8,128)S(1)}, bf16[64,512]{1,0:T(8,128)(2,1)S(1)}, f32[64,128]{1,0:T(8,128)S(1)}, f32[64,3456]{1,0:T(8,128)S(1)}, f32[64,3456]{1,0:T(8,128)S(1)}) custom-call(f32[64,512]{1,0:T(8,128)S(1)} %get-tuple-element.97.state_ref, bf16[64,512]{1,0:T(8,128)(2,1)S(1)} %collective-permute-done.17.refs_0_, ...), custom_call_target="tpu_custom_call" | custom-call | flops 452984832 | bytes 7077888 | tf_op jit(solution)/shard_map/begin/pallas_call | solution.py:239
  64.7 1.4 %end.1 = (f32[2,16,3584]{2,1,0:T(8,128)S(1)}, bf16[2,16,3584]{2,1,0:T(8,128)(2,1)S(1)}, bf16[2,16,3584]{2,1,0:T(8,128)(2,1)S(1)}, bf16[2,16,3584]{2,1,0:T(8,128)...) custom-call(f32[64,512]{1,0:T(8,128)S(1)} %get-tuple-element.94.state_ref, ...), custom_call_target="tpu_custom_call" | custom-call | flops 452984832 | bytes 7077888 | tf_op jit(solution)/shard_map/end/pallas_call | solution.py:248
  66.1 1.4 %collective-permute-start.22 = (bf16[2,16,3584]{2,1,0:T(8,128)(2,1)S(1)}, bf16[2,16,3584]{2,1,0:T(8,128)(2,1)S(1)}, u32[]{:S(2)}, u32[]{:S(2)}) collective-permute-start(bf16[2,16,3584]{2,1,0:T(8,128)(2,1)S(1)} %get-tuple-element.117), channel_id=1, source_target_pairs={{0,4},{2,6},{4,0},{6,2},{8,12},{10,14},{12,8},{14,10},{1,5},{3,7},... | collective-permute-start | bytes 688136 | tf_op jit(solution)/shard_map/ppermute | solution.py:56
  68.4 1.3 %collective-permute-start.24 = (bf16[2,16,3584]{2,1,0:T(8,128)(2,1)S(1)}, bf16[2,16,3584]{2,1,0:T(8,128)(2,1)S(1)}, u32[]{:S(2)}, u32[]{:S(2)}) collective-permute-start(bf16[2,16,3584]{2,1,0:T(8,128)(2,1)S(1)} %get-tuple-element.119), channel_id=1, source_target_pairs={{0,6},{2,4},{4,2},{6,0},{8,14},{10,12},{12,10},{14,8},{1,7},{3,5},... | collective-permute-start | bytes 688136 | tf_op jit(solution)/shard_map/ppermute | solution.py:56
  69.7 2.3 %gate_up.5 = (f32[2,16,3200]{2,1,0:T(8,128)S(1)}, bf16[2,16,3200]{2,1,0:T(8,128)(2,1)S(1)}, bf16[2,16,3200]{2,1,0:T(8,128)(2,1)S(1)}, bf16[2,16,3200]{2,1,0:T(8,128)(2,1)S(1)}) custom-call(s32[1]{0:T(128)} %bitcast.2.base_ref, bf16[64,1024]{1,0:T(8,128)(2,1)S(1)} %get-tuple-element.106.x_ref, bf16[1024,3200]{1,0:T(8,128)(2,1)S(1)} %get-tuple-element.107.refs_0_, ...), custom_call_target="tpu_custom_call" | custom-call | flops 838860800 | bytes 13107200 | tf_op jit(solution)/shard_map/gate_up/pallas_call | solution.py:266
  72.0 1.4 %collective-permute-start.18 = (bf16[2,16,3200]{2,1,0:T(8,128)(2,1)S(1)}, bf16[2,16,3200]{2,1,0:T(8,128)(2,1)S(1)}, u32[]{:S(2)}, u32[]{:S(2)}) collective-permute-start(bf16[2,16,3200]{2,1,0:T(8,128)(2,1)S(1)} %get-tuple-element.110), channel_id=1, source_target_pairs={{0,4},{2,6},{4,0},{6,2},{8,12},{10,14},{12,8},{14,10},{1,5},{3,7},... | collective-permute-start | bytes 614408 | tf_op jit(solution)/shard_map/ppermute | solution.py:56
  74.7 1.7 %collective-permute-start.20 = (bf16[2,16,3200]{2,1,0:T(8,128)(2,1)S(1)}, bf16[2,16,3200]{2,1,0:T(8,128)(2,1)S(1)}, u32[]{:S(2)}, u32[]{:S(2)}) collective-permute-start(bf16[2,16,3200]{2,1,0:T(8,128)(2,1)S(1)} %get-tuple-element.112), channel_id=1, source_target_pairs={{0,6},{2,4},{4,2},{6,0},{8,14},{10,12},{12,10},{14,8},{1,7},{3,5},... | collective-permute-start | bytes 614408 | tf_op jit(solution)/shard_map/ppermute | solution.py:56
  76.4 3.0 %collective-permute-done.23.refs_1_ = bf16[2,16,3584]{2,1,0:T(8,128)(2,1)S(1)} collective-permute-done((bf16[2,16,3584]{2,1,0:T(8,128)(2,1)S(1)}, bf16[2,16,3584]{2,1,0:T(8,128)(2,1)S(1)}, u32[]{:S(2)}, u32[]{:S(2)}) %collective-permute-start.23) | collective-permute-done | bytes 229408 | tf_op jit(solution)/shard_map/ppermute | solution.py:56
  80.3 2.9 %collective-permute-start.25 = (bf16[2,16,3584]{2,1,0:T(8,128)(2,1)S(1)}, bf16[2,16,3584]{2,1,0:T(8,128)(2,1)S(1)}, u32[]{:S(2)}, u32[]{:S(2)}) collective-permute-start(bf16[2,16,3584]{2,1,0:T(8,128)(2,1)S(1)} %get-tuple-element.122), channel_id=1, source_target_pairs={{0,8},{2,10},{4,12},{6,14},{8,0},{10,2},{12,4},{14,6},{1,9},{3,11}... | collective-permute-start | bytes 688136 | tf_op jit(solution)/shard_map/ppermute | solution.py:56
  83.1 4.7 %collective-permute-done.18.refs_0_ = bf16[2,16,3200]{2,1,0:T(8,128)(2,1)S(1)} collective-permute-done((bf16[2,16,3200]{2,1,0:T(8,128)(2,1)S(1)}, bf16[2,16,3200]{2,1,0:T(8,128)(2,1)S(1)}, u32[]{:S(2)}, u32[]{:S(2)}) %collective-permute-start.18) | collective-permute-done | bytes 204832 | tf_op jit(solution)/shard_map/ppermute | solution.py:56
  87.8 3.6 %collective-permute-done.20.refs_2_ = bf16[2,16,3200]{2,1,0:T(8,128)(2,1)S(1)} collective-permute-done((bf16[2,16,3200]{2,1,0:T(8,128)(2,1)S(1)}, bf16[2,16,3200]{2,1,0:T(8,128)(2,1)S(1)}, u32[]{:S(2)}, u32[]{:S(2)}) %collective-permute-start.20) | collective-permute-done | bytes 204832 | tf_op jit(solution)/shard_map/ppermute | solution.py:56
  91.8 2.5 %collective-permute-done.25.refs_0_ = bf16[2,16,3584]{2,1,0:T(8,128)(2,1)S(1)} collective-permute-done((bf16[2,16,3584]{2,1,0:T(8,128)(2,1)S(1)}, bf16[2,16,3584]{2,1,0:T(8,128)(2,1)S(1)}, u32[]{:S(2)}, u32[]{:S(2)}) %collective-permute-start.25) | collective-permute-done | bytes 229408 | tf_op jit(solution)/shard_map/ppermute | solution.py:56
  94.6 1.4 %collective-permute-start.31 = (bf16[16,3456]{1,0:T(8,128)(2,1)S(1)}, bf16[16,3456]{1,0:T(8,128)(2,1)S(1)}, u32[]{:S(2)}, u32[]{:S(2)}) collective-permute-start(bf16[16,3456]{1,0:T(8,128)(2,1)S(1)} %get-tuple-element.125.refs_0_), channel_id=1, source_target_pairs={{0,6},{2,4},{4,2},{6,0},{8,14},{10,12},{12,10},{14,8},{1,7},{3,5},... | collective-permute-start | bytes 331784 | tf_op jit(solution)/shard_map/ppermute | solution.py:56
  96.0 2.1 %collective-permute-start.29 = (bf16[16,3456]{1,0:T(8,128)(2,1)S(1)}, bf16[16,3456]{1,0:T(8,128)(2,1)S(1)}, u32[]{:S(2)}, u32[]{:S(2)}) collective-permute-start(bf16[16,3456]{1,0:T(8,128)(2,1)S(1)} %get-tuple-element.125.refs_0_), channel_id=1, source_target_pairs={{0,4},{2,6},{4,0},{6,2},{8,12},{10,14},{12,8},{14,10},{1,5},{3,7},... | collective-permute-start | bytes 331784 | tf_op jit(solution)/shard_map/ppermute | solution.py:56
  98.1 2.8 %collective-permute-done.21.refs_0_ = bf16[2,16,3200]{2,1,0:T(8,128)(2,1)S(1)} collective-permute-done((bf16[2,16,3200]{2,1,0:T(8,128)(2,1)S(1)}, bf16[2,16,3200]{2,1,0:T(8,128)(2,1)S(1)}, u32[]{:S(2)}, u32[]{:S(2)}) %collective-permute-start.21) | collective-permute-done | bytes 204832 | tf_op jit(solution)/shard_map/ppermute | solution.py:56
  101.4 1.5 %collective-permute-start.27 = (bf16[16,3200]{1,0:T(8,128)(2,1)S(1)}, bf16[16,3200]{1,0:T(8,128)(2,1)S(1)}, u32[]{:S(2)}, u32[]{:S(2)}) collective-permute-start(bf16[16,3200]{1,0:T(8,128)(2,1)S(1)} %hidden.7.refs_0_), channel_id=1, source_target_pairs={{0,2},{2,0},{4,6},{6,4},{8,10},{10,8},{12,14},{14,12},{1,3},{3,1},... | collective-permute-start | bytes 307208 | tf_op jit(solution)/shard_map/ppermute | solution.py:56
  102.9 1.8 %collective-permute-start.26 = (bf16[16,3200]{1,0:T(8,128)(2,1)S(1)}, bf16[16,3200]{1,0:T(8,128)(2,1)S(1)}, u32[]{:S(2)}, u32[]{:S(2)}) collective-permute-start(bf16[16,3200]{1,0:T(8,128)(2,1)S(1)} %hidden.7.refs_0_), channel_id=1, source_target_pairs={{0,4},{2,6},{4,0},{6,2},{8,12},{10,14},{12,8},{14,10},{1,5},{3,7},... | collective-permute-start | bytes 307208 | tf_op jit(solution)/shard_map/ppermute | solution.py:56
  104.6 1.4 %down.6.refs_5_ = f32[64,1024]{1,0:T(8,128)S(1)} custom-call(s32[1]{0:T(128)} %bitcast.2.base_ref, bf16[16,3456]{1,0:T(8,128)(2,1)S(1)} %get-tuple-element.125.refs_0_, bf16[16,3456]{1,0:T(8,128)(2,1)S(1)} %collective-permute-done.29.refs_1_, bf16[16,3456]{1,0:T(8,128)(2,1)S(1)} %collective-permute-done.30.refs_2_, ...), custom_call_target="tpu_custom_call" | custom-call | flops 452984832 | bytes 7077888 | tf_op jit(solution)/shard_map/down/pallas_call | solution.py:419
  106.0 1.5 %collective-permute-done.28.refs_3_ = bf16[16,3200]{1,0:T(8,128)(2,1)S(1)} collective-permute-done((bf16[16,3200]{1,0:T(8,128)(2,1)S(1)}, bf16[16,3200]{1,0:T(8,128)(2,1)S(1)}, u32[]{:S(2)}, u32[]{:S(2)}) %collective-permute-start.28) | collective-permute-done | bytes 102432 | tf_op jit(solution)/shard_map/ppermute | solution.py:56
  107.6 1.0 collective-permute-done.26.refs_1_
  108.6 1.3 %down.7 = (f32[64,1024]{1,0:T(8,128)S(1)}, bf16[64,1024]{1,0:T(8,128)(2,1)S(1)}) custom-call(s32[1]{0:T(128)} %bitcast.2.base_ref, bf16[16,3200]{1,0:T(8,128)(2,1)S(1)} %hidden.7.refs_0_, bf16[16,3200]{1,0:T(8,128)(2,1)S(1)} %collective-permute-done.26.refs_1_, bf16[16,3200]{1,0:T(8,128)(2,1)S(1)} %collective-permute-done.27.refs_2_, ...), custom_call_target="tpu_custom_call" | custom-call | flops 419430400 | bytes 6553600 | tf_op jit(solution)/shard_map/down/pallas_call | solution.py:419
  110.0 1.3 %collective-permute-done.32.b_ref = bf16[64,1024]{1,0:T(8,128)(2,1)S(1)} collective-permute-done((bf16[64,1024]{1,0:T(8,128)(2,1)S(1)}, bf16[64,1024]{1,0:T(8,128)(2,1)S(1)}, u32[]{:S(2)}, u32[]{:S(2)}) %collective-permute-start.32) | collective-permute-done | bytes 131104 | tf_op jit(solution)/shard_map/ppermute | solution.py:56
  112.5 3.8 %collective-permute-done.33 = bf16[32,1024]{1,0:T(8,128)(2,1)S(1)} collective-permute-done((bf16[32,1024]{1,0:T(8,128)(2,1)S(1)}, bf16[32,1024]{1,0:T(8,128)(2,1)S(1)}, u32[]{:S(2)}, u32[]{:S(2)}) %collective-permute-start.33) | collective-permute-done | bytes 65568 | tf_op jit(solution)/shard_map/ppermute | solution.py:477
  (54 shorter events, 11.3 us)
Async XLA Ops:
  0.0 6.2 %collective-permute-start = (bf16[32,1024]{1,0:T(8,128)(2,1)}, bf16[32,1024]{1,0:T(8,128)(2,1)S(1)}, u32[]{:S(2)}, u32[]{:S(2)}) collective-permute-start(bf16[32,1024]{1,0:T(8,128)(2,1)} %own_ref.1), channel_id=1, source_target_pairs={{16,0},{0,16},{17,1},{1,17},{18,2},{2,18},{19,3},{3,19},{20,4},{4,... | collective-permute-start | bytes 196616 | tf_op jit(solution)/shard_map/ppermute | solution.py:477
  2.9 3.2 %copy-start.1 = (bf16[32,1024]{1,0:T(8,128)(2,1)S(1)}, bf16[32,1024]{1,0:T(8,128)(2,1)}, u32[]{:S(2)}) copy-start(bf16[32,1024]{1,0:T(8,128)(2,1)} %own_ref.1) | copy-start | bytes 196612
  10.4 14.7 %collective-permute-start.1 = (bf16[2,16,3584]{2,1,0:T(8,128)(2,1)S(1)}, bf16[2,16,3584]{2,1,0:T(8,128)(2,1)S(1)}, u32[]{:S(2)}, u32[]{:S(2)}) collective-permute-start(bf16[2,16,3584]{2,1,0:T(8,128)(2,1)S(1)} %get-tuple-element.75), channel_id=1, source_target_pairs={{0,4},{2,6},{4,0},{6,2},{8,12},{10,14},{12,8},{14,10},{1,5},{3,7},... | collective-permute-start | bytes 688136 | tf_op jit(solution)/shard_map/ppermute | solution.py:56
  12.1 13.5 %collective-permute-start.2 = (bf16[2,16,3584]{2,1,0:T(8,128)(2,1)S(1)}, bf16[2,16,3584]{2,1,0:T(8,128)(2,1)S(1)}, u32[]{:S(2)}, u32[]{:S(2)}) collective-permute-start(bf16[2,16,3584]{2,1,0:T(8,128)(2,1)S(1)} %get-tuple-element.76), channel_id=1, source_target_pairs={{0,2},{2,0},{4,6},{6,4},{8,10},{10,8},{12,14},{14,12},{1,3},{3,1},... | collective-permute-start | bytes 688136 | tf_op jit(solution)/shard_map/ppermute | solution.py:56
  13.6 11.9 %collective-permute-start.3 = (bf16[2,16,3584]{2,1,0:T(8,128)(2,1)S(1)}, bf16[2,16,3584]{2,1,0:T(8,128)(2,1)S(1)}, u32[]{:S(2)}, u32[]{:S(2)}) collective-permute-start(bf16[2,16,3584]{2,1,0:T(8,128)(2,1)S(1)} %get-tuple-element.77), channel_id=1, source_target_pairs={{0,6},{2,4},{4,2},{6,0},{8,14},{10,12},{12,10},{14,8},{1,7},{3,5},... | collective-permute-start | bytes 688136 | tf_op jit(solution)/shard_map/ppermute | solution.py:56
  19.3 2.7 %copy-start = (bf16[1024,3200]{1,0:T(8,128)(2,1)}, bf16[1024,3200]{1,0:T(8,128)(2,1)S(1)}, u32[]{:S(2)}) copy-start(bf16[1024,3200]{1,0:T(8,128)(2,1)S(1)} %get-tuple-element.108.refs_1_) | copy-start | bytes 19660804
  22.0 12.6 %collective-permute-start.4 = (bf16[2,16,3200]{2,1,0:T(8,128)(2,1)S(1)}, bf16[2,16,3200]{2,1,0:T(8,128)(2,1)S(1)}, u32[]{:S(2)}, u32[]{:S(2)}) collective-permute-start(bf16[2,16,3200]{2,1,0:T(8,128)(2,1)S(1)} %get-tuple-element.80), channel_id=1, source_target_pairs={{0,4},{2,6},{4,0},{6,2},{8,12},{10,14},{12,8},{14,10},{1,5},{3,7},... | collective-permute-start | bytes 614408 | tf_op jit(solution)/shard_map/ppermute | solution.py:56
  23.6 11.1 %collective-permute-start.5 = (bf16[2,16,3200]{2,1,0:T(8,128)(2,1)S(1)}, bf16[2,16,3200]{2,1,0:T(8,128)(2,1)S(1)}, u32[]{:S(2)}, u32[]{:S(2)}) collective-permute-start(bf16[2,16,3200]{2,1,0:T(8,128)(2,1)S(1)} %get-tuple-element.81), channel_id=1, source_target_pairs={{0,2},{2,0},{4,6},{6,4},{8,10},{10,8},{12,14},{14,12},{1,3},{3,1},... | collective-permute-start | bytes 614408 | tf_op jit(solution)/shard_map/ppermute | solution.py:56
  25.1 12.9 %collective-permute-start.6 = (bf16[2,16,3200]{2,1,0:T(8,128)(2,1)S(1)}, bf16[2,16,3200]{2,1,0:T(8,128)(2,1)S(1)}, u32[]{:S(2)}, u32[]{:S(2)}) collective-permute-start(bf16[2,16,3200]{2,1,0:T(8,128)(2,1)S(1)} %get-tuple-element.82), channel_id=1, source_target_pairs={{0,6},{2,4},{4,2},{6,0},{8,14},{10,12},{12,10},{14,8},{1,7},{3,5},... | collective-permute-start | bytes 614408 | tf_op jit(solution)/shard_map/ppermute | solution.py:56
  26.1 12.4 %collective-permute-start.8 = (bf16[2,16,3584]{2,1,0:T(8,128)(2,1)S(1)}, bf16[2,16,3584]{2,1,0:T(8,128)(2,1)S(1)}, u32[]{:S(2)}, u32[]{:S(2)}) collective-permute-start(bf16[2,16,3584]{2,1,0:T(8,128)(2,1)S(1)} %get-tuple-element.87), channel_id=1, source_target_pairs={{0,8},{2,10},{4,12},{6,14},{8,0},{10,2},{12,4},{14,6},{1,9},{3,11}... | collective-permute-start | bytes 688136 | tf_op jit(solution)/shard_map/ppermute | solution.py:56
  38.3 10.3 %collective-permute-start.7 = (bf16[2,16,3200]{2,1,0:T(8,128)(2,1)S(1)}, bf16[2,16,3200]{2,1,0:T(8,128)(2,1)S(1)}, u32[]{:S(2)}, u32[]{:S(2)}) collective-permute-start(bf16[2,16,3200]{2,1,0:T(8,128)(2,1)S(1)} %get-tuple-element.85), channel_id=1, source_target_pairs={{0,8},{2,10},{4,12},{6,14},{8,0},{10,2},{12,4},{14,6},{1,9},{3,11}... | collective-permute-start | bytes 614408 | tf_op jit(solution)/shard_map/ppermute | solution.py:56
  38.8 11.6 %collective-permute-start.14 = (bf16[16,3456]{1,0:T(8,128)(2,1)S(1)}, bf16[16,3456]{1,0:T(8,128)(2,1)S(1)}, u32[]{:S(2)}, u32[]{:S(2)}) collective-permute-start(bf16[16,3456]{1,0:T(8,128)(2,1)S(1)} %get-tuple-element.90.refs_0_), channel_id=1, source_target_pairs={{0,6},{2,4},{4,2},{6,0},{8,14},{10,12},{12,10},{14,8},{1,7},{3,5},... | collective-permute-start | bytes 331784 | tf_op jit(solution)/shard_map/ppermute | solution.py:56
  42.3 10.1 %collective-permute-start.13 = (bf16[16,3456]{1,0:T(8,128)(2,1)S(1)}, bf16[16,3456]{1,0:T(8,128)(2,1)S(1)}, u32[]{:S(2)}, u32[]{:S(2)}) collective-permute-start(bf16[16,3456]{1,0:T(8,128)(2,1)S(1)} %get-tuple-element.90.refs_0_), channel_id=1, source_target_pairs={{0,2},{2,0},{4,6},{6,4},{8,10},{10,8},{12,14},{14,12},{1,3},{3,1},... | collective-permute-start | bytes 331784 | tf_op jit(solution)/shard_map/ppermute | solution.py:56
  43.8 8.6 %collective-permute-start.12 = (bf16[16,3456]{1,0:T(8,128)(2,1)S(1)}, bf16[16,3456]{1,0:T(8,128)(2,1)S(1)}, u32[]{:S(2)}, u32[]{:S(2)}) collective-permute-start(bf16[16,3456]{1,0:T(8,128)(2,1)S(1)} %get-tuple-element.90.refs_0_), channel_id=1, source_target_pairs={{0,4},{2,6},{4,0},{6,2},{8,12},{10,14},{12,8},{14,10},{1,5},{3,7},... | collective-permute-start | bytes 331784 | tf_op jit(solution)/shard_map/ppermute | solution.py:56
  48.8 6.0 %collective-permute-start.11 = (bf16[16,3200]{1,0:T(8,128)(2,1)S(1)}, bf16[16,3200]{1,0:T(8,128)(2,1)S(1)}, u32[]{:S(2)}, u32[]{:S(2)}) collective-permute-start(bf16[16,3200]{1,0:T(8,128)(2,1)S(1)} %hidden.5.refs_0_), channel_id=1, source_target_pairs={{0,6},{2,4},{4,2},{6,0},{8,14},{10,12},{12,10},{14,8},{1,7},{3,5},... | collective-permute-start | bytes 307208 | tf_op jit(solution)/shard_map/ppermute | solution.py:56
  48.9 6.0 %collective-permute-start.10 = (bf16[16,3200]{1,0:T(8,128)(2,1)S(1)}, bf16[16,3200]{1,0:T(8,128)(2,1)S(1)}, u32[]{:S(2)}, u32[]{:S(2)}) collective-permute-start(bf16[16,3200]{1,0:T(8,128)(2,1)S(1)} %hidden.5.refs_0_), channel_id=1, source_target_pairs={{0,2},{2,0},{4,6},{6,4},{8,10},{10,8},{12,14},{14,12},{1,3},{3,1},... | collective-permute-start | bytes 307208 | tf_op jit(solution)/shard_map/ppermute | solution.py:56
  50.4 5.3 %collective-permute-start.9 = (bf16[16,3200]{1,0:T(8,128)(2,1)S(1)}, bf16[16,3200]{1,0:T(8,128)(2,1)S(1)}, u32[]{:S(2)}, u32[]{:S(2)}) collective-permute-start(bf16[16,3200]{1,0:T(8,128)(2,1)S(1)} %hidden.5.refs_0_), channel_id=1, source_target_pairs={{0,4},{2,6},{4,0},{6,2},{8,12},{10,14},{12,8},{14,10},{1,5},{3,7},... | collective-permute-start | bytes 307208 | tf_op jit(solution)/shard_map/ppermute | solution.py:56
  57.0 1.4 %collective-permute-start.15 = (bf16[64,1024]{1,0:T(8,128)(2,1)S(1)}, bf16[64,1024]{1,0:T(8,128)(2,1)S(1)}, u32[]{:S(2)}, u32[]{:S(2)}) collective-permute-start(bf16[64,1024]{1,0:T(8,128)(2,1)S(1)} %get-tuple-element.92), channel_id=1, source_target_pairs={{0,1},{1,0},{2,3},{3,2},{4,5},{5,4},{6,7},{7,6},{8,9},{9,8},{10,11... | collective-permute-start | bytes 393224 | tf_op jit(solution)/shard_map/ppermute | solution.py:56
  58.5 4.9 %collective-permute-start.17 = (bf16[64,512]{1,0:T(8,128)(2,1)S(1)}, bf16[64,512]{1,0:T(8,128)(2,1)S(1)}, u32[]{:S(2)}, u32[]{:S(2)}) collective-permute-start(bf16[64,512]{1,0:T(8,128)(2,1)S(1)} %get-tuple-element.98), channel_id=1, source_target_pairs={{16,0},{0,16},{17,1},{1,17},{18,2},{2,18},{19,3},{3,19},{20,4},{4,... | collective-permute-start | bytes 196616 | tf_op jit(solution)/shard_map/ppermute | solution.py:477
  59.4 5.4 %collective-permute-start.16 = (bf16[64,512]{1,0:T(8,128)(2,1)S(1)}, bf16[64,512]{1,0:T(8,128)(2,1)S(1)}, u32[]{:S(2)}, u32[]{:S(2)}) collective-permute-start(bf16[64,512]{1,0:T(8,128)(2,1)S(1)} %get-tuple-element.95), channel_id=1, source_target_pairs={{16,0},{0,16},{17,1},{1,17},{18,2},{2,18},{19,3},{3,19},{20,4},{4,... | collective-permute-start | bytes 196616 | tf_op jit(solution)/shard_map/ppermute | solution.py:477
  63.4 6.3 %slice-start = ((s8[6553600]{0:T(1024)(128)(4,1)}), s8[4194304]{0:T(1024)(128)(4,1)S(1)}, s32[]{:S(2)}) async-start(s8[6553600]{0:T(1024)(128)(4,1)} %bitcast.3), calls=%async_computation | async-start | bytes 8388608
  64.7 4.9 %slice-start.1 = ((s8[6553600]{0:T(1024)(128)(4,1)}), s8[2359296]{0:T(1024)(128)(4,1)S(1)}, s32[]{:S(2)}) async-start(s8[6553600]{0:T(1024)(128)(4,1)} %bitcast.3), calls=%async_computation.1 | async-start | bytes 4718592
  66.1 8.6 %collective-permute-start.22 = (bf16[2,16,3584]{2,1,0:T(8,128)(2,1)S(1)}, bf16[2,16,3584]{2,1,0:T(8,128)(2,1)S(1)}, u32[]{:S(2)}, u32[]{:S(2)}) collective-permute-start(bf16[2,16,3584]{2,1,0:T(8,128)(2,1)S(1)} %get-tuple-element.117), channel_id=1, source_target_pairs={{0,4},{2,6},{4,0},{6,2},{8,12},{10,14},{12,8},{14,10},{1,5},{3,7},... | collective-permute-start | bytes 688136 | tf_op jit(solution)/shard_map/ppermute | solution.py:56
  67.5 11.8 %collective-permute-start.23 = (bf16[2,16,3584]{2,1,0:T(8,128)(2,1)S(1)}, bf16[2,16,3584]{2,1,0:T(8,128)(2,1)S(1)}, u32[]{:S(2)}, u32[]{:S(2)}) collective-permute-start(bf16[2,16,3584]{2,1,0:T(8,128)(2,1)S(1)} %get-tuple-element.118), channel_id=1, source_target_pairs={{0,2},{2,0},{4,6},{6,4},{8,10},{10,8},{12,14},{14,12},{1,3},{3,1},... | collective-permute-start | bytes 688136 | tf_op jit(solution)/shard_map/ppermute | solution.py:56
  68.4 11.3 %collective-permute-start.24 = (bf16[2,16,3584]{2,1,0:T(8,128)(2,1)S(1)}, bf16[2,16,3584]{2,1,0:T(8,128)(2,1)S(1)}, u32[]{:S(2)}, u32[]{:S(2)}) collective-permute-start(bf16[2,16,3584]{2,1,0:T(8,128)(2,1)S(1)} %get-tuple-element.119), channel_id=1, source_target_pairs={{0,6},{2,4},{4,2},{6,0},{8,14},{10,12},{12,10},{14,8},{1,7},{3,5},... | collective-permute-start | bytes 688136 | tf_op jit(solution)/shard_map/ppermute | solution.py:56
  72.0 15.9 %collective-permute-start.18 = (bf16[2,16,3200]{2,1,0:T(8,128)(2,1)S(1)}, bf16[2,16,3200]{2,1,0:T(8,128)(2,1)S(1)}, u32[]{:S(2)}, u32[]{:S(2)}) collective-permute-start(bf16[2,16,3200]{2,1,0:T(8,128)(2,1)S(1)} %get-tuple-element.110), channel_id=1, source_target_pairs={{0,4},{2,6},{4,0},{6,2},{8,12},{10,14},{12,8},{14,10},{1,5},{3,7},... | collective-permute-start | bytes 614408 | tf_op jit(solution)/shard_map/ppermute | solution.py:56
  73.4 14.5 %collective-permute-start.19 = (bf16[2,16,3200]{2,1,0:T(8,128)(2,1)S(1)}, bf16[2,16,3200]{2,1,0:T(8,128)(2,1)S(1)}, u32[]{:S(2)}, u32[]{:S(2)}) collective-permute-start(bf16[2,16,3200]{2,1,0:T(8,128)(2,1)S(1)} %get-tuple-element.111), channel_id=1, source_target_pairs={{0,2},{2,0},{4,6},{6,4},{8,10},{10,8},{12,14},{14,12},{1,3},{3,1},... | collective-permute-start | bytes 614408 | tf_op jit(solution)/shard_map/ppermute | solution.py:56
  74.7 16.7 %collective-permute-start.20 = (bf16[2,16,3200]{2,1,0:T(8,128)(2,1)S(1)}, bf16[2,16,3200]{2,1,0:T(8,128)(2,1)S(1)}, u32[]{:S(2)}, u32[]{:S(2)}) collective-permute-start(bf16[2,16,3200]{2,1,0:T(8,128)(2,1)S(1)} %get-tuple-element.112), channel_id=1, source_target_pairs={{0,6},{2,4},{4,2},{6,0},{8,14},{10,12},{12,10},{14,8},{1,7},{3,5},... | collective-permute-start | bytes 614408 | tf_op jit(solution)/shard_map/ppermute | solution.py:56
  80.3 14.0 %collective-permute-start.25 = (bf16[2,16,3584]{2,1,0:T(8,128)(2,1)S(1)}, bf16[2,16,3584]{2,1,0:T(8,128)(2,1)S(1)}, u32[]{:S(2)}, u32[]{:S(2)}) collective-permute-start(bf16[2,16,3584]{2,1,0:T(8,128)(2,1)S(1)} %get-tuple-element.122), channel_id=1, source_target_pairs={{0,8},{2,10},{4,12},{6,14},{8,0},{10,2},{12,4},{14,6},{1,9},{3,11}... | collective-permute-start | bytes 688136 | tf_op jit(solution)/shard_map/ppermute | solution.py:56
  91.7 9.2 %collective-permute-start.21 = (bf16[2,16,3200]{2,1,0:T(8,128)(2,1)S(1)}, bf16[2,16,3200]{2,1,0:T(8,128)(2,1)S(1)}, u32[]{:S(2)}, u32[]{:S(2)}) collective-permute-start(bf16[2,16,3200]{2,1,0:T(8,128)(2,1)S(1)} %get-tuple-element.115), channel_id=1, source_target_pairs={{0,8},{2,10},{4,12},{6,14},{8,0},{10,2},{12,4},{14,6},{1,9},{3,11}... | collective-permute-start | bytes 614408 | tf_op jit(solution)/shard_map/ppermute | solution.py:56
  94.6 8.3 %collective-permute-start.31 = (bf16[16,3456]{1,0:T(8,128)(2,1)S(1)}, bf16[16,3456]{1,0:T(8,128)(2,1)S(1)}, u32[]{:S(2)}, u32[]{:S(2)}) collective-permute-start(bf16[16,3456]{1,0:T(8,128)(2,1)S(1)} %get-tuple-element.125.refs_0_), channel_id=1, source_target_pairs={{0,6},{2,4},{4,2},{6,0},{8,14},{10,12},{12,10},{14,8},{1,7},{3,5},... | collective-permute-start | bytes 331784 | tf_op jit(solution)/shard_map/ppermute | solution.py:56
  96.0 8.6 %collective-permute-start.30 = (bf16[16,3456]{1,0:T(8,128)(2,1)S(1)}, bf16[16,3456]{1,0:T(8,128)(2,1)S(1)}, u32[]{:S(2)}, u32[]{:S(2)}) collective-permute-start(bf16[16,3456]{1,0:T(8,128)(2,1)S(1)} %get-tuple-element.125.refs_0_), channel_id=1, source_target_pairs={{0,2},{2,0},{4,6},{6,4},{8,10},{10,8},{12,14},{14,12},{1,3},{3,1},... | collective-permute-start | bytes 331784 | tf_op jit(solution)/shard_map/ppermute | solution.py:56
  96.0 8.6 %collective-permute-start.29 = (bf16[16,3456]{1,0:T(8,128)(2,1)S(1)}, bf16[16,3456]{1,0:T(8,128)(2,1)S(1)}, u32[]{:S(2)}, u32[]{:S(2)}) collective-permute-start(bf16[16,3456]{1,0:T(8,128)(2,1)S(1)} %get-tuple-element.125.refs_0_), channel_id=1, source_target_pairs={{0,4},{2,6},{4,0},{6,2},{8,12},{10,14},{12,8},{14,10},{1,5},{3,7},... | collective-permute-start | bytes 331784 | tf_op jit(solution)/shard_map/ppermute | solution.py:56
  101.1 6.5 %collective-permute-start.28 = (bf16[16,3200]{1,0:T(8,128)(2,1)S(1)}, bf16[16,3200]{1,0:T(8,128)(2,1)S(1)}, u32[]{:S(2)}, u32[]{:S(2)}) collective-permute-start(bf16[16,3200]{1,0:T(8,128)(2,1)S(1)} %hidden.7.refs_0_), channel_id=1, source_target_pairs={{0,6},{2,4},{4,2},{6,0},{8,14},{10,12},{12,10},{14,8},{1,7},{3,5},... | collective-permute-start | bytes 307208 | tf_op jit(solution)/shard_map/ppermute | solution.py:56
  101.4 6.1 %collective-permute-start.27 = (bf16[16,3200]{1,0:T(8,128)(2,1)S(1)}, bf16[16,3200]{1,0:T(8,128)(2,1)S(1)}, u32[]{:S(2)}, u32[]{:S(2)}) collective-permute-start(bf16[16,3200]{1,0:T(8,128)(2,1)S(1)} %hidden.7.refs_0_), channel_id=1, source_target_pairs={{0,2},{2,0},{4,6},{6,4},{8,10},{10,8},{12,14},{14,12},{1,3},{3,1},... | collective-permute-start | bytes 307208 | tf_op jit(solution)/shard_map/ppermute | solution.py:56
  102.9 5.7 %collective-permute-start.26 = (bf16[16,3200]{1,0:T(8,128)(2,1)S(1)}, bf16[16,3200]{1,0:T(8,128)(2,1)S(1)}, u32[]{:S(2)}, u32[]{:S(2)}) collective-permute-start(bf16[16,3200]{1,0:T(8,128)(2,1)S(1)} %hidden.7.refs_0_), channel_id=1, source_target_pairs={{0,4},{2,6},{4,0},{6,2},{8,12},{10,14},{12,8},{14,10},{1,5},{3,7},... | collective-permute-start | bytes 307208 | tf_op jit(solution)/shard_map/ppermute | solution.py:56
  109.9 1.4 %collective-permute-start.32 = (bf16[64,1024]{1,0:T(8,128)(2,1)S(1)}, bf16[64,1024]{1,0:T(8,128)(2,1)S(1)}, u32[]{:S(2)}, u32[]{:S(2)}) collective-permute-start(bf16[64,1024]{1,0:T(8,128)(2,1)S(1)} %get-tuple-element.127), channel_id=1, source_target_pairs={{0,1},{1,0},{2,3},{3,2},{4,5},{5,4},{6,7},{7,6},{8,9},{9,8},{10,11... | collective-permute-start | bytes 393224 | tf_op jit(solution)/shard_map/ppermute | solution.py:56
  112.0 4.3 %collective-permute-start.33 = (bf16[32,1024]{1,0:T(8,128)(2,1)S(1)}, bf16[32,1024]{1,0:T(8,128)(2,1)S(1)}, u32[]{:S(2)}, u32[]{:S(2)}) collective-permute-start(bf16[32,1024]{1,0:T(8,128)(2,1)S(1)} %get-tuple-element.130), channel_id=1, source_target_pairs={{16,0},{0,16},{17,1},{1,17},{18,2},{2,18},{19,3},{3,19},{20,4},{4,... | collective-permute-start | bytes 196616 | tf_op jit(solution)/shard_map/ppermute | solution.py:477

commit v7 on v6

--- a/solution.py
+++ b/solution.py
@@ -282,9 +282,8 @@
     if keep.shape[-1] == width:
         return total, None
     square = keep[..., width:]
-    for ref in refs:
-        square = square + jnp.sum(ref[:, :, width:].astype(F32), axis=-1, keepdims=True)
-    return total, square
+    lanes = sum(ref[:, :, width:].astype(F32) for ref in refs)
+    return total, square + jnp.sum(lanes, axis=-1, keepdims=True)
 
 
 def add_kernel(count, width, pair, keep_ref, *refs):

time: 117 us -> 117 us (level)
  no operation moved by 1% of the time
where the time goes in v7:
time: 117 us
  starting transfers between devices  41.6 us (36%)
  waiting for transfers between devices  39.5 us (34%)
  Pallas kernels  32.2 us (28%)
  local copies, waits for them, and re-layouts  2.72 us (2%)
    ppermute x30, starting transfers between devices, swap(): return lax.ppermute(value, axis, [(i, i ^ flip) for i in range(count)])  36 us
    ppermute x30, waiting for transfers between devices, swap(): return lax.ppermute(value, axis, [(i, i ^ flip) for i in range(count)])  32.9 us
    pallas_call x3, Pallas kernels, gate_up(): pl.pallas_call(functools.partial(gate_up_kernel, first, per, size, fresh,...  11.2 us
    ppermute x4, waiting for transfers between devices, from_group(): lax.ppermute(value, 'groups', [((i + k) % groups, i) for i in range(group...  6.62 us
    pallas_call x2, Pallas kernels, load_down(): pl.pallas_call(functools.partial(load_down_kernel, first), out_shape=stru...  5.95 us
    ppermute x4, starting transfers between devices, from_group(): lax.ppermute(value, 'groups', [((i + k) % groups, i) for i in range(group...  5.56 us
    pallas_call x4, Pallas kernels, down(): pl.pallas_call(functools.partial(down_kernel, first, len(parts), added, f...  5.29 us
    pallas_call x1, Pallas kernels, load(): pl.pallas_call(functools.partial(load_kernel, first), out_shape=struct((d...  3.13 us
  transfers between devices with their start and end apart: 34, of which 19 were waited for; matrix products, arithmetic and copies ran while one was open for 0% of the time, Pallas kernels for 20%

profile of v7, /device:TPU:0, one launch (start us, length us, event | category | flops | bytes accessed | tf_op | source)
XLA Modules:
  0.0 117.0 jit_solution(7963403952761651887)
XLA Ops:
  0.0 2.9 %collective-permute-start = (bf16[32,1024]{1,0:T(8,128)(2,1)}, bf16[32,1024]{1,0:T(8,128)(2,1)S(1)}, u32[]{:S(2)}, u32[]{:S(2)}) collective-permute-start(bf16[32,1024]{1,0:T(8,128)(2,1)} %own_ref.1), channel_id=1, source_target_pairs={{16,0},{0,16},{17,1},{1,17},{18,2},{2,18},{19,3},{3,19},{20,4},{4,... | collective-permute-start | bytes 196616 | tf_op jit(solution)/shard_map/ppermute | solution.py:476
  2.9 3.1 %load.1.refs_1_ = bf16[1024,3456]{1,0:T(8,128)(2,1)S(1)} custom-call(s32[1]{0:T(128)} %bitcast.2.base_ref, bf16[1024,13312]{1,0:T(8,128)(2,1)} %refs_0_.1), custom_call_target="tpu_custom_call" | custom-call | bytes 14155776 | tf_op jit(solution)/shard_map/load/pallas_call | solution.py:144
  6.8 3.6 %gate_up.3 = (f32[2,16,3584]{2,1,0:T(8,128)S(1)}, bf16[2,16,3584]{2,1,0:T(8,128)(2,1)S(1)}, bf16[2,16,3584]{2,1,0:T(8,128)(2,1)S(1)}, bf16[2,16,3584]{2,1,0:T(8,128)(2,1)S(1)}, bf16[1024,3456]{1,0:T(8,128)(2,1)S(1)}) custom-call(s32[1]{0:T(128)} %bitcast.2.base_ref, bf16[64,1024]{1,0:T(8,128)(2,1)S(1)} %get-tuple-element.72.x_ref, ...), custom_call_target="tpu_custom_call" | custom-call | flops 905969664 | bytes 14155776 | tf_op jit(solution)/shard_map/gate_up/pallas_call | solution.py:266
  10.4 1.6 %collective-permute-start.1 = (bf16[2,16,3584]{2,1,0:T(8,128)(2,1)S(1)}, bf16[2,16,3584]{2,1,0:T(8,128)(2,1)S(1)}, u32[]{:S(2)}, u32[]{:S(2)}) collective-permute-start(bf16[2,16,3584]{2,1,0:T(8,128)(2,1)S(1)} %get-tuple-element.75), channel_id=1, source_target_pairs={{0,4},{2,6},{4,0},{6,2},{8,12},{10,14},{12,8},{14,10},{1,5},{3,7},... | collective-permute-start | bytes 688136 | tf_op jit(solution)/shard_map/ppermute | solution.py:56
  12.1 1.5 %collective-permute-start.2 = (bf16[2,16,3584]{2,1,0:T(8,128)(2,1)S(1)}, bf16[2,16,3584]{2,1,0:T(8,128)(2,1)S(1)}, u32[]{:S(2)}, u32[]{:S(2)}) collective-permute-start(bf16[2,16,3584]{2,1,0:T(8,128)(2,1)S(1)} %get-tuple-element.76), channel_id=1, source_target_pairs={{0,2},{2,0},{4,6},{6,4},{8,10},{10,8},{12,14},{14,12},{1,3},{3,1},... | collective-permute-start | bytes 688136 | tf_op jit(solution)/shard_map/ppermute | solution.py:56
  14.0 5.3 %gate_up.4 = (f32[2,16,3200]{2,1,0:T(8,128)S(1)}, bf16[2,16,3200]{2,1,0:T(8,128)(2,1)S(1)}, bf16[2,16,3200]{2,1,0:T(8,128)(2,1)S(1)}, bf16[2,16,3200]{2,1,0:T(8,...) custom-call(s32[1]{0:T(128)} %bitcast.2.base_ref, ...), custom_call_target="tpu_custom_call" | custom-call | flops 838860800 | bytes 13107200 | tf_op jit(solution)/shard_map/gate_up/pallas_call | solution.py:266
  19.3 2.7 %copy-done = bf16[1024,3200]{1,0:T(8,128)(2,1)} copy-done((bf16[1024,3200]{1,0:T(8,128)(2,1)}, bf16[1024,3200]{1,0:T(8,128)(2,1)S(1)}, u32[]{:S(2)}) %copy-start) | copy-done | bytes 6553624
  22.0 1.6 %collective-permute-start.4 = (bf16[2,16,3200]{2,1,0:T(8,128)(2,1)S(1)}, bf16[2,16,3200]{2,1,0:T(8,128)(2,1)S(1)}, u32[]{:S(2)}, u32[]{:S(2)}) collective-permute-start(bf16[2,16,3200]{2,1,0:T(8,128)(2,1)S(1)} %get-tuple-element.80), channel_id=1, source_target_pairs={{0,4},{2,6},{4,0},{6,2},{8,12},{10,14},{12,8},{14,10},{1,5},{3,7},... | collective-permute-start | bytes 614408 | tf_op jit(solution)/shard_map/ppermute | solution.py:56
  23.6 1.5 %collective-permute-start.5 = (bf16[2,16,3200]{2,1,0:T(8,128)(2,1)S(1)}, bf16[2,16,3200]{2,1,0:T(8,128)(2,1)S(1)}, u32[]{:S(2)}, u32[]{:S(2)}) collective-permute-start(bf16[2,16,3200]{2,1,0:T(8,128)(2,1)S(1)} %get-tuple-element.81), channel_id=1, source_target_pairs={{0,2},{2,0},{4,6},{6,4},{8,10},{10,8},{12,14},{14,12},{1,3},{3,1},... | collective-permute-start | bytes 614408 | tf_op jit(solution)/shard_map/ppermute | solution.py:56
  26.1 2.7 %collective-permute-start.8 = (bf16[2,16,3584]{2,1,0:T(8,128)(2,1)S(1)}, bf16[2,16,3584]{2,1,0:T(8,128)(2,1)S(1)}, u32[]{:S(2)}, u32[]{:S(2)}) collective-permute-start(bf16[2,16,3584]{2,1,0:T(8,128)(2,1)S(1)} %get-tuple-element.87), channel_id=1, source_target_pairs={{0,8},{2,10},{4,12},{6,14},{8,0},{10,2},{12,4},{14,6},{1,9},{3,11}... | collective-permute-start | bytes 688136 | tf_op jit(solution)/shard_map/ppermute | solution.py:56
  28.7 3.1 %load_down.2.refs_4_ = bf16[3456,1024]{1,0:T(8,128)(2,1)S(1)} custom-call(s32[1]{0:T(128)} %bitcast.2.base_ref, bf16[13312,1024]{1,0:T(8,128)(2,1)} %down_hbm.3, f32[2,16,3584]{2,1,0:T(8,128)S(1)} %get-tuple-element.86.after_ref.keep_ref), custom_call_target="tpu_custom_call" | custom-call | bytes 7077888 | tf_op jit(solution)/shard_map/load_down/pallas_call | solution.py:377
  31.8 2.9 %collective-permute-done.4.refs_0_ = bf16[2,16,3200]{2,1,0:T(8,128)(2,1)S(1)} collective-permute-done((bf16[2,16,3200]{2,1,0:T(8,128)(2,1)S(1)}, bf16[2,16,3200]{2,1,0:T(8,128)(2,1)S(1)}, u32[]{:S(2)}, u32[]{:S(2)}) %collective-permute-start.4) | collective-permute-done | bytes 204832 | tf_op jit(solution)/shard_map/ppermute | solution.py:56
  34.7 3.4 %collective-permute-done.6.refs_2_ = bf16[2,16,3200]{2,1,0:T(8,128)(2,1)S(1)} collective-permute-done((bf16[2,16,3200]{2,1,0:T(8,128)(2,1)S(1)}, bf16[2,16,3200]{2,1,0:T(8,128)(2,1)S(1)}, u32[]{:S(2)}, u32[]{:S(2)}) %collective-permute-start.6) | collective-permute-done | bytes 204832 | tf_op jit(solution)/shard_map/ppermute | solution.py:56
  38.8 3.4 %collective-permute-start.14 = (bf16[16,3456]{1,0:T(8,128)(2,1)S(1)}, bf16[16,3456]{1,0:T(8,128)(2,1)S(1)}, u32[]{:S(2)}, u32[]{:S(2)}) collective-permute-start(bf16[16,3456]{1,0:T(8,128)(2,1)S(1)} %get-tuple-element.90.refs_0_), channel_id=1, source_target_pairs={{0,6},{2,4},{4,2},{6,0},{8,14},{10,12},{12,10},{14,8},{1,7},{3,5},... | collective-permute-start | bytes 331784 | tf_op jit(solution)/shard_map/ppermute | solution.py:56
  42.3 1.5 %collective-permute-start.13 = (bf16[16,3456]{1,0:T(8,128)(2,1)S(1)}, bf16[16,3456]{1,0:T(8,128)(2,1)S(1)}, u32[]{:S(2)}, u32[]{:S(2)}) collective-permute-start(bf16[16,3456]{1,0:T(8,128)(2,1)S(1)} %get-tuple-element.90.refs_0_), channel_id=1, source_target_pairs={{0,2},{2,0},{4,6},{6,4},{8,10},{10,8},{12,14},{14,12},{1,3},{3,1},... | collective-permute-start | bytes 331784 | tf_op jit(solution)/shard_map/ppermute | solution.py:56
  43.8 2.9 %load_down.3.refs_4_ = bf16[3200,1024]{1,0:T(8,128)(2,1)S(1)} custom-call(s32[1]{0:T(128)} %bitcast.2.base_ref, bf16[13312,1024]{1,0:T(8,128)(2,1)} %down_hbm.3, f32[2,16,3200]{2,1,0:T(8,128)S(1)} %get-tuple-element.84.after_ref.keep_ref), custom_call_target="tpu_custom_call" | custom-call | bytes 6553600 | tf_op jit(solution)/shard_map/load_down/pallas_call | solution.py:377
  46.7 2.0 %collective-permute-done.7.refs_0_ = bf16[2,16,3200]{2,1,0:T(8,128)(2,1)S(1)} collective-permute-done((bf16[2,16,3200]{2,1,0:T(8,128)(2,1)S(1)}, bf16[2,16,3200]{2,1,0:T(8,128)(2,1)S(1)}, u32[]{:S(2)}, u32[]{:S(2)}) %collective-permute-start.7) | collective-permute-done | bytes 204832 | tf_op jit(solution)/shard_map/ppermute | solution.py:56
  48.9 1.5 %collective-permute-start.10 = (bf16[16,3200]{1,0:T(8,128)(2,1)S(1)}, bf16[16,3200]{1,0:T(8,128)(2,1)S(1)}, u32[]{:S(2)}, u32[]{:S(2)}) collective-permute-start(bf16[16,3200]{1,0:T(8,128)(2,1)S(1)} %hidden.5.refs_0_), channel_id=1, source_target_pairs={{0,2},{2,0},{4,6},{6,4},{8,10},{10,8},{12,14},{14,12},{1,3},{3,1},... | collective-permute-start | bytes 307208 | tf_op jit(solution)/shard_map/ppermute | solution.py:56
  50.4 2.0 %collective-permute-start.9 = (bf16[16,3200]{1,0:T(8,128)(2,1)S(1)}, bf16[16,3200]{1,0:T(8,128)(2,1)S(1)}, u32[]{:S(2)}, u32[]{:S(2)}) collective-permute-start(bf16[16,3200]{1,0:T(8,128)(2,1)S(1)} %hidden.5.refs_0_), channel_id=1, source_target_pairs={{0,4},{2,6},{4,0},{6,2},{8,12},{10,14},{12,8},{14,10},{1,5},{3,7},... | collective-permute-start | bytes 307208 | tf_op jit(solution)/shard_map/ppermute | solution.py:56
  52.4 1.4 %down.4.refs_5_ = f32[64,1024]{1,0:T(8,128)S(1)} custom-call(s32[1]{0:T(128)} %bitcast.2.base_ref, bf16[16,3456]{1,0:T(8,128)(2,1)S(1)} %get-tuple-element.90.refs_0_, bf16[16,3456]{1,0:T(8,128)(2,1)S(1)} %collective-permute-done.12.refs_1_, bf16[16,3456]{1,0:T(8,128)(2,1)S(1)} %collective-permute-done.13.refs_2_, ...), custom_call_target="tpu_custom_call" | custom-call | flops 452984832 | bytes 7077888 | tf_op jit(solution)/shard_map/down/pallas_call | solution.py:418
  53.8 1.1 collective-permute-done.11.refs_3_
  55.7 1.3 %down.5 = (f32[64,1024]{1,0:T(8,128)S(1)}, bf16[64,1024]{1,0:T(8,128)(2,1)S(1)}) custom-call(s32[1]{0:T(128)} %bitcast.2.base_ref, bf16[16,3200]{1,0:T(8,128)(2,1)S(1)} %hidden.5.refs_0_, bf16[16,3200]{1,0:T(8,128)(2,1)S(1)} %collective-permute-done.9.refs_1_, bf16[16,3200]{1,0:T(8,128)(2,1)S(1)} %collective-permute-done.10.refs_2_, ...), custom_call_target="tpu_custom_call" | custom-call | flops 419430400 | bytes 6553600 | tf_op jit(solution)/shard_map/down/pallas_call | solution.py:418
  57.1 1.3 %collective-permute-done.15.b_ref = bf16[64,1024]{1,0:T(8,128)(2,1)S(1)} collective-permute-done((bf16[64,1024]{1,0:T(8,128)(2,1)S(1)}, bf16[64,1024]{1,0:T(8,128)(2,1)S(1)}, u32[]{:S(2)}, u32[]{:S(2)}) %collective-permute-start.15) | collective-permute-done | bytes 131104 | tf_op jit(solution)/shard_map/ppermute | solution.py:56
  59.4 1.2 %collective-permute-start.16 = (bf16[64,512]{1,0:T(8,128)(2,1)S(1)}, bf16[64,512]{1,0:T(8,128)(2,1)S(1)}, u32[]{:S(2)}, u32[]{:S(2)}) collective-permute-start(bf16[64,512]{1,0:T(8,128)(2,1)S(1)} %get-tuple-element.95), channel_id=1, source_target_pairs={{16,0},{0,16},{17,1},{1,17},{18,2},{2,18},{19,3},{3,19},{20,4},{4,... | collective-permute-start | bytes 196616 | tf_op jit(solution)/shard_map/ppermute | solution.py:476
  60.6 2.8 %collective-permute-done.17.refs_0_ = bf16[64,512]{1,0:T(8,128)(2,1)S(1)} collective-permute-done((bf16[64,512]{1,0:T(8,128)(2,1)S(1)}, bf16[64,512]{1,0:T(8,128)(2,1)S(1)}, u32[]{:S(2)}, u32[]{:S(2)}) %collective-permute-start.17) | collective-permute-done | bytes 65568 | tf_op jit(solution)/shard_map/ppermute | solution.py:476
  63.4 1.3 %begin.1 = (f32[64,512]{1,0:T(8,128)S(1)}, bf16[64,512]{1,0:T(8,128)(2,1)S(1)}, f32[64,128]{1,0:T(8,128)S(1)}, f32[64,3456]{1,0:T(8,128)S(1)}, f32[64,3456]{1,0:T(8,128)S(1)}) custom-call(f32[64,512]{1,0:T(8,128)S(1)} %get-tuple-element.97.state_ref, bf16[64,512]{1,0:T(8,128)(2,1)S(1)} %collective-permute-done.17.refs_0_, ...), custom_call_target="tpu_custom_call" | custom-call | flops 452984832 | bytes 7077888 | tf_op jit(solution)/shard_map/begin/pallas_call | solution.py:239
  64.7 1.4 %end.1 = (f32[2,16,3584]{2,1,0:T(8,128)S(1)}, bf16[2,16,3584]{2,1,0:T(8,128)(2,1)S(1)}, bf16[2,16,3584]{2,1,0:T(8,128)(2,1)S(1)}, bf16[2,16,3584]{2,1,0:T(8,128)...) custom-call(f32[64,512]{1,0:T(8,128)S(1)} %get-tuple-element.94.state_ref, ...), custom_call_target="tpu_custom_call" | custom-call | flops 452984832 | bytes 7077888 | tf_op jit(solution)/shard_map/end/pallas_call | solution.py:248
  66.1 1.4 %collective-permute-start.22 = (bf16[2,16,3584]{2,1,0:T(8,128)(2,1)S(1)}, bf16[2,16,3584]{2,1,0:T(8,128)(2,1)S(1)}, u32[]{:S(2)}, u32[]{:S(2)}) collective-permute-start(bf16[2,16,3584]{2,1,0:T(8,128)(2,1)S(1)} %get-tuple-element.117), channel_id=1, source_target_pairs={{0,4},{2,6},{4,0},{6,2},{8,12},{10,14},{12,8},{14,10},{1,5},{3,7},... | collective-permute-start | bytes 688136 | tf_op jit(solution)/shard_map/ppermute | solution.py:56
  68.4 1.3 %collective-permute-start.24 = (bf16[2,16,3584]{2,1,0:T(8,128)(2,1)S(1)}, bf16[2,16,3584]{2,1,0:T(8,128)(2,1)S(1)}, u32[]{:S(2)}, u32[]{:S(2)}) collective-permute-start(bf16[2,16,3584]{2,1,0:T(8,128)(2,1)S(1)} %get-tuple-element.119), channel_id=1, source_target_pairs={{0,6},{2,4},{4,2},{6,0},{8,14},{10,12},{12,10},{14,8},{1,7},{3,5},... | collective-permute-start | bytes 688136 | tf_op jit(solution)/shard_map/ppermute | solution.py:56
  69.7 2.3 %gate_up.5 = (f32[2,16,3200]{2,1,0:T(8,128)S(1)}, bf16[2,16,3200]{2,1,0:T(8,128)(2,1)S(1)}, bf16[2,16,3200]{2,1,0:T(8,128)(2,1)S(1)}, bf16[2,16,3200]{2,1,0:T(8,128)(2,1)S(1)}) custom-call(s32[1]{0:T(128)} %bitcast.2.base_ref, bf16[64,1024]{1,0:T(8,128)(2,1)S(1)} %get-tuple-element.106.x_ref, bf16[1024,3200]{1,0:T(8,128)(2,1)S(1)} %get-tuple-element.107.refs_0_, ...), custom_call_target="tpu_custom_call" | custom-call | flops 838860800 | bytes 13107200 | tf_op jit(solution)/shard_map/gate_up/pallas_call | solution.py:266
  72.0 1.4 %collective-permute-start.18 = (bf16[2,16,3200]{2,1,0:T(8,128)(2,1)S(1)}, bf16[2,16,3200]{2,1,0:T(8,128)(2,1)S(1)}, u32[]{:S(2)}, u32[]{:S(2)}) collective-permute-start(bf16[2,16,3200]{2,1,0:T(8,128)(2,1)S(1)} %get-tuple-element.110), channel_id=1, source_target_pairs={{0,4},{2,6},{4,0},{6,2},{8,12},{10,14},{12,8},{14,10},{1,5},{3,7},... | collective-permute-start | bytes 614408 | tf_op jit(solution)/shard_map/ppermute | solution.py:56
  74.7 1.7 %collective-permute-start.20 = (bf16[2,16,3200]{2,1,0:T(8,128)(2,1)S(1)}, bf16[2,16,3200]{2,1,0:T(8,128)(2,1)S(1)}, u32[]{:S(2)}, u32[]{:S(2)}) collective-permute-start(bf16[2,16,3200]{2,1,0:T(8,128)(2,1)S(1)} %get-tuple-element.112), channel_id=1, source_target_pairs={{0,6},{2,4},{4,2},{6,0},{8,14},{10,12},{12,10},{14,8},{1,7},{3,5},... | collective-permute-start | bytes 614408 | tf_op jit(solution)/shard_map/ppermute | solution.py:56
  76.4 2.9 %collective-permute-done.23.refs_1_ = bf16[2,16,3584]{2,1,0:T(8,128)(2,1)S(1)} collective-permute-done((bf16[2,16,3584]{2,1,0:T(8,128)(2,1)S(1)}, bf16[2,16,3584]{2,1,0:T(8,128)(2,1)S(1)}, u32[]{:S(2)}, u32[]{:S(2)}) %collective-permute-start.23) | collective-permute-done | bytes 229408 | tf_op jit(solution)/shard_map/ppermute | solution.py:56
  80.3 2.8 %collective-permute-start.25 = (bf16[2,16,3584]{2,1,0:T(8,128)(2,1)S(1)}, bf16[2,16,3584]{2,1,0:T(8,128)(2,1)S(1)}, u32[]{:S(2)}, u32[]{:S(2)}) collective-permute-start(bf16[2,16,3584]{2,1,0:T(8,128)(2,1)S(1)} %get-tuple-element.122), channel_id=1, source_target_pairs={{0,8},{2,10},{4,12},{6,14},{8,0},{10,2},{12,4},{14,6},{1,9},{3,11}... | collective-permute-start | bytes 688136 | tf_op jit(solution)/shard_map/ppermute | solution.py:56
  83.1 4.7 %collective-permute-done.18.refs_0_ = bf16[2,16,3200]{2,1,0:T(8,128)(2,1)S(1)} collective-permute-done((bf16[2,16,3200]{2,1,0:T(8,128)(2,1)S(1)}, bf16[2,16,3200]{2,1,0:T(8,128)(2,1)S(1)}, u32[]{:S(2)}, u32[]{:S(2)}) %collective-permute-start.18) | collective-permute-done | bytes 204832 | tf_op jit(solution)/shard_map/ppermute | solution.py:56
  87.8 3.7 %collective-permute-done.20.refs_2_ = bf16[2,16,3200]{2,1,0:T(8,128)(2,1)S(1)} collective-permute-done((bf16[2,16,3200]{2,1,0:T(8,128)(2,1)S(1)}, bf16[2,16,3200]{2,1,0:T(8,128)(2,1)S(1)}, u32[]{:S(2)}, u32[]{:S(2)}) %collective-permute-start.20) | collective-permute-done | bytes 204832 | tf_op jit(solution)/shard_map/ppermute | solution.py:56
  91.8 2.5 %collective-permute-done.25.refs_0_ = bf16[2,16,3584]{2,1,0:T(8,128)(2,1)S(1)} collective-permute-done((bf16[2,16,3584]{2,1,0:T(8,128)(2,1)S(1)}, bf16[2,16,3584]{2,1,0:T(8,128)(2,1)S(1)}, u32[]{:S(2)}, u32[]{:S(2)}) %collective-permute-start.25) | collective-permute-done | bytes 229408 | tf_op jit(solution)/shard_map/ppermute | solution.py:56
  94.6 1.3 %collective-permute-start.31 = (bf16[16,3456]{1,0:T(8,128)(2,1)S(1)}, bf16[16,3456]{1,0:T(8,128)(2,1)S(1)}, u32[]{:S(2)}, u32[]{:S(2)}) collective-permute-start(bf16[16,3456]{1,0:T(8,128)(2,1)S(1)} %get-tuple-element.125.refs_0_), channel_id=1, source_target_pairs={{0,6},{2,4},{4,2},{6,0},{8,14},{10,12},{12,10},{14,8},{1,7},{3,5},... | collective-permute-start | bytes 331784 | tf_op jit(solution)/shard_map/ppermute | solution.py:56
  96.0 2.2 %collective-permute-start.29 = (bf16[16,3456]{1,0:T(8,128)(2,1)S(1)}, bf16[16,3456]{1,0:T(8,128)(2,1)S(1)}, u32[]{:S(2)}, u32[]{:S(2)}) collective-permute-start(bf16[16,3456]{1,0:T(8,128)(2,1)S(1)} %get-tuple-element.125.refs_0_), channel_id=1, source_target_pairs={{0,4},{2,6},{4,0},{6,2},{8,12},{10,14},{12,8},{14,10},{1,5},{3,7},... | collective-permute-start | bytes 331784 | tf_op jit(solution)/shard_map/ppermute | solution.py:56
  98.2 2.7 %collective-permute-done.21.refs_0_ = bf16[2,16,3200]{2,1,0:T(8,128)(2,1)S(1)} collective-permute-done((bf16[2,16,3200]{2,1,0:T(8,128)(2,1)S(1)}, bf16[2,16,3200]{2,1,0:T(8,128)(2,1)S(1)}, u32[]{:S(2)}, u32[]{:S(2)}) %collective-permute-start.21) | collective-permute-done | bytes 204832 | tf_op jit(solution)/shard_map/ppermute | solution.py:56
  101.4 1.5 %collective-permute-start.27 = (bf16[16,3200]{1,0:T(8,128)(2,1)S(1)}, bf16[16,3200]{1,0:T(8,128)(2,1)S(1)}, u32[]{:S(2)}, u32[]{:S(2)}) collective-permute-start(bf16[16,3200]{1,0:T(8,128)(2,1)S(1)} %hidden.7.refs_0_), channel_id=1, source_target_pairs={{0,2},{2,0},{4,6},{6,4},{8,10},{10,8},{12,14},{14,12},{1,3},{3,1},... | collective-permute-start | bytes 307208 | tf_op jit(solution)/shard_map/ppermute | solution.py:56
  102.9 1.8 %collective-permute-start.26 = (bf16[16,3200]{1,0:T(8,128)(2,1)S(1)}, bf16[16,3200]{1,0:T(8,128)(2,1)S(1)}, u32[]{:S(2)}, u32[]{:S(2)}) collective-permute-start(bf16[16,3200]{1,0:T(8,128)(2,1)S(1)} %hidden.7.refs_0_), channel_id=1, source_target_pairs={{0,4},{2,6},{4,0},{6,2},{8,12},{10,14},{12,8},{14,10},{1,5},{3,7},... | collective-permute-start | bytes 307208 | tf_op jit(solution)/shard_map/ppermute | solution.py:56
  104.7 1.4 %down.6.refs_5_ = f32[64,1024]{1,0:T(8,128)S(1)} custom-call(s32[1]{0:T(128)} %bitcast.2.base_ref, bf16[16,3456]{1,0:T(8,128)(2,1)S(1)} %get-tuple-element.125.refs_0_, bf16[16,3456]{1,0:T(8,128)(2,1)S(1)} %collective-permute-done.29.refs_1_, bf16[16,3456]{1,0:T(8,128)(2,1)S(1)} %collective-permute-done.30.refs_2_, ...), custom_call_target="tpu_custom_call" | custom-call | flops 452984832 | bytes 7077888 | tf_op jit(solution)/shard_map/down/pallas_call | solution.py:418
  106.0 1.5 %collective-permute-done.28.refs_3_ = bf16[16,3200]{1,0:T(8,128)(2,1)S(1)} collective-permute-done((bf16[16,3200]{1,0:T(8,128)(2,1)S(1)}, bf16[16,3200]{1,0:T(8,128)(2,1)S(1)}, u32[]{:S(2)}, u32[]{:S(2)}) %collective-permute-start.28) | collective-permute-done | bytes 102432 | tf_op jit(solution)/shard_map/ppermute | solution.py:56
  107.5 1.0 collective-permute-done.26.refs_1_
  108.6 1.3 %down.7 = (f32[64,1024]{1,0:T(8,128)S(1)}, bf16[64,1024]{1,0:T(8,128)(2,1)S(1)}) custom-call(s32[1]{0:T(128)} %bitcast.2.base_ref, bf16[16,3200]{1,0:T(8,128)(2,1)S(1)} %hidden.7.refs_0_, bf16[16,3200]{1,0:T(8,128)(2,1)S(1)} %collective-permute-done.26.refs_1_, bf16[16,3200]{1,0:T(8,128)(2,1)S(1)} %collective-permute-done.27.refs_2_, ...), custom_call_target="tpu_custom_call" | custom-call | flops 419430400 | bytes 6553600 | tf_op jit(solution)/shard_map/down/pallas_call | solution.py:418
  110.0 1.3 %collective-permute-done.32.b_ref = bf16[64,1024]{1,0:T(8,128)(2,1)S(1)} collective-permute-done((bf16[64,1024]{1,0:T(8,128)(2,1)S(1)}, bf16[64,1024]{1,0:T(8,128)(2,1)S(1)}, u32[]{:S(2)}, u32[]{:S(2)}) %collective-permute-start.32) | collective-permute-done | bytes 131104 | tf_op jit(solution)/shard_map/ppermute | solution.py:56
  112.5 3.8 %collective-permute-done.33 = bf16[32,1024]{1,0:T(8,128)(2,1)S(1)} collective-permute-done((bf16[32,1024]{1,0:T(8,128)(2,1)S(1)}, bf16[32,1024]{1,0:T(8,128)(2,1)S(1)}, u32[]{:S(2)}, u32[]{:S(2)}) %collective-permute-start.33) | collective-permute-done | bytes 65568 | tf_op jit(solution)/shard_map/ppermute | solution.py:476
  (54 shorter events, 11.3 us)
Async XLA Ops:
  0.0 6.2 %collective-permute-start = (bf16[32,1024]{1,0:T(8,128)(2,1)}, bf16[32,1024]{1,0:T(8,128)(2,1)S(1)}, u32[]{:S(2)}, u32[]{:S(2)}) collective-permute-start(bf16[32,1024]{1,0:T(8,128)(2,1)} %own_ref.1), channel_id=1, source_target_pairs={{16,0},{0,16},{17,1},{1,17},{18,2},{2,18},{19,3},{3,19},{20,4},{4,... | collective-permute-start | bytes 196616 | tf_op jit(solution)/shard_map/ppermute | solution.py:476
  2.9 3.2 %copy-start.1 = (bf16[32,1024]{1,0:T(8,128)(2,1)S(1)}, bf16[32,1024]{1,0:T(8,128)(2,1)}, u32[]{:S(2)}) copy-start(bf16[32,1024]{1,0:T(8,128)(2,1)} %own_ref.1) | copy-start | bytes 196612
  10.4 14.7 %collective-permute-start.1 = (bf16[2,16,3584]{2,1,0:T(8,128)(2,1)S(1)}, bf16[2,16,3584]{2,1,0:T(8,128)(2,1)S(1)}, u32[]{:S(2)}, u32[]{:S(2)}) collective-permute-start(bf16[2,16,3584]{2,1,0:T(8,128)(2,1)S(1)} %get-tuple-element.75), channel_id=1, source_target_pairs={{0,4},{2,6},{4,0},{6,2},{8,12},{10,14},{12,8},{14,10},{1,5},{3,7},... | collective-permute-start | bytes 688136 | tf_op jit(solution)/shard_map/ppermute | solution.py:56
  12.1 13.5 %collective-permute-start.2 = (bf16[2,16,3584]{2,1,0:T(8,128)(2,1)S(1)}, bf16[2,16,3584]{2,1,0:T(8,128)(2,1)S(1)}, u32[]{:S(2)}, u32[]{:S(2)}) collective-permute-start(bf16[2,16,3584]{2,1,0:T(8,128)(2,1)S(1)} %get-tuple-element.76), channel_id=1, source_target_pairs={{0,2},{2,0},{4,6},{6,4},{8,10},{10,8},{12,14},{14,12},{1,3},{3,1},... | collective-permute-start | bytes 688136 | tf_op jit(solution)/shard_map/ppermute | solution.py:56
  13.6 11.9 %collective-permute-start.3 = (bf16[2,16,3584]{2,1,0:T(8,128)(2,1)S(1)}, bf16[2,16,3584]{2,1,0:T(8,128)(2,1)S(1)}, u32[]{:S(2)}, u32[]{:S(2)}) collective-permute-start(bf16[2,16,3584]{2,1,0:T(8,128)(2,1)S(1)} %get-tuple-element.77), channel_id=1, source_target_pairs={{0,6},{2,4},{4,2},{6,0},{8,14},{10,12},{12,10},{14,8},{1,7},{3,5},... | collective-permute-start | bytes 688136 | tf_op jit(solution)/shard_map/ppermute | solution.py:56
  19.3 2.7 %copy-start = (bf16[1024,3200]{1,0:T(8,128)(2,1)}, bf16[1024,3200]{1,0:T(8,128)(2,1)S(1)}, u32[]{:S(2)}) copy-start(bf16[1024,3200]{1,0:T(8,128)(2,1)S(1)} %get-tuple-element.108.refs_1_) | copy-start | bytes 19660804
  22.0 12.6 %collective-permute-start.4 = (bf16[2,16,3200]{2,1,0:T(8,128)(2,1)S(1)}, bf16[2,16,3200]{2,1,0:T(8,128)(2,1)S(1)}, u32[]{:S(2)}, u32[]{:S(2)}) collective-permute-start(bf16[2,16,3200]{2,1,0:T(8,128)(2,1)S(1)} %get-tuple-element.80), channel_id=1, source_target_pairs={{0,4},{2,6},{4,0},{6,2},{8,12},{10,14},{12,8},{14,10},{1,5},{3,7},... | collective-permute-start | bytes 614408 | tf_op jit(solution)/shard_map/ppermute | solution.py:56
  23.6 11.1 %collective-permute-start.5 = (bf16[2,16,3200]{2,1,0:T(8,128)(2,1)S(1)}, bf16[2,16,3200]{2,1,0:T(8,128)(2,1)S(1)}, u32[]{:S(2)}, u32[]{:S(2)}) collective-permute-start(bf16[2,16,3200]{2,1,0:T(8,128)(2,1)S(1)} %get-tuple-element.81), channel_id=1, source_target_pairs={{0,2},{2,0},{4,6},{6,4},{8,10},{10,8},{12,14},{14,12},{1,3},{3,1},... | collective-permute-start | bytes 614408 | tf_op jit(solution)/shard_map/ppermute | solution.py:56
  25.1 12.9 %collective-permute-start.6 = (bf16[2,16,3200]{2,1,0:T(8,128)(2,1)S(1)}, bf16[2,16,3200]{2,1,0:T(8,128)(2,1)S(1)}, u32[]{:S(2)}, u32[]{:S(2)}) collective-permute-start(bf16[2,16,3200]{2,1,0:T(8,128)(2,1)S(1)} %get-tuple-element.82), channel_id=1, source_target_pairs={{0,6},{2,4},{4,2},{6,0},{8,14},{10,12},{12,10},{14,8},{1,7},{3,5},... | collective-permute-start | bytes 614408 | tf_op jit(solution)/shard_map/ppermute | solution.py:56
  26.1 12.5 %collective-permute-start.8 = (bf16[2,16,3584]{2,1,0:T(8,128)(2,1)S(1)}, bf16[2,16,3584]{2,1,0:T(8,128)(2,1)S(1)}, u32[]{:S(2)}, u32[]{:S(2)}) collective-permute-start(bf16[2,16,3584]{2,1,0:T(8,128)(2,1)S(1)} %get-tuple-element.87), channel_id=1, source_target_pairs={{0,8},{2,10},{4,12},{6,14},{8,0},{10,2},{12,4},{14,6},{1,9},{3,11}... | collective-permute-start | bytes 688136 | tf_op jit(solution)/shard_map/ppermute | solution.py:56
  38.3 10.3 %collective-permute-start.7 = (bf16[2,16,3200]{2,1,0:T(8,128)(2,1)S(1)}, bf16[2,16,3200]{2,1,0:T(8,128)(2,1)S(1)}, u32[]{:S(2)}, u32[]{:S(2)}) collective-permute-start(bf16[2,16,3200]{2,1,0:T(8,128)(2,1)S(1)} %get-tuple-element.85), channel_id=1, source_target_pairs={{0,8},{2,10},{4,12},{6,14},{8,0},{10,2},{12,4},{14,6},{1,9},{3,11}... | collective-permute-start | bytes 614408 | tf_op jit(solution)/shard_map/ppermute | solution.py:56
  38.8 11.6 %collective-permute-start.14 = (bf16[16,3456]{1,0:T(8,128)(2,1)S(1)}, bf16[16,3456]{1,0:T(8,128)(2,1)S(1)}, u32[]{:S(2)}, u32[]{:S(2)}) collective-permute-start(bf16[16,3456]{1,0:T(8,128)(2,1)S(1)} %get-tuple-element.90.refs_0_), channel_id=1, source_target_pairs={{0,6},{2,4},{4,2},{6,0},{8,14},{10,12},{12,10},{14,8},{1,7},{3,5},... | collective-permute-start | bytes 331784 | tf_op jit(solution)/shard_map/ppermute | solution.py:56
  42.3 10.1 %collective-permute-start.13 = (bf16[16,3456]{1,0:T(8,128)(2,1)S(1)}, bf16[16,3456]{1,0:T(8,128)(2,1)S(1)}, u32[]{:S(2)}, u32[]{:S(2)}) collective-permute-start(bf16[16,3456]{1,0:T(8,128)(2,1)S(1)} %get-tuple-element.90.refs_0_), channel_id=1, source_target_pairs={{0,2},{2,0},{4,6},{6,4},{8,10},{10,8},{12,14},{14,12},{1,3},{3,1},... | collective-permute-start | bytes 331784 | tf_op jit(solution)/shard_map/ppermute | solution.py:56
  43.8 8.6 %collective-permute-start.12 = (bf16[16,3456]{1,0:T(8,128)(2,1)S(1)}, bf16[16,3456]{1,0:T(8,128)(2,1)S(1)}, u32[]{:S(2)}, u32[]{:S(2)}) collective-permute-start(bf16[16,3456]{1,0:T(8,128)(2,1)S(1)} %get-tuple-element.90.refs_0_), channel_id=1, source_target_pairs={{0,4},{2,6},{4,0},{6,2},{8,12},{10,14},{12,8},{14,10},{1,5},{3,7},... | collective-permute-start | bytes 331784 | tf_op jit(solution)/shard_map/ppermute | solution.py:56
  48.8 6.0 %collective-permute-start.11 = (bf16[16,3200]{1,0:T(8,128)(2,1)S(1)}, bf16[16,3200]{1,0:T(8,128)(2,1)S(1)}, u32[]{:S(2)}, u32[]{:S(2)}) collective-permute-start(bf16[16,3200]{1,0:T(8,128)(2,1)S(1)} %hidden.5.refs_0_), channel_id=1, source_target_pairs={{0,6},{2,4},{4,2},{6,0},{8,14},{10,12},{12,10},{14,8},{1,7},{3,5},... | collective-permute-start | bytes 307208 | tf_op jit(solution)/shard_map/ppermute | solution.py:56
  48.9 6.1 %collective-permute-start.10 = (bf16[16,3200]{1,0:T(8,128)(2,1)S(1)}, bf16[16,3200]{1,0:T(8,128)(2,1)S(1)}, u32[]{:S(2)}, u32[]{:S(2)}) collective-permute-start(bf16[16,3200]{1,0:T(8,128)(2,1)S(1)} %hidden.5.refs_0_), channel_id=1, source_target_pairs={{0,2},{2,0},{4,6},{6,4},{8,10},{10,8},{12,14},{14,12},{1,3},{3,1},... | collective-permute-start | bytes 307208 | tf_op jit(solution)/shard_map/ppermute | solution.py:56
  50.4 5.3 %collective-permute-start.9 = (bf16[16,3200]{1,0:T(8,128)(2,1)S(1)}, bf16[16,3200]{1,0:T(8,128)(2,1)S(1)}, u32[]{:S(2)}, u32[]{:S(2)}) collective-permute-start(bf16[16,3200]{1,0:T(8,128)(2,1)S(1)} %hidden.5.refs_0_), channel_id=1, source_target_pairs={{0,4},{2,6},{4,0},{6,2},{8,12},{10,14},{12,8},{14,10},{1,5},{3,7},... | collective-permute-start | bytes 307208 | tf_op jit(solution)/shard_map/ppermute | solution.py:56
  57.0 1.4 %collective-permute-start.15 = (bf16[64,1024]{1,0:T(8,128)(2,1)S(1)}, bf16[64,1024]{1,0:T(8,128)(2,1)S(1)}, u32[]{:S(2)}, u32[]{:S(2)}) collective-permute-start(bf16[64,1024]{1,0:T(8,128)(2,1)S(1)} %get-tuple-element.92), channel_id=1, source_target_pairs={{0,1},{1,0},{2,3},{3,2},{4,5},{5,4},{6,7},{7,6},{8,9},{9,8},{10,11... | collective-permute-start | bytes 393224 | tf_op jit(solution)/shard_map/ppermute | solution.py:56
  58.5 4.9 %collective-permute-start.17 = (bf16[64,512]{1,0:T(8,128)(2,1)S(1)}, bf16[64,512]{1,0:T(8,128)(2,1)S(1)}, u32[]{:S(2)}, u32[]{:S(2)}) collective-permute-start(bf16[64,512]{1,0:T(8,128)(2,1)S(1)} %get-tuple-element.98), channel_id=1, source_target_pairs={{16,0},{0,16},{17,1},{1,17},{18,2},{2,18},{19,3},{3,19},{20,4},{4,... | collective-permute-start | bytes 196616 | tf_op jit(solution)/shard_map/ppermute | solution.py:476
  59.4 5.4 %collective-permute-start.16 = (bf16[64,512]{1,0:T(8,128)(2,1)S(1)}, bf16[64,512]{1,0:T(8,128)(2,1)S(1)}, u32[]{:S(2)}, u32[]{:S(2)}) collective-permute-start(bf16[64,512]{1,0:T(8,128)(2,1)S(1)} %get-tuple-element.95), channel_id=1, source_target_pairs={{16,0},{0,16},{17,1},{1,17},{18,2},{2,18},{19,3},{3,19},{20,4},{4,... | collective-permute-start | bytes 196616 | tf_op jit(solution)/shard_map/ppermute | solution.py:476
  63.4 6.3 %slice-start = ((s8[6553600]{0:T(1024)(128)(4,1)}), s8[4194304]{0:T(1024)(128)(4,1)S(1)}, s32[]{:S(2)}) async-start(s8[6553600]{0:T(1024)(128)(4,1)} %bitcast.3), calls=%async_computation | async-start | bytes 8388608
  64.7 4.9 %slice-start.1 = ((s8[6553600]{0:T(1024)(128)(4,1)}), s8[2359296]{0:T(1024)(128)(4,1)S(1)}, s32[]{:S(2)}) async-start(s8[6553600]{0:T(1024)(128)(4,1)} %bitcast.3), calls=%async_computation.1 | async-start | bytes 4718592
  66.1 8.6 %collective-permute-start.22 = (bf16[2,16,3584]{2,1,0:T(8,128)(2,1)S(1)}, bf16[2,16,3584]{2,1,0:T(8,128)(2,1)S(1)}, u32[]{:S(2)}, u32[]{:S(2)}) collective-permute-start(bf16[2,16,3584]{2,1,0:T(8,128)(2,1)S(1)} %get-tuple-element.117), channel_id=1, source_target_pairs={{0,4},{2,6},{4,0},{6,2},{8,12},{10,14},{12,8},{14,10},{1,5},{3,7},... | collective-permute-start | bytes 688136 | tf_op jit(solution)/shard_map/ppermute | solution.py:56
  67.5 11.7 %collective-permute-start.23 = (bf16[2,16,3584]{2,1,0:T(8,128)(2,1)S(1)}, bf16[2,16,3584]{2,1,0:T(8,128)(2,1)S(1)}, u32[]{:S(2)}, u32[]{:S(2)}) collective-permute-start(bf16[2,16,3584]{2,1,0:T(8,128)(2,1)S(1)} %get-tuple-element.118), channel_id=1, source_target_pairs={{0,2},{2,0},{4,6},{6,4},{8,10},{10,8},{12,14},{14,12},{1,3},{3,1},... | collective-permute-start | bytes 688136 | tf_op jit(solution)/shard_map/ppermute | solution.py:56
  68.4 11.4 %collective-permute-start.24 = (bf16[2,16,3584]{2,1,0:T(8,128)(2,1)S(1)}, bf16[2,16,3584]{2,1,0:T(8,128)(2,1)S(1)}, u32[]{:S(2)}, u32[]{:S(2)}) collective-permute-start(bf16[2,16,3584]{2,1,0:T(8,128)(2,1)S(1)} %get-tuple-element.119), channel_id=1, source_target_pairs={{0,6},{2,4},{4,2},{6,0},{8,14},{10,12},{12,10},{14,8},{1,7},{3,5},... | collective-permute-start | bytes 688136 | tf_op jit(solution)/shard_map/ppermute | solution.py:56
  72.0 15.8 %collective-permute-start.18 = (bf16[2,16,3200]{2,1,0:T(8,128)(2,1)S(1)}, bf16[2,16,3200]{2,1,0:T(8,128)(2,1)S(1)}, u32[]{:S(2)}, u32[]{:S(2)}) collective-permute-start(bf16[2,16,3200]{2,1,0:T(8,128)(2,1)S(1)} %get-tuple-element.110), channel_id=1, source_target_pairs={{0,4},{2,6},{4,0},{6,2},{8,12},{10,14},{12,8},{14,10},{1,5},{3,7},... | collective-permute-start | bytes 614408 | tf_op jit(solution)/shard_map/ppermute | solution.py:56
  73.4 14.4 %collective-permute-start.19 = (bf16[2,16,3200]{2,1,0:T(8,128)(2,1)S(1)}, bf16[2,16,3200]{2,1,0:T(8,128)(2,1)S(1)}, u32[]{:S(2)}, u32[]{:S(2)}) collective-permute-start(bf16[2,16,3200]{2,1,0:T(8,128)(2,1)S(1)} %get-tuple-element.111), channel_id=1, source_target_pairs={{0,2},{2,0},{4,6},{6,4},{8,10},{10,8},{12,14},{14,12},{1,3},{3,1},... | collective-permute-start | bytes 614408 | tf_op jit(solution)/shard_map/ppermute | solution.py:56
  74.7 16.8 %collective-permute-start.20 = (bf16[2,16,3200]{2,1,0:T(8,128)(2,1)S(1)}, bf16[2,16,3200]{2,1,0:T(8,128)(2,1)S(1)}, u32[]{:S(2)}, u32[]{:S(2)}) collective-permute-start(bf16[2,16,3200]{2,1,0:T(8,128)(2,1)S(1)} %get-tuple-element.112), channel_id=1, source_target_pairs={{0,6},{2,4},{4,2},{6,0},{8,14},{10,12},{12,10},{14,8},{1,7},{3,5},... | collective-permute-start | bytes 614408 | tf_op jit(solution)/shard_map/ppermute | solution.py:56
  80.3 14.0 %collective-permute-start.25 = (bf16[2,16,3584]{2,1,0:T(8,128)(2,1)S(1)}, bf16[2,16,3584]{2,1,0:T(8,128)(2,1)S(1)}, u32[]{:S(2)}, u32[]{:S(2)}) collective-permute-start(bf16[2,16,3584]{2,1,0:T(8,128)(2,1)S(1)} %get-tuple-element.122), channel_id=1, source_target_pairs={{0,8},{2,10},{4,12},{6,14},{8,0},{10,2},{12,4},{14,6},{1,9},{3,11}... | collective-permute-start | bytes 688136 | tf_op jit(solution)/shard_map/ppermute | solution.py:56
  91.8 9.1 %collective-permute-start.21 = (bf16[2,16,3200]{2,1,0:T(8,128)(2,1)S(1)}, bf16[2,16,3200]{2,1,0:T(8,128)(2,1)S(1)}, u32[]{:S(2)}, u32[]{:S(2)}) collective-permute-start(bf16[2,16,3200]{2,1,0:T(8,128)(2,1)S(1)} %get-tuple-element.115), channel_id=1, source_target_pairs={{0,8},{2,10},{4,12},{6,14},{8,0},{10,2},{12,4},{14,6},{1,9},{3,11}... | collective-permute-start | bytes 614408 | tf_op jit(solution)/shard_map/ppermute | solution.py:56
  94.6 8.2 %collective-permute-start.31 = (bf16[16,3456]{1,0:T(8,128)(2,1)S(1)}, bf16[16,3456]{1,0:T(8,128)(2,1)S(1)}, u32[]{:S(2)}, u32[]{:S(2)}) collective-permute-start(bf16[16,3456]{1,0:T(8,128)(2,1)S(1)} %get-tuple-element.125.refs_0_), channel_id=1, source_target_pairs={{0,6},{2,4},{4,2},{6,0},{8,14},{10,12},{12,10},{14,8},{1,7},{3,5},... | collective-permute-start | bytes 331784 | tf_op jit(solution)/shard_map/ppermute | solution.py:56
  96.0 8.7 %collective-permute-start.30 = (bf16[16,3456]{1,0:T(8,128)(2,1)S(1)}, bf16[16,3456]{1,0:T(8,128)(2,1)S(1)}, u32[]{:S(2)}, u32[]{:S(2)}) collective-permute-start(bf16[16,3456]{1,0:T(8,128)(2,1)S(1)} %get-tuple-element.125.refs_0_), channel_id=1, source_target_pairs={{0,2},{2,0},{4,6},{6,4},{8,10},{10,8},{12,14},{14,12},{1,3},{3,1},... | collective-permute-start | bytes 331784 | tf_op jit(solution)/shard_map/ppermute | solution.py:56
  96.0 8.7 %collective-permute-start.29 = (bf16[16,3456]{1,0:T(8,128)(2,1)S(1)}, bf16[16,3456]{1,0:T(8,128)(2,1)S(1)}, u32[]{:S(2)}, u32[]{:S(2)}) collective-permute-start(bf16[16,3456]{1,0:T(8,128)(2,1)S(1)} %get-tuple-element.125.refs_0_), channel_id=1, source_target_pairs={{0,4},{2,6},{4,0},{6,2},{8,12},{10,14},{12,8},{14,10},{1,5},{3,7},... | collective-permute-start | bytes 331784 | tf_op jit(solution)/shard_map/ppermute | solution.py:56
  101.1 6.4 %collective-permute-start.28 = (bf16[16,3200]{1,0:T(8,128)(2,1)S(1)}, bf16[16,3200]{1,0:T(8,128)(2,1)S(1)}, u32[]{:S(2)}, u32[]{:S(2)}) collective-permute-start(bf16[16,3200]{1,0:T(8,128)(2,1)S(1)} %hidden.7.refs_0_), channel_id=1, source_target_pairs={{0,6},{2,4},{4,2},{6,0},{8,14},{10,12},{12,10},{14,8},{1,7},{3,5},... | collective-permute-start | bytes 307208 | tf_op jit(solution)/shard_map/ppermute | solution.py:56
  101.4 6.1 %collective-permute-start.27 = (bf16[16,3200]{1,0:T(8,128)(2,1)S(1)}, bf16[16,3200]{1,0:T(8,128)(2,1)S(1)}, u32[]{:S(2)}, u32[]{:S(2)}) collective-permute-start(bf16[16,3200]{1,0:T(8,128)(2,1)S(1)} %hidden.7.refs_0_), channel_id=1, source_target_pairs={{0,2},{2,0},{4,6},{6,4},{8,10},{10,8},{12,14},{14,12},{1,3},{3,1},... | collective-permute-start | bytes 307208 | tf_op jit(solution)/shard_map/ppermute | solution.py:56
  102.9 5.7 %collective-permute-start.26 = (bf16[16,3200]{1,0:T(8,128)(2,1)S(1)}, bf16[16,3200]{1,0:T(8,128)(2,1)S(1)}, u32[]{:S(2)}, u32[]{:S(2)}) collective-permute-start(bf16[16,3200]{1,0:T(8,128)(2,1)S(1)} %hidden.7.refs_0_), channel_id=1, source_target_pairs={{0,4},{2,6},{4,0},{6,2},{8,12},{10,14},{12,8},{14,10},{1,5},{3,7},... | collective-permute-start | bytes 307208 | tf_op jit(solution)/shard_map/ppermute | solution.py:56
  109.9 1.4 %collective-permute-start.32 = (bf16[64,1024]{1,0:T(8,128)(2,1)S(1)}, bf16[64,1024]{1,0:T(8,128)(2,1)S(1)}, u32[]{:S(2)}, u32[]{:S(2)}) collective-permute-start(bf16[64,1024]{1,0:T(8,128)(2,1)S(1)} %get-tuple-element.127), channel_id=1, source_target_pairs={{0,1},{1,0},{2,3},{3,2},{4,5},{5,4},{6,7},{7,6},{8,9},{9,8},{10,11... | collective-permute-start | bytes 393224 | tf_op jit(solution)/shard_map/ppermute | solution.py:56
  111.9 4.3 %collective-permute-start.33 = (bf16[32,1024]{1,0:T(8,128)(2,1)S(1)}, bf16[32,1024]{1,0:T(8,128)(2,1)S(1)}, u32[]{:S(2)}, u32[]{:S(2)}) collective-permute-start(bf16[32,1024]{1,0:T(8,128)(2,1)S(1)} %get-tuple-element.130), channel_id=1, source_target_pairs={{16,0},{0,16},{17,1},{1,17},{18,2},{2,18},{19,3},{3,19},{20,4},{4,... | collective-permute-start | bytes 196616 | tf_op jit(solution)/shard_map/ppermute | solution.py:476
